TPU v7x, 512 devices: a whole 4x4x16 slice. The times are simulated.
512 devices in a mesh: fsdp: 8 (over x, core), ctx: 64 (over z, y).
Axes of the slice: x: 4, y: 4, z: 16, core: 2. Of those that a mesh axis runs over, the one named last changes fastest.
Arguments:
- tokens: bfloat16 [8, 8192, 4096], P('fsdp', 'ctx'), may hold values from -64 to 64
- doc_start: int32 [8, 8192], P('fsdp', 'ctx'), may hold values from 0 to 8191, as said below
- out_grad: bfloat16 [8, 8192, 1024], P('fsdp', 'ctx'), may hold values from -6 to 6
- w_qkv: bfloat16 [4096, 1280], P(('fsdp', 'ctx')), may hold values from -1 to 1
Outputs:
- grad_tokens: bfloat16 [8, 8192, 4096], P('fsdp', 'ctx')
Inputs may be any that keep to these rules, and one draw needn't show every extreme that they name: Documents are runs of consecutive tokens of 1 to 385 tokens; doc_start gives each token the position in its sequence of its document's first token, and every sequence holds a document of exactly 385 tokens.
All inputs are finite; a program needn't handle non-finite values.
Results may differ from a plain program's by a relative error of at most 0.04.
Values may be sent and summed in bfloat16 or wider, within the bound.
No kernel may reach another device: no remote copies, remote signals or barrier semaphores. Data moves between devices by JAX's collectives and lax.ppermute only.
A program may use at most 64 MiB of HBM per device.

v0:
```python
import math

import jax
import jax.numpy as jnp
from jax import lax
from jax.sharding import PartitionSpec as P

HQ = 8
HD = 128
REACH = 4


ROPE_BASE = 500000.0
MASKED = -1e30


def shifted(block, axis, distance):
    devices = range(lax.axis_size(axis))
    route = [(i - distance, i) for i in devices if i - distance in devices]
    return lax.ppermute(block, axis, route)


def angles_for(positions, head_size):
    half_size = head_size // 2
    inverse = jnp.power(
        jnp.float32(ROPE_BASE), -jnp.arange(half_size, dtype=jnp.float32) / half_size
    )
    phase_angle = positions.astype(jnp.float32)[:, None] * inverse[None, :]
    return (jnp.cos(phase_angle), jnp.sin(phase_angle))


def rotate(vectors, cos_part, sin_part):
    half_size = vectors.shape[-1] // 2
    first_half = vectors[..., :half_size]
    second_half = vectors[..., half_size:]
    return jnp.concatenate(
        [
            first_half * cos_part - second_half * sin_part,
            second_half * cos_part + first_half * sin_part,
        ],
        axis=-1,
    )


def unrotate(vectors, cos_part, sin_part):
    half_size = vectors.shape[-1] // 2
    first_half = vectors[..., :half_size]
    second_half = vectors[..., half_size:]
    return jnp.concatenate(
        [
            first_half * cos_part + second_half * sin_part,
            second_half * cos_part - first_half * sin_part,
        ],
        axis=-1,
    )


def allowed_pairs(query_index, begin_rows, key_start, row_count):
    key_index = key_start + jnp.arange(row_count, dtype=jnp.int32)
    return (key_index[None, :] <= query_index[:, None]) & (
        key_index[None, :] >= begin_rows[:, None]
    )


def forward_block(running, query_block, pair_block, allowed, score_scale):
    top_run, total_run, weighted = running
    key_block = pair_block[:, :HD]
    value_block = pair_block[:, HD:]
    scores = (
        jnp.einsum("qhd,kd->hqk", query_block, key_block, preferred_element_type=jnp.float32)
        * score_scale
    )
    scores = jnp.where(allowed[None], scores, MASKED)
    top_new = jnp.maximum(top_run, jnp.max(scores, axis=-1))
    factor = jnp.exp(top_run - top_new)
    unnormed = jnp.where(allowed[None], jnp.exp(scores - top_new[..., None]), 0.0)
    total_new = total_run * factor + jnp.sum(unnormed, axis=-1)
    weighted = weighted * factor[..., None] + jnp.einsum(
        "hqk,kd->hqd", unnormed, value_block.astype(jnp.float32)
    )
    return (top_new, total_new, weighted)


def backward_block(query_block, pair_block, allowed, log_total, grad_block, row_delta, score_scale):
    key_block = pair_block[:, :HD]
    value_block = pair_block[:, HD:]
    scores = (
        jnp.einsum("qhd,kd->hqk", query_block, key_block, preferred_element_type=jnp.float32)
        * score_scale
    )
    probs = jnp.where(allowed[None], jnp.exp(scores - log_total[..., None]), 0.0)
    probs_low = probs.astype(jnp.bfloat16)
    grad_value = jnp.einsum(
        "hqk,qhd->kd", probs_low, grad_block, preferred_element_type=jnp.float32
    )
    grad_probs = jnp.einsum(
        "qhd,kd->hqk", grad_block, value_block, preferred_element_type=jnp.float32
    )
    grad_scores = (probs * (grad_probs - row_delta[..., None])).astype(jnp.bfloat16)
    grad_query = (
        jnp.einsum("hqk,kd->qhd", grad_scores, key_block, preferred_element_type=jnp.float32)
        * score_scale
    )
    grad_key = (
        jnp.einsum("hqk,qhd->kd", grad_scores, query_block, preferred_element_type=jnp.float32)
        * score_scale
    )
    return (grad_query, jnp.concatenate([grad_key, grad_value], axis=1))


def local(tokens, doc_start, out_grad, w_qkv):
    row_count = tokens.shape[1]
    score_scale = 1.0 / math.sqrt(HD)
    panel_all = lax.all_gather(w_qkv, ("fsdp", "ctx"), axis=0, tiled=True)
    features = tokens[0]
    begin_rows = doc_start[0]
    grad_rows = out_grad[0].reshape(row_count, HQ, HD)
    first_row = lax.axis_index("ctx") * row_count
    query_index = first_row + jnp.arange(row_count, dtype=jnp.int32)
    projected = jnp.dot(features, panel_all, preferred_element_type=jnp.float32)
    cos_part, sin_part = angles_for(query_index - begin_rows, HD)
    queries = rotate(
        projected[:, : HQ * HD].reshape(row_count, HQ, HD),
        cos_part[:, None, :],
        sin_part[:, None, :],
    ).astype(jnp.bfloat16)
    own_keys = rotate(projected[:, HQ * HD : HQ * HD + HD], cos_part, sin_part)
    pair_rows = jnp.concatenate([own_keys, projected[:, HQ * HD + HD :]], axis=1).astype(
        jnp.bfloat16
    )
    pair_blocks = [pair_rows]
    moving = pair_rows
    for distance in range(1, REACH):
        moving = shifted(moving, "ctx", 1)
        pair_blocks.append(moving)
    pair_masks = [
        allowed_pairs(query_index, begin_rows, first_row - distance * row_count, row_count)
        for distance in range(REACH)
    ]
    running = (
        jnp.full((HQ, row_count), MASKED, jnp.float32),
        jnp.zeros((HQ, row_count), jnp.float32),
        jnp.zeros((HQ, row_count, HD), jnp.float32),
    )
    for distance in range(REACH):
        pair_block = pair_blocks[distance]
        allowed = pair_masks[distance]
        running = forward_block(running, queries, pair_block, allowed, score_scale)
    top_run, total_run, weighted = running
    log_total = top_run + jnp.log(total_run)
    attn_out = lax.optimization_barrier(
        jnp.transpose(weighted / total_run[..., None], (1, 0, 2)).astype(jnp.bfloat16)
    )
    row_delta = jnp.sum(grad_rows.astype(jnp.float32) * attn_out.astype(jnp.float32), axis=-1).T
    grad_query = jnp.zeros((row_count, HQ, HD), jnp.float32)
    pair_grads = []
    for distance in range(REACH):
        pair_block = pair_blocks[distance]
        allowed = pair_masks[distance]
        step_query, step_pairs = backward_block(
            queries, pair_block, allowed, log_total, grad_rows, row_delta, score_scale
        )
        grad_query = grad_query + step_query
        pair_grads.append(step_pairs)
    pair_total = pair_grads[REACH - 1]
    for distance in range(REACH - 2, -1, -1):
        pair_total = shifted(pair_total, "ctx", -1) + pair_grads[distance]
    grad_q_pre = unrotate(grad_query, cos_part[:, None, :], sin_part[:, None, :]).reshape(
        row_count, HQ * HD
    )
    grad_k_pre = unrotate(pair_total[:, :HD], cos_part, sin_part)
    all_grads = jnp.concatenate(
        [
            grad_q_pre.astype(jnp.bfloat16),
            grad_k_pre.astype(jnp.bfloat16),
            pair_total[:, HD:].astype(jnp.bfloat16),
        ],
        axis=1,
    )
    result = lax.dot_general(
        all_grads, panel_all, (((1,), (1,)), ((), ())), preferred_element_type=jnp.float32
    )
    return result.astype(jnp.bfloat16)[None]


def solution(mesh):
    placed = (
        P("fsdp", "ctx", None),
        P("fsdp", "ctx"),
        P("fsdp", "ctx", None),
        P(("fsdp", "ctx"), None),
    )
    return jax.shard_map(
        local, mesh=mesh, in_specs=placed, out_specs=P("fsdp", "ctx", None), check_vma=False
    )
```

profile of v0, /device:TPU:24, one launch (start us, length us, event | category | flops | bytes accessed | tf_op | source)
XLA Modules:
  0.0 315.8 jit_solution(14078913883701712490)
XLA Ops:
  6.5 0.7 all-gather.2.cloned.1.call-update
  7.3 1.1 copy.104
  8.4 0.9 copy.106
  9.3 0.7 subtract_convert_fusion.2
  9.9 1.4 compare_and_fusion.3
  11.3 218.7 %all-gather.2.cloned.1.call-done = bf16[4096,1280]{1,0:T(8,128)(2,1)} async-done(((bf16[8,1280]{1,0:T(8,128)(2,1)}), bf16[4096,1280]{1,0:T(8,128)(2,1)}) %all-gather.2.cloned.1.call-update) | async-done | bytes 10485776 | tf_op jit(solution)/shard_map/all_gather | solution.py:114
  230.1 5.5 %fusion.32 = f32[128,1280]{1,0:T(8,128)S(1)} fusion(bf16[4096,1280]{1,0:T(8,128)(2,1)} %all-gather.2.cloned.1.call-done, bf16[1,128,4096]{2,1,0:T(8,128)(2,1)S(1)} %copy-done), kind=kOutput, calls=%fused_computation.56 | convolution fusion | flops 1342177280 | bytes 12189696 | tf_op jit(solution)/shard_map/dot_general | solution.py:120
  237.0 3.4 %collective-permute-start = (bf16[128,256]{1,0:T(8,128)(2,1)S(1)}, bf16[128,256]{1,0:T(8,128)(2,1)S(1)}, u32[]{:S(2)}, u32[]{:S(2)}) collective-permute-start(bf16[128,256]{1,0:T(8,128)(2,1)S(1)} %pad_maximum_fusion.3), channel_id=1, source_target_pairs={{0,1},{1,2},{2,3},{3,4},{4,5},{5,6},{6,7},{7,8},{8,9},{9,10},{10,1... | collective-permute-start | bytes 196616 | tf_op jit(solution)/shard_map/ppermute | solution.py:20
  240.8 0.3 select_reduce_fusion.3
  241.0 2.1 collective-permute-done
  243.2 5.5 %collective-permute-start.1 = (bf16[128,256]{1,0:T(8,128)(2,1)S(1)}, bf16[128,256]{1,0:T(8,128)(2,1)S(1)}, u32[]{:S(2)}, u32[]{:S(2)}) collective-permute-start(bf16[128,256]{1,0:T(8,128)(2,1)S(1)} %collective-permute-done), channel_id=1, source_target_pairs={{0,1},{1,2},{2,3},{3,4},{4,5},{5,6},{6,7},{7,8},{8,9},{9,10},{10,1... | collective-permute-start | bytes 196616 | tf_op jit(solution)/shard_map/ppermute | solution.py:20
  248.9 1.6 collective-permute-done.1
  250.5 6.4 %collective-permute-start.2 = (bf16[128,256]{1,0:T(8,128)(2,1)S(1)}, bf16[128,256]{1,0:T(8,128)(2,1)S(1)}, u32[]{:S(2)}, u32[]{:S(2)}) collective-permute-start(bf16[128,256]{1,0:T(8,128)(2,1)S(1)} %collective-permute-done.1), channel_id=1, source_target_pairs={{0,1},{1,2},{2,3},{3,4},{4,5},{5,6},{6,7},{7,8},{8,9},{9,10},{10,1... | collective-permute-start | bytes 196616 | tf_op jit(solution)/shard_map/ppermute | solution.py:20
  257.0 1.0 select_reduce_fusion.1
  257.9 0.8 collective-permute-done.2
  258.8 1.0 select_reduce_fusion
  259.8 0.8 fusion.41
  260.6 0.8 fusion.40
  261.4 0.8 fusion.39
  262.5 1.0 convolution_bitcast_fusion.14
  263.5 0.5 fusion.10
  263.9 1.1 fusion.12
  265.0 1.1 fusion.14
  266.1 1.1 fusion.27
  267.2 1.2 multiply_reduce_fusion
  268.6 0.3 fusion.28
  268.9 0.3 fusion.99
  269.1 1.0 fusion.23
  270.1 0.3 fusion.31
  270.4 0.7 pad_maximum_fusion.2
  271.0 1.9 collective-permute-start.3
  273.2 0.9 fusion.30
  274.4 0.3 fusion.29
  274.7 0.3 convolution_add_fusion.2
  274.9 0.3 convolution_add_fusion.1
  275.2 0.3 fusion.22
  275.5 0.3 add_convert_fusion
  276.1 1.0 convolution_bitcast_fusion.12
  277.1 3.6 %collective-permute-done.3 = f32[128,256]{0,1:T(8,128)} collective-permute-done((f32[128,256]{0,1:T(8,128)}, f32[128,256]{0,1:T(8,128)}, u32[]{:S(2)}, u32[]{:S(2)}) %collective-permute-start.3) | collective-permute-done | bytes 131104 | tf_op jit(solution)/shard_map/ppermute | solution.py:20
  280.7 0.9 maximum_add_fusion
  281.6 1.9 collective-permute-start.4
  283.5 1.0 convolution_bitcast_fusion.10
  284.5 6.1 %collective-permute-done.4 = f32[128,256]{0,1:T(8,128)S(1)} collective-permute-done((f32[128,256]{0,1:T(8,128)S(1)}, f32[128,256]{0,1:T(8,128)S(1)}, u32[]{:S(2)}, u32[]{:S(2)}) %collective-permute-start.4) | collective-permute-done | bytes 131104 | tf_op jit(solution)/shard_map/ppermute | solution.py:20
  290.6 2.1 collective-permute-start.5
  292.7 0.9 convolution_bitcast_fusion.8
  293.6 5.9 %collective-permute-done.5 = f32[128,256]{0,1:T(8,128)S(1)} collective-permute-done((f32[128,256]{0,1:T(8,128)S(1)}, f32[128,256]{0,1:T(8,128)S(1)}, u32[]{:S(2)}, u32[]{:S(2)}) %collective-permute-start.5) | collective-permute-done | bytes 131104 | tf_op jit(solution)/shard_map/ppermute | solution.py:20
  299.6 0.8 fusion.94
  300.4 8.5 %fusion = bf16[1,128,4096]{2,1,0:T(8,128)(2,1)} fusion(bf16[4096,1280]{1,0:T(8,128)(2,1)} %all-gather.2.cloned.1.call-done, bf16[128,128]{0,1:T(8,128)(2,1)S(1)} %slice.133, bf16[128,64]{0,1:T(8,128)(2,1)S(1)} %get-tuple-element.20, bf16[128,64]{0,1:T(8,128)(2,1)S(1)} %get-tuple-element.19, bf16[128,1024]{0,1:T(8,128)(2,1)S(1)} %bitcast.251), kind=kOutput, calls=%fused_computation.1 | convolution fusion | flops 1344012288 | bytes 11862016 | tf_op jit(solution)/shard_map/dot_general | solution.py:180
  (62 shorter events, 3.2 us)
Async XLA Ops:
  6.5 223.5 %copy-start = (bf16[1,128,4096]{2,1,0:T(8,128)(2,1)S(1)}, bf16[1,128,4096]{2,1,0:T(8,128)(2,1)}, u32[]{:S(2)}) copy-start(bf16[1,128,4096]{2,1,0:T(8,128)(2,1)} %param.4) | copy-start | bytes 3145732
  6.5 223.5 %all-gather.2.cloned.1.call-start = ((), (), s32[]{:S(2)}) async-start(), calls=%async_computation | async-start | bytes 10506240 | tf_op jit(solution)/shard_map/all_gather | solution.py:114
  9.3 227.0 %copy-start.14 = (f32[64]{0:T(128)}, f32[64]{0:T(128)S(1)}, u32[]{:S(2)}) copy-start(f32[64]{0:T(128)S(1)} %multiply_power_fusion) | copy-start | bytes 772
  9.9 226.3 %copy-start.13 = (f32[128]{0:T(128)}, f32[128]{0:T(128)S(1)}, u32[]{:S(2)}) copy-start(f32[128]{0:T(128)S(1)} %get-tuple-element.40) | copy-start | bytes 1540
  11.3 237.3 %copy-start.1 = (pred[128,128]{0,1:T(8,128)(4,1)}, pred[128,128]{0,1:T(8,128)(4,1)S(1)}, u32[]{:S(2)}) copy-start(pred[128,128]{0,1:T(8,128)(4,1)S(1)} %get-tuple-element.29) | copy-start | bytes 49156
  236.4 20.5 %copy-start.9 = (bf16[128,64]{0,1:T(8,128)(2,1)}, bf16[128,64]{0,1:T(8,128)(2,1)S(1)}, u32[]{:S(2)}) copy-start(bf16[128,64]{0,1:T(8,128)(2,1)S(1)} %get-tuple-element.21) | copy-start | bytes 49156
  236.5 20.5 %copy-start.11 = (bf16[128,64]{0,1:T(8,128)(2,1)}, bf16[128,64]{0,1:T(8,128)(2,1)S(1)}, u32[]{:S(2)}) copy-start(bf16[128,64]{0,1:T(8,128)(2,1)S(1)} %get-tuple-element.22) | copy-start | bytes 49156
  236.6 20.4 %copy-start.4 = (f32[128,64]{1,0:T(8,128)}, f32[128,64]{1,0:T(8,128)S(1)}, u32[]{:S(2)}) copy-start(f32[128,64]{1,0:T(8,128)S(1)} %copy.100) | copy-start | bytes 98308
  236.7 20.3 %copy-start.6 = (f32[128,64]{1,0:T(8,128)}, f32[128,64]{1,0:T(8,128)S(1)}, u32[]{:S(2)}) copy-start(f32[128,64]{1,0:T(8,128)S(1)} %copy.98) | copy-start | bytes 98308
  237.0 6.2 %collective-permute-start = (bf16[128,256]{1,0:T(8,128)(2,1)S(1)}, bf16[128,256]{1,0:T(8,128)(2,1)S(1)}, u32[]{:S(2)}, u32[]{:S(2)}) collective-permute-start(bf16[128,256]{1,0:T(8,128)(2,1)S(1)} %pad_maximum_fusion.3), channel_id=1, source_target_pairs={{0,1},{1,2},{2,3},{3,4},{4,5},{5,6},{6,7},{7,8},{8,9},{9,10},{10,1... | collective-permute-start | bytes 196616 | tf_op jit(solution)/shard_map/ppermute | solution.py:20
  240.4 32.6 %copy-start.3 = (pred[128,128]{0,1:T(8,128)(4,1)S(1)}, pred[128,128]{0,1:T(8,128)(4,1)}, u32[]{:S(2)}) copy-start(pred[128,128]{0,1:T(8,128)(4,1)} %get-tuple-element.27) | copy-start | bytes 49156
  243.2 7.3 %collective-permute-start.1 = (bf16[128,256]{1,0:T(8,128)(2,1)S(1)}, bf16[128,256]{1,0:T(8,128)(2,1)S(1)}, u32[]{:S(2)}, u32[]{:S(2)}) collective-permute-start(bf16[128,256]{1,0:T(8,128)(2,1)S(1)} %collective-permute-done), channel_id=1, source_target_pairs={{0,1},{1,2},{2,3},{3,4},{4,5},{5,6},{6,7},{7,8},{8,9},{9,10},{10,1... | collective-permute-start | bytes 196616 | tf_op jit(solution)/shard_map/ppermute | solution.py:20
  248.9 25.2 %copy-start.2 = (pred[128,128]{0,1:T(8,128)(4,1)S(1)}, pred[128,128]{0,1:T(8,128)(4,1)}, u32[]{:S(2)}) copy-start(pred[128,128]{0,1:T(8,128)(4,1)} %copy-done.1) | copy-start | bytes 49156
  250.5 8.3 %collective-permute-start.2 = (bf16[128,256]{1,0:T(8,128)(2,1)S(1)}, bf16[128,256]{1,0:T(8,128)(2,1)S(1)}, u32[]{:S(2)}, u32[]{:S(2)}) collective-permute-start(bf16[128,256]{1,0:T(8,128)(2,1)S(1)} %collective-permute-done.1), channel_id=1, source_target_pairs={{0,1},{1,2},{2,3},{3,4},{4,5},{5,6},{6,7},{7,8},{8,9},{9,10},{10,1... | collective-permute-start | bytes 196616 | tf_op jit(solution)/shard_map/ppermute | solution.py:20
  256.9 11.9 %copy-start.10 = (bf16[128,64]{0,1:T(8,128)(2,1)S(1)}, bf16[128,64]{0,1:T(8,128)(2,1)}, u32[]{:S(2)}) copy-start(bf16[128,64]{0,1:T(8,128)(2,1)} %copy-done.9) | copy-start | bytes 49156
  256.9 11.9 %copy-start.12 = (bf16[128,64]{0,1:T(8,128)(2,1)S(1)}, bf16[128,64]{0,1:T(8,128)(2,1)}, u32[]{:S(2)}) copy-start(bf16[128,64]{0,1:T(8,128)(2,1)} %copy-done.11) | copy-start | bytes 49156
  262.3 13.2 %copy-start.5 = (f32[128,64]{1,0:T(8,128)S(1)}, f32[128,64]{1,0:T(8,128)}, u32[]{:S(2)}) copy-start(f32[128,64]{1,0:T(8,128)} %copy-done.4) | copy-start | bytes 98308
  262.3 13.2 %copy-start.7 = (f32[128,64]{1,0:T(8,128)S(1)}, f32[128,64]{1,0:T(8,128)}, u32[]{:S(2)}) copy-start(f32[128,64]{1,0:T(8,128)} %copy-done.6) | copy-start | bytes 98308
  262.5 11.9 %copy-start.8 = (f32[8,128]{1,0:T(8,128)}, f32[8,128]{1,0:T(8,128)S(1)}, u32[]{:S(2)}) copy-start(f32[8,128]{1,0:T(8,128)S(1)} %log_add_fusion) | copy-start | bytes 12292
  271.0 9.6 %collective-permute-start.3 = (f32[128,256]{0,1:T(8,128)}, f32[128,256]{0,1:T(8,128)}, u32[]{:S(2)}, u32[]{:S(2)}) collective-permute-start(f32[128,256]{0,1:T(8,128)} %pad_maximum_fusion.2), channel_id=1, source_target_pairs={{1,0},{2,1},{3,2},{4,3},{5,4},{6,5},{7,6},{8,7},{9,8},{10,9},{11,1... | collective-permute-start | bytes 393224 | tf_op jit(solution)/shard_map/ppermute | solution.py:20
  281.6 9.0 %collective-permute-start.4 = (f32[128,256]{0,1:T(8,128)S(1)}, f32[128,256]{0,1:T(8,128)S(1)}, u32[]{:S(2)}, u32[]{:S(2)}) collective-permute-start(f32[128,256]{0,1:T(8,128)S(1)} %maximum_add_fusion), channel_id=1, source_target_pairs={{1,0},{2,1},{3,2},{4,3},{5,4},{6,5},{7,6},{8,7},{9,8},{10,9},{11,1... | collective-permute-start | bytes 393224 | tf_op jit(solution)/shard_map/ppermute | solution.py:20
  290.6 9.0 %collective-permute-start.5 = (f32[128,256]{0,1:T(8,128)S(1)}, f32[128,256]{0,1:T(8,128)S(1)}, u32[]{:S(2)}, u32[]{:S(2)}) collective-permute-start(f32[128,256]{0,1:T(8,128)S(1)} %maximum_add_fusion.1), channel_id=1, source_target_pairs={{1,0},{2,1},{3,2},{4,3},{5,4},{6,5},{7,6},{8,7},{9,8},{10,9},{11,1... | collective-permute-start | bytes 393224 | tf_op jit(solution)/shard_map/ppermute | solution.py:20
Sparse Core Ops, SparseCore 0:
  12.0 218.0 all-gather.1
where the time goes:
time: 321 us; the launch traced here: 316 us
  waiting for transfers between devices  240 us (75%)
  matrix products  28.4 us (9%)
  starting transfers between devices  21.1 us (7%)
  between operations  14 us (4%)
  other arithmetic  9.45 us (3%)
  local copies, waits for them, and re-layouts  3.22 us (1%)
    all_gather x1, waiting for transfers between devices, local(): panel_all = lax.all_gather(w_qkv, ('fsdp', 'ctx'), axis=0, tiled=True)  219 us
    ppermute x6, starting transfers between devices, shifted(): return lax.ppermute(block, axis, route)  21.1 us
    ppermute x6, waiting for transfers between devices, shifted(): return lax.ppermute(block, axis, route)  20.2 us
    dot_general x1, matrix products, local(): lax.dot_general(all_grads, panel_all, (((1,), (1,)), ((), ())), preferred...  8.49 us
  transfers between devices with their start and end apart: 7, of which 7 were waited for; matrix products, arithmetic and copies ran while one was open for 4% of the time, Pallas kernels for 0%

commit v1 on v0

v1 whole, which is shorter than its diff:
```python
import math

import jax
import jax.numpy as jnp
from jax import lax
from jax.sharding import PartitionSpec as P

HQ = 8
HD = 128
REACH = 4
ROPE_BASE = 500000.0
MASKED = -1e30
NX, NC, NZ, NY = 4, 2, 16, 4
ALL = ("fsdp", "ctx")


def place(x, c, z, y):
    return (x * NC + c) * (NZ * NY) + z * NY + y


def route(move):
    return [
        (place(x, c, z, y), place(*move(x, c, z, y)))
        for x in range(NX)
        for c in range(NC)
        for z in range(NZ)
        for y in range(NY)
    ]


def hop(block, distance, x_core):
    def move(x, c, z, y):
        if c == x_core:
            return (x + distance) % NX, c, z, y
        return x, c, z, (y + distance) % NY

    return lax.ppermute(block, ALL, route(move))


def swap_cores(block):
    return lax.ppermute(block, ALL, route(lambda x, c, z, y: (x, 1 - c, z, y)))


def shifted(block, axis, distance):
    devices = range(lax.axis_size(axis))
    return lax.ppermute(block, axis, [(i - distance, i) for i in devices if i - distance in devices])


def angles_for(positions, head_size):
    half_size = head_size // 2
    inverse = jnp.power(
        jnp.float32(ROPE_BASE), -jnp.arange(half_size, dtype=jnp.float32) / half_size
    )
    phase_angle = positions.astype(jnp.float32)[:, None] * inverse[None, :]
    return (jnp.cos(phase_angle), jnp.sin(phase_angle))


def rotate(vectors, cos_part, sin_part):
    half_size = vectors.shape[-1] // 2
    a = vectors[..., :half_size]
    b = vectors[..., half_size:]
    return jnp.concatenate([a * cos_part - b * sin_part, b * cos_part + a * sin_part], axis=-1)


def local(tokens, doc_start, out_grad, w_qkv):
    row_count = tokens.shape[1]
    score_scale = 1.0 / math.sqrt(HD)
    features = tokens[0]
    begin_rows = doc_start[0]
    grad_rows = out_grad[0].reshape(row_count, HQ, HD)
    fsdp, ctx = lax.axis_index("fsdp"), lax.axis_index("ctx")
    x_me, core = fsdp // NC, fsdp % NC
    y_me = ctx % NY

    column = lax.all_gather(
        w_qkv, "ctx", axis=0, tiled=True,
        axis_index_groups=[[z * NY + y for z in range(NZ)] for y in range(NY)],
    )
    second, first, third = (hop(column, d, 0) for d in (2, 1, 3))
    plane = jnp.concatenate([column, first, second, third], axis=0)

    def spread(part):
        two, one, three = (hop(part, d, 1) for d in (2, 1, 3))
        mine = [part, one, two, three]
        return mine + [swap_cores(piece) for piece in mine]

    pair_w = spread(plane[:, HQ * HD :])
    query_w = spread(plane[:, : HQ * HD])

    block = NZ * NY * 8
    slot = lax.broadcasted_iota(jnp.int32, (block, block), 1)
    source = lax.broadcasted_iota(jnp.int32, (block, block), 0)
    wanted = slot // 8 % NZ * (NY * 8) + (y_me - slot // (NZ * 8) + NY) % NY * 8 + slot % 8
    order = (source == wanted).astype(jnp.bfloat16)

    def taken(shift, c):
        at = ((x_me - shift + NX) % NX * NC + c) * block
        return jnp.dot(
            lax.dynamic_slice_in_dim(features, at, block, 1), order,
            preferred_element_type=jnp.float32,
        ).astype(jnp.bfloat16)

    by_x = [taken(s, 0) for s in range(NX)]
    span = NZ * 8
    order0 = [
        jnp.concatenate([by_x[d][:, e * span : (e + 1) * span] for d in range(NX)], axis=1)
        for e in range(NY)
    ]
    order1 = [taken(e, 1) for e in range(NX)]
    own = [jnp.where(core == 0, a, b) for a, b in zip(order0, order1)]
    other = [jnp.where(core == 0, b, a) for a, b in zip(order0, order1)]
    features_in = own + other

    def project(weights):
        total = 0.0
        for part, w in zip(features_in, weights):
            total = total + jnp.dot(part, w, preferred_element_type=jnp.float32)
        return total

    first_row = ctx * row_count
    query_index = first_row + jnp.arange(row_count, dtype=jnp.int32)
    cos_part, sin_part = angles_for(query_index - begin_rows, HD)
    pair_pre = project(pair_w)
    pair_rows = jnp.concatenate(
        [rotate(pair_pre[:, :HD], cos_part, sin_part), pair_pre[:, HD:]], axis=1
    ).astype(jnp.bfloat16)
    near = jnp.concatenate([shifted(pair_rows, "ctx", 1), pair_rows], axis=0)
    window = jnp.concatenate([shifted(near, "ctx", 2), near], axis=0)

    queries = rotate(
        project(query_w).reshape(row_count, HQ, HD), cos_part[:, None, :], sin_part[:, None, :]
    ).astype(jnp.bfloat16)
    keys, values = window[:, :HD], window[:, HD:]
    key_index = first_row - (REACH - 1) * row_count + jnp.arange(REACH * row_count, dtype=jnp.int32)
    allowed = (key_index[None, :] <= query_index[:, None]) & (
        key_index[None, :] >= begin_rows[:, None]
    )
    scores = (
        jnp.einsum("qhd,kd->hqk", queries, keys, preferred_element_type=jnp.float32) * score_scale
    )
    scores = jnp.where(allowed[None], scores, MASKED)
    top = jnp.max(scores, axis=-1, keepdims=True)
    unnormed = jnp.where(allowed[None], jnp.exp(scores - top), 0.0)
    probs = unnormed / jnp.sum(unnormed, axis=-1, keepdims=True)
    probs_low = probs.astype(jnp.bfloat16)
    grad_probs = jnp.einsum("qhd,kd->hqk", grad_rows, values, preferred_element_type=jnp.float32)
    attn_out = jnp.einsum(
        "hqk,kd->hqd", probs_low, values, preferred_element_type=jnp.float32
    ).astype(jnp.bfloat16)
    row_delta = jnp.sum(
        jnp.transpose(grad_rows, (1, 0, 2)).astype(jnp.float32) * attn_out.astype(jnp.float32),
        axis=-1, keepdims=True,
    )
    grad_value = jnp.einsum("hqk,qhd->kd", probs_low, grad_rows, preferred_element_type=jnp.float32)
    grad_scores = (probs * (grad_probs - row_delta)).astype(jnp.bfloat16)
    grad_query = (
        jnp.einsum("hqk,kd->qhd", grad_scores, keys, preferred_element_type=jnp.float32)
        * score_scale
    )
    grad_key = (
        jnp.einsum("hqk,qhd->kd", grad_scores, queries, preferred_element_type=jnp.float32)
        * score_scale
    )
    pair_grad = jnp.concatenate([grad_key, grad_value], axis=1)
    far, near = pair_grad[: 2 * row_count], pair_grad[2 * row_count :]
    near = near + shifted(far, "ctx", -2)
    pair_total = near[row_count:] + shifted(near[:row_count], "ctx", -1)

    query_out = rotate(grad_query, cos_part[:, None, :], -sin_part[:, None, :]).reshape(
        row_count, HQ * HD
    ).astype(jnp.bfloat16)
    pair_out = jnp.concatenate(
        [rotate(pair_total[:, :HD], cos_part, -sin_part), pair_total[:, HD:]], axis=1
    ).astype(jnp.bfloat16)

    turn = (((1,), (1,)), ((), ()))
    arrived = [
        (
            lax.dot_general(query_out, wq, turn, preferred_element_type=jnp.float32)
            + lax.dot_general(pair_out, wp, turn, preferred_element_type=jnp.float32)
        ).astype(jnp.bfloat16)
        for wq, wp in zip(query_w, pair_w)
    ]
    own, other = arrived[:NX], arrived[NX:]
    order0 = [jnp.where(core == 0, a, b) for a, b in zip(own, other)]
    order1 = [jnp.where(core == 0, b, a) for a, b in zip(own, other)]
    by_x = [
        jnp.concatenate([order0[e][:, d * span : (d + 1) * span] for e in range(NY)], axis=1)
        for d in range(NX)
    ]
    result = jnp.zeros(features.shape, jnp.bfloat16)
    for s in range(NX):
        for c, part in ((0, by_x[s]), (1, order1[s])):
            at = ((x_me - s + NX) % NX * NC + c) * block
            back = lax.dot_general(part, order, turn, preferred_element_type=jnp.float32)
            result = lax.dynamic_update_slice_in_dim(result, back.astype(jnp.bfloat16), at, 1)
    return result[None]


def solution(mesh):
    placed = (
        P("fsdp", "ctx", None),
        P("fsdp", "ctx"),
        P("fsdp", "ctx", None),
        P(("fsdp", "ctx"), None),
    )
    return jax.shard_map(
        local, mesh=mesh, in_specs=placed, out_specs=P("fsdp", "ctx", None), check_vma=False
    )
```

time: 321 us -> 188 us (0.59); the launches traced: 316 us -> 186 us
  waiting for transfers between devices: 240 us -> 44.3 us
  blocking collectives: 0 us -> 37.6 us
  starting transfers between devices: 21.1 us -> 56.1 us
  between operations: 14 us -> 1.78 us
  local copies, waits for them, and re-layouts: 3.22 us -> 14.2 us
    all_gather x1 -> x0, waiting for transfers between devices: 219 us -> none  [local(): panel_all = lax.all_gather(w_qkv, ('fsdp', 'ctx'), axis=0, tiled=True)]
    all_gather x0 -> x1, blocking collectives: none -> 37.6 us  [local(): lax.all_gather(w_qkv, 'ctx', axis=0, tiled=True, axis_index_groups=[[z *...]
    ppermute x6 -> x21, starting transfers between devices: 21.1 us -> 56.1 us  [the longest x9 31.1 us: hop(): return lax.ppermute(block, ALL, route(move))]
    ppermute x6 -> x21, waiting for transfers between devices: 20.2 us -> 44.3 us  [the longest x4 24.4 us: shifted(): lax.ppermute(block, axis, [(i - distance, i) for i in devices if i - dist...]
    unnamed x35 -> x121, local copies, waits for them, and re-layouts: 1.48 us -> 8.42 us
    dot_general x26 -> x53, matrix products: 28.4 us -> 23.3 us  [the longest x16 6.87 us: project(): total = total + jnp.dot(part, w, preferred_element_type=jnp.float32)]
    slice x4 -> x14, local copies, waits for them, and re-layouts: 0.3 us -> 4.47 us  [the longest x4 2.64 us: local(): by_x[d][:, e * span:(e + 1) * span]]
    reduce_sum x5 -> x0, other arithmetic: 3.8 us -> none  [the longest x4 2.64 us: forward_block(): total_new = total_run * factor + jnp.sum(unnormed, axis=-1)]
  transfers between devices with their start and end apart: 7 -> 21, of which waited for: 7 -> 6; matrix products, arithmetic and copies ran while one was open for 4% -> 10% of each run, Pallas kernels for 0% -> 0%
where the time goes in v1:
time: 188 us; the launch traced here: 186 us
  starting transfers between devices  56.1 us (30%)
  waiting for transfers between devices  44.3 us (24%)
  blocking collectives  37.6 us (20%)
  matrix products  25.6 us (14%)
  local copies, waits for them, and re-layouts  14.2 us (8%)
  other arithmetic  6.73 us (4%)
    all_gather x1, blocking collectives, local(): lax.all_gather(w_qkv, 'ctx', axis=0, tiled=True, axis_index_groups=[[z *...  37.6 us
    ppermute x9, starting transfers between devices, hop(): return lax.ppermute(block, ALL, route(move))  31.1 us
    ppermute x4, waiting for transfers between devices, shifted(): lax.ppermute(block, axis, [(i - distance, i) for i in devices if i - dist...  24.4 us
    ppermute x9, waiting for transfers between devices, hop(): return lax.ppermute(block, ALL, route(move))  18.6 us
    ppermute x8, starting transfers between devices, swap_cores(): return lax.ppermute(block, ALL, route(lambda x, c, z, y: (x, 1 - c, z, y)))  16.4 us
    ppermute x4, starting transfers between devices, shifted(): lax.ppermute(block, axis, [(i - distance, i) for i in devices if i - dist...  8.52 us
    unnamed x121, local copies, waits for them, and re-layouts  8.42 us
    dot_general x16, matrix products, project(): total = total + jnp.dot(part, w, preferred_element_type=jnp.float32)  6.87 us
  transfers between devices with their start and end apart: 21, of which 6 were waited for; matrix products, arithmetic and copies ran while one was open for 10% of the time, Pallas kernels for 0%

profile of v1, /device:TPU:24, one launch (start us, length us, event | category | flops | bytes accessed | tf_op | source)
XLA Modules:
  0.0 186.2 jit_solution(13931892626687819293)
XLA Ops:
  0.0 37.6 %all_gather.3 = bf16[128,1280]{1,0:T(8,128)(2,1)S(1)} all-gather(bf16[8,1280]{1,0:T(8,128)(2,1)} %param.7), channel_id=1, replica_groups={{0,4,8,12,16,20,24,28,32,36,40,44,48,52,56,60},{1,5,9,13,17,21,25,29,33..., dimensions={0}, use_global_device_ids=true | all-gather | bytes 348160 | tf_op jit(solution)/shard_map/all_gather | solution.py:75
  37.6 3.4 %collective-permute-start = (bf16[128,1280]{1,0:T(8,128)(2,1)S(1)}, bf16[128,1280]{1,0:T(8,128)(2,1)}, u32[]{:S(2)}, u32[]{:S(2)}) collective-permute-start(bf16[128,1280]{1,0:T(8,128)(2,1)S(1)} %all_gather.3), channel_id=1, source_target_pairs={{0,128},{1,129},{2,130},{3,131},{4,132},{5,133},{6,134},{7,135},{8... | collective-permute-start | bytes 983048 | tf_op jit(solution)/shard_map/ppermute | solution.py:37
  41.0 4.6 %collective-permute-start.1 = (bf16[128,1280]{1,0:T(8,128)(2,1)S(1)}, bf16[128,1280]{1,0:T(8,128)(2,1)}, u32[]{:S(2)}, u32[]{:S(2)}) collective-permute-start(bf16[128,1280]{1,0:T(8,128)(2,1)S(1)} %all_gather.3), channel_id=1, source_target_pairs={{0,256},{1,257},{2,258},{3,259},{4,260},{5,261},{6,262},{7,263},{8... | collective-permute-start | bytes 983048 | tf_op jit(solution)/shard_map/ppermute | solution.py:37
  45.6 3.3 %collective-permute-start.2 = (bf16[128,1280]{1,0:T(8,128)(2,1)S(1)}, bf16[128,1280]{1,0:T(8,128)(2,1)}, u32[]{:S(2)}, u32[]{:S(2)}) collective-permute-start(bf16[128,1280]{1,0:T(8,128)(2,1)S(1)} %all_gather.3), channel_id=1, source_target_pairs={{0,384},{1,385},{2,386},{3,387},{4,388},{5,389},{6,390},{7,391},{8... | collective-permute-start | bytes 983048 | tf_op jit(solution)/shard_map/ppermute | solution.py:37
  54.2 1.0 constant_dynamic-update-slice_fusion.2
  55.2 1.0 constant_dynamic-update-slice_fusion.1
  56.3 1.0 constant_dynamic-update-slice_fusion
  58.0 2.2 %collective-permute-start.3 = (bf16[512,256]{1,0:T(8,128)(2,1)}, bf16[512,256]{1,0:T(8,128)(2,1)}, u32[]{:S(2)}, u32[]{:S(2)}) collective-permute-start(bf16[512,256]{1,0:T(8,128)(2,1)} %slice.212), channel_id=1, source_target_pairs={{0,1},{1,2},{2,3},{3,0},{4,5},{5,6},{6,7},{7,4},{8,9},{9,10},{10,1... | collective-permute-start | bytes 786440 | tf_op jit(solution)/shard_map/ppermute | solution.py:37
  60.6 4.5 %collective-permute-start.4 = (bf16[512,256]{1,0:T(8,128)(2,1)}, bf16[512,256]{1,0:T(8,128)(2,1)}, u32[]{:S(2)}, u32[]{:S(2)}) collective-permute-start(bf16[512,256]{1,0:T(8,128)(2,1)} %slice.212), channel_id=1, source_target_pairs={{0,2},{1,3},{2,0},{3,1},{4,6},{5,7},{6,4},{7,5},{8,10},{9,11},{10,... | collective-permute-start | bytes 786440 | tf_op jit(solution)/shard_map/ppermute | solution.py:37
  65.1 1.8 copy.21
  67.1 3.8 %collective-permute-start.12 = (bf16[512,1024]{1,0:T(8,128)(2,1)S(1)}, bf16[512,1024]{1,0:T(8,128)(2,1)S(1)}, u32[]{:S(2)}, u32[]{:S(2)}) collective-permute-start(bf16[512,1024]{1,0:T(8,128)(2,1)S(1)} %slice.229), channel_id=1, source_target_pairs={{0,1},{1,2},{2,3},{3,0},{4,5},{5,6},{6,7},{7,4},{8,9},{9,10},{10,1... | collective-permute-start | bytes 3145736 | tf_op jit(solution)/shard_map/ppermute | solution.py:37
  70.9 1.9 %collective-permute-start.13 = (bf16[512,1024]{1,0:T(8,128)(2,1)S(1)}, bf16[512,1024]{1,0:T(8,128)(2,1)S(1)}, u32[]{:S(2)}, u32[]{:S(2)}) collective-permute-start(bf16[512,1024]{1,0:T(8,128)(2,1)S(1)} %slice.229), channel_id=1, source_target_pairs={{0,2},{1,3},{2,0},{3,1},{4,6},{5,7},{6,4},{7,5},{8,10},{9,11},{10,... | collective-permute-start | bytes 3145736 | tf_op jit(solution)/shard_map/ppermute | solution.py:37
  72.8 2.8 %collective-permute-start.14 = (bf16[512,1024]{1,0:T(8,128)(2,1)S(1)}, bf16[512,1024]{1,0:T(8,128)(2,1)S(1)}, u32[]{:S(2)}, u32[]{:S(2)}) collective-permute-start(bf16[512,1024]{1,0:T(8,128)(2,1)S(1)} %slice.229), channel_id=1, source_target_pairs={{0,3},{1,0},{2,1},{3,2},{4,7},{5,4},{6,5},{7,6},{8,11},{9,8},{10,9... | collective-permute-start | bytes 3145736 | tf_op jit(solution)/shard_map/ppermute | solution.py:37
  75.6 4.5 %collective-permute-start.5 = (bf16[512,256]{1,0:T(8,128)(2,1)}, bf16[512,256]{1,0:T(8,128)(2,1)S(1)}, u32[]{:S(2)}, u32[]{:S(2)}) collective-permute-start(bf16[512,256]{1,0:T(8,128)(2,1)} %slice.212), channel_id=1, source_target_pairs={{0,3},{1,0},{2,1},{3,2},{4,7},{5,4},{6,5},{7,6},{8,11},{9,8},{10,9... | collective-permute-start | bytes 786440 | tf_op jit(solution)/shard_map/ppermute | solution.py:37
  80.2 1.1 fusion.128
  81.4 1.9 %collective-permute-start.6 = (bf16[512,256]{1,0:T(8,128)(2,1)}, bf16[512,256]{1,0:T(8,128)(2,1)}, u32[]{:S(2)}, u32[]{:S(2)}) collective-permute-start(bf16[512,256]{1,0:T(8,128)(2,1)} %slice.212), channel_id=1, source_target_pairs={{0,64},{1,65},{2,66},{3,67},{4,68},{5,69},{6,70},{7,71},{8,72},{9,... | collective-permute-start | bytes 786440 | tf_op jit(solution)/shard_map/ppermute | solution.py:41
  83.3 1.1 fusion.130
  84.5 18.6 %collective-permute-done.5 = bf16[512,256]{1,0:T(8,128)(2,1)S(1)} collective-permute-done((bf16[512,256]{1,0:T(8,128)(2,1)}, bf16[512,256]{1,0:T(8,128)(2,1)S(1)}, u32[]{:S(2)}, u32[]{:S(2)}) %collective-permute-start.5) | collective-permute-done | bytes 262176 | tf_op jit(solution)/shard_map/ppermute | solution.py:37
  103.1 1.9 %collective-permute-start.8 = (bf16[512,256]{1,0:T(8,128)(2,1)}, bf16[512,256]{1,0:T(8,128)(2,1)S(1)}, u32[]{:S(2)}, u32[]{:S(2)}) collective-permute-start(bf16[512,256]{1,0:T(8,128)(2,1)} %collective-permute-done.4), channel_id=1, source_target_pairs={{0,64},{1,65},{2,66},{3,67},{4,68},{5,69},{6,70},{7,71},{8,72},{9,... | collective-permute-start | bytes 786440 | tf_op jit(solution)/shard_map/ppermute | solution.py:41
  105.3 2.4 %collective-permute-start.9 = (bf16[512,256]{1,0:T(8,128)(2,1)S(1)}, bf16[512,256]{1,0:T(8,128)(2,1)S(1)}, u32[]{:S(2)}, u32[]{:S(2)}) collective-permute-start(bf16[512,256]{1,0:T(8,128)(2,1)S(1)} %collective-permute-done.5), channel_id=1, source_target_pairs={{0,64},{1,65},{2,66},{3,67},{4,68},{5,69},{6,70},{7,71},{8,72},{9,... | collective-permute-start | bytes 786440 | tf_op jit(solution)/shard_map/ppermute | solution.py:41
  107.8 1.1 fusion.134
  109.2 1.9 %collective-permute-start.7 = (bf16[512,256]{1,0:T(8,128)(2,1)}, bf16[512,256]{1,0:T(8,128)(2,1)S(1)}, u32[]{:S(2)}, u32[]{:S(2)}) collective-permute-start(bf16[512,256]{1,0:T(8,128)(2,1)} %collective-permute-done.3), channel_id=1, source_target_pairs={{0,64},{1,65},{2,66},{3,67},{4,68},{5,69},{6,70},{7,71},{8,72},{9,... | collective-permute-start | bytes 786440 | tf_op jit(solution)/shard_map/ppermute | solution.py:41
  111.6 1.2 collective-permute-done.7
  113.0 1.0 fusion.115
  114.1 1.9 %collective-permute-start.10 = (bf16[128,256]{1,0:T(8,128)(2,1)S(1)}, bf16[128,256]{1,0:T(8,128)(2,1)S(1)}, u32[]{:S(2)}, u32[]{:S(2)}) collective-permute-start(bf16[128,256]{1,0:T(8,128)(2,1)S(1)} %pad_maximum_fusion.7), channel_id=1, source_target_pairs={{0,1},{1,2},{2,3},{3,4},{4,5},{5,6},{6,7},{7,8},{8,9},{9,10},{10,1... | collective-permute-start | bytes 196616 | tf_op jit(solution)/shard_map/ppermute | solution.py:46
  116.0 2.0 %collective-permute-start.15 = (bf16[512,1024]{1,0:T(8,128)(2,1)S(1)}, bf16[512,1024]{1,0:T(8,128)(2,1)S(1)}, u32[]{:S(2)}, u32[]{:S(2)}) collective-permute-start(bf16[512,1024]{1,0:T(8,128)(2,1)S(1)} %slice.229), channel_id=1, source_target_pairs={{0,64},{1,65},{2,66},{3,67},{4,68},{5,69},{6,70},{7,71},{8,72},{9,... | collective-permute-start | bytes 3145736 | tf_op jit(solution)/shard_map/ppermute | solution.py:41
  118.1 2.2 %collective-permute-done.10 = bf16[128,256]{1,0:T(8,128)(2,1)S(1)} collective-permute-done((bf16[128,256]{1,0:T(8,128)(2,1)S(1)}, bf16[128,256]{1,0:T(8,128)(2,1)S(1)}, u32[]{:S(2)}, u32[]{:S(2)}) %collective-permute-start.10) | collective-permute-done | bytes 65568 | tf_op jit(solution)/shard_map/ppermute | solution.py:46
  120.3 1.9 %collective-permute-start.11 = (bf16[256,256]{1,0:T(8,128)(2,1)S(1)}, bf16[256,256]{1,0:T(8,128)(2,1)S(1)}, u32[]{:S(2)}, u32[]{:S(2)}) collective-permute-start(bf16[256,256]{1,0:T(8,128)(2,1)S(1)} %maximum_maximum_fusion.1), channel_id=1, source_target_pairs={{0,2},{1,3},{2,4},{3,5},{4,6},{5,7},{6,8},{7,9},{8,10},{9,11},{10,... | collective-permute-start | bytes 393224 | tf_op jit(solution)/shard_map/ppermute | solution.py:46
  122.3 0.8 compare_and_fusion
  123.0 5.7 %collective-permute-done.11 = bf16[256,256]{1,0:T(8,128)(2,1)S(1)} collective-permute-done((bf16[256,256]{1,0:T(8,128)(2,1)S(1)}, bf16[256,256]{1,0:T(8,128)(2,1)S(1)}, u32[]{:S(2)}, u32[]{:S(2)}) %collective-permute-start.11) | collective-permute-done | bytes 131104 | tf_op jit(solution)/shard_map/ppermute | solution.py:46
  128.7 0.8 maximum_maximum_fusion
  129.5 1.9 %collective-permute-start.17 = (bf16[512,1024]{1,0:T(8,128)(2,1)S(1)}, bf16[512,1024]{1,0:T(8,128)(2,1)S(1)}, u32[]{:S(2)}, u32[]{:S(2)}) collective-permute-start(bf16[512,1024]{1,0:T(8,128)(2,1)S(1)} %collective-permute-done.13), channel_id=1, source_target_pairs={{0,64},{1,65},{2,66},{3,67},{4,68},{5,69},{6,70},{7,71},{8,72},{9,... | collective-permute-start | bytes 3145736 | tf_op jit(solution)/shard_map/ppermute | solution.py:41
  131.4 2.4 %collective-permute-start.18 = (bf16[512,1024]{1,0:T(8,128)(2,1)S(1)}, bf16[512,1024]{1,0:T(8,128)(2,1)S(1)}, u32[]{:S(2)}, u32[]{:S(2)}) collective-permute-start(bf16[512,1024]{1,0:T(8,128)(2,1)S(1)} %collective-permute-done.14), channel_id=1, source_target_pairs={{0,64},{1,65},{2,66},{3,67},{4,68},{5,69},{6,70},{7,71},{8,72},{9,... | collective-permute-start | bytes 3145736 | tf_op jit(solution)/shard_map/ppermute | solution.py:41
  133.9 1.9 %collective-permute-start.16 = (bf16[512,1024]{1,0:T(8,128)(2,1)S(1)}, bf16[512,1024]{1,0:T(8,128)(2,1)S(1)}, u32[]{:S(2)}, u32[]{:S(2)}) collective-permute-start(bf16[512,1024]{1,0:T(8,128)(2,1)S(1)} %collective-permute-done.12), channel_id=1, source_target_pairs={{0,64},{1,65},{2,66},{3,67},{4,68},{5,69},{6,70},{7,71},{8,72},{9,... | collective-permute-start | bytes 3145736 | tf_op jit(solution)/shard_map/ppermute | solution.py:41
  136.8 1.1 copy-done.11
  141.3 2.3 %fusion.175 = (f32[8,128]{1,0:T(8,128)S(1)}, f32[8,128,512]{1,2,0:T(8,128)}) fusion(pred[128,512]{0,1:T(8,128)(4,1)S(1)} %copy-done.56, bf16[512,256]{1,0:T(8,128)(2,1)S(1)} %copy-done.20, bf16[128,8,64]{2,0,1:T(8,128)(2,1)S(1)} %get-tuple-element.6, bf16[128,8,64]{2,0,1:T(8,128)(2,1)S(1)} %get-tuple-element.5), kind=kOutput, calls=%fused_computation.270 | convolution fusion | flops 137363968 | bytes 2887680 | tf_op jit(solution)/shard_map/sub | solution.py:143
  143.6 1.8 fusion.54
  146.3 0.8 copy-done.15
  148.1 2.1 %collective-permute-start.19 = (f32[256,256]{1,0:T(8,128)S(1)}, f32[256,256]{1,0:T(8,128)S(1)}, u32[]{:S(2)}, u32[]{:S(2)}) collective-permute-start(f32[256,256]{1,0:T(8,128)S(1)} %pad_maximum_fusion), channel_id=1, source_target_pairs={{2,0},{3,1},{4,2},{5,3},{6,4},{7,5},{8,6},{9,7},{10,8},{11,9},{12,... | collective-permute-start | bytes 786440 | tf_op jit(solution)/shard_map/ppermute | solution.py:46
  150.7 10.3 %collective-permute-done.19 = f32[256,256]{1,0:T(8,128)S(1)} collective-permute-done((f32[256,256]{1,0:T(8,128)S(1)}, f32[256,256]{1,0:T(8,128)S(1)}, u32[]{:S(2)}, u32[]{:S(2)}) %collective-permute-start.19) | collective-permute-done | bytes 262176 | tf_op jit(solution)/shard_map/ppermute | solution.py:46
  161.8 2.6 %collective-permute-start.20 = (f32[128,256]{1,0:T(8,128)}, f32[128,256]{1,0:T(8,128)}, u32[]{:S(2)}, u32[]{:S(2)}) collective-permute-start(f32[128,256]{1,0:T(8,128)} %slice.238), channel_id=1, source_target_pairs={{1,0},{2,1},{3,2},{4,3},{5,4},{6,5},{7,6},{8,7},{9,8},{10,9},{11,1... | collective-permute-start | bytes 393224 | tf_op jit(solution)/shard_map/ppermute | solution.py:46
  165.0 6.2 %collective-permute-done.20 = f32[128,256]{1,0:T(8,128)} collective-permute-done((f32[128,256]{1,0:T(8,128)}, f32[128,256]{1,0:T(8,128)}, u32[]{:S(2)}, u32[]{:S(2)}) %collective-permute-start.20) | collective-permute-done | bytes 131104 | tf_op jit(solution)/shard_map/ppermute | solution.py:46
  171.2 0.9 slice_add_fusion
  172.8 1.2 fusion.176
  175.0 1.3 fusion.177
  177.6 1.2 fusion.179
  184.3 1.0 copy-done.16
  185.2 1.0 fusion.38
  (211 shorter events, 23.3 us)
Async XLA Ops:
  0.0 49.4 %copy-start = (bf16[1,128,4096]{2,1,0:T(8,128)(2,1)S(1)}, bf16[1,128,4096]{2,1,0:T(8,128)(2,1)}, u32[]{:S(2)}) copy-start(bf16[1,128,4096]{2,1,0:T(8,128)(2,1)} %param.4) | copy-start | bytes 3145732
  37.6 16.6 %collective-permute-start = (bf16[128,1280]{1,0:T(8,128)(2,1)S(1)}, bf16[128,1280]{1,0:T(8,128)(2,1)}, u32[]{:S(2)}, u32[]{:S(2)}) collective-permute-start(bf16[128,1280]{1,0:T(8,128)(2,1)S(1)} %all_gather.3), channel_id=1, source_target_pairs={{0,128},{1,129},{2,130},{3,131},{4,132},{5,133},{6,134},{7,135},{8... | collective-permute-start | bytes 983048 | tf_op jit(solution)/shard_map/ppermute | solution.py:37
  41.0 14.2 %collective-permute-start.1 = (bf16[128,1280]{1,0:T(8,128)(2,1)S(1)}, bf16[128,1280]{1,0:T(8,128)(2,1)}, u32[]{:S(2)}, u32[]{:S(2)}) collective-permute-start(bf16[128,1280]{1,0:T(8,128)(2,1)S(1)} %all_gather.3), channel_id=1, source_target_pairs={{0,256},{1,257},{2,258},{3,259},{4,260},{5,261},{6,262},{7,263},{8... | collective-permute-start | bytes 983048 | tf_op jit(solution)/shard_map/ppermute | solution.py:37
  45.6 10.6 %collective-permute-start.2 = (bf16[128,1280]{1,0:T(8,128)(2,1)S(1)}, bf16[128,1280]{1,0:T(8,128)(2,1)}, u32[]{:S(2)}, u32[]{:S(2)}) collective-permute-start(bf16[128,1280]{1,0:T(8,128)(2,1)S(1)} %all_gather.3), channel_id=1, source_target_pairs={{0,384},{1,385},{2,386},{3,387},{4,388},{5,389},{6,390},{7,391},{8... | collective-permute-start | bytes 983048 | tf_op jit(solution)/shard_map/ppermute | solution.py:37
  50.4 58.5 %copy-start.21 = (bf16[128,128]{1,0:T(8,128)(2,1)}, bf16[128,128]{1,0:T(8,128)(2,1)S(1)}, u32[]{:S(2)}) copy-start(bf16[128,128]{1,0:T(8,128)(2,1)S(1)} %get-tuple-element.38) | copy-start | bytes 98308
  51.3 57.6 %copy-start.23 = (bf16[128,128]{1,0:T(8,128)(2,1)}, bf16[128,128]{1,0:T(8,128)(2,1)S(1)}, u32[]{:S(2)}) copy-start(bf16[128,128]{1,0:T(8,128)(2,1)S(1)} %get-tuple-element.42) | copy-start | bytes 98308
  56.2 23.9 %copy-start.27 = (bf16[128,128]{1,0:T(8,128)(2,1)S(1)}, bf16[128,128]{1,0:T(8,128)(2,1)}, u32[]{:S(2)}) copy-start(bf16[128,128]{1,0:T(8,128)(2,1)} %get-tuple-element.35) | copy-start | bytes 98308
  56.2 23.9 %copy-start.29 = (bf16[128,128]{1,0:T(8,128)(2,1)S(1)}, bf16[128,128]{1,0:T(8,128)(2,1)}, u32[]{:S(2)}) copy-start(bf16[128,128]{1,0:T(8,128)(2,1)} %get-tuple-element.39) | copy-start | bytes 98308
  56.2 23.9 %copy-start.31 = (bf16[128,128]{1,0:T(8,128)(2,1)S(1)}, bf16[128,128]{1,0:T(8,128)(2,1)}, u32[]{:S(2)}) copy-start(bf16[128,128]{1,0:T(8,128)(2,1)} %get-tuple-element.43) | copy-start | bytes 98308
  56.2 23.9 %copy-start.33 = (bf16[128,128]{1,0:T(8,128)(2,1)S(1)}, bf16[128,128]{1,0:T(8,128)(2,1)}, u32[]{:S(2)}) copy-start(bf16[128,128]{1,0:T(8,128)(2,1)} %get-tuple-element.31) | copy-start | bytes 98308
  58.0 25.3 %copy-start.37 = (bf16[128,128]{1,0:T(8,128)(2,1)S(1)}, bf16[128,128]{1,0:T(8,128)(2,1)}, u32[]{:S(2)}) copy-start(bf16[128,128]{1,0:T(8,128)(2,1)} %get-tuple-element.37) | copy-start | bytes 98308
  58.0 25.3 %copy-start.41 = (bf16[128,128]{1,0:T(8,128)(2,1)S(1)}, bf16[128,128]{1,0:T(8,128)(2,1)}, u32[]{:S(2)}) copy-start(bf16[128,128]{1,0:T(8,128)(2,1)} %get-tuple-element.41) | copy-start | bytes 98308
  58.0 25.3 %copy-start.45 = (bf16[128,128]{1,0:T(8,128)(2,1)S(1)}, bf16[128,128]{1,0:T(8,128)(2,1)}, u32[]{:S(2)}) copy-start(bf16[128,128]{1,0:T(8,128)(2,1)} %get-tuple-element.45) | copy-start | bytes 98308
  58.0 17.6 %collective-permute-start.3 = (bf16[512,256]{1,0:T(8,128)(2,1)}, bf16[512,256]{1,0:T(8,128)(2,1)}, u32[]{:S(2)}, u32[]{:S(2)}) collective-permute-start(bf16[512,256]{1,0:T(8,128)(2,1)} %slice.212), channel_id=1, source_target_pairs={{0,1},{1,2},{2,3},{3,0},{4,5},{5,6},{6,7},{7,4},{8,9},{9,10},{10,1... | collective-permute-start | bytes 786440 | tf_op jit(solution)/shard_map/ppermute | solution.py:37
  60.6 20.8 %collective-permute-start.4 = (bf16[512,256]{1,0:T(8,128)(2,1)}, bf16[512,256]{1,0:T(8,128)(2,1)}, u32[]{:S(2)}, u32[]{:S(2)}) collective-permute-start(bf16[512,256]{1,0:T(8,128)(2,1)} %slice.212), channel_id=1, source_target_pairs={{0,2},{1,3},{2,0},{3,1},{4,6},{5,7},{6,4},{7,5},{8,10},{9,11},{10,... | collective-permute-start | bytes 786440 | tf_op jit(solution)/shard_map/ppermute | solution.py:37
  65.1 39.9 %copy-start.35 = (bf16[128,128]{1,0:T(8,128)(2,1)S(1)}, bf16[128,128]{1,0:T(8,128)(2,1)}, u32[]{:S(2)}) copy-start(bf16[128,128]{1,0:T(8,128)(2,1)} %get-tuple-element.36) | copy-start | bytes 98308
  65.1 39.9 %copy-start.39 = (bf16[128,128]{1,0:T(8,128)(2,1)S(1)}, bf16[128,128]{1,0:T(8,128)(2,1)}, u32[]{:S(2)}) copy-start(bf16[128,128]{1,0:T(8,128)(2,1)} %get-tuple-element.40) | copy-start | bytes 98308
  65.1 39.9 %copy-start.43 = (bf16[128,128]{1,0:T(8,128)(2,1)S(1)}, bf16[128,128]{1,0:T(8,128)(2,1)}, u32[]{:S(2)}) copy-start(bf16[128,128]{1,0:T(8,128)(2,1)} %get-tuple-element.44) | copy-start | bytes 98308
  66.9 16.4 %copy-start.48 = (bf16[128,128]{1,0:T(8,128)(2,1)S(1)}, bf16[128,128]{1,0:T(8,128)(2,1)}, u32[]{:S(2)}) copy-start(bf16[128,128]{1,0:T(8,128)(2,1)} %get-tuple-element.33) | copy-start | bytes 98308
  66.9 38.1 %copy-start.47 = (bf16[128,128]{1,0:T(8,128)(2,1)S(1)}, bf16[128,128]{1,0:T(8,128)(2,1)}, u32[]{:S(2)}) copy-start(bf16[128,128]{1,0:T(8,128)(2,1)} %get-tuple-element.32) | copy-start | bytes 98308
  66.9 40.8 %copy-start.25 = (bf16[128,128]{1,0:T(8,128)(2,1)S(1)}, bf16[128,128]{1,0:T(8,128)(2,1)}, u32[]{:S(2)}) copy-start(bf16[128,128]{1,0:T(8,128)(2,1)} %get-tuple-element.46) | copy-start | bytes 98308
  67.0 40.8 %copy-start.26 = (bf16[128,128]{1,0:T(8,128)(2,1)S(1)}, bf16[128,128]{1,0:T(8,128)(2,1)}, u32[]{:S(2)}) copy-start(bf16[128,128]{1,0:T(8,128)(2,1)} %get-tuple-element.34) | copy-start | bytes 98308
  67.1 66.8 %collective-permute-start.12 = (bf16[512,1024]{1,0:T(8,128)(2,1)S(1)}, bf16[512,1024]{1,0:T(8,128)(2,1)S(1)}, u32[]{:S(2)}, u32[]{:S(2)}) collective-permute-start(bf16[512,1024]{1,0:T(8,128)(2,1)S(1)} %slice.229), channel_id=1, source_target_pairs={{0,1},{1,2},{2,3},{3,0},{4,5},{5,6},{6,7},{7,4},{8,9},{9,10},{10,1... | collective-permute-start | bytes 3145736 | tf_op jit(solution)/shard_map/ppermute | solution.py:37
  70.9 58.6 %collective-permute-start.13 = (bf16[512,1024]{1,0:T(8,128)(2,1)S(1)}, bf16[512,1024]{1,0:T(8,128)(2,1)S(1)}, u32[]{:S(2)}, u32[]{:S(2)}) collective-permute-start(bf16[512,1024]{1,0:T(8,128)(2,1)S(1)} %slice.229), channel_id=1, source_target_pairs={{0,2},{1,3},{2,0},{3,1},{4,6},{5,7},{6,4},{7,5},{8,10},{9,11},{10,... | collective-permute-start | bytes 3145736 | tf_op jit(solution)/shard_map/ppermute | solution.py:37
  72.8 58.6 %collective-permute-start.14 = (bf16[512,1024]{1,0:T(8,128)(2,1)S(1)}, bf16[512,1024]{1,0:T(8,128)(2,1)S(1)}, u32[]{:S(2)}, u32[]{:S(2)}) collective-permute-start(bf16[512,1024]{1,0:T(8,128)(2,1)S(1)} %slice.229), channel_id=1, source_target_pairs={{0,3},{1,0},{2,1},{3,2},{4,7},{5,4},{6,5},{7,6},{8,11},{9,8},{10,9... | collective-permute-start | bytes 3145736 | tf_op jit(solution)/shard_map/ppermute | solution.py:37
  75.6 27.5 %collective-permute-start.5 = (bf16[512,256]{1,0:T(8,128)(2,1)}, bf16[512,256]{1,0:T(8,128)(2,1)S(1)}, u32[]{:S(2)}, u32[]{:S(2)}) collective-permute-start(bf16[512,256]{1,0:T(8,128)(2,1)} %slice.212), channel_id=1, source_target_pairs={{0,3},{1,0},{2,1},{3,2},{4,7},{5,4},{6,5},{7,6},{8,11},{9,8},{10,9... | collective-permute-start | bytes 786440 | tf_op jit(solution)/shard_map/ppermute | solution.py:37
  81.3 29.8 %copy-start.38 = (bf16[128,128]{1,0:T(8,128)(2,1)S(1)}, bf16[128,128]{1,0:T(8,128)(2,1)}, u32[]{:S(2)}) copy-start(bf16[128,128]{1,0:T(8,128)(2,1)} %get-tuple-element.37) | copy-start | bytes 98308
  81.3 29.8 %copy-start.42 = (bf16[128,128]{1,0:T(8,128)(2,1)S(1)}, bf16[128,128]{1,0:T(8,128)(2,1)}, u32[]{:S(2)}) copy-start(bf16[128,128]{1,0:T(8,128)(2,1)} %get-tuple-element.41) | copy-start | bytes 98308
  81.4 29.8 %copy-start.46 = (bf16[128,128]{1,0:T(8,128)(2,1)S(1)}, bf16[128,128]{1,0:T(8,128)(2,1)}, u32[]{:S(2)}) copy-start(bf16[128,128]{1,0:T(8,128)(2,1)} %get-tuple-element.45) | copy-start | bytes 98308
  81.4 23.9 %collective-permute-start.6 = (bf16[512,256]{1,0:T(8,128)(2,1)}, bf16[512,256]{1,0:T(8,128)(2,1)}, u32[]{:S(2)}, u32[]{:S(2)}) collective-permute-start(bf16[512,256]{1,0:T(8,128)(2,1)} %slice.212), channel_id=1, source_target_pairs={{0,64},{1,65},{2,66},{3,67},{4,68},{5,69},{6,70},{7,71},{8,72},{9,... | collective-permute-start | bytes 786440 | tf_op jit(solution)/shard_map/ppermute | solution.py:41
  84.5 26.8 %copy-start.36 = (bf16[128,128]{1,0:T(8,128)(2,1)S(1)}, bf16[128,128]{1,0:T(8,128)(2,1)}, u32[]{:S(2)}) copy-start(bf16[128,128]{1,0:T(8,128)(2,1)} %get-tuple-element.36) | copy-start | bytes 98308
  84.5 26.8 %copy-start.40 = (bf16[128,128]{1,0:T(8,128)(2,1)S(1)}, bf16[128,128]{1,0:T(8,128)(2,1)}, u32[]{:S(2)}) copy-start(bf16[128,128]{1,0:T(8,128)(2,1)} %get-tuple-element.40) | copy-start | bytes 98308
  84.5 26.8 %copy-start.44 = (bf16[128,128]{1,0:T(8,128)(2,1)S(1)}, bf16[128,128]{1,0:T(8,128)(2,1)}, u32[]{:S(2)}) copy-start(bf16[128,128]{1,0:T(8,128)(2,1)} %get-tuple-element.44) | copy-start | bytes 98308
  103.1 6.0 %collective-permute-start.8 = (bf16[512,256]{1,0:T(8,128)(2,1)}, bf16[512,256]{1,0:T(8,128)(2,1)S(1)}, u32[]{:S(2)}, u32[]{:S(2)}) collective-permute-start(bf16[512,256]{1,0:T(8,128)(2,1)} %collective-permute-done.4), channel_id=1, source_target_pairs={{0,64},{1,65},{2,66},{3,67},{4,68},{5,69},{6,70},{7,71},{8,72},{9,... | collective-permute-start | bytes 786440 | tf_op jit(solution)/shard_map/ppermute | solution.py:41
  105.3 6.0 %collective-permute-start.9 = (bf16[512,256]{1,0:T(8,128)(2,1)S(1)}, bf16[512,256]{1,0:T(8,128)(2,1)S(1)}, u32[]{:S(2)}, u32[]{:S(2)}) collective-permute-start(bf16[512,256]{1,0:T(8,128)(2,1)S(1)} %collective-permute-done.5), channel_id=1, source_target_pairs={{0,64},{1,65},{2,66},{3,67},{4,68},{5,69},{6,70},{7,71},{8,72},{9,... | collective-permute-start | bytes 786440 | tf_op jit(solution)/shard_map/ppermute | solution.py:41
  109.1 11.1 %copy-start.53 = (bf16[512,256]{1,0:T(8,128)(2,1)}, bf16[512,256]{1,0:T(8,128)(2,1)S(1)}, u32[]{:S(2)}) copy-start(bf16[512,256]{1,0:T(8,128)(2,1)S(1)} %collective-permute-done.8) | copy-start | bytes 786436
  109.2 3.6 %collective-permute-start.7 = (bf16[512,256]{1,0:T(8,128)(2,1)}, bf16[512,256]{1,0:T(8,128)(2,1)S(1)}, u32[]{:S(2)}, u32[]{:S(2)}) collective-permute-start(bf16[512,256]{1,0:T(8,128)(2,1)} %collective-permute-done.3), channel_id=1, source_target_pairs={{0,64},{1,65},{2,66},{3,67},{4,68},{5,69},{6,70},{7,71},{8,72},{9,... | collective-permute-start | bytes 786440 | tf_op jit(solution)/shard_map/ppermute | solution.py:41
  112.8 23.3 %copy-start.17 = (bf16[512,256]{1,0:T(8,128)(2,1)}, bf16[512,256]{1,0:T(8,128)(2,1)S(1)}, u32[]{:S(2)}) copy-start(bf16[512,256]{1,0:T(8,128)(2,1)S(1)} %collective-permute-done.7) | copy-start | bytes 786436
  114.1 6.2 %collective-permute-start.10 = (bf16[128,256]{1,0:T(8,128)(2,1)S(1)}, bf16[128,256]{1,0:T(8,128)(2,1)S(1)}, u32[]{:S(2)}, u32[]{:S(2)}) collective-permute-start(bf16[128,256]{1,0:T(8,128)(2,1)S(1)} %pad_maximum_fusion.7), channel_id=1, source_target_pairs={{0,1},{1,2},{2,3},{3,4},{4,5},{5,6},{6,7},{7,8},{8,9},{9,10},{10,1... | collective-permute-start | bytes 196616 | tf_op jit(solution)/shard_map/ppermute | solution.py:46
  116.0 20.8 %collective-permute-start.15 = (bf16[512,1024]{1,0:T(8,128)(2,1)S(1)}, bf16[512,1024]{1,0:T(8,128)(2,1)S(1)}, u32[]{:S(2)}, u32[]{:S(2)}) collective-permute-start(bf16[512,1024]{1,0:T(8,128)(2,1)S(1)} %slice.229), channel_id=1, source_target_pairs={{0,64},{1,65},{2,66},{3,67},{4,68},{5,69},{6,70},{7,71},{8,72},{9,... | collective-permute-start | bytes 3145736 | tf_op jit(solution)/shard_map/ppermute | solution.py:41
  120.3 8.4 %collective-permute-start.11 = (bf16[256,256]{1,0:T(8,128)(2,1)S(1)}, bf16[256,256]{1,0:T(8,128)(2,1)S(1)}, u32[]{:S(2)}, u32[]{:S(2)}) collective-permute-start(bf16[256,256]{1,0:T(8,128)(2,1)S(1)} %maximum_maximum_fusion.1), channel_id=1, source_target_pairs={{0,2},{1,3},{2,4},{3,5},{4,6},{5,7},{6,8},{7,9},{8,10},{9,11},{10,... | collective-permute-start | bytes 393224 | tf_op jit(solution)/shard_map/ppermute | solution.py:46
  129.5 9.1 %collective-permute-start.17 = (bf16[512,1024]{1,0:T(8,128)(2,1)S(1)}, bf16[512,1024]{1,0:T(8,128)(2,1)S(1)}, u32[]{:S(2)}, u32[]{:S(2)}) collective-permute-start(bf16[512,1024]{1,0:T(8,128)(2,1)S(1)} %collective-permute-done.13), channel_id=1, source_target_pairs={{0,64},{1,65},{2,66},{3,67},{4,68},{5,69},{6,70},{7,71},{8,72},{9,... | collective-permute-start | bytes 3145736 | tf_op jit(solution)/shard_map/ppermute | solution.py:41
  131.4 7.5 %collective-permute-start.18 = (bf16[512,1024]{1,0:T(8,128)(2,1)S(1)}, bf16[512,1024]{1,0:T(8,128)(2,1)S(1)}, u32[]{:S(2)}, u32[]{:S(2)}) collective-permute-start(bf16[512,1024]{1,0:T(8,128)(2,1)S(1)} %collective-permute-done.14), channel_id=1, source_target_pairs={{0,64},{1,65},{2,66},{3,67},{4,68},{5,69},{6,70},{7,71},{8,72},{9,... | collective-permute-start | bytes 3145736 | tf_op jit(solution)/shard_map/ppermute | solution.py:41
  133.9 5.4 %collective-permute-start.16 = (bf16[512,1024]{1,0:T(8,128)(2,1)S(1)}, bf16[512,1024]{1,0:T(8,128)(2,1)S(1)}, u32[]{:S(2)}, u32[]{:S(2)}) collective-permute-start(bf16[512,1024]{1,0:T(8,128)(2,1)S(1)} %collective-permute-done.12), channel_id=1, source_target_pairs={{0,64},{1,65},{2,66},{3,67},{4,68},{5,69},{6,70},{7,71},{8,72},{9,... | collective-permute-start | bytes 3145736 | tf_op jit(solution)/shard_map/ppermute | solution.py:41
  148.0 16.3 %copy-start.55 = (f32[128,64]{1,0:T(8,128)S(1)}, f32[128,64]{1,0:T(8,128)}, u32[]{:S(2)}) copy-start(f32[128,64]{1,0:T(8,128)} %get-tuple-element.47) | copy-start | bytes 98308
  148.1 13.0 %collective-permute-start.19 = (f32[256,256]{1,0:T(8,128)S(1)}, f32[256,256]{1,0:T(8,128)S(1)}, u32[]{:S(2)}, u32[]{:S(2)}) collective-permute-start(f32[256,256]{1,0:T(8,128)S(1)} %pad_maximum_fusion), channel_id=1, source_target_pairs={{2,0},{3,1},{4,2},{5,3},{6,4},{7,5},{8,6},{9,7},{10,8},{11,9},{12,... | collective-permute-start | bytes 786440 | tf_op jit(solution)/shard_map/ppermute | solution.py:46
  161.8 9.4 %collective-permute-start.20 = (f32[128,256]{1,0:T(8,128)}, f32[128,256]{1,0:T(8,128)}, u32[]{:S(2)}, u32[]{:S(2)}) collective-permute-start(f32[128,256]{1,0:T(8,128)} %slice.238), channel_id=1, source_target_pairs={{1,0},{2,1},{3,2},{4,3},{5,4},{6,5},{7,6},{8,7},{9,8},{10,9},{11,1... | collective-permute-start | bytes 393224 | tf_op jit(solution)/shard_map/ppermute | solution.py:46
  165.0 9.0 %copy-start.12 = (bf16[512,1024]{1,0:T(8,128)(2,1)S(1)}, bf16[512,1024]{1,0:T(8,128)(2,1)}, u32[]{:S(2)}) copy-start(bf16[512,1024]{1,0:T(8,128)(2,1)} %copy-done.11) | copy-start | bytes 3145732
  (31 other events, 85.0 us)

commit v2 on v1

--- a/solution.py
+++ b/solution.py
@@ -3,6 +3,8 @@
 import jax
 import jax.numpy as jnp
 from jax import lax
+from jax.experimental import pallas as pl
+from jax.experimental.pallas import tpu as pltpu
 from jax.sharding import PartitionSpec as P
 
 HQ = 8
@@ -39,6 +41,119 @@
 
 def swap_cores(block):
     return lax.ppermute(block, ALL, route(lambda x, c, z, y: (x, 1 - c, z, y)))
+
+
+BLOCK = NZ * NY * 8
+SPAN = NZ * 8
+TURN = (((1,), (1,)), ((), ()))
+VMEM_LIMIT = 48 * 1024 * 1024
+
+
+def order_matrix(y_me):
+    slot = lax.broadcasted_iota(jnp.int32, (BLOCK, BLOCK), 1)
+    source = lax.broadcasted_iota(jnp.int32, (BLOCK, BLOCK), 0)
+    step, inner = slot // SPAN, slot % SPAN
+    wanted = inner // 8 * (NY * 8) + (y_me - step + NY) % NY * 8 + inner % 8
+    return (source == wanted).astype(jnp.bfloat16)
+
+
+def block_at(x_me, s, c):
+    return pl.multiple_of(((x_me - s + NX) % NX * NC + c) * BLOCK, BLOCK)
+
+
+def arrange_body(at, features, theirs, out_ref):
+    x_me, y_me, core = at[0], at[1], at[2]
+    order = order_matrix(y_me)
+    for s in range(NX):
+        own = features[:, pl.ds(block_at(x_me, s, core), BLOCK)]
+        other = theirs[:, pl.ds(pl.multiple_of((x_me - s + NX) % NX * BLOCK, BLOCK), BLOCK)]
+        both = jnp.concatenate([own, other], axis=0)
+        rows = both.shape[0]
+        got = jnp.dot(both, order, preferred_element_type=jnp.float32).astype(jnp.bfloat16)
+
+        @pl.when(core == 1)
+        def _():
+            out_ref[pl.ds(s * rows, rows), :] = got
+
+        @pl.when(core == 0)
+        def _():
+            for e in range(NY):
+                out_ref[pl.ds(e * rows, rows), pl.ds(s * SPAN, SPAN)] = got[
+                    :, e * SPAN : (e + 1) * SPAN
+                ]
+
+
+def arrange(at, features, theirs):
+    return pl.pallas_call(
+        arrange_body,
+        in_specs=[pl.BlockSpec(memory_space=pltpu.SMEM)]
+        + [pl.BlockSpec(memory_space=pltpu.VMEM)] * 2,
+        out_shape=jax.ShapeDtypeStruct((NX * 2 * features.shape[0], BLOCK), jnp.bfloat16),
+        compiler_params=pltpu.CompilerParams(vmem_limit_bytes=VMEM_LIMIT),
+        cost_estimate=pl.CostEstimate(
+            flops=4 * 2 * 256 * BLOCK * BLOCK, bytes_accessed=4 << 20, transcendentals=0
+        ),
+    )(at, features, theirs)
+
+
+def stack_body(own, first, second, third, query_ref, pair_ref):
+    rows = own.shape[0]
+    for i, piece in enumerate((own, first, second, third)):
+        at = pl.ds(i * rows, rows)
+        query_ref[at, :] = piece[:, : HQ * HD]
+        pair_ref[at, :] = piece[:, HQ * HD :]
+
+
+def stack_planes(*pieces):
+    rows = sum(piece.shape[0] for piece in pieces)
+    return pl.pallas_call(
+        stack_body,
+        out_shape=[
+            pltpu.VMEM((rows, HQ * HD), jnp.bfloat16),
+            pltpu.VMEM((rows, 2 * HD), jnp.bfloat16),
+        ],
+    )(*[pltpu.with_memory_space_constraint(p, pltpu.VMEM) for p in pieces])
+
+
+def query_part_body(at, grads, *refs):
+    pieces, out_ref, held = refs[:8], refs[8], refs[9]
+    x_me, y_me, core = at[0], at[1], at[2]
+    order = order_matrix(y_me)
+    for i, piece in enumerate(pieces):
+        held[i] = lax.dot_general(
+            grads[...], piece[...], TURN, preferred_element_type=jnp.float32
+        )
+    rows = grads.shape[0]
+    by_x, by_y = core * NX, (1 - core) * NX
+    for s in range(NX):
+        even = jnp.concatenate(
+            [held[by_x + e, :, s * SPAN : (s + 1) * SPAN] for e in range(NY)], axis=1
+        )
+        for c, part in ((0, even), (1, held[by_y + s])):
+            high = part.astype(jnp.bfloat16)
+            low = (part - high.astype(jnp.float32)).astype(jnp.bfloat16)
+            back = lax.dot_general(
+                jnp.concatenate([high, low], axis=0), order, TURN,
+                preferred_element_type=jnp.float32,
+            )
+            out_ref[:, pl.ds(block_at(x_me, s, c), BLOCK)] = back[:rows] + back[rows:]
+
+
+def query_part_of(at, grads, pieces):
+    rows = grads.shape[0]
+    return pl.pallas_call(
+        query_part_body,
+        in_specs=[pl.BlockSpec(memory_space=pltpu.SMEM)]
+        + [pl.BlockSpec(memory_space=pltpu.VMEM)] * 9,
+        out_shape=jax.ShapeDtypeStruct((rows, 8 * BLOCK), jnp.float32),
+        scratch_shapes=[pltpu.VMEM((8, rows, BLOCK), jnp.float32)],
+        compiler_params=pltpu.CompilerParams(vmem_limit_bytes=VMEM_LIMIT),
+        cost_estimate=pl.CostEstimate(
+            flops=8 * 2 * rows * BLOCK * (HQ * HD + 2 * BLOCK),
+            bytes_accessed=12 << 20,
+            transcendentals=0,
+        ),
+    )(at, grads, *pieces)
 
 
 def shifted(block, axis, distance):
@@ -77,58 +192,44 @@
         axis_index_groups=[[z * NY + y for z in range(NZ)] for y in range(NY)],
     )
     second, first, third = (hop(column, d, 0) for d in (2, 1, 3))
-    plane = jnp.concatenate([column, first, second, third], axis=0)
-
-    def spread(part):
-        two, one, three = (hop(part, d, 1) for d in (2, 1, 3))
-        mine = [part, one, two, three]
-        return mine + [swap_cores(piece) for piece in mine]
-
-    pair_w = spread(plane[:, HQ * HD :])
-    query_w = spread(plane[:, : HQ * HD])
-
-    block = NZ * NY * 8
-    slot = lax.broadcasted_iota(jnp.int32, (block, block), 1)
-    source = lax.broadcasted_iota(jnp.int32, (block, block), 0)
-    wanted = slot // 8 % NZ * (NY * 8) + (y_me - slot // (NZ * 8) + NY) % NY * 8 + slot % 8
-    order = (source == wanted).astype(jnp.bfloat16)
-
-    def taken(shift, c):
-        at = ((x_me - shift + NX) % NX * NC + c) * block
-        return jnp.dot(
-            lax.dynamic_slice_in_dim(features, at, block, 1), order,
-            preferred_element_type=jnp.float32,
-        ).astype(jnp.bfloat16)
-
-    by_x = [taken(s, 0) for s in range(NX)]
-    span = NZ * 8
-    order0 = [
-        jnp.concatenate([by_x[d][:, e * span : (e + 1) * span] for d in range(NX)], axis=1)
-        for e in range(NY)
-    ]
-    order1 = [taken(e, 1) for e in range(NX)]
-    own = [jnp.where(core == 0, a, b) for a, b in zip(order0, order1)]
-    other = [jnp.where(core == 0, b, a) for a, b in zip(order0, order1)]
-    features_in = own + other
-
-    def project(weights):
+
+    at = jnp.stack([x_me, y_me, core]).astype(jnp.int32)
+    blocks = [features[:, i * BLOCK : (i + 1) * BLOCK] for i in range(NX * NC)]
+    halves = [jnp.concatenate(blocks[c::NC], axis=1) for c in range(NC)]
+    theirs = swap_cores(jnp.where(core == 0, halves[1], halves[0]))
+    arranged = arrange(at, features, theirs)
+
+    def project(pieces):
         total = 0.0
-        for part, w in zip(features_in, weights):
-            total = total + jnp.dot(part, w, preferred_element_type=jnp.float32)
-        return total
+        rows = 2 * row_count
+        for e, piece in enumerate(pieces):
+            total = total + jnp.dot(
+                arranged[e * rows : (e + 1) * rows], piece, preferred_element_type=jnp.float32
+            )
+        return total[:row_count] + swap_cores(total[row_count:])
+
+    plane_q, plane_p = stack_planes(column, first, second, third)
+    two, one, three = (hop(plane_p, d, 1) for d in (2, 1, 3))
+    two_q, one_q, three_q = (hop(plane_q, d, 1) for d in (2, 1, 3))
+    pair_pre = project([plane_p, one, two, three])
 
     first_row = ctx * row_count
     query_index = first_row + jnp.arange(row_count, dtype=jnp.int32)
     cos_part, sin_part = angles_for(query_index - begin_rows, HD)
-    pair_pre = project(pair_w)
     pair_rows = jnp.concatenate(
         [rotate(pair_pre[:, :HD], cos_part, sin_part), pair_pre[:, HD:]], axis=1
     ).astype(jnp.bfloat16)
     near = jnp.concatenate([shifted(pair_rows, "ctx", 1), pair_rows], axis=0)
-    window = jnp.concatenate([shifted(near, "ctx", 2), near], axis=0)
+    near, one_q, two_q, three_q = lax.optimization_barrier((near, one_q, two_q, three_q))
+    query_pre = project([plane_q, one_q, two_q, three_q])
+    far, query_pre = lax.optimization_barrier((shifted(near, "ctx", 2), query_pre))
+    window = jnp.concatenate([far, near], axis=0)
+    pair_own = jnp.concatenate([plane_p, one, two, three], axis=0)
+    pair_other = swap_cores(pair_own)
+    plane_q_other = swap_cores(plane_q)
 
     queries = rotate(
-        project(query_w).reshape(row_count, HQ, HD), cos_part[:, None, :], sin_part[:, None, :]
+        query_pre.reshape(row_count, HQ, HD), cos_part[:, None, :], sin_part[:, None, :]
     ).astype(jnp.bfloat16)
     keys, values = window[:, :HD], window[:, HD:]
     key_index = first_row - (REACH - 1) * row_count + jnp.arange(REACH * row_count, dtype=jnp.int32)
@@ -162,39 +263,42 @@
         * score_scale
     )
     pair_grad = jnp.concatenate([grad_key, grad_value], axis=1)
-    far, near = pair_grad[: 2 * row_count], pair_grad[2 * row_count :]
-    near = near + shifted(far, "ctx", -2)
-    pair_total = near[row_count:] + shifted(near[:row_count], "ctx", -1)
-
     query_out = rotate(grad_query, cos_part[:, None, :], -sin_part[:, None, :]).reshape(
         row_count, HQ * HD
     ).astype(jnp.bfloat16)
+    far, near = pair_grad[: 2 * row_count], pair_grad[2 * row_count :]
+    one_q, two_q, three_q, query_out = lax.optimization_barrier((one_q, two_q, three_q, query_out))
+    swapped = [swap_cores(piece) for piece in (one_q, two_q, three_q)]
+    near = near + shifted(far, "ctx", -2)
+    query_part = query_part_of(
+        at, query_out, [plane_q, one_q, two_q, three_q, plane_q_other] + swapped
+    )
+
+    pair_w = [
+        w[i * BLOCK : (i + 1) * BLOCK] for w in (pair_own, pair_other) for i in range(NX)
+    ]
+    order = order_matrix(y_me)
+    order0 = [jnp.where(core == 0, a, b) for a, b in zip(pair_w[:NX], pair_w[NX:])]
+    order1 = [jnp.where(core == 0, b, a) for a, b in zip(pair_w[:NX], pair_w[NX:])]
+    pair_all = jnp.zeros((features.shape[1], 2 * HD), jnp.bfloat16)
+    for s in range(NX):
+        even = jnp.concatenate([order0[e][s * SPAN : (s + 1) * SPAN] for e in range(NY)], axis=0)
+        for c, part in ((0, even), (1, order1[s])):
+            back = jnp.dot(order, part, preferred_element_type=jnp.float32).astype(jnp.bfloat16)
+            place_at = ((x_me - s + NX) % NX * NC + c) * BLOCK
+            pair_all = lax.dynamic_update_slice_in_dim(pair_all, back, place_at, 0)
+
+    came, query_part, pair_all = lax.optimization_barrier(
+        (shifted(near[:row_count], "ctx", -1), query_part, pair_all)
+    )
+    pair_total = near[row_count:] + came
     pair_out = jnp.concatenate(
         [rotate(pair_total[:, :HD], cos_part, -sin_part), pair_total[:, HD:]], axis=1
     ).astype(jnp.bfloat16)
-
-    turn = (((1,), (1,)), ((), ()))
-    arrived = [
-        (
-            lax.dot_general(query_out, wq, turn, preferred_element_type=jnp.float32)
-            + lax.dot_general(pair_out, wp, turn, preferred_element_type=jnp.float32)
-        ).astype(jnp.bfloat16)
-        for wq, wp in zip(query_w, pair_w)
-    ]
-    own, other = arrived[:NX], arrived[NX:]
-    order0 = [jnp.where(core == 0, a, b) for a, b in zip(own, other)]
-    order1 = [jnp.where(core == 0, b, a) for a, b in zip(own, other)]
-    by_x = [
-        jnp.concatenate([order0[e][:, d * span : (d + 1) * span] for e in range(NY)], axis=1)
-        for d in range(NX)
-    ]
-    result = jnp.zeros(features.shape, jnp.bfloat16)
-    for s in range(NX):
-        for c, part in ((0, by_x[s]), (1, order1[s])):
-            at = ((x_me - s + NX) % NX * NC + c) * block
-            back = lax.dot_general(part, order, turn, preferred_element_type=jnp.float32)
-            result = lax.dynamic_update_slice_in_dim(result, back.astype(jnp.bfloat16), at, 1)
-    return result[None]
+    result = query_part + lax.dot_general(
+        pair_out, pair_all, TURN, preferred_element_type=jnp.float32
+    )
+    return result.astype(jnp.bfloat16)[None]
 
 
 def solution(mesh):

time: 188 us -> 170 us (0.904)
  the two profiles are of different devices: /device:TPU:24 before, /device:TPU:34 now
where the time goes in v2:
time: 170 us; the launch traced here: 169 us
  starting transfers between devices  62.4 us (37%)
  blocking collectives  35.3 us (21%)
  waiting for transfers between devices  18.5 us (11%)
  matrix products  14.7 us (9%)
  local copies, waits for them, and re-layouts  13.1 us (8%)
  other arithmetic  12.2 us (7%)
  Pallas kernels  11.8 us (7%)
    all_gather x1, blocking collectives, local(): lax.all_gather(w_qkv, 'ctx', axis=0, tiled=True, axis_index_groups=[[z *...  35.3 us
    ppermute x9, starting transfers between devices, hop(): return lax.ppermute(block, ALL, route(move))  30.3 us
    ppermute x8, starting transfers between devices, swap_cores(): return lax.ppermute(block, ALL, route(lambda x, c, z, y: (x, 1 - c, z, y)))  16.8 us
    ppermute x4, starting transfers between devices, shifted(): lax.ppermute(block, axis, [(i - distance, i) for i in devices if i - dist...  15.4 us
    ppermute x4, waiting for transfers between devices, shifted(): lax.ppermute(block, axis, [(i - distance, i) for i in devices if i - dist...  12 us
    pallas_call x1, Pallas kernels, query_part_of(): pl.pallas_call(query_part_body, in_specs=[pl.BlockSpec(memory_space=pltpu...  8.32 us
    unnamed x59, local copies, waits for them, and re-layouts  7.44 us
    ppermute x9, waiting for transfers between devices, hop(): return lax.ppermute(block, ALL, route(move))  6.51 us
  transfers between devices with their start and end apart: 21, of which 7 were waited for; matrix products, arithmetic and copies ran while one was open for 18% of the time, Pallas kernels for 7%

profile of v2, /device:TPU:34, one launch (start us, length us, event | category | flops | bytes accessed | tf_op | source)
XLA Modules:
  0.0 169.0 jit_solution(12578695045239375141)
XLA Ops:
  0.0 35.3 %all_gather.3.own = bf16[128,1280]{1,0:T(8,128)(2,1)S(1)} all-gather(bf16[8,1280]{1,0:T(8,128)(2,1)} %param.7), channel_id=1, replica_groups={{0,4,8,12,16,20,24,28,32,36,40,44,48,52,56,60},{1,5,9,13,17,21,25,29,33..., dimensions={0}, use_global_device_ids=true | all-gather | bytes 348160 | tf_op jit(solution)/shard_map/all_gather | solution.py:190
  35.4 3.4 %collective-permute-start.1 = (bf16[128,1280]{1,0:T(8,128)(2,1)S(1)}, bf16[128,1280]{1,0:T(8,128)(2,1)S(1)}, u32[]{:S(2)}, u32[]{:S(2)}) collective-permute-start(bf16[128,1280]{1,0:T(8,128)(2,1)S(1)} %all_gather.3.own), channel_id=1, source_target_pairs={{0,128},{1,129},{2,130},{3,131},{4,132},{5,133},{6,134},{7,135},{8... | collective-permute-start | bytes 983048 | tf_op jit(solution)/shard_map/ppermute | solution.py:39
  38.7 3.0 %collective-permute-start.2 = (bf16[128,1280]{1,0:T(8,128)(2,1)S(1)}, bf16[128,1280]{1,0:T(8,128)(2,1)S(1)}, u32[]{:S(2)}, u32[]{:S(2)}) collective-permute-start(bf16[128,1280]{1,0:T(8,128)(2,1)S(1)} %all_gather.3.own), channel_id=1, source_target_pairs={{0,256},{1,257},{2,258},{3,259},{4,260},{5,261},{6,262},{7,263},{8... | collective-permute-start | bytes 983048 | tf_op jit(solution)/shard_map/ppermute | solution.py:39
  41.8 4.1 %collective-permute-start.3 = (bf16[128,1280]{1,0:T(8,128)(2,1)S(1)}, bf16[128,1280]{1,0:T(8,128)(2,1)S(1)}, u32[]{:S(2)}, u32[]{:S(2)}) collective-permute-start(bf16[128,1280]{1,0:T(8,128)(2,1)S(1)} %all_gather.3.own), channel_id=1, source_target_pairs={{0,384},{1,385},{2,386},{3,387},{4,388},{5,389},{6,390},{7,391},{8... | collective-permute-start | bytes 983048 | tf_op jit(solution)/shard_map/ppermute | solution.py:39
  45.9 1.4 fusion.137
  47.4 1.9 %collective-permute-start = (bf16[128,2048]{1,0:T(8,128)(2,1)S(1)}, bf16[128,2048]{1,0:T(8,128)(2,1)}, u32[]{:S(2)}, u32[]{:S(2)}) collective-permute-start(bf16[128,2048]{1,0:T(8,128)(2,1)S(1)} %maximum_select_fusion), channel_id=1, source_target_pairs={{0,64},{1,65},{2,66},{3,67},{4,68},{5,69},{6,70},{7,71},{8,72},{9,... | collective-permute-start | bytes 1572872 | tf_op jit(solution)/shard_map/ppermute | solution.py:43
  51.3 1.4 collective-permute-done.3.third
  52.7 1.1 shard_map.47
  53.8 4.9 %collective-permute-start.6 = (bf16[512,256]{1,0:T(8,128)(2,1)S(1)}, bf16[512,256]{1,0:T(8,128)(2,1)S(1)}, u32[]{:S(2)}, u32[]{:S(2)}) collective-permute-start(bf16[512,256]{1,0:T(8,128)(2,1)S(1)} %get-tuple-element.20), channel_id=1, source_target_pairs={{0,3},{1,0},{2,1},{3,2},{4,7},{5,4},{6,5},{7,6},{8,11},{9,8},{10,9... | collective-permute-start | bytes 786440 | tf_op jit(solution)/shard_map/ppermute | solution.py:39
  58.7 2.5 %collective-permute-start.5 = (bf16[512,256]{1,0:T(8,128)(2,1)S(1)}, bf16[512,256]{1,0:T(8,128)(2,1)S(1)}, u32[]{:S(2)}, u32[]{:S(2)}) collective-permute-start(bf16[512,256]{1,0:T(8,128)(2,1)S(1)} %get-tuple-element.20), channel_id=1, source_target_pairs={{0,2},{1,3},{2,0},{3,1},{4,6},{5,7},{6,4},{7,5},{8,10},{9,11},{10,... | collective-permute-start | bytes 786440 | tf_op jit(solution)/shard_map/ppermute | solution.py:39
  61.3 2.9 %collective-permute-start.4 = (bf16[512,256]{1,0:T(8,128)(2,1)S(1)}, bf16[512,256]{1,0:T(8,128)(2,1)S(1)}, u32[]{:S(2)}, u32[]{:S(2)}) collective-permute-start(bf16[512,256]{1,0:T(8,128)(2,1)S(1)} %get-tuple-element.20), channel_id=1, source_target_pairs={{0,1},{1,2},{2,3},{3,0},{4,5},{5,6},{6,7},{7,4},{8,9},{9,10},{10,1... | collective-permute-start | bytes 786440 | tf_op jit(solution)/shard_map/ppermute | solution.py:39
  64.2 1.2 copy-done
  65.4 2.4 %shard_map.46 = bf16[1024,512]{1,0:T(8,128)(2,1)S(1)} custom-call(s32[3]{0:T(128)S(1)} %pad_add_fusion.at, bf16[128,4096]{1,0:T(8,128)(2,1)S(1)} %bitcast.71, bf16[128,2048]{1,0:T(8,128)(2,1)} %collective-permute-done.theirs), custom_call_target="tpu_custom_call" | custom-call | flops 536870912 | bytes 4194304 | tf_op jit(solution)/shard_map/pallas_call | solution.py:87
  68.8 2.5 %collective-permute-done.4 = bf16[512,256]{1,0:T(8,128)(2,1)S(1)} collective-permute-done((bf16[512,256]{1,0:T(8,128)(2,1)S(1)}, bf16[512,256]{1,0:T(8,128)(2,1)S(1)}, u32[]{:S(2)}, u32[]{:S(2)}) %collective-permute-start.4) | collective-permute-done | bytes 262176 | tf_op jit(solution)/shard_map/ppermute | solution.py:39
  72.6 1.9 %collective-permute-start.7 = (f32[128,256]{0,1:T(8,128)}, f32[128,256]{0,1:T(8,128)S(1)}, u32[]{:S(2)}, u32[]{:S(2)}) collective-permute-start(f32[128,256]{0,1:T(8,128)} %slice.233), channel_id=1, source_target_pairs={{0,64},{1,65},{2,66},{3,67},{4,68},{5,69},{6,70},{7,71},{8,72},{9,... | collective-permute-start | bytes 393224 | tf_op jit(solution)/shard_map/ppermute | solution.py:43
  75.1 0.9 copy.10
  76.0 1.9 %collective-permute-start.9 = (bf16[512,1024]{1,0:T(8,128)(2,1)}, bf16[512,1024]{1,0:T(8,128)(2,1)S(1)}, u32[]{:S(2)}, u32[]{:S(2)}) collective-permute-start(bf16[512,1024]{1,0:T(8,128)(2,1)} %get-tuple-element.21.refs_0_), channel_id=1, source_target_pairs={{0,1},{1,2},{2,3},{3,0},{4,5},{5,6},{6,7},{7,4},{8,9},{9,10},{10,1... | collective-permute-start | bytes 3145736 | tf_op jit(solution)/shard_map/ppermute | solution.py:39
  77.9 3.9 %collective-permute-start.10 = (bf16[512,1024]{1,0:T(8,128)(2,1)}, bf16[512,1024]{1,0:T(8,128)(2,1)S(1)}, u32[]{:S(2)}, u32[]{:S(2)}) collective-permute-start(bf16[512,1024]{1,0:T(8,128)(2,1)} %get-tuple-element.21.refs_0_), channel_id=1, source_target_pairs={{0,2},{1,3},{2,0},{3,1},{4,6},{5,7},{6,4},{7,5},{8,10},{9,11},{10,... | collective-permute-start | bytes 3145736 | tf_op jit(solution)/shard_map/ppermute | solution.py:39
  81.8 3.6 %collective-permute-start.11 = (bf16[512,1024]{1,0:T(8,128)(2,1)}, bf16[512,1024]{1,0:T(8,128)(2,1)}, u32[]{:S(2)}, u32[]{:S(2)}) collective-permute-start(bf16[512,1024]{1,0:T(8,128)(2,1)} %get-tuple-element.21.refs_0_), channel_id=1, source_target_pairs={{0,3},{1,0},{2,1},{3,2},{4,7},{5,4},{6,5},{7,6},{8,11},{9,8},{10,9... | collective-permute-start | bytes 3145736 | tf_op jit(solution)/shard_map/ppermute | solution.py:39
  85.5 2.1 %collective-permute-start.16 = (bf16[512,1024]{1,0:T(8,128)(2,1)}, bf16[512,1024]{1,0:T(8,128)(2,1)}, u32[]{:S(2)}, u32[]{:S(2)}) collective-permute-start(bf16[512,1024]{1,0:T(8,128)(2,1)} %get-tuple-element.21.refs_0_), channel_id=1, source_target_pairs={{0,64},{1,65},{2,66},{3,67},{4,68},{5,69},{6,70},{7,71},{8,72},{9,... | collective-permute-start | bytes 3145736 | tf_op jit(solution)/shard_map/ppermute | solution.py:43
  87.6 0.9 slice_add_fusion.2
  88.5 0.8 fusion.105
  90.0 2.1 %collective-permute-start.8 = (bf16[128,256]{0,1:T(8,128)(2,1)}, bf16[128,256]{0,1:T(8,128)(2,1)}, u32[]{:S(2)}, u32[]{:S(2)}) collective-permute-start(bf16[128,256]{0,1:T(8,128)(2,1)} %pad_maximum_fusion.3), channel_id=1, source_target_pairs={{0,1},{1,2},{2,3},{3,4},{4,5},{5,6},{6,7},{7,8},{8,9},{9,10},{10,1... | collective-permute-start | bytes 196616 | tf_op jit(solution)/shard_map/ppermute | solution.py:161
  92.1 2.2 %pad_maximum_fusion = bf16[2048,256]{1,0:T(8,128)(2,1)} fusion(bf16[512,256]{1,0:T(8,128)(2,1)} %copy-done.5, bf16[512,256]{1,0:T(8,128)(2,1)} %copy-done.8, bf16[512,256]{1,0:T(8,128)(2,1)} %copy-done.10, bf16[512,256]{1,0:T(8,128)(2,1)S(1)} %get-tuple-element.20), kind=kLoop, calls=%fused_computation.60 | loop fusion | flops 4194304 | bytes 2097152 | tf_op jit(solution)/shard_map/concatenate | solution.py:227
  95.0 0.8 copy.6
  95.8 1.5 copy.19
  97.3 5.9 %collective-permute-done.8 = bf16[128,256]{0,1:T(8,128)(2,1)} collective-permute-done((bf16[128,256]{0,1:T(8,128)(2,1)}, bf16[128,256]{0,1:T(8,128)(2,1)}, u32[]{:S(2)}, u32[]{:S(2)}) %collective-permute-start.8) | collective-permute-done | bytes 65568 | tf_op jit(solution)/shard_map/ppermute | solution.py:161
  103.2 1.9 %collective-permute-start.20 = (bf16[2048,256]{1,0:T(8,128)(2,1)}, bf16[2048,256]{1,0:T(8,128)(2,1)S(1)}, u32[]{:S(2)}, u32[]{:S(2)}) collective-permute-start(bf16[2048,256]{1,0:T(8,128)(2,1)} %pad_maximum_fusion), channel_id=1, source_target_pairs={{0,64},{1,65},{2,66},{3,67},{4,68},{5,69},{6,70},{7,71},{8,72},{9,... | collective-permute-start | bytes 3145736 | tf_op jit(solution)/shard_map/ppermute | solution.py:43
  105.1 0.9 maximum_maximum_fusion
  106.7 1.5 collective-permute-done.11.refs_3_
  108.2 3.9 %collective-permute-start.12 = (bf16[256,256]{0,1:T(8,128)(2,1)S(1)}, bf16[256,256]{0,1:T(8,128)(2,1)S(1)}, u32[]{:S(2)}, u32[]{:S(2)}) collective-permute-start(bf16[256,256]{0,1:T(8,128)(2,1)S(1)} %maximum_maximum_fusion), channel_id=1, source_target_pairs={{0,2},{1,3},{2,4},{3,5},{4,6},{5,7},{6,8},{7,9},{8,10},{9,11},{10,... | collective-permute-start | bytes 393224 | tf_op jit(solution)/shard_map/ppermute | solution.py:161
  112.1 1.7 fusion.78
  114.7 1.8 %fusion.5 = f32[256,1024]{1,0:T(8,128)S(1)} fusion(f32[256,1024]{1,0:T(8,128)S(1)} %fusion.78, f32[256,1024]{1,0:T(8,128)S(1)} %fusion.82, f32[256,1024]{1,0:T(8,128)S(1)} %fusion.86, bf16[512,1024]{1,0:T(8,128)(2,1)} %get-tuple-element.21.refs_0_, bf16[1024,512]{1,0:T(8,128)(2,1)S(1)} %shard_map.46), kind=kOutput, calls=%fused_computation.21 | convolution fusion | flops 269221888 | bytes 5505024 | tf_op jit(solution)/shard_map/dot_general | solution.py:206
  116.6 2.3 %collective-permute-start.13 = (f32[128,1024]{1,0:T(8,128)S(1)}, f32[128,1024]{1,0:T(8,128)S(1)}, u32[]{:S(2)}, u32[]{:S(2)}) collective-permute-start(f32[128,1024]{1,0:T(8,128)S(1)} %slice.238), channel_id=1, source_target_pairs={{0,64},{1,65},{2,66},{3,67},{4,68},{5,69},{6,70},{7,71},{8,72},{9,... | collective-permute-start | bytes 1572872 | tf_op jit(solution)/shard_map/ppermute | solution.py:43
  122.7 0.9 copy-done.1
  123.8 2.4 %fusion.143 = (f32[8,128]{1,0:T(8,128)S(1)}, f32[8,128,512]{1,2,0:T(8,128)}) fusion(pred[128,512]{0,1:T(8,128)(4,1)S(1)} %copy-done.21, bf16[512,256]{0,1:T(8,128)(2,1)S(1)} %constant_dynamic-update-slice_fusion, bf16[128,8,64]{2,0,1:T(8,128)(2,1)S(1)} %get-tuple-element.36, bf16[128,8,64]{2,0,1:T(8,128)(2,1)S(1)} %get-tuple-element.35), kind=kOutput, calls=%fused_computation.203 | convolution fusion | flops 137363968 | bytes 2887680 | tf_op jit(solution)/shard_map/sub | solution.py:244
  126.2 1.8 %fusion.35 = bf16[8,128,512]{1,2,0:T(8,128)(2,1)S(1)} fusion(f32[8,128,512]{1,2,0:T(8,128)} %get-tuple-element.79, f32[8,128]{1,0:T(8,128)S(1)} %get-tuple-element.78), kind=kLoop, calls=%fused_computation.66 | loop fusion | flops 1048576 | bytes 3149824 | tf_op jit(solution)/shard_map/convert_element_type | solution.py:246
  131.1 2.3 %collective-permute-start.17 = (bf16[512,1024]{1,0:T(8,128)(2,1)S(1)}, bf16[512,1024]{1,0:T(8,128)(2,1)S(1)}, u32[]{:S(2)}, u32[]{:S(2)}) collective-permute-start(bf16[512,1024]{1,0:T(8,128)(2,1)S(1)} %collective-permute-done.9.refs_1_), channel_id=1, source_target_pairs={{0,64},{1,65},{2,66},{3,67},{4,68},{5,69},{6,70},{7,71},{8,72},{9,... | collective-permute-start | bytes 3145736 | tf_op jit(solution)/shard_map/ppermute | solution.py:43
  133.4 2.1 %collective-permute-start.18 = (bf16[512,1024]{1,0:T(8,128)(2,1)S(1)}, bf16[512,1024]{1,0:T(8,128)(2,1)S(1)}, u32[]{:S(2)}, u32[]{:S(2)}) collective-permute-start(bf16[512,1024]{1,0:T(8,128)(2,1)S(1)} %collective-permute-done.10.refs_2_), channel_id=1, source_target_pairs={{0,64},{1,65},{2,66},{3,67},{4,68},{5,69},{6,70},{7,71},{8,72},{9,... | collective-permute-start | bytes 3145736 | tf_op jit(solution)/shard_map/ppermute | solution.py:43
  135.5 2.2 %collective-permute-start.19 = (bf16[512,1024]{1,0:T(8,128)(2,1)}, bf16[512,1024]{1,0:T(8,128)(2,1)S(1)}, u32[]{:S(2)}, u32[]{:S(2)}) collective-permute-start(bf16[512,1024]{1,0:T(8,128)(2,1)} %collective-permute-done.11.refs_3_), channel_id=1, source_target_pairs={{0,64},{1,65},{2,66},{3,67},{4,68},{5,69},{6,70},{7,71},{8,72},{9,... | collective-permute-start | bytes 3145736 | tf_op jit(solution)/shard_map/ppermute | solution.py:43
  138.3 4.4 %collective-permute-start.14 = (f32[256,256]{0,1:T(8,128)S(1)}, f32[256,256]{0,1:T(8,128)S(1)}, u32[]{:S(2)}, u32[]{:S(2)}) collective-permute-start(f32[256,256]{0,1:T(8,128)S(1)} %pad_maximum_fusion.1), channel_id=1, source_target_pairs={{2,0},{3,1},{4,2},{5,3},{6,4},{7,5},{8,6},{9,7},{10,8},{11,9},{12,... | collective-permute-start | bytes 786440 | tf_op jit(solution)/shard_map/ppermute | solution.py:161
  142.8 1.3 fusion.7
  144.1 6.1 %collective-permute-done.14 = f32[256,256]{0,1:T(8,128)S(1)} collective-permute-done((f32[256,256]{0,1:T(8,128)S(1)}, f32[256,256]{0,1:T(8,128)S(1)}, u32[]{:S(2)}, u32[]{:S(2)}) %collective-permute-start.14) | collective-permute-done | bytes 262176 | tf_op jit(solution)/shard_map/ppermute | solution.py:161
  150.2 5.1 %collective-permute-start.15 = (f32[128,256]{0,1:T(8,128)S(1)}, f32[128,256]{0,1:T(8,128)S(1)}, u32[]{:S(2)}, u32[]{:S(2)}) collective-permute-start(f32[128,256]{0,1:T(8,128)S(1)} %slice.245), channel_id=1, source_target_pairs={{1,0},{2,1},{3,2},{4,3},{5,4},{6,5},{7,6},{8,7},{9,8},{10,9},{11,1... | collective-permute-start | bytes 393224 | tf_op jit(solution)/shard_map/ppermute | solution.py:161
  155.4 0.9 copy-done.15
  156.7 1.0 copy-done.17
  157.6 8.3 %shard_map.48 = f32[128,4096]{1,0:T(8,128)} custom-call(s32[3]{0:T(128)S(1)} %pad_add_fusion.at, bf16[128,1024]{1,0:T(8,128)(2,1)S(1)} %copy_bitcast_fusion.grads, bf16[512,1024]{1,0:T(8,128)(2,1)} %get-tuple-element.21.refs_0_, bf16[512,1024]{1,0:T(8,128)(2,1)S(1)} %collective-permute-done.9.refs_1_, bf16[512,1024]{1,0:T(8,128)(2,1)S(1)} %collective-permute-done.10.refs_2_, ...), custom_call_target="tpu_custom_call" | custom-call | flops 2147483648 | bytes 12582912 | tf_op jit(solution)/shard_map/pallas_call | solution.py:144
  167.8 1.2 fusion.27
  (120 shorter events, 17.7 us)
Async XLA Ops:
  0.0 50.6 %copy-start.25 = (s32[1,128]{1,0:T(1,128)S(1)}, s32[1,128]{1,0:T(1,128)}, u32[]{:S(2)}) copy-start(s32[1,128]{1,0:T(1,128)} %param.5) | copy-start | bytes 1540
  35.4 16.0 %collective-permute-start.1 = (bf16[128,1280]{1,0:T(8,128)(2,1)S(1)}, bf16[128,1280]{1,0:T(8,128)(2,1)S(1)}, u32[]{:S(2)}, u32[]{:S(2)}) collective-permute-start(bf16[128,1280]{1,0:T(8,128)(2,1)S(1)} %all_gather.3.own), channel_id=1, source_target_pairs={{0,128},{1,129},{2,130},{3,131},{4,132},{5,133},{6,134},{7,135},{8... | collective-permute-start | bytes 983048 | tf_op jit(solution)/shard_map/ppermute | solution.py:39
  38.7 12.6 %collective-permute-start.2 = (bf16[128,1280]{1,0:T(8,128)(2,1)S(1)}, bf16[128,1280]{1,0:T(8,128)(2,1)S(1)}, u32[]{:S(2)}, u32[]{:S(2)}) collective-permute-start(bf16[128,1280]{1,0:T(8,128)(2,1)S(1)} %all_gather.3.own), channel_id=1, source_target_pairs={{0,256},{1,257},{2,258},{3,259},{4,260},{5,261},{6,262},{7,263},{8... | collective-permute-start | bytes 983048 | tf_op jit(solution)/shard_map/ppermute | solution.py:39
  41.8 11.0 %collective-permute-start.3 = (bf16[128,1280]{1,0:T(8,128)(2,1)S(1)}, bf16[128,1280]{1,0:T(8,128)(2,1)S(1)}, u32[]{:S(2)}, u32[]{:S(2)}) collective-permute-start(bf16[128,1280]{1,0:T(8,128)(2,1)S(1)} %all_gather.3.own), channel_id=1, source_target_pairs={{0,384},{1,385},{2,386},{3,387},{4,388},{5,389},{6,390},{7,391},{8... | collective-permute-start | bytes 983048 | tf_op jit(solution)/shard_map/ppermute | solution.py:39
  47.4 16.8 %collective-permute-start = (bf16[128,2048]{1,0:T(8,128)(2,1)S(1)}, bf16[128,2048]{1,0:T(8,128)(2,1)}, u32[]{:S(2)}, u32[]{:S(2)}) collective-permute-start(bf16[128,2048]{1,0:T(8,128)(2,1)S(1)} %maximum_select_fusion), channel_id=1, source_target_pairs={{0,64},{1,65},{2,66},{3,67},{4,68},{5,69},{6,70},{7,71},{8,72},{9,... | collective-permute-start | bytes 1572872 | tf_op jit(solution)/shard_map/ppermute | solution.py:43
  53.8 14.1 %collective-permute-start.6 = (bf16[512,256]{1,0:T(8,128)(2,1)S(1)}, bf16[512,256]{1,0:T(8,128)(2,1)S(1)}, u32[]{:S(2)}, u32[]{:S(2)}) collective-permute-start(bf16[512,256]{1,0:T(8,128)(2,1)S(1)} %get-tuple-element.20), channel_id=1, source_target_pairs={{0,3},{1,0},{2,1},{3,2},{4,7},{5,4},{6,5},{7,6},{8,11},{9,8},{10,9... | collective-permute-start | bytes 786440 | tf_op jit(solution)/shard_map/ppermute | solution.py:39
  58.7 9.8 %collective-permute-start.5 = (bf16[512,256]{1,0:T(8,128)(2,1)S(1)}, bf16[512,256]{1,0:T(8,128)(2,1)S(1)}, u32[]{:S(2)}, u32[]{:S(2)}) collective-permute-start(bf16[512,256]{1,0:T(8,128)(2,1)S(1)} %get-tuple-element.20), channel_id=1, source_target_pairs={{0,2},{1,3},{2,0},{3,1},{4,6},{5,7},{6,4},{7,5},{8,10},{9,11},{10,... | collective-permute-start | bytes 786440 | tf_op jit(solution)/shard_map/ppermute | solution.py:39
  61.3 10.0 %collective-permute-start.4 = (bf16[512,256]{1,0:T(8,128)(2,1)S(1)}, bf16[512,256]{1,0:T(8,128)(2,1)S(1)}, u32[]{:S(2)}, u32[]{:S(2)}) collective-permute-start(bf16[512,256]{1,0:T(8,128)(2,1)S(1)} %get-tuple-element.20), channel_id=1, source_target_pairs={{0,1},{1,2},{2,3},{3,0},{4,5},{5,6},{6,7},{7,4},{8,9},{9,10},{10,1... | collective-permute-start | bytes 786440 | tf_op jit(solution)/shard_map/ppermute | solution.py:39
  64.2 1.2 copy-start
  67.8 7.3 %copy-start.18 = (bf16[1,128,1024]{2,1,0:T(8,128)(2,1)S(1)}, bf16[1,128,1024]{2,1,0:T(8,128)(2,1)}, u32[]{:S(2)}) copy-start(bf16[1,128,1024]{2,1,0:T(8,128)(2,1)} %param.6) | copy-start | bytes 786436
  67.9 4.7 %copy-start.5 = (bf16[512,256]{1,0:T(8,128)(2,1)}, bf16[512,256]{1,0:T(8,128)(2,1)S(1)}, u32[]{:S(2)}) copy-start(bf16[512,256]{1,0:T(8,128)(2,1)S(1)} %collective-permute-done.6) | copy-start | bytes 786436
  68.5 6.0 %copy-start.8 = (bf16[512,256]{1,0:T(8,128)(2,1)}, bf16[512,256]{1,0:T(8,128)(2,1)S(1)}, u32[]{:S(2)}) copy-start(bf16[512,256]{1,0:T(8,128)(2,1)S(1)} %collective-permute-done.5) | copy-start | bytes 786436
  71.3 3.2 %copy-start.10 = (bf16[512,256]{1,0:T(8,128)(2,1)}, bf16[512,256]{1,0:T(8,128)(2,1)S(1)}, u32[]{:S(2)}) copy-start(bf16[512,256]{1,0:T(8,128)(2,1)S(1)} %collective-permute-done.4) | copy-start | bytes 786436
  71.9 2.7 %copy-start.14 = (f32[256,256]{0,1:T(8,128)}, f32[256,256]{0,1:T(8,128)S(1)}, u32[]{:S(2)}) copy-start(f32[256,256]{0,1:T(8,128)S(1)} %fusion.20) | copy-start | bytes 786436
  72.6 15.0 %collective-permute-start.7 = (f32[128,256]{0,1:T(8,128)}, f32[128,256]{0,1:T(8,128)S(1)}, u32[]{:S(2)}, u32[]{:S(2)}) collective-permute-start(f32[128,256]{0,1:T(8,128)} %slice.233), channel_id=1, source_target_pairs={{0,64},{1,65},{2,66},{3,67},{4,68},{5,69},{6,70},{7,71},{8,72},{9,... | collective-permute-start | bytes 393224 | tf_op jit(solution)/shard_map/ppermute | solution.py:43
  76.0 30.7 %collective-permute-start.9 = (bf16[512,1024]{1,0:T(8,128)(2,1)}, bf16[512,1024]{1,0:T(8,128)(2,1)S(1)}, u32[]{:S(2)}, u32[]{:S(2)}) collective-permute-start(bf16[512,1024]{1,0:T(8,128)(2,1)} %get-tuple-element.21.refs_0_), channel_id=1, source_target_pairs={{0,1},{1,2},{2,3},{3,0},{4,5},{5,6},{6,7},{7,4},{8,9},{9,10},{10,1... | collective-permute-start | bytes 3145736 | tf_op jit(solution)/shard_map/ppermute | solution.py:39
  77.9 28.8 %collective-permute-start.10 = (bf16[512,1024]{1,0:T(8,128)(2,1)}, bf16[512,1024]{1,0:T(8,128)(2,1)S(1)}, u32[]{:S(2)}, u32[]{:S(2)}) collective-permute-start(bf16[512,1024]{1,0:T(8,128)(2,1)} %get-tuple-element.21.refs_0_), channel_id=1, source_target_pairs={{0,2},{1,3},{2,0},{3,1},{4,6},{5,7},{6,4},{7,5},{8,10},{9,11},{10,... | collective-permute-start | bytes 3145736 | tf_op jit(solution)/shard_map/ppermute | solution.py:39
  81.8 26.4 %collective-permute-start.11 = (bf16[512,1024]{1,0:T(8,128)(2,1)}, bf16[512,1024]{1,0:T(8,128)(2,1)}, u32[]{:S(2)}, u32[]{:S(2)}) collective-permute-start(bf16[512,1024]{1,0:T(8,128)(2,1)} %get-tuple-element.21.refs_0_), channel_id=1, source_target_pairs={{0,3},{1,0},{2,1},{3,2},{4,7},{5,4},{6,5},{7,6},{8,11},{9,8},{10,9... | collective-permute-start | bytes 3145736 | tf_op jit(solution)/shard_map/ppermute | solution.py:39
  85.5 69.8 %collective-permute-start.16 = (bf16[512,1024]{1,0:T(8,128)(2,1)}, bf16[512,1024]{1,0:T(8,128)(2,1)}, u32[]{:S(2)}, u32[]{:S(2)}) collective-permute-start(bf16[512,1024]{1,0:T(8,128)(2,1)} %get-tuple-element.21.refs_0_), channel_id=1, source_target_pairs={{0,64},{1,65},{2,66},{3,67},{4,68},{5,69},{6,70},{7,71},{8,72},{9,... | collective-permute-start | bytes 3145736 | tf_op jit(solution)/shard_map/ppermute | solution.py:43
  90.0 13.2 %collective-permute-start.8 = (bf16[128,256]{0,1:T(8,128)(2,1)}, bf16[128,256]{0,1:T(8,128)(2,1)}, u32[]{:S(2)}, u32[]{:S(2)}) collective-permute-start(bf16[128,256]{0,1:T(8,128)(2,1)} %pad_maximum_fusion.3), channel_id=1, source_target_pairs={{0,1},{1,2},{2,3},{3,4},{4,5},{5,6},{6,7},{7,8},{8,9},{9,10},{10,1... | collective-permute-start | bytes 196616 | tf_op jit(solution)/shard_map/ppermute | solution.py:161
  103.2 15.7 %collective-permute-start.20 = (bf16[2048,256]{1,0:T(8,128)(2,1)}, bf16[2048,256]{1,0:T(8,128)(2,1)S(1)}, u32[]{:S(2)}, u32[]{:S(2)}) collective-permute-start(bf16[2048,256]{1,0:T(8,128)(2,1)} %pad_maximum_fusion), channel_id=1, source_target_pairs={{0,64},{1,65},{2,66},{3,67},{4,68},{5,69},{6,70},{7,71},{8,72},{9,... | collective-permute-start | bytes 3145736 | tf_op jit(solution)/shard_map/ppermute | solution.py:43
  108.2 14.1 %collective-permute-start.12 = (bf16[256,256]{0,1:T(8,128)(2,1)S(1)}, bf16[256,256]{0,1:T(8,128)(2,1)S(1)}, u32[]{:S(2)}, u32[]{:S(2)}) collective-permute-start(bf16[256,256]{0,1:T(8,128)(2,1)S(1)} %maximum_maximum_fusion), channel_id=1, source_target_pairs={{0,2},{1,3},{2,4},{3,5},{4,6},{5,7},{6,8},{7,9},{8,10},{9,11},{10,... | collective-permute-start | bytes 393224 | tf_op jit(solution)/shard_map/ppermute | solution.py:161
  114.7 4.2 %copy-start.6 = (bf16[512,256]{1,0:T(8,128)(2,1)S(1)}, bf16[512,256]{1,0:T(8,128)(2,1)}, u32[]{:S(2)}) copy-start(bf16[512,256]{1,0:T(8,128)(2,1)} %copy-done.5) | copy-start | bytes 786436
  114.7 4.2 %copy-start.9 = (bf16[512,256]{1,0:T(8,128)(2,1)S(1)}, bf16[512,256]{1,0:T(8,128)(2,1)}, u32[]{:S(2)}) copy-start(bf16[512,256]{1,0:T(8,128)(2,1)} %copy-done.8) | copy-start | bytes 786436
  114.7 4.2 %copy-start.11 = (bf16[512,256]{1,0:T(8,128)(2,1)S(1)}, bf16[512,256]{1,0:T(8,128)(2,1)}, u32[]{:S(2)}) copy-start(bf16[512,256]{1,0:T(8,128)(2,1)} %copy-done.10) | copy-start | bytes 786436
  116.6 5.7 %collective-permute-start.13 = (f32[128,1024]{1,0:T(8,128)S(1)}, f32[128,1024]{1,0:T(8,128)S(1)}, u32[]{:S(2)}, u32[]{:S(2)}) collective-permute-start(f32[128,1024]{1,0:T(8,128)S(1)} %slice.238), channel_id=1, source_target_pairs={{0,64},{1,65},{2,66},{3,67},{4,68},{5,69},{6,70},{7,71},{8,72},{9,... | collective-permute-start | bytes 1572872 | tf_op jit(solution)/shard_map/ppermute | solution.py:43
  118.9 2.6 %copy-start.13 = (bf16[2048,256]{1,0:T(8,128)(2,1)}, bf16[2048,256]{1,0:T(8,128)(2,1)S(1)}, u32[]{:S(2)}) copy-start(bf16[2048,256]{1,0:T(8,128)(2,1)S(1)} %collective-permute-done.20) | copy-start | bytes 3145732
  119.1 0.7 copy-start.22
  119.1 0.7 copy-start.24
  119.1 0.7 copy-start.26
  119.1 0.7 copy-start.27
  122.2 1.3 copy-start.1
  122.3 1.3 copy-start.20
  122.5 1.3 copy-start.21
  126.2 1.8 %copy-start.4 = (bf16[1,128,1024]{1,2,0:T(8,128)(2,1)S(1)}, bf16[1,128,1024]{1,2,0:T(8,128)(2,1)}, u32[]{:S(2)}) copy-start(bf16[1,128,1024]{1,2,0:T(8,128)(2,1)} %copy.10) | copy-start | bytes 786436
  128.0 1.6 copy-start.12
  129.6 1.0 copy-start.19
  130.9 11.8 %copy-start.2 = (bf16[4096,256]{1,0:T(8,128)(2,1)S(1)}, bf16[4096,256]{1,0:T(8,128)(2,1)}, u32[]{:S(2)}) copy-start(bf16[4096,256]{1,0:T(8,128)(2,1)} %copy-done.1) | copy-start | bytes 6291460
  130.9 11.8 %copy-start.7 = (bf16[512,256]{1,0:T(8,128)(2,1)S(1)}, bf16[512,256]{1,0:T(8,128)(2,1)}, u32[]{:S(2)}) copy-start(bf16[512,256]{1,0:T(8,128)(2,1)} %copy-done.5) | copy-start | bytes 786436
  131.1 24.2 %collective-permute-start.17 = (bf16[512,1024]{1,0:T(8,128)(2,1)S(1)}, bf16[512,1024]{1,0:T(8,128)(2,1)S(1)}, u32[]{:S(2)}, u32[]{:S(2)}) collective-permute-start(bf16[512,1024]{1,0:T(8,128)(2,1)S(1)} %collective-permute-done.9.refs_1_), channel_id=1, source_target_pairs={{0,64},{1,65},{2,66},{3,67},{4,68},{5,69},{6,70},{7,71},{8,72},{9,... | collective-permute-start | bytes 3145736 | tf_op jit(solution)/shard_map/ppermute | solution.py:43
  133.4 21.9 %collective-permute-start.18 = (bf16[512,1024]{1,0:T(8,128)(2,1)S(1)}, bf16[512,1024]{1,0:T(8,128)(2,1)S(1)}, u32[]{:S(2)}, u32[]{:S(2)}) collective-permute-start(bf16[512,1024]{1,0:T(8,128)(2,1)S(1)} %collective-permute-done.10.refs_2_), channel_id=1, source_target_pairs={{0,64},{1,65},{2,66},{3,67},{4,68},{5,69},{6,70},{7,71},{8,72},{9,... | collective-permute-start | bytes 3145736 | tf_op jit(solution)/shard_map/ppermute | solution.py:43
  135.5 19.8 %collective-permute-start.19 = (bf16[512,1024]{1,0:T(8,128)(2,1)}, bf16[512,1024]{1,0:T(8,128)(2,1)S(1)}, u32[]{:S(2)}, u32[]{:S(2)}) collective-permute-start(bf16[512,1024]{1,0:T(8,128)(2,1)} %collective-permute-done.11.refs_3_), channel_id=1, source_target_pairs={{0,64},{1,65},{2,66},{3,67},{4,68},{5,69},{6,70},{7,71},{8,72},{9,... | collective-permute-start | bytes 3145736 | tf_op jit(solution)/shard_map/ppermute | solution.py:43
  138.3 11.8 %collective-permute-start.14 = (f32[256,256]{0,1:T(8,128)S(1)}, f32[256,256]{0,1:T(8,128)S(1)}, u32[]{:S(2)}, u32[]{:S(2)}) collective-permute-start(f32[256,256]{0,1:T(8,128)S(1)} %pad_maximum_fusion.1), channel_id=1, source_target_pairs={{2,0},{3,1},{4,2},{5,3},{6,4},{7,5},{8,6},{9,7},{10,8},{11,9},{12,... | collective-permute-start | bytes 786440 | tf_op jit(solution)/shard_map/ppermute | solution.py:161
  150.2 15.7 %collective-permute-start.15 = (f32[128,256]{0,1:T(8,128)S(1)}, f32[128,256]{0,1:T(8,128)S(1)}, u32[]{:S(2)}, u32[]{:S(2)}) collective-permute-start(f32[128,256]{0,1:T(8,128)S(1)} %slice.245), channel_id=1, source_target_pairs={{1,0},{2,1},{3,2},{4,3},{5,4},{6,5},{7,6},{8,7},{9,8},{10,9},{11,1... | collective-permute-start | bytes 393224 | tf_op jit(solution)/shard_map/ppermute | solution.py:161
  155.3 1.0 copy-start.15
  155.3 1.3 copy-start.16
  156.7 1.0 copy-start.17
  166.2 1.6 copy-start.3
  (1 other events, 0.7 us)

commit v3 on v2

--- a/solution.py
+++ b/solution.py
@@ -96,32 +96,97 @@
     )(at, features, theirs)
 
 
-def stack_body(own, first, second, third, query_ref, pair_ref):
+def stack_body(at, features, own, first, second, third, plane_ref, theirs_ref):
     rows = own.shape[0]
     for i, piece in enumerate((own, first, second, third)):
-        at = pl.ds(i * rows, rows)
-        query_ref[at, :] = piece[:, : HQ * HD]
-        pair_ref[at, :] = piece[:, HQ * HD :]
-
-
-def stack_planes(*pieces):
+        plane_ref[pl.ds(i * rows, rows), :] = piece[...]
+    for x in range(NX):
+        from_block = pl.ds(pl.multiple_of((x * NC + 1 - at[2]) * BLOCK, BLOCK), BLOCK)
+        theirs_ref[:, x * BLOCK : (x + 1) * BLOCK] = features[:, from_block]
+
+
+def stack_plane(at, features, pieces):
     rows = sum(piece.shape[0] for piece in pieces)
     return pl.pallas_call(
         stack_body,
+        in_specs=[pl.BlockSpec(memory_space=pltpu.SMEM)]
+        + [pl.BlockSpec(memory_space=pltpu.VMEM)] * 5,
         out_shape=[
-            pltpu.VMEM((rows, HQ * HD), jnp.bfloat16),
-            pltpu.VMEM((rows, 2 * HD), jnp.bfloat16),
-        ],
-    )(*[pltpu.with_memory_space_constraint(p, pltpu.VMEM) for p in pieces])
-
-
-def query_part_body(at, grads, *refs):
-    pieces, out_ref, held = refs[:8], refs[8], refs[9]
+            pltpu.VMEM((rows, pieces[0].shape[1]), jnp.bfloat16),
+            pltpu.VMEM((features.shape[0], NX * BLOCK), jnp.bfloat16),
+        ],
+        compiler_params=pltpu.CompilerParams(vmem_limit_bytes=VMEM_LIMIT),
+    )(at, in_vmem(features), *[in_vmem(p) for p in pieces])
+
+
+def in_vmem(array):
+    return pltpu.with_memory_space_constraint(array, pltpu.VMEM)
+
+
+def project_body(arranged, *refs):
+    pieces, mine_ref, theirs_ref, rows_ref = refs[:4], refs[4], refs[5], refs[6]
+    held, in_sems, out_sems = refs[7:]
+    count = arranged.shape[0] // NX
+    loads = [
+        pltpu.make_async_copy(piece, held.at[e], in_sems.at[e]) for e, piece in enumerate(pieces)
+    ]
+    for load in loads:
+        load.start()
+    stores = []
+    for e in range(NX):
+        loads[e].wait()
+        store = pltpu.make_async_copy(
+            held.at[e], rows_ref.at[pl.ds(e * BLOCK, BLOCK)], out_sems.at[e]
+        )
+        store.start()
+        stores.append(store)
+        part = jnp.dot(
+            arranged[e * count : (e + 1) * count, :], held[e], preferred_element_type=jnp.float32
+        )
+        for ref, half in ((mine_ref, part[: count // 2]), (theirs_ref, part[count // 2 :])):
+            ref[...] = half if e == 0 else ref[...] + half
+    for store in stores:
+        store.wait()
+
+
+def project(arranged, pieces):
+    count, columns = arranged.shape[0] // NX // 2, pieces[0].shape[1]
+    whole = pl.BlockSpec(memory_space=pltpu.VMEM)
+    left = pl.BlockSpec(memory_space=pl.ANY)
+    return pl.pallas_call(
+        project_body,
+        in_specs=[whole] + [left] * 4,
+        out_specs=[whole, whole, left],
+        out_shape=[
+            jax.ShapeDtypeStruct((count, columns), jnp.float32),
+            jax.ShapeDtypeStruct((count, columns), jnp.float32),
+            jax.ShapeDtypeStruct((NX * BLOCK, columns), jnp.bfloat16),
+        ],
+        scratch_shapes=[
+            pltpu.VMEM((NX, BLOCK, columns), jnp.bfloat16),
+            pltpu.SemaphoreType.DMA((NX,)),
+            pltpu.SemaphoreType.DMA((NX,)),
+        ],
+        compiler_params=pltpu.CompilerParams(vmem_limit_bytes=VMEM_LIMIT),
+        cost_estimate=pl.CostEstimate(
+            flops=NX * 4 * count * BLOCK * columns, bytes_accessed=12 << 20, transcendentals=0
+        ),
+    )(arranged, *pieces)
+
+
+def query_part_body(at, grads, own, other, out_ref, pair_ref, weights, held, sems):
     x_me, y_me, core = at[0], at[1], at[2]
+    loads = []
+    for i in range(2 * NX):
+        source = (own, other)[i // NX].at[pl.ds(i % NX * BLOCK, BLOCK)]
+        loads.append(pltpu.make_async_copy(source, weights.at[i], sems.at[i]))
+        loads[-1].start()
     order = order_matrix(y_me)
-    for i, piece in enumerate(pieces):
+    queries = HQ * HD
+    for i in range(2 * NX):
+        loads[i].wait()
         held[i] = lax.dot_general(
-            grads[...], piece[...], TURN, preferred_element_type=jnp.float32
+            grads[...], weights[i, :, :queries], TURN, preferred_element_type=jnp.float32
         )
     rows = grads.shape[0]
     by_x, by_y = core * NX, (1 - core) * NX
@@ -137,23 +202,39 @@
                 preferred_element_type=jnp.float32,
             )
             out_ref[:, pl.ds(block_at(x_me, s, c), BLOCK)] = back[:rows] + back[rows:]
-
-
-def query_part_of(at, grads, pieces):
-    rows = grads.shape[0]
+    for s in range(NX):
+        even = jnp.concatenate(
+            [weights[by_x + e, s * SPAN : (s + 1) * SPAN, queries:] for e in range(NY)], axis=0
+        )
+        for c, part in ((0, even), (1, weights[by_y + s, :, queries:])):
+            pair_ref[pl.ds(block_at(x_me, s, c), BLOCK), :] = jnp.dot(
+                order, part, preferred_element_type=jnp.float32
+            ).astype(jnp.bfloat16)
+
+
+def query_part_of(at, grads, own, other):
+    rows, columns = grads.shape[0], own.shape[1]
+    whole = pl.BlockSpec(memory_space=pltpu.VMEM)
+    left = pl.BlockSpec(memory_space=pl.ANY)
     return pl.pallas_call(
         query_part_body,
-        in_specs=[pl.BlockSpec(memory_space=pltpu.SMEM)]
-        + [pl.BlockSpec(memory_space=pltpu.VMEM)] * 9,
-        out_shape=jax.ShapeDtypeStruct((rows, 8 * BLOCK), jnp.float32),
-        scratch_shapes=[pltpu.VMEM((8, rows, BLOCK), jnp.float32)],
+        in_specs=[pl.BlockSpec(memory_space=pltpu.SMEM), whole, left, left],
+        out_shape=[
+            pltpu.VMEM((rows, 8 * BLOCK), jnp.float32),
+            pltpu.VMEM((8 * BLOCK, columns - HQ * HD), jnp.bfloat16),
+        ],
+        scratch_shapes=[
+            pltpu.VMEM((8, BLOCK, columns), jnp.bfloat16),
+            pltpu.VMEM((8, rows, BLOCK), jnp.float32),
+            pltpu.SemaphoreType.DMA((8,)),
+        ],
         compiler_params=pltpu.CompilerParams(vmem_limit_bytes=VMEM_LIMIT),
         cost_estimate=pl.CostEstimate(
-            flops=8 * 2 * rows * BLOCK * (HQ * HD + 2 * BLOCK),
+            flops=8 * 2 * rows * BLOCK * (HQ * HD + 4 * BLOCK),
             bytes_accessed=12 << 20,
             transcendentals=0,
         ),
-    )(at, grads, *pieces)
+    )(at, grads, own, other)
 
 
 def shifted(block, axis, distance):
@@ -194,24 +275,13 @@
     second, first, third = (hop(column, d, 0) for d in (2, 1, 3))
 
     at = jnp.stack([x_me, y_me, core]).astype(jnp.int32)
-    blocks = [features[:, i * BLOCK : (i + 1) * BLOCK] for i in range(NX * NC)]
-    halves = [jnp.concatenate(blocks[c::NC], axis=1) for c in range(NC)]
-    theirs = swap_cores(jnp.where(core == 0, halves[1], halves[0]))
-    arranged = arrange(at, features, theirs)
-
-    def project(pieces):
-        total = 0.0
-        rows = 2 * row_count
-        for e, piece in enumerate(pieces):
-            total = total + jnp.dot(
-                arranged[e * rows : (e + 1) * rows], piece, preferred_element_type=jnp.float32
-            )
-        return total[:row_count] + swap_cores(total[row_count:])
-
-    plane_q, plane_p = stack_planes(column, first, second, third)
-    two, one, three = (hop(plane_p, d, 1) for d in (2, 1, 3))
-    two_q, one_q, three_q = (hop(plane_q, d, 1) for d in (2, 1, 3))
-    pair_pre = project([plane_p, one, two, three])
+    plane, theirs = stack_plane(at, features, [column, first, second, third])
+    two, one, three = (hop(plane, d, 1) for d in (2, 1, 3))
+    arranged = arrange(at, features, swap_cores(theirs))
+    mine, theirs, own_w = project(arranged, [plane, one, two, three])
+    projected, own_w = lax.optimization_barrier((mine + swap_cores(theirs), own_w))
+    other_w = swap_cores(own_w)
+    pair_pre, query_pre = projected[:, HQ * HD :], projected[:, : HQ * HD]
 
     first_row = ctx * row_count
     query_index = first_row + jnp.arange(row_count, dtype=jnp.int32)
@@ -220,14 +290,7 @@
         [rotate(pair_pre[:, :HD], cos_part, sin_part), pair_pre[:, HD:]], axis=1
     ).astype(jnp.bfloat16)
     near = jnp.concatenate([shifted(pair_rows, "ctx", 1), pair_rows], axis=0)
-    near, one_q, two_q, three_q = lax.optimization_barrier((near, one_q, two_q, three_q))
-    query_pre = project([plane_q, one_q, two_q, three_q])
-    far, query_pre = lax.optimization_barrier((shifted(near, "ctx", 2), query_pre))
-    window = jnp.concatenate([far, near], axis=0)
-    pair_own = jnp.concatenate([plane_p, one, two, three], axis=0)
-    pair_other = swap_cores(pair_own)
-    plane_q_other = swap_cores(plane_q)
-
+    window = jnp.concatenate([shifted(near, "ctx", 2), near], axis=0)
     queries = rotate(
         query_pre.reshape(row_count, HQ, HD), cos_part[:, None, :], sin_part[:, None, :]
     ).astype(jnp.bfloat16)
@@ -267,31 +330,12 @@
         row_count, HQ * HD
     ).astype(jnp.bfloat16)
     far, near = pair_grad[: 2 * row_count], pair_grad[2 * row_count :]
-    one_q, two_q, three_q, query_out = lax.optimization_barrier((one_q, two_q, three_q, query_out))
-    swapped = [swap_cores(piece) for piece in (one_q, two_q, three_q)]
-    near = near + shifted(far, "ctx", -2)
-    query_part = query_part_of(
-        at, query_out, [plane_q, one_q, two_q, three_q, plane_q_other] + swapped
-    )
-
-    pair_w = [
-        w[i * BLOCK : (i + 1) * BLOCK] for w in (pair_own, pair_other) for i in range(NX)
-    ]
-    order = order_matrix(y_me)
-    order0 = [jnp.where(core == 0, a, b) for a, b in zip(pair_w[:NX], pair_w[NX:])]
-    order1 = [jnp.where(core == 0, b, a) for a, b in zip(pair_w[:NX], pair_w[NX:])]
-    pair_all = jnp.zeros((features.shape[1], 2 * HD), jnp.bfloat16)
-    for s in range(NX):
-        even = jnp.concatenate([order0[e][s * SPAN : (s + 1) * SPAN] for e in range(NY)], axis=0)
-        for c, part in ((0, even), (1, order1[s])):
-            back = jnp.dot(order, part, preferred_element_type=jnp.float32).astype(jnp.bfloat16)
-            place_at = ((x_me - s + NX) % NX * NC + c) * BLOCK
-            pair_all = lax.dynamic_update_slice_in_dim(pair_all, back, place_at, 0)
-
+    query_part, pair_all = query_part_of(at, query_out, own_w, other_w)
     came, query_part, pair_all = lax.optimization_barrier(
-        (shifted(near[:row_count], "ctx", -1), query_part, pair_all)
-    )
-    pair_total = near[row_count:] + came
+        (shifted(far, "ctx", -2), query_part, pair_all)
+    )
+    near = near + came
+    pair_total = near[row_count:] + shifted(near[:row_count], "ctx", -1)
     pair_out = jnp.concatenate(
         [rotate(pair_total[:, :HD], cos_part, -sin_part), pair_total[:, HD:]], axis=1
     ).astype(jnp.bfloat16)

time: 170 us -> 151 us (0.89)
  the two profiles are of different devices: /device:TPU:34 before, /device:TPU:24 now
where the time goes in v3:
time: 151 us; the launch traced here: 150 us
  waiting for transfers between devices  48.3 us (32%)
  starting transfers between devices  37.9 us (25%)
  blocking collectives  37.4 us (25%)
  Pallas kernels  14.8 us (10%)
  matrix products  4.17 us (3%)
  other arithmetic  3.34 us (2%)
  local copies, waits for them, and re-layouts  3.22 us (2%)
    all_gather x1, blocking collectives, local(): lax.all_gather(w_qkv, 'ctx', axis=0, tiled=True, axis_index_groups=[[z *...  37.4 us
    ppermute x6, waiting for transfers between devices, hop(): return lax.ppermute(block, ALL, route(move))  30.6 us
    ppermute x6, starting transfers between devices, hop(): return lax.ppermute(block, ALL, route(move))  19.7 us
    ppermute x4, waiting for transfers between devices, shifted(): lax.ppermute(block, axis, [(i - distance, i) for i in devices if i - dist...  13.8 us
    ppermute x4, starting transfers between devices, shifted(): lax.ppermute(block, axis, [(i - distance, i) for i in devices if i - dist...  12.1 us
    pallas_call x1, Pallas kernels, query_part_of(): pl.pallas_call(query_part_body, in_specs=[pl.BlockSpec(memory_space=pltpu...  8.21 us
    ppermute x3, starting transfers between devices, swap_cores(): return lax.ppermute(block, ALL, route(lambda x, c, z, y: (x, 1 - c, z, y)))  6.02 us
    pallas_call x1, Pallas kernels, project(): pl.pallas_call(project_body, in_specs=[whole] + [left] * 4, out_specs=[wh...  3.99 us
  transfers between devices with their start and end apart: 13, of which 10 were waited for; matrix products, arithmetic and copies ran while one was open for 4% of the time, Pallas kernels for 7%

profile of v3, /device:TPU:24, one launch (start us, length us, event | category | flops | bytes accessed | tf_op | source)
XLA Modules:
  0.0 149.6 jit_solution(5770234199719240380)
XLA Ops:
  0.0 37.4 %all_gather.3.own = bf16[128,1280]{1,0:T(8,128)(2,1)S(1)} all-gather(bf16[8,1280]{1,0:T(8,128)(2,1)} %param.7), channel_id=1, replica_groups={{0,4,8,12,16,20,24,28,32,36,40,44,48,52,56,60},{1,5,9,13,17,21,25,29,33..., dimensions={0}, use_global_device_ids=true | all-gather | bytes 348160 | tf_op jit(solution)/shard_map/all_gather | solution.py:271
  37.4 4.7 %collective-permute-start.2 = (bf16[128,1280]{1,0:T(8,128)(2,1)S(1)}, bf16[128,1280]{1,0:T(8,128)(2,1)S(1)}, u32[]{:S(2)}, u32[]{:S(2)}) collective-permute-start(bf16[128,1280]{1,0:T(8,128)(2,1)S(1)} %all_gather.3.own), channel_id=1, source_target_pairs={{0,384},{1,385},{2,386},{3,387},{4,388},{5,389},{6,390},{7,391},{8... | collective-permute-start | bytes 983048 | tf_op jit(solution)/shard_map/ppermute | solution.py:39
  42.1 2.7 %collective-permute-start.1 = (bf16[128,1280]{1,0:T(8,128)(2,1)S(1)}, bf16[128,1280]{1,0:T(8,128)(2,1)S(1)}, u32[]{:S(2)}, u32[]{:S(2)}) collective-permute-start(bf16[128,1280]{1,0:T(8,128)(2,1)S(1)} %all_gather.3.own), channel_id=1, source_target_pairs={{0,256},{1,257},{2,258},{3,259},{4,260},{5,261},{6,262},{7,263},{8... | collective-permute-start | bytes 983048 | tf_op jit(solution)/shard_map/ppermute | solution.py:39
  44.8 2.8 %collective-permute-start = (bf16[128,1280]{1,0:T(8,128)(2,1)S(1)}, bf16[128,1280]{1,0:T(8,128)(2,1)S(1)}, u32[]{:S(2)}, u32[]{:S(2)}) collective-permute-start(bf16[128,1280]{1,0:T(8,128)(2,1)S(1)} %all_gather.3.own), channel_id=1, source_target_pairs={{0,128},{1,129},{2,130},{3,131},{4,132},{5,133},{6,134},{7,135},{8... | collective-permute-start | bytes 983048 | tf_op jit(solution)/shard_map/ppermute | solution.py:39
  47.7 2.5 %collective-permute-done.2.third = bf16[128,1280]{1,0:T(8,128)(2,1)S(1)} collective-permute-done((bf16[128,1280]{1,0:T(8,128)(2,1)S(1)}, bf16[128,1280]{1,0:T(8,128)(2,1)S(1)}, u32[]{:S(2)}, u32[]{:S(2)}) %collective-permute-start.2) | collective-permute-done | bytes 327712 | tf_op jit(solution)/shard_map/ppermute | solution.py:39
  50.2 2.5 %collective-permute-done.1.second = bf16[128,1280]{1,0:T(8,128)(2,1)S(1)} collective-permute-done((bf16[128,1280]{1,0:T(8,128)(2,1)S(1)}, bf16[128,1280]{1,0:T(8,128)(2,1)S(1)}, u32[]{:S(2)}, u32[]{:S(2)}) %collective-permute-start.1) | collective-permute-done | bytes 327712 | tf_op jit(solution)/shard_map/ppermute | solution.py:39
  52.7 3.4 %collective-permute-done.first = bf16[128,1280]{1,0:T(8,128)(2,1)S(1)} collective-permute-done((bf16[128,1280]{1,0:T(8,128)(2,1)S(1)}, bf16[128,1280]{1,0:T(8,128)(2,1)S(1)}, u32[]{:S(2)}, u32[]{:S(2)}) %collective-permute-start) | collective-permute-done | bytes 327712 | tf_op jit(solution)/shard_map/ppermute | solution.py:39
  56.1 1.2 copy-done
  57.3 0.7 shard_map.46
  58.0 2.7 %collective-permute-start.6 = (bf16[512,1280]{1,0:T(8,128)(2,1)S(1)}, bf16[512,1280]{1,0:T(8,128)(2,1)S(1)}, u32[]{:S(2)}, u32[]{:S(2)}) collective-permute-start(bf16[512,1280]{1,0:T(8,128)(2,1)S(1)} %get-tuple-element.18.refs_0_), channel_id=1, source_target_pairs={{0,3},{1,0},{2,1},{3,2},{4,7},{5,4},{6,5},{7,6},{8,11},{9,8},{10,9... | collective-permute-start | bytes 3932168 | tf_op jit(solution)/shard_map/ppermute | solution.py:39
  60.6 2.8 %collective-permute-start.5 = (bf16[512,1280]{1,0:T(8,128)(2,1)S(1)}, bf16[512,1280]{1,0:T(8,128)(2,1)S(1)}, u32[]{:S(2)}, u32[]{:S(2)}) collective-permute-start(bf16[512,1280]{1,0:T(8,128)(2,1)S(1)} %get-tuple-element.18.refs_0_), channel_id=1, source_target_pairs={{0,2},{1,3},{2,0},{3,1},{4,6},{5,7},{6,4},{7,5},{8,10},{9,11},{10,... | collective-permute-start | bytes 3932168 | tf_op jit(solution)/shard_map/ppermute | solution.py:39
  63.5 4.1 %collective-permute-start.4 = (bf16[512,1280]{1,0:T(8,128)(2,1)S(1)}, bf16[512,1280]{1,0:T(8,128)(2,1)S(1)}, u32[]{:S(2)}, u32[]{:S(2)}) collective-permute-start(bf16[512,1280]{1,0:T(8,128)(2,1)S(1)} %get-tuple-element.18.refs_0_), channel_id=1, source_target_pairs={{0,1},{1,2},{2,3},{3,0},{4,5},{5,6},{6,7},{7,4},{8,9},{9,10},{10,1... | collective-permute-start | bytes 3932168 | tf_op jit(solution)/shard_map/ppermute | solution.py:39
  67.6 1.9 %collective-permute-start.3 = (bf16[128,2048]{1,0:T(8,128)(2,1)S(1)}, bf16[128,2048]{1,0:T(8,128)(2,1)S(1)}, u32[]{:S(2)}, u32[]{:S(2)}) collective-permute-start(bf16[128,2048]{1,0:T(8,128)(2,1)S(1)} %get-tuple-element.17), channel_id=1, source_target_pairs={{0,64},{1,65},{2,66},{3,67},{4,68},{5,69},{6,70},{7,71},{8,72},{9,... | collective-permute-start | bytes 1572872 | tf_op jit(solution)/shard_map/ppermute | solution.py:43
  69.5 1.9 %collective-permute-done.3.theirs = bf16[128,2048]{1,0:T(8,128)(2,1)S(1)} collective-permute-done((bf16[128,2048]{1,0:T(8,128)(2,1)S(1)}, bf16[128,2048]{1,0:T(8,128)(2,1)S(1)}, u32[]{:S(2)}, u32[]{:S(2)}) %collective-permute-start.3) | collective-permute-done | bytes 524320 | tf_op jit(solution)/shard_map/ppermute | solution.py:43
  71.4 1.9 %shard_map.47.arranged = bf16[1024,512]{1,0:T(8,128)(2,1)S(1)} custom-call(s32[3]{0:T(128)S(1)} %pad_add_fusion.at, bf16[128,4096]{1,0:T(8,128)(2,1)S(1)} %bitcast.64, bf16[128,2048]{1,0:T(8,128)(2,1)S(1)} %collective-permute-done.3.theirs), custom_call_target="tpu_custom_call" | custom-call | flops 536870912 | bytes 4194304 | tf_op jit(solution)/shard_map/pallas_call | solution.py:87
  73.4 19.4 %collective-permute-done.6.refs_3_ = bf16[512,1280]{1,0:T(8,128)(2,1)S(1)} collective-permute-done((bf16[512,1280]{1,0:T(8,128)(2,1)S(1)}, bf16[512,1280]{1,0:T(8,128)(2,1)S(1)}, u32[]{:S(2)}, u32[]{:S(2)}) %collective-permute-start.6) | collective-permute-done | bytes 1310752 | tf_op jit(solution)/shard_map/ppermute | solution.py:39
  92.8 2.8 %collective-permute-done.4.refs_1_ = bf16[512,1280]{1,0:T(8,128)(2,1)S(1)} collective-permute-done((bf16[512,1280]{1,0:T(8,128)(2,1)S(1)}, bf16[512,1280]{1,0:T(8,128)(2,1)S(1)}, u32[]{:S(2)}, u32[]{:S(2)}) %collective-permute-start.4) | collective-permute-done | bytes 1310752 | tf_op jit(solution)/shard_map/ppermute | solution.py:39
  95.6 4.0 %shard_map.48 = (f32[128,1280]{1,0:T(8,128)S(1)}, f32[128,1280]{1,0:T(8,128)S(1)}, bf16[2048,1280]{1,0:T(8,128)(2,1)}) custom-call(bf16[1024,512]{1,0:T(8,128)(2,1)S(1)} %shard_map.47.arranged, bf16[512,1280]{1,0:T(8,128)(2,1)S(1)} %get-tuple-element.18.refs_0_, bf16[512,1280]{1,0:T(8,128)(2,1)S(1)} %collective-permute-done.4.refs_1_, ...), custom_call_target="tpu_custom_call" | custom-call | flops 1342177280 | bytes 12582912 | tf_op jit(solution)/shard_map/pallas_call | solution.py:156
  99.6 2.1 %collective-permute-start.7 = (f32[128,1280]{1,0:T(8,128)S(1)}, f32[128,1280]{1,0:T(8,128)S(1)}, u32[]{:S(2)}, u32[]{:S(2)}) collective-permute-start(f32[128,1280]{1,0:T(8,128)S(1)} %get-tuple-element.20), channel_id=1, source_target_pairs={{0,64},{1,65},{2,66},{3,67},{4,68},{5,69},{6,70},{7,71},{8,72},{9,... | collective-permute-start | bytes 1966088 | tf_op jit(solution)/shard_map/ppermute | solution.py:43
  101.6 2.1 %collective-permute-done.7 = f32[128,1280]{1,0:T(8,128)S(1)} collective-permute-done((f32[128,1280]{1,0:T(8,128)S(1)}, f32[128,1280]{1,0:T(8,128)S(1)}, u32[]{:S(2)}, u32[]{:S(2)}) %collective-permute-start.7) | collective-permute-done | bytes 655392 | tf_op jit(solution)/shard_map/ppermute | solution.py:43
  103.8 2.0 %collective-permute-start.11 = (bf16[2048,1280]{1,0:T(8,128)(2,1)}, bf16[2048,1280]{1,0:T(8,128)(2,1)}, u32[]{:S(2)}, u32[]{:S(2)}) collective-permute-start(bf16[2048,1280]{1,0:T(8,128)(2,1)} %get-tuple-element.23.own), channel_id=1, source_target_pairs={{0,64},{1,65},{2,66},{3,67},{4,68},{5,69},{6,70},{7,71},{8,72},{9,... | collective-permute-start | bytes 15728648 | tf_op jit(solution)/shard_map/ppermute | solution.py:43
  105.8 0.8 copy.7
  106.7 0.1 compare_and_fusion
  107.0 0.1 copy.38
  107.1 0.3 fusion.22
  107.5 3.7 %collective-permute-start.8 = (bf16[128,256]{1,0:T(8,128)(2,1)S(1)}, bf16[128,256]{1,0:T(8,128)(2,1)S(1)}, u32[]{:S(2)}, u32[]{:S(2)}) collective-permute-start(bf16[128,256]{1,0:T(8,128)(2,1)S(1)} %pad_maximum_fusion.2), channel_id=1, source_target_pairs={{0,1},{1,2},{2,3},{3,4},{4,5},{5,6},{6,7},{7,8},{8,9},{9,10},{10,1... | collective-permute-start | bytes 196616 | tf_op jit(solution)/shard_map/ppermute | solution.py:242
  111.2 0.2 fusion.43
  111.4 2.4 %collective-permute-done.8 = bf16[128,256]{1,0:T(8,128)(2,1)S(1)} collective-permute-done((bf16[128,256]{1,0:T(8,128)(2,1)S(1)}, bf16[128,256]{1,0:T(8,128)(2,1)S(1)}, u32[]{:S(2)}, u32[]{:S(2)}) %collective-permute-start.8) | collective-permute-done | bytes 65568 | tf_op jit(solution)/shard_map/ppermute | solution.py:242
  113.8 3.4 %collective-permute-start.9 = (bf16[256,256]{1,0:T(8,128)(2,1)S(1)}, bf16[256,256]{1,0:T(8,128)(2,1)S(1)}, u32[]{:S(2)}, u32[]{:S(2)}) collective-permute-start(bf16[256,256]{1,0:T(8,128)(2,1)S(1)} %maximum_maximum_fusion.1), channel_id=1, source_target_pairs={{0,2},{1,3},{2,4},{3,5},{4,6},{5,7},{6,8},{7,9},{8,10},{9,11},{10,... | collective-permute-start | bytes 393224 | tf_op jit(solution)/shard_map/ppermute | solution.py:242
  117.2 0.2 subtract_convert_fusion.1
  117.5 4.8 %collective-permute-done.9 = bf16[256,256]{1,0:T(8,128)(2,1)S(1)} collective-permute-done((bf16[256,256]{1,0:T(8,128)(2,1)S(1)}, bf16[256,256]{1,0:T(8,128)(2,1)S(1)}, u32[]{:S(2)}, u32[]{:S(2)}) %collective-permute-start.9) | collective-permute-done | bytes 131104 | tf_op jit(solution)/shard_map/ppermute | solution.py:242
  122.3 1.0 fusion.44
  123.4 0.2 fusion.13
  123.5 0.8 copy-done.3
  124.3 0.4 convolution_bitcast_fusion
  124.7 0.4 fusion.7
  125.1 0.4 fusion.2
  125.6 0.5 fusion.8
  126.1 2.1 %collective-permute-start.10 = (f32[256,256]{1,0:T(8,128)S(1)}, f32[256,256]{1,0:T(8,128)S(1)}, u32[]{:S(2)}, u32[]{:S(2)}) collective-permute-start(f32[256,256]{1,0:T(8,128)S(1)} %fusion.14), channel_id=1, source_target_pairs={{2,0},{3,1},{4,2},{5,3},{6,4},{7,5},{8,6},{9,7},{10,8},{11,9},{12,... | collective-permute-start | bytes 786440 | tf_op jit(solution)/shard_map/ppermute | solution.py:242
  128.2 0.6 fusion.4
  128.8 0.3 subtract_convert_fusion
  129.1 0.1 copy_bitcast_fusion.grads
  129.2 8.2 %shard_map.49 = (f32[128,4096]{1,0:T(8,128)S(1)}, bf16[4096,256]{1,0:T(8,128)(2,1)S(1)}) custom-call(s32[3]{0:T(128)S(1)} %pad_add_fusion.at, bf16[128,1024]{1,0:T(8,128)(2,1)S(1)} %copy_bitcast_fusion.grads, bf16[2048,1280]{1,0:T(8,128)(2,1)} %get-tuple-element.23.own, bf16[2048,1280]{1,0:T(8,128)(2,1)} %collective-permute-done.11.other), custom_call_target="tpu_custom_call" | custom-call | flops 3221225472 | bytes 12582912 | tf_op jit(solution)/shard_map/pallas_call | solution.py:219
  137.5 3.0 %collective-permute-start.12 = (f32[128,256]{1,0:T(8,128)S(1)}, f32[128,256]{1,0:T(8,128)S(1)}, u32[]{:S(2)}, u32[]{:S(2)}) collective-permute-start(f32[128,256]{1,0:T(8,128)S(1)} %slice.89), channel_id=1, source_target_pairs={{1,0},{2,1},{3,2},{4,3},{5,4},{6,5},{7,6},{8,7},{9,8},{10,9},{11,1... | collective-permute-start | bytes 393224 | tf_op jit(solution)/shard_map/ppermute | solution.py:242
  140.5 6.6 %collective-permute-done.12 = f32[128,256]{1,0:T(8,128)S(1)} collective-permute-done((f32[128,256]{1,0:T(8,128)S(1)}, f32[128,256]{1,0:T(8,128)S(1)}, u32[]{:S(2)}, u32[]{:S(2)}) %collective-permute-start.12) | collective-permute-done | bytes 131104 | tf_op jit(solution)/shard_map/ppermute | solution.py:242
  147.2 0.3 fusion.31
  147.5 0.8 fusion.34
  148.3 1.3 fusion.9
  (29 shorter events, 0.6 us)
Async XLA Ops:
  37.4 12.8 %collective-permute-start.2 = (bf16[128,1280]{1,0:T(8,128)(2,1)S(1)}, bf16[128,1280]{1,0:T(8,128)(2,1)S(1)}, u32[]{:S(2)}, u32[]{:S(2)}) collective-permute-start(bf16[128,1280]{1,0:T(8,128)(2,1)S(1)} %all_gather.3.own), channel_id=1, source_target_pairs={{0,384},{1,385},{2,386},{3,387},{4,388},{5,389},{6,390},{7,391},{8... | collective-permute-start | bytes 983048 | tf_op jit(solution)/shard_map/ppermute | solution.py:39
  42.1 10.6 %collective-permute-start.1 = (bf16[128,1280]{1,0:T(8,128)(2,1)S(1)}, bf16[128,1280]{1,0:T(8,128)(2,1)S(1)}, u32[]{:S(2)}, u32[]{:S(2)}) collective-permute-start(bf16[128,1280]{1,0:T(8,128)(2,1)S(1)} %all_gather.3.own), channel_id=1, source_target_pairs={{0,256},{1,257},{2,258},{3,259},{4,260},{5,261},{6,262},{7,263},{8... | collective-permute-start | bytes 983048 | tf_op jit(solution)/shard_map/ppermute | solution.py:39
  44.8 11.3 %collective-permute-start = (bf16[128,1280]{1,0:T(8,128)(2,1)S(1)}, bf16[128,1280]{1,0:T(8,128)(2,1)S(1)}, u32[]{:S(2)}, u32[]{:S(2)}) collective-permute-start(bf16[128,1280]{1,0:T(8,128)(2,1)S(1)} %all_gather.3.own), channel_id=1, source_target_pairs={{0,128},{1,129},{2,130},{3,131},{4,132},{5,133},{6,134},{7,135},{8... | collective-permute-start | bytes 983048 | tf_op jit(solution)/shard_map/ppermute | solution.py:39
  56.1 1.2 copy-start
  58.0 34.8 %collective-permute-start.6 = (bf16[512,1280]{1,0:T(8,128)(2,1)S(1)}, bf16[512,1280]{1,0:T(8,128)(2,1)S(1)}, u32[]{:S(2)}, u32[]{:S(2)}) collective-permute-start(bf16[512,1280]{1,0:T(8,128)(2,1)S(1)} %get-tuple-element.18.refs_0_), channel_id=1, source_target_pairs={{0,3},{1,0},{2,1},{3,2},{4,7},{5,4},{6,5},{7,6},{8,11},{9,8},{10,9... | collective-permute-start | bytes 3932168 | tf_op jit(solution)/shard_map/ppermute | solution.py:39
  60.6 32.1 %collective-permute-start.5 = (bf16[512,1280]{1,0:T(8,128)(2,1)S(1)}, bf16[512,1280]{1,0:T(8,128)(2,1)S(1)}, u32[]{:S(2)}, u32[]{:S(2)}) collective-permute-start(bf16[512,1280]{1,0:T(8,128)(2,1)S(1)} %get-tuple-element.18.refs_0_), channel_id=1, source_target_pairs={{0,2},{1,3},{2,0},{3,1},{4,6},{5,7},{6,4},{7,5},{8,10},{9,11},{10,... | collective-permute-start | bytes 3932168 | tf_op jit(solution)/shard_map/ppermute | solution.py:39
  63.5 32.1 %collective-permute-start.4 = (bf16[512,1280]{1,0:T(8,128)(2,1)S(1)}, bf16[512,1280]{1,0:T(8,128)(2,1)S(1)}, u32[]{:S(2)}, u32[]{:S(2)}) collective-permute-start(bf16[512,1280]{1,0:T(8,128)(2,1)S(1)} %get-tuple-element.18.refs_0_), channel_id=1, source_target_pairs={{0,1},{1,2},{2,3},{3,0},{4,5},{5,6},{6,7},{7,4},{8,9},{9,10},{10,1... | collective-permute-start | bytes 3932168 | tf_op jit(solution)/shard_map/ppermute | solution.py:39
  67.6 3.8 %collective-permute-start.3 = (bf16[128,2048]{1,0:T(8,128)(2,1)S(1)}, bf16[128,2048]{1,0:T(8,128)(2,1)S(1)}, u32[]{:S(2)}, u32[]{:S(2)}) collective-permute-start(bf16[128,2048]{1,0:T(8,128)(2,1)S(1)} %get-tuple-element.17), channel_id=1, source_target_pairs={{0,64},{1,65},{2,66},{3,67},{4,68},{5,69},{6,70},{7,71},{8,72},{9,... | collective-permute-start | bytes 1572872 | tf_op jit(solution)/shard_map/ppermute | solution.py:43
  92.7 2.8 %copy-start.1 = (bf16[512,1280]{1,0:T(8,128)(2,1)}, bf16[512,1280]{1,0:T(8,128)(2,1)S(1)}, u32[]{:S(2)}) copy-start(bf16[512,1280]{1,0:T(8,128)(2,1)S(1)} %collective-permute-done.6.refs_3_) | copy-start | bytes 3932164
  92.8 2.8 %copy-start.2 = (bf16[512,1280]{1,0:T(8,128)(2,1)}, bf16[512,1280]{1,0:T(8,128)(2,1)S(1)}, u32[]{:S(2)}) copy-start(bf16[512,1280]{1,0:T(8,128)(2,1)S(1)} %collective-permute-done.5.refs_2_) | copy-start | bytes 3932164
  99.6 6.3 %copy-start.4 = (bf16[1,128,1024]{2,1,0:T(8,128)(2,1)S(1)}, bf16[1,128,1024]{2,1,0:T(8,128)(2,1)}, u32[]{:S(2)}) copy-start(bf16[1,128,1024]{2,1,0:T(8,128)(2,1)} %param.6) | copy-start | bytes 786436
  99.6 7.1 %copy-start.5 = (s32[1,128]{1,0:T(1,128)S(1)}, s32[1,128]{1,0:T(1,128)}, u32[]{:S(2)}) copy-start(s32[1,128]{1,0:T(1,128)} %param.5) | copy-start | bytes 1540
  99.6 4.1 %collective-permute-start.7 = (f32[128,1280]{1,0:T(8,128)S(1)}, f32[128,1280]{1,0:T(8,128)S(1)}, u32[]{:S(2)}, u32[]{:S(2)}) collective-permute-start(f32[128,1280]{1,0:T(8,128)S(1)} %get-tuple-element.20), channel_id=1, source_target_pairs={{0,64},{1,65},{2,66},{3,67},{4,68},{5,69},{6,70},{7,71},{8,72},{9,... | collective-permute-start | bytes 1966088 | tf_op jit(solution)/shard_map/ppermute | solution.py:43
  103.8 25.4 %collective-permute-start.11 = (bf16[2048,1280]{1,0:T(8,128)(2,1)}, bf16[2048,1280]{1,0:T(8,128)(2,1)}, u32[]{:S(2)}, u32[]{:S(2)}) collective-permute-start(bf16[2048,1280]{1,0:T(8,128)(2,1)} %get-tuple-element.23.own), channel_id=1, source_target_pairs={{0,64},{1,65},{2,66},{3,67},{4,68},{5,69},{6,70},{7,71},{8,72},{9,... | collective-permute-start | bytes 15728648 | tf_op jit(solution)/shard_map/ppermute | solution.py:43
  107.5 6.3 %collective-permute-start.8 = (bf16[128,256]{1,0:T(8,128)(2,1)S(1)}, bf16[128,256]{1,0:T(8,128)(2,1)S(1)}, u32[]{:S(2)}, u32[]{:S(2)}) collective-permute-start(bf16[128,256]{1,0:T(8,128)(2,1)S(1)} %pad_maximum_fusion.2), channel_id=1, source_target_pairs={{0,1},{1,2},{2,3},{3,4},{4,5},{5,6},{6,7},{7,8},{8,9},{9,10},{10,1... | collective-permute-start | bytes 196616 | tf_op jit(solution)/shard_map/ppermute | solution.py:242
  113.8 8.4 %collective-permute-start.9 = (bf16[256,256]{1,0:T(8,128)(2,1)S(1)}, bf16[256,256]{1,0:T(8,128)(2,1)S(1)}, u32[]{:S(2)}, u32[]{:S(2)}) collective-permute-start(bf16[256,256]{1,0:T(8,128)(2,1)S(1)} %maximum_maximum_fusion.1), channel_id=1, source_target_pairs={{0,2},{1,3},{2,4},{3,5},{4,6},{5,7},{6,8},{7,9},{8,10},{9,11},{10,... | collective-permute-start | bytes 393224 | tf_op jit(solution)/shard_map/ppermute | solution.py:242
  123.3 1.0 copy-start.3
  126.1 11.3 %collective-permute-start.10 = (f32[256,256]{1,0:T(8,128)S(1)}, f32[256,256]{1,0:T(8,128)S(1)}, u32[]{:S(2)}, u32[]{:S(2)}) collective-permute-start(f32[256,256]{1,0:T(8,128)S(1)} %fusion.14), channel_id=1, source_target_pairs={{2,0},{3,1},{4,2},{5,3},{6,4},{7,5},{8,6},{9,7},{10,8},{11,9},{12,... | collective-permute-start | bytes 786440 | tf_op jit(solution)/shard_map/ppermute | solution.py:242
  137.5 9.6 %collective-permute-start.12 = (f32[128,256]{1,0:T(8,128)S(1)}, f32[128,256]{1,0:T(8,128)S(1)}, u32[]{:S(2)}, u32[]{:S(2)}) collective-permute-start(f32[128,256]{1,0:T(8,128)S(1)} %slice.89), channel_id=1, source_target_pairs={{1,0},{2,1},{3,2},{4,3},{5,4},{6,5},{7,6},{8,7},{9,8},{10,9},{11,1... | collective-permute-start | bytes 393224 | tf_op jit(solution)/shard_map/ppermute | solution.py:242

commit v4 on v3

v4 whole, which is shorter than its diff:
```python
import functools
import math

import jax
import jax.numpy as jnp
from jax import lax
from jax.experimental import pallas as pl
from jax.experimental.pallas import tpu as pltpu
from jax.sharding import PartitionSpec as P

HQ = 8
HD = 128
REACH = 4
ROPE_BASE = 500000.0
MASKED = -1e30
NX, NC, NZ, NY = 4, 2, 16, 4
ALL = ("fsdp", "ctx")


def place(x, c, z, y):
    return (x * NC + c) * (NZ * NY) + z * NY + y


def route(move):
    return [
        (place(x, c, z, y), place(*move(x, c, z, y)))
        for x in range(NX)
        for c in range(NC)
        for z in range(NZ)
        for y in range(NY)
    ]


def hop(block, distance, x_core):
    def move(x, c, z, y):
        if c == x_core:
            return (x + distance) % NX, c, z, y
        return x, c, z, (y + distance) % NY

    return lax.ppermute(block, ALL, route(move))


def swap_cores(block):
    return lax.ppermute(block, ALL, route(lambda x, c, z, y: (x, 1 - c, z, y)))


BLOCK = NZ * NY * 8
SPAN = NZ * 8
TURN = (((1,), (1,)), ((), ()))
VMEM_LIMIT = 48 * 1024 * 1024


def order_matrix(y_me):
    slot = lax.broadcasted_iota(jnp.int32, (BLOCK, BLOCK), 1)
    source = lax.broadcasted_iota(jnp.int32, (BLOCK, BLOCK), 0)
    step, inner = slot // SPAN, slot % SPAN
    place_z = inner // 8
    z = place_z // 8 + place_z // 4 % 2 * 2 + place_z // 2 % 2 * 4 + place_z % 2 * 8
    wanted = z * (NY * 8) + (y_me - step + NY) % NY * 8 + inner % 8
    return (source == wanted).astype(jnp.bfloat16)


def block_at(x_me, s, c):
    return pl.multiple_of(((x_me - s + NX) % NX * NC + c) * BLOCK, BLOCK)


def arrange_body(at, features, theirs, out_ref):
    x_me, y_me, core = at[0], at[1], at[2]
    order = order_matrix(y_me)
    for s in range(NX):
        own = features[:, pl.ds(block_at(x_me, s, core), BLOCK)]
        other = theirs[:, pl.ds(pl.multiple_of((x_me - s + NX) % NX * BLOCK, BLOCK), BLOCK)]
        both = jnp.concatenate([own, other], axis=0)
        rows = both.shape[0]
        got = jnp.dot(both, order, preferred_element_type=jnp.float32).astype(jnp.bfloat16)

        @pl.when(core == 1)
        def _():
            out_ref[pl.ds(s * rows, rows), :] = got

        @pl.when(core == 0)
        def _():
            for e in range(NY):
                out_ref[pl.ds(e * rows, rows), pl.ds(s * SPAN, SPAN)] = got[
                    :, e * SPAN : (e + 1) * SPAN
                ]


def arrange(at, features, theirs):
    return pl.pallas_call(
        arrange_body,
        in_specs=[pl.BlockSpec(memory_space=pltpu.SMEM)]
        + [pl.BlockSpec(memory_space=pltpu.VMEM)] * 2,
        out_shape=jax.ShapeDtypeStruct((NX * 2 * features.shape[0], BLOCK), jnp.bfloat16),
        compiler_params=pltpu.CompilerParams(vmem_limit_bytes=VMEM_LIMIT),
        cost_estimate=pl.CostEstimate(
            flops=4 * 2 * 256 * BLOCK * BLOCK, bytes_accessed=4 << 20, transcendentals=0
        ),
    )(at, features, theirs)


def pick_body(at, features, theirs_ref):
    for x in range(NX):
        from_block = pl.ds(pl.multiple_of((x * NC + 1 - at[2]) * BLOCK, BLOCK), BLOCK)
        theirs_ref[:, x * BLOCK : (x + 1) * BLOCK] = features[:, from_block]


def pick(at, features):
    return pl.pallas_call(
        pick_body,
        in_specs=[pl.BlockSpec(memory_space=pltpu.SMEM), pl.BlockSpec(memory_space=pltpu.VMEM)],
        out_shape=jax.ShapeDtypeStruct((features.shape[0], NX * BLOCK), jnp.bfloat16),
        compiler_params=pltpu.CompilerParams(vmem_limit_bytes=VMEM_LIMIT),
    )(at, features)


def stack_body(own, first, second, third, plane_ref):
    rows = own.shape[0]
    for i, piece in enumerate((own, first, second, third)):
        plane_ref[pl.ds(i * rows, rows), :] = piece[...]


def stack_plane(pieces):
    rows = sum(piece.shape[0] for piece in pieces)
    return pl.pallas_call(
        stack_body,
        out_shape=pltpu.VMEM((rows, pieces[0].shape[1]), jnp.bfloat16),
        compiler_params=pltpu.CompilerParams(vmem_limit_bytes=VMEM_LIMIT),
    )(*[in_vmem(p) for p in pieces])


def in_vmem(array):
    return pltpu.with_memory_space_constraint(array, pltpu.VMEM)


def first_body(arranged, piece, mine_ref, theirs_ref):
    count = mine_ref.shape[0]
    part = jnp.dot(arranged[: 2 * count, :], piece[...], preferred_element_type=jnp.float32)
    mine_ref[...] = part[:count]
    theirs_ref[...] = part[count:]


def first_sums(arranged, plane):
    count, columns = arranged.shape[0] // NX // 2, plane.shape[1]
    return pl.pallas_call(
        first_body,
        out_shape=[pltpu.VMEM((count, columns), jnp.float32)] * 2,
        compiler_params=pltpu.CompilerParams(vmem_limit_bytes=VMEM_LIMIT),
        cost_estimate=pl.CostEstimate(
            flops=4 * count * BLOCK * columns, bytes_accessed=3 << 20, transcendentals=0
        ),
    )(arranged, in_vmem(plane))


def rest_body(steps, arranged, mine_in, theirs_in, plane, *refs):
    pieces, refs = refs[: len(steps)], refs[len(steps) :]
    mine_ref, theirs_ref, rows_ref, held, in_sems, out_sems = refs
    count = mine_ref.shape[0]
    loads = [
        pltpu.make_async_copy(piece, held.at[i], in_sems.at[i]) for i, piece in enumerate(pieces)
    ]
    for load in loads:
        load.start()
    stores = [pltpu.make_async_copy(plane, rows_ref.at[pl.ds(0, BLOCK)], out_sems.at[0])]
    stores[0].start()
    mine_ref[...] = mine_in[...]
    theirs_ref[...] = theirs_in[...]
    for i, step in enumerate(steps):
        loads[i].wait()
        store = pltpu.make_async_copy(
            held.at[i], rows_ref.at[pl.ds((i + 1) * BLOCK, BLOCK)], out_sems.at[i + 1]
        )
        store.start()
        stores.append(store)
        at = step * 2 * count
        part = jnp.dot(
            arranged[at : at + 2 * count, :], held[i], preferred_element_type=jnp.float32
        )
        mine_ref[...] += part[:count]
        theirs_ref[...] += part[count:]
    for store in stores:
        store.wait()


def rest_sums(arranged, sums, plane, pieces, steps):
    count, columns = sums[0].shape
    whole = pl.BlockSpec(memory_space=pltpu.VMEM)
    left = pl.BlockSpec(memory_space=pl.ANY)
    n = len(pieces)
    return pl.pallas_call(
        functools.partial(rest_body, steps),
        in_specs=[whole] * 3 + [left] * (n + 1),
        out_specs=[whole, whole, left],
        out_shape=[
            pltpu.VMEM((count, columns), jnp.float32),
            pltpu.VMEM((count, columns), jnp.float32),
            jax.ShapeDtypeStruct(((n + 1) * BLOCK, columns), jnp.bfloat16),
        ],
        scratch_shapes=[
            pltpu.VMEM((n, BLOCK, columns), jnp.bfloat16),
            pltpu.SemaphoreType.DMA((n,)),
            pltpu.SemaphoreType.DMA((n + 1,)),
        ],
        compiler_params=pltpu.CompilerParams(vmem_limit_bytes=VMEM_LIMIT),
        cost_estimate=pl.CostEstimate(
            flops=n * 4 * count * BLOCK * columns, bytes_accessed=n * 3 << 20, transcendentals=0
        ),
    )(arranged, *[in_vmem(x) for x in sums], plane, *pieces)


def by_source(pieces, steps, parity, cut, join):
    at = {step: piece for step, piece in zip(steps, pieces)}
    for s in range(NX):
        turned = join([cut(at[e], s) for e in range(NY)])
        yield s, jnp.where(parity == 0, turned, at[s])


def query_part_body(steps, flip, at, grads, all_rows, out_ref, weights, held, sems):
    x_me, y_me = at[0], at[1]
    parity = at[2] if flip == 0 else 1 - at[2]
    rows = grads.shape[0]
    loads = []
    for i in range(NX):
        source = all_rows.at[pl.ds(i * BLOCK, BLOCK), pl.ds(0, HQ * HD)]
        loads.append(pltpu.make_async_copy(source, weights.at[i], sems.at[i]))
        loads[-1].start()
    order = order_matrix(y_me)
    for i in range(NX):
        loads[i].wait()
        held[i] = lax.dot_general(
            grads[...], weights[i], TURN, preferred_element_type=jnp.float32
        )
    for s, part in by_source(
        [held[i] for i in range(NX)], steps, parity,
        lambda piece, d: piece[:, d * SPAN : (d + 1) * SPAN],
        lambda parts: jnp.concatenate(parts, axis=1),
    ):
        high = part.astype(jnp.bfloat16)
        low = (part - high.astype(jnp.float32)).astype(jnp.bfloat16)
        back = lax.dot_general(
            jnp.concatenate([high, low], axis=0), order, TURN, preferred_element_type=jnp.float32
        )
        to_block = pl.ds(pl.multiple_of((x_me - s + NX) % NX * BLOCK, BLOCK), BLOCK)
        out_ref[:, to_block] = back[:rows] + back[rows:]


def query_part_of(at, grads, all_rows, steps, flip):
    rows = grads.shape[0]
    whole = pl.BlockSpec(memory_space=pltpu.VMEM)
    left = pl.BlockSpec(memory_space=pl.ANY)
    return pl.pallas_call(
        functools.partial(query_part_body, steps, flip),
        in_specs=[pl.BlockSpec(memory_space=pltpu.SMEM), whole, left],
        out_shape=pltpu.VMEM((rows, NX * BLOCK), jnp.float32),
        scratch_shapes=[
            pltpu.VMEM((NX, BLOCK, HQ * HD), jnp.bfloat16),
            pltpu.VMEM((NX, rows, BLOCK), jnp.float32),
            pltpu.SemaphoreType.DMA((NX,)),
        ],
        compiler_params=pltpu.CompilerParams(vmem_limit_bytes=VMEM_LIMIT),
        cost_estimate=pl.CostEstimate(
            flops=NX * 2 * rows * BLOCK * (HQ * HD + 2 * BLOCK),
            bytes_accessed=6 << 20,
            transcendentals=0,
        ),
    )(at, grads, all_rows)


def pair_weights_body(steps, flip, at, all_rows, out_ref, weights, sem):
    x_me, y_me = at[0], at[1]
    parity = at[2] if flip == 0 else 1 - at[2]
    load = pltpu.make_async_copy(all_rows.at[:, pl.ds(HQ * HD, 2 * HD)], weights, sem)
    load.start()
    order = order_matrix(y_me)
    load.wait()
    for s, part in by_source(
        [weights[i * BLOCK : (i + 1) * BLOCK, :] for i in range(NX)], steps, parity,
        lambda piece, d: piece[d * SPAN : (d + 1) * SPAN],
        lambda parts: jnp.concatenate(parts, axis=0),
    ):
        to_block = pl.ds(pl.multiple_of((x_me - s + NX) % NX * BLOCK, BLOCK), BLOCK)
        out_ref[to_block, :] = jnp.dot(
            order, part, preferred_element_type=jnp.float32
        ).astype(jnp.bfloat16)


def pair_weights_of(at, all_rows, steps, flip):
    left = pl.BlockSpec(memory_space=pl.ANY)
    return pl.pallas_call(
        functools.partial(pair_weights_body, steps, flip),
        in_specs=[pl.BlockSpec(memory_space=pltpu.SMEM), left],
        out_shape=pltpu.VMEM((NX * BLOCK, 2 * HD), jnp.bfloat16),
        scratch_shapes=[
            pltpu.VMEM((NX * BLOCK, 2 * HD), jnp.bfloat16),
            pltpu.SemaphoreType.DMA,
        ],
        compiler_params=pltpu.CompilerParams(vmem_limit_bytes=VMEM_LIMIT),
        cost_estimate=pl.CostEstimate(
            flops=NX * 2 * BLOCK * BLOCK * 2 * HD, bytes_accessed=3 << 20, transcendentals=0
        ),
    )(at, all_rows)


def finish_body(at, pair_out, own_part, other_part, own_w, other_w, out_ref):
    for x in range(NX):
        cut = slice(x * BLOCK, (x + 1) * BLOCK)
        for flip, part, w in ((0, own_part, own_w), (1, other_part, other_w)):
            parity = at[2] if flip == 0 else 1 - at[2]
            total = part[:, cut] + lax.dot_general(
                pair_out[...], w[cut, :], TURN, preferred_element_type=jnp.float32
            )
            to_block = pl.ds(pl.multiple_of((x * NC + parity) * BLOCK, BLOCK), BLOCK)
            out_ref[:, to_block] = total.astype(jnp.bfloat16)


def finish(at, pair_out, parts, weights):
    whole = pl.BlockSpec(memory_space=pltpu.VMEM)
    return pl.pallas_call(
        finish_body,
        in_specs=[pl.BlockSpec(memory_space=pltpu.SMEM)] + [whole] * 5,
        out_shape=jax.ShapeDtypeStruct((pair_out.shape[0], NX * NC * BLOCK), jnp.bfloat16),
        compiler_params=pltpu.CompilerParams(vmem_limit_bytes=VMEM_LIMIT),
    )(at, pair_out, *[in_vmem(p) for p in parts], *[in_vmem(w) for w in weights])


def shifted(block, axis, distance):
    devices = range(lax.axis_size(axis))
    return lax.ppermute(block, axis, [(i - distance, i) for i in devices if i - distance in devices])


def angles_for(positions, head_size):
    half_size = head_size // 2
    inverse = jnp.power(
        jnp.float32(ROPE_BASE), -jnp.arange(half_size, dtype=jnp.float32) / half_size
    )
    phase_angle = positions.astype(jnp.float32)[:, None] * inverse[None, :]
    return (jnp.cos(phase_angle), jnp.sin(phase_angle))


def rotate(vectors, cos_part, sin_part):
    half_size = vectors.shape[-1] // 2
    a = vectors[..., :half_size]
    b = vectors[..., half_size:]
    return jnp.concatenate([a * cos_part - b * sin_part, b * cos_part + a * sin_part], axis=-1)


def local(tokens, doc_start, out_grad, w_qkv):
    row_count = tokens.shape[1]
    score_scale = 1.0 / math.sqrt(HD)
    features = tokens[0]
    begin_rows = doc_start[0]
    grad_rows = out_grad[0].reshape(row_count, HQ, HD)
    fsdp, ctx = lax.axis_index("fsdp"), lax.axis_index("ctx")
    x_me, core = fsdp // NC, fsdp % NC
    y_me = ctx % NY

    column = w_qkv
    for far in (8, 4, 2, 1):
        column = lax.all_gather(
            column, "ctx", axis=0, tiled=True,
            axis_index_groups=[
                [z * NY + y, (z + far) * NY + y] for z in range(NZ) if not z & far for y in range(NY)
            ],
        )
    second, first, third = (hop(column, d, 0) for d in (2, 1, 3))

    at = jnp.stack([x_me, y_me, core]).astype(jnp.int32)
    plane, theirs = lax.optimization_barrier(
        (stack_plane([column, first, second, third]), pick(at, features))
    )
    two, one, three = (hop(plane, d, 1) for d in (2, 1, 3))
    arranged = arrange(at, features, swap_cores(theirs))
    steps = (0, 3, 1, 2)
    sums = first_sums(arranged, plane)
    mine, theirs, own_w = rest_sums(arranged, sums, plane, [three, one, two], steps[1:])
    projected = mine + swap_cores(theirs)
    other_w = swap_cores(own_w)
    pair_pre, query_pre = projected[:, HQ * HD :], projected[:, : HQ * HD]

    first_row = ctx * row_count
    query_index = first_row + jnp.arange(row_count, dtype=jnp.int32)
    cos_part, sin_part = angles_for(query_index - begin_rows, HD)
    pair_rows = jnp.concatenate(
        [rotate(pair_pre[:, :HD], cos_part, sin_part), pair_pre[:, HD:]], axis=1
    ).astype(jnp.bfloat16)
    back2 = shifted(pair_rows, "ctx", 2)
    back2, at_later = lax.optimization_barrier((back2, at))
    back31, pair_w_own = lax.optimization_barrier(
        (
            shifted(jnp.concatenate([back2, pair_rows], axis=0), "ctx", 1),
            pair_weights_of(at_later, own_w, steps, 0),
        )
    )
    window = jnp.concatenate([back31[:row_count], back2, back31[row_count:], pair_rows], axis=0)

    queries = rotate(
        query_pre.reshape(row_count, HQ, HD), cos_part[:, None, :], sin_part[:, None, :]
    ).astype(jnp.bfloat16)
    keys, values = window[:, :HD], window[:, HD:]
    key_index = first_row - (REACH - 1) * row_count + jnp.arange(REACH * row_count, dtype=jnp.int32)
    allowed = (key_index[None, :] <= query_index[:, None]) & (
        key_index[None, :] >= begin_rows[:, None]
    )
    scores = (
        jnp.einsum("qhd,kd->hqk", queries, keys, preferred_element_type=jnp.float32) * score_scale
    )
    scores = jnp.where(allowed[None], scores, MASKED)
    top = jnp.max(scores, axis=-1, keepdims=True)
    unnormed = jnp.where(allowed[None], jnp.exp(scores - top), 0.0)
    probs = unnormed / jnp.sum(unnormed, axis=-1, keepdims=True)
    probs_low = probs.astype(jnp.bfloat16)
    grad_probs = jnp.einsum("qhd,kd->hqk", grad_rows, values, preferred_element_type=jnp.float32)
    attn_out = jnp.einsum(
        "hqk,kd->hqd", probs_low, values, preferred_element_type=jnp.float32
    ).astype(jnp.bfloat16)
    row_delta = jnp.sum(
        jnp.transpose(grad_rows, (1, 0, 2)).astype(jnp.float32) * attn_out.astype(jnp.float32),
        axis=-1, keepdims=True,
    )
    grad_value = jnp.einsum("hqk,qhd->kd", probs_low, grad_rows, preferred_element_type=jnp.float32)
    grad_scores = (probs * (grad_probs - row_delta)).astype(jnp.bfloat16)
    grad_query = (
        jnp.einsum("hqk,kd->qhd", grad_scores, keys, preferred_element_type=jnp.float32)
        * score_scale
    )
    grad_key = (
        jnp.einsum("hqk,qhd->kd", grad_scores, queries, preferred_element_type=jnp.float32)
        * score_scale
    )
    pair_grad = jnp.concatenate([grad_key, grad_value], axis=1)
    query_out = rotate(grad_query, cos_part[:, None, :], -sin_part[:, None, :]).reshape(
        row_count, HQ * HD
    ).astype(jnp.bfloat16)
    back3, back2, back1, own_grad = (
        pair_grad[i * row_count : (i + 1) * row_count] for i in range(REACH)
    )
    came, part_own = lax.optimization_barrier(
        (
            shifted(jnp.concatenate([back3, back1], axis=0).astype(jnp.bfloat16), "ctx", -1),
            query_part_of(at, query_out, own_w, steps, 0),
        )
    )
    came = came.astype(jnp.float32)
    last, part_other, pair_w_other = lax.optimization_barrier(
        (
            shifted((back2 + came[:row_count]).astype(jnp.bfloat16), "ctx", -2),
            query_part_of(at, query_out, other_w, steps, 1),
            pair_weights_of(at, other_w, steps, 1),
        )
    )
    pair_total = own_grad + came[row_count:] + last.astype(jnp.float32)
    pair_out = jnp.concatenate(
        [rotate(pair_total[:, :HD], cos_part, -sin_part), pair_total[:, HD:]], axis=1
    ).astype(jnp.bfloat16)
    return finish(at, pair_out, [part_own, part_other], [pair_w_own, pair_w_other])[None]


def solution(mesh):
    placed = (
        P("fsdp", "ctx", None),
        P("fsdp", "ctx"),
        P("fsdp", "ctx", None),
        P(("fsdp", "ctx"), None),
    )
    return jax.shard_map(
        local, mesh=mesh, in_specs=placed, out_specs=P("fsdp", "ctx", None), check_vma=False
    )
```

time: 151 us -> 154 us (1.020)
  the two profiles are of different devices: /device:TPU:24 before, /device:TPU:394 now
where the time goes in v4:
time: 154 us; the launch traced here: 153 us
  starting transfers between devices  49 us (32%)
  blocking collectives  35 us (23%)
  waiting for transfers between devices  27.9 us (18%)
  Pallas kernels  23.7 us (15%)
  local copies, waits for them, and re-layouts  8.04 us (5%)
  matrix products  4.35 us (3%)
  other arithmetic  4.24 us (3%)
    all_gather x4, blocking collectives, local(): lax.all_gather(column, 'ctx', axis=0, tiled=True, axis_index_groups=[[z *...  35 us
    ppermute x6, starting transfers between devices, hop(): return lax.ppermute(block, ALL, route(move))  21.7 us
    ppermute x4, starting transfers between devices, shifted(): lax.ppermute(block, axis, [(i - distance, i) for i in devices if i - dist...  21 us
    ppermute x6, waiting for transfers between devices, hop(): return lax.ppermute(block, ALL, route(move))  20.7 us
    pallas_call x2, Pallas kernels, query_part_of(): pl.pallas_call(functools.partial(query_part_body, steps, flip), in_specs=...  8.73 us
    unnamed x23, local copies, waits for them, and re-layouts  7.8 us
    ppermute x4, waiting for transfers between devices, shifted(): lax.ppermute(block, axis, [(i - distance, i) for i in devices if i - dist...  6.97 us
    ppermute x3, starting transfers between devices, swap_cores(): return lax.ppermute(block, ALL, route(lambda x, c, z, y: (x, 1 - c, z, y)))  6.25 us
  transfers between devices with their start and end apart: 13, of which 8 were waited for; matrix products, arithmetic and copies ran while one was open for 7% of the time, Pallas kernels for 11%

profile of v4, /device:TPU:394, one launch (start us, length us, event | category | flops | bytes accessed | tf_op | source)
XLA Modules:
  0.0 152.7 jit_solution(15052390470828934133)
XLA Ops:
  0.0 13.4 %all_gather.12 = bf16[16,1280]{1,0:T(8,128)(2,1)S(1)} all-gather(bf16[8,1280]{1,0:T(8,128)(2,1)} %param.7), channel_id=1, replica_groups={{0,32},{1,33},{2,34},{3,35},{4,36},{5,37},{6,38},{7,39},{8,40},{9,41},{..., dimensions={0}, use_global_device_ids=true | all-gather | bytes 61440 | tf_op jit(solution)/shard_map/all_gather | solution.py:359
  13.4 8.7 %all_gather.13 = bf16[32,1280]{1,0:T(8,128)(2,1)S(1)} all-gather(bf16[16,1280]{1,0:T(8,128)(2,1)S(1)} %all_gather.12), channel_id=1, replica_groups={{0,16},{1,17},{2,18},{3,19},{4,20},{5,21},{6,22},{7,23},{8,24},{9,25},{..., dimensions={0}, use_global_device_ids=true | all-gather | bytes 122880 | tf_op jit(solution)/shard_map/all_gather | solution.py:359
  22.0 7.0 %all_gather.14 = bf16[64,1280]{1,0:T(8,128)(2,1)S(1)} all-gather(bf16[32,1280]{1,0:T(8,128)(2,1)S(1)} %all_gather.13), channel_id=1, replica_groups={{0,8},{1,9},{2,10},{3,11},{4,12},{5,13},{6,14},{7,15},{16,24},{17,25},{..., dimensions={0}, use_global_device_ids=true | all-gather | bytes 245760 | tf_op jit(solution)/shard_map/all_gather | solution.py:359
  29.0 6.0 %all_gather.15.own = bf16[128,1280]{1,0:T(8,128)(2,1)S(1)} all-gather(bf16[64,1280]{1,0:T(8,128)(2,1)S(1)} %all_gather.14), channel_id=1, replica_groups={{0,4},{1,5},{2,6},{3,7},{8,12},{9,13},{10,14},{11,15},{16,20},{17,21},{..., dimensions={0}, use_global_device_ids=true | all-gather | bytes 491520 | tf_op jit(solution)/shard_map/all_gather | solution.py:359
  35.0 3.4 %collective-permute-start = (bf16[128,1280]{1,0:T(8,128)(2,1)S(1)}, bf16[128,1280]{1,0:T(8,128)(2,1)S(1)}, u32[]{:S(2)}, u32[]{:S(2)}) collective-permute-start(bf16[128,1280]{1,0:T(8,128)(2,1)S(1)} %all_gather.15.own), channel_id=1, source_target_pairs={{0,128},{1,129},{2,130},{3,131},{4,132},{5,133},{6,134},{7,135},{8... | collective-permute-start | bytes 983048 | tf_op jit(solution)/shard_map/ppermute | solution.py:40
  38.4 3.0 %collective-permute-start.1 = (bf16[128,1280]{1,0:T(8,128)(2,1)S(1)}, bf16[128,1280]{1,0:T(8,128)(2,1)S(1)}, u32[]{:S(2)}, u32[]{:S(2)}) collective-permute-start(bf16[128,1280]{1,0:T(8,128)(2,1)S(1)} %all_gather.15.own), channel_id=1, source_target_pairs={{0,256},{1,257},{2,258},{3,259},{4,260},{5,261},{6,262},{7,263},{8... | collective-permute-start | bytes 983048 | tf_op jit(solution)/shard_map/ppermute | solution.py:40
  41.4 4.1 %collective-permute-start.2 = (bf16[128,1280]{1,0:T(8,128)(2,1)S(1)}, bf16[128,1280]{1,0:T(8,128)(2,1)S(1)}, u32[]{:S(2)}, u32[]{:S(2)}) collective-permute-start(bf16[128,1280]{1,0:T(8,128)(2,1)S(1)} %all_gather.15.own), channel_id=1, source_target_pairs={{0,384},{1,385},{2,386},{3,387},{4,388},{5,389},{6,390},{7,391},{8... | collective-permute-start | bytes 983048 | tf_op jit(solution)/shard_map/ppermute | solution.py:40
  45.6 1.2 copy-done
  46.8 0.6 shard_map.47
  47.4 1.5 %collective-permute-done.1.second = bf16[128,1280]{1,0:T(8,128)(2,1)S(1)} collective-permute-done((bf16[128,1280]{1,0:T(8,128)(2,1)S(1)}, bf16[128,1280]{1,0:T(8,128)(2,1)S(1)}, u32[]{:S(2)}, u32[]{:S(2)}) %collective-permute-start.1) | collective-permute-done | bytes 327712 | tf_op jit(solution)/shard_map/ppermute | solution.py:40
  49.0 0.7 copy-done.2
  49.7 2.7 %collective-permute-done.2.third = bf16[128,1280]{1,0:T(8,128)(2,1)S(1)} collective-permute-done((bf16[128,1280]{1,0:T(8,128)(2,1)S(1)}, bf16[128,1280]{1,0:T(8,128)(2,1)S(1)}, u32[]{:S(2)}, u32[]{:S(2)}) %collective-permute-start.2) | collective-permute-done | bytes 327712 | tf_op jit(solution)/shard_map/ppermute | solution.py:40
  52.4 0.7 copy-done.4
  53.1 1.0 copy-done.3
  54.1 1.0 copy-done.5
  55.1 2.4 %collective-permute-start.4 = (bf16[512,1280]{1,0:T(8,128)(2,1)S(1)}, bf16[512,1280]{1,0:T(8,128)(2,1)}, u32[]{:S(2)}, u32[]{:S(2)}) collective-permute-start(bf16[512,1280]{1,0:T(8,128)(2,1)S(1)} %shard_map.46.piece.plane), channel_id=1, source_target_pairs={{0,3},{1,0},{2,1},{3,2},{4,7},{5,4},{6,5},{7,6},{8,11},{9,8},{10,9... | collective-permute-start | bytes 3932168 | tf_op jit(solution)/shard_map/ppermute | solution.py:40
  57.5 3.5 %collective-permute-start.5 = (bf16[512,1280]{1,0:T(8,128)(2,1)S(1)}, bf16[512,1280]{1,0:T(8,128)(2,1)}, u32[]{:S(2)}, u32[]{:S(2)}) collective-permute-start(bf16[512,1280]{1,0:T(8,128)(2,1)S(1)} %shard_map.46.piece.plane), channel_id=1, source_target_pairs={{0,1},{1,2},{2,3},{3,0},{4,5},{5,6},{6,7},{7,4},{8,9},{9,10},{10,1... | collective-permute-start | bytes 3932168 | tf_op jit(solution)/shard_map/ppermute | solution.py:40
  61.0 5.4 %collective-permute-start.6 = (bf16[512,1280]{1,0:T(8,128)(2,1)S(1)}, bf16[512,1280]{1,0:T(8,128)(2,1)}, u32[]{:S(2)}, u32[]{:S(2)}) collective-permute-start(bf16[512,1280]{1,0:T(8,128)(2,1)S(1)} %shard_map.46.piece.plane), channel_id=1, source_target_pairs={{0,2},{1,3},{2,0},{3,1},{4,6},{5,7},{6,4},{7,5},{8,10},{9,11},{10,... | collective-permute-start | bytes 3932168 | tf_op jit(solution)/shard_map/ppermute | solution.py:40
  66.4 1.9 %collective-permute-start.3 = (bf16[128,2048]{1,0:T(8,128)(2,1)S(1)}, bf16[128,2048]{1,0:T(8,128)(2,1)}, u32[]{:S(2)}, u32[]{:S(2)}) collective-permute-start(bf16[128,2048]{1,0:T(8,128)(2,1)S(1)} %shard_map.47), channel_id=1, source_target_pairs={{0,64},{1,65},{2,66},{3,67},{4,68},{5,69},{6,70},{7,71},{8,72},{9,... | collective-permute-start | bytes 1572872 | tf_op jit(solution)/shard_map/ppermute | solution.py:44
  68.4 1.8 %copy.7 = bf16[1,128,1024]{1,2,0:T(8,128)(2,1)} copy(bf16[1,128,1024]{2,1,0:T(8,128)(2,1)} %param.6) | data formatting | bytes 524288 | tf_op args[2]
  70.4 2.5 %shard_map.48.arranged = bf16[1024,512]{1,0:T(8,128)(2,1)S(1)} custom-call(s32[3]{0:T(128)S(1)} %pad_add_fusion.at, bf16[128,4096]{1,0:T(8,128)(2,1)S(1)} %bitcast.62, bf16[128,2048]{1,0:T(8,128)(2,1)} %collective-permute-done.3.theirs), custom_call_target="tpu_custom_call" | custom-call | flops 536870912 | bytes 4194304 | tf_op jit(solution)/shard_map/pallas_call | solution.py:90
  72.8 0.5 shard_map.49
  73.4 1.4 collective-permute-done.4.refs_0_
  74.8 3.4 %collective-permute-done.5.refs_1_ = bf16[512,1280]{1,0:T(8,128)(2,1)} collective-permute-done((bf16[512,1280]{1,0:T(8,128)(2,1)S(1)}, bf16[512,1280]{1,0:T(8,128)(2,1)}, u32[]{:S(2)}, u32[]{:S(2)}) %collective-permute-start.5) | collective-permute-done | bytes 1310752 | tf_op jit(solution)/shard_map/ppermute | solution.py:40
  78.1 11.7 %collective-permute-done.6.refs_2_ = bf16[512,1280]{1,0:T(8,128)(2,1)} collective-permute-done((bf16[512,1280]{1,0:T(8,128)(2,1)S(1)}, bf16[512,1280]{1,0:T(8,128)(2,1)}, u32[]{:S(2)}, u32[]{:S(2)}) %collective-permute-start.6) | collective-permute-done | bytes 1310752 | tf_op jit(solution)/shard_map/ppermute | solution.py:40
  89.8 4.0 %shard_map.50 = (f32[128,1280]{1,0:T(8,128)S(1)}, f32[128,1280]{1,0:T(8,128)S(1)}, bf16[2048,1280]{1,0:T(8,128)(2,1)}) custom-call(bf16[1024,512]{1,0:T(8,128)(2,1)S(1)} %shard_map.48.arranged, f32[128,1280]{1,0:T(8,128)S(1)} %get-tuple-element.23.mine_in, f32[128,1280]{1,0:T(8,128)S(1)} %get-tuple-element.24.theirs_in, ...), custom_call_target="tpu_custom_call" | custom-call | flops 1006632960 | bytes 9437184 | tf_op jit(solution)/shard_map/pallas_call | solution.py:190
  93.8 1.9 %collective-permute-start.7 = (f32[128,1280]{1,0:T(8,128)S(1)}, f32[128,1280]{1,0:T(8,128)S(1)}, u32[]{:S(2)}, u32[]{:S(2)}) collective-permute-start(f32[128,1280]{1,0:T(8,128)S(1)} %get-tuple-element.26), channel_id=1, source_target_pairs={{0,64},{1,65},{2,66},{3,67},{4,68},{5,69},{6,70},{7,71},{8,72},{9,... | collective-permute-start | bytes 1966088 | tf_op jit(solution)/shard_map/ppermute | solution.py:44
  95.7 2.4 %collective-permute-start.12 = (bf16[2048,1280]{1,0:T(8,128)(2,1)}, bf16[2048,1280]{1,0:T(8,128)(2,1)}, u32[]{:S(2)}, u32[]{:S(2)}) collective-permute-start(bf16[2048,1280]{1,0:T(8,128)(2,1)} %get-tuple-element.29.all_rows), channel_id=1, source_target_pairs={{0,64},{1,65},{2,66},{3,67},{4,68},{5,69},{6,70},{7,71},{8,72},{9,... | collective-permute-start | bytes 15728648 | tf_op jit(solution)/shard_map/ppermute | solution.py:44
  98.2 0.8 compare_and_fusion
  99.4 5.8 %collective-permute-start.8 = (bf16[128,256]{1,0:T(8,128)(2,1)S(1)}, bf16[128,256]{1,0:T(8,128)(2,1)S(1)}, u32[]{:S(2)}, u32[]{:S(2)}) collective-permute-start(bf16[128,256]{1,0:T(8,128)(2,1)S(1)} %pad_maximum_fusion.3), channel_id=1, source_target_pairs={{0,2},{1,3},{2,4},{3,5},{4,6},{5,7},{6,8},{7,9},{8,10},{9,11},{10,... | collective-permute-start | bytes 196616 | tf_op jit(solution)/shard_map/ppermute | solution.py:328
  105.6 3.6 %collective-permute-done.8 = bf16[128,256]{1,0:T(8,128)(2,1)S(1)} collective-permute-done((bf16[128,256]{1,0:T(8,128)(2,1)S(1)}, bf16[128,256]{1,0:T(8,128)(2,1)S(1)}, u32[]{:S(2)}, u32[]{:S(2)}) %collective-permute-start.8) | collective-permute-done | bytes 65568 | tf_op jit(solution)/shard_map/ppermute | solution.py:328
  109.3 3.6 %collective-permute-start.9 = (bf16[256,256]{1,0:T(8,128)(2,1)S(1)}, bf16[256,256]{1,0:T(8,128)(2,1)S(1)}, u32[]{:S(2)}, u32[]{:S(2)}) collective-permute-start(bf16[256,256]{1,0:T(8,128)(2,1)S(1)} %maximum_maximum_fusion.1), channel_id=1, source_target_pairs={{0,1},{1,2},{2,3},{3,4},{4,5},{5,6},{6,7},{7,8},{8,9},{9,10},{10,1... | collective-permute-start | bytes 393224 | tf_op jit(solution)/shard_map/ppermute | solution.py:328
  112.9 0.9 subtract_convert_fusion.1
  113.9 2.5 %shard_map.51.own_w = bf16[2048,256]{1,0:T(8,128)(2,1)S(1)} custom-call(s32[3]{0:T(128)S(1)} %pad_add_fusion.at, bf16[2048,1280]{1,0:T(8,128)(2,1)} %get-tuple-element.29.all_rows), custom_call_target="tpu_custom_call" | custom-call | flops 536870912 | bytes 3145728 | tf_op jit(solution)/shard_map/pallas_call | solution.py:289
  116.4 3.4 %collective-permute-done.9 = bf16[256,256]{1,0:T(8,128)(2,1)S(1)} collective-permute-done((bf16[256,256]{1,0:T(8,128)(2,1)S(1)}, bf16[256,256]{1,0:T(8,128)(2,1)S(1)}, u32[]{:S(2)}, u32[]{:S(2)}) %collective-permute-start.9) | collective-permute-done | bytes 131104 | tf_op jit(solution)/shard_map/ppermute | solution.py:328
  119.8 0.8 maximum_maximum_fusion
  120.6 2.0 %fusion.43 = (f32[8,128]{1,0:T(8,128)S(1)}, f32[8,128,512]{1,2,0:T(8,128)S(1)}) fusion(pred[128,512]{0,1:T(8,128)(4,1)} %compare_and_fusion, bf16[512,256]{1,0:T(8,128)(2,1)} %maximum_maximum_fusion, bf16[128,8,64]{2,0,1:T(8,128)(2,1)} %get-tuple-element.38, bf16[128,8,64]{2,0,1:T(8,128)(2,1)S(1)} %get-tuple-element.37), kind=kOutput, calls=%fused_computation.80 | convolution fusion | flops 137363968 | bytes 2756608 | tf_op jit(solution)/shard_map/sub | solution.py:409
  122.8 0.7 copy-done.7
  124.4 0.4 fusion.2
  124.8 0.5 copy-done.6
  125.3 0.5 fusion.8
  125.9 7.2 %collective-permute-start.10 = (bf16[256,256]{1,0:T(8,128)(2,1)S(1)}, bf16[256,256]{1,0:T(8,128)(2,1)S(1)}, u32[]{:S(2)}, u32[]{:S(2)}) collective-permute-start(bf16[256,256]{1,0:T(8,128)(2,1)S(1)} %pad_maximum_fusion.2), channel_id=1, source_target_pairs={{1,0},{2,1},{3,2},{4,3},{5,4},{6,5},{7,6},{8,7},{9,8},{10,9},{11,1... | collective-permute-start | bytes 393224 | tf_op jit(solution)/shard_map/ppermute | solution.py:328
  133.2 0.5 fusion.4
  134.2 4.4 %shard_map.52.own_part = f32[128,2048]{1,0:T(8,128)S(1)} custom-call(s32[3]{0:T(128)S(1)} %pad_add_fusion.at, bf16[128,1024]{1,0:T(8,128)(2,1)S(1)} %copy_bitcast_fusion.grads, bf16[2048,1280]{1,0:T(8,128)(2,1)} %get-tuple-element.29.all_rows), custom_call_target="tpu_custom_call" | custom-call | flops 1073741824 | bytes 6291456 | tf_op jit(solution)/shard_map/pallas_call | solution.py:251
  138.6 4.4 %collective-permute-start.11 = (bf16[128,256]{1,0:T(8,128)(2,1)S(1)}, bf16[128,256]{1,0:T(8,128)(2,1)S(1)}, u32[]{:S(2)}, u32[]{:S(2)}) collective-permute-start(bf16[128,256]{1,0:T(8,128)(2,1)S(1)} %fusion.21), channel_id=1, source_target_pairs={{2,0},{3,1},{4,2},{5,3},{6,4},{7,5},{8,6},{9,7},{10,8},{11,9},{12,... | collective-permute-start | bytes 196616 | tf_op jit(solution)/shard_map/ppermute | solution.py:328
  143.0 4.4 %shard_map.53.other_part = f32[128,2048]{1,0:T(8,128)S(1)} custom-call(s32[3]{0:T(128)S(1)} %pad_add_fusion.at, bf16[128,1024]{1,0:T(8,128)(2,1)S(1)} %copy_bitcast_fusion.grads, bf16[2048,1280]{1,0:T(8,128)(2,1)} %collective-permute-done.12.all_rows), custom_call_target="tpu_custom_call" | custom-call | flops 1073741824 | bytes 6291456 | tf_op jit(solution)/shard_map/pallas_call | solution.py:251
  147.4 2.5 %shard_map.54.other_w = bf16[2048,256]{1,0:T(8,128)(2,1)S(1)} custom-call(s32[3]{0:T(128)S(1)} %pad_add_fusion.at, bf16[2048,1280]{1,0:T(8,128)(2,1)} %collective-permute-done.12.all_rows), custom_call_target="tpu_custom_call" | custom-call | flops 536870912 | bytes 3145728 | tf_op jit(solution)/shard_map/pallas_call | solution.py:289
  150.4 2.3 %shard_map.55 = bf16[128,4096]{1,0:T(8,128)(2,1)} custom-call(s32[3]{0:T(128)S(1)} %pad_add_fusion.at, bf16[128,256]{1,0:T(8,128)(2,1)S(1)} %pad_maximum_fusion.4.pair_out, f32[128,2048]{1,0:T(8,128)S(1)} %shard_map.52.own_part, f32[128,2048]{1,0:T(8,128)S(1)} %shard_map.53.other_part, bf16[2048,256]{1,0:T(8,128)(2,1)S(1)} %shard_map.51.own_w, ...), custom_call_target="tpu_custom_call" | custom-call | tf_op jit(solution)/shard_map/pallas_call | solution.py:318
  (47 shorter events, 3.3 us)
Async XLA Ops:
  35.0 12.4 %collective-permute-start = (bf16[128,1280]{1,0:T(8,128)(2,1)S(1)}, bf16[128,1280]{1,0:T(8,128)(2,1)S(1)}, u32[]{:S(2)}, u32[]{:S(2)}) collective-permute-start(bf16[128,1280]{1,0:T(8,128)(2,1)S(1)} %all_gather.15.own), channel_id=1, source_target_pairs={{0,128},{1,129},{2,130},{3,131},{4,132},{5,133},{6,134},{7,135},{8... | collective-permute-start | bytes 983048 | tf_op jit(solution)/shard_map/ppermute | solution.py:40
  38.4 10.6 %collective-permute-start.1 = (bf16[128,1280]{1,0:T(8,128)(2,1)S(1)}, bf16[128,1280]{1,0:T(8,128)(2,1)S(1)}, u32[]{:S(2)}, u32[]{:S(2)}) collective-permute-start(bf16[128,1280]{1,0:T(8,128)(2,1)S(1)} %all_gather.15.own), channel_id=1, source_target_pairs={{0,256},{1,257},{2,258},{3,259},{4,260},{5,261},{6,262},{7,263},{8... | collective-permute-start | bytes 983048 | tf_op jit(solution)/shard_map/ppermute | solution.py:40
  41.4 11.0 %collective-permute-start.2 = (bf16[128,1280]{1,0:T(8,128)(2,1)S(1)}, bf16[128,1280]{1,0:T(8,128)(2,1)S(1)}, u32[]{:S(2)}, u32[]{:S(2)}) collective-permute-start(bf16[128,1280]{1,0:T(8,128)(2,1)S(1)} %all_gather.15.own), channel_id=1, source_target_pairs={{0,384},{1,385},{2,386},{3,387},{4,388},{5,389},{6,390},{7,391},{8... | collective-permute-start | bytes 983048 | tf_op jit(solution)/shard_map/ppermute | solution.py:40
  45.6 1.2 copy-start
  46.8 23.5 %copy-start.1 = (bf16[1,128,4096]{2,1,0:T(8,128)(2,1)S(1)}, bf16[1,128,4096]{2,1,0:T(8,128)(2,1)}, u32[]{:S(2)}) copy-start(bf16[1,128,4096]{2,1,0:T(8,128)(2,1)} %param.4) | copy-start | bytes 3145732
  49.0 0.7 copy-start.2
  52.4 0.7 copy-start.4
  53.1 1.0 copy-start.3
  54.1 1.0 copy-start.5
  55.1 19.6 %collective-permute-start.4 = (bf16[512,1280]{1,0:T(8,128)(2,1)S(1)}, bf16[512,1280]{1,0:T(8,128)(2,1)}, u32[]{:S(2)}, u32[]{:S(2)}) collective-permute-start(bf16[512,1280]{1,0:T(8,128)(2,1)S(1)} %shard_map.46.piece.plane), channel_id=1, source_target_pairs={{0,3},{1,0},{2,1},{3,2},{4,7},{5,4},{6,5},{7,6},{8,11},{9,8},{10,9... | collective-permute-start | bytes 3932168 | tf_op jit(solution)/shard_map/ppermute | solution.py:40
  57.5 20.6 %collective-permute-start.5 = (bf16[512,1280]{1,0:T(8,128)(2,1)S(1)}, bf16[512,1280]{1,0:T(8,128)(2,1)}, u32[]{:S(2)}, u32[]{:S(2)}) collective-permute-start(bf16[512,1280]{1,0:T(8,128)(2,1)S(1)} %shard_map.46.piece.plane), channel_id=1, source_target_pairs={{0,1},{1,2},{2,3},{3,0},{4,5},{5,6},{6,7},{7,4},{8,9},{9,10},{10,1... | collective-permute-start | bytes 3932168 | tf_op jit(solution)/shard_map/ppermute | solution.py:40
  61.0 28.8 %collective-permute-start.6 = (bf16[512,1280]{1,0:T(8,128)(2,1)S(1)}, bf16[512,1280]{1,0:T(8,128)(2,1)}, u32[]{:S(2)}, u32[]{:S(2)}) collective-permute-start(bf16[512,1280]{1,0:T(8,128)(2,1)S(1)} %shard_map.46.piece.plane), channel_id=1, source_target_pairs={{0,2},{1,3},{2,0},{3,1},{4,6},{5,7},{6,4},{7,5},{8,10},{9,11},{10,... | collective-permute-start | bytes 3932168 | tf_op jit(solution)/shard_map/ppermute | solution.py:40
  66.4 3.9 %collective-permute-start.3 = (bf16[128,2048]{1,0:T(8,128)(2,1)S(1)}, bf16[128,2048]{1,0:T(8,128)(2,1)}, u32[]{:S(2)}, u32[]{:S(2)}) collective-permute-start(bf16[128,2048]{1,0:T(8,128)(2,1)S(1)} %shard_map.47), channel_id=1, source_target_pairs={{0,64},{1,65},{2,66},{3,67},{4,68},{5,69},{6,70},{7,71},{8,72},{9,... | collective-permute-start | bytes 1572872 | tf_op jit(solution)/shard_map/ppermute | solution.py:44
  89.8 8.3 %copy-start.9 = (s32[1,128]{1,0:T(1,128)S(1)}, s32[1,128]{1,0:T(1,128)}, u32[]{:S(2)}) copy-start(s32[1,128]{1,0:T(1,128)} %param.5) | copy-start | bytes 1540
  93.8 5.2 %collective-permute-start.7 = (f32[128,1280]{1,0:T(8,128)S(1)}, f32[128,1280]{1,0:T(8,128)S(1)}, u32[]{:S(2)}, u32[]{:S(2)}) collective-permute-start(f32[128,1280]{1,0:T(8,128)S(1)} %get-tuple-element.26), channel_id=1, source_target_pairs={{0,64},{1,65},{2,66},{3,67},{4,68},{5,69},{6,70},{7,71},{8,72},{9,... | collective-permute-start | bytes 1966088 | tf_op jit(solution)/shard_map/ppermute | solution.py:44
  95.7 47.3 %collective-permute-start.12 = (bf16[2048,1280]{1,0:T(8,128)(2,1)}, bf16[2048,1280]{1,0:T(8,128)(2,1)}, u32[]{:S(2)}, u32[]{:S(2)}) collective-permute-start(bf16[2048,1280]{1,0:T(8,128)(2,1)} %get-tuple-element.29.all_rows), channel_id=1, source_target_pairs={{0,64},{1,65},{2,66},{3,67},{4,68},{5,69},{6,70},{7,71},{8,72},{9,... | collective-permute-start | bytes 15728648 | tf_op jit(solution)/shard_map/ppermute | solution.py:44
  99.4 9.8 %collective-permute-start.8 = (bf16[128,256]{1,0:T(8,128)(2,1)S(1)}, bf16[128,256]{1,0:T(8,128)(2,1)S(1)}, u32[]{:S(2)}, u32[]{:S(2)}) collective-permute-start(bf16[128,256]{1,0:T(8,128)(2,1)S(1)} %pad_maximum_fusion.3), channel_id=1, source_target_pairs={{0,2},{1,3},{2,4},{3,5},{4,6},{5,7},{6,8},{7,9},{8,10},{9,11},{10,... | collective-permute-start | bytes 196616 | tf_op jit(solution)/shard_map/ppermute | solution.py:328
  109.3 10.4 %collective-permute-start.9 = (bf16[256,256]{1,0:T(8,128)(2,1)S(1)}, bf16[256,256]{1,0:T(8,128)(2,1)S(1)}, u32[]{:S(2)}, u32[]{:S(2)}) collective-permute-start(bf16[256,256]{1,0:T(8,128)(2,1)S(1)} %maximum_maximum_fusion.1), channel_id=1, source_target_pairs={{0,1},{1,2},{2,3},{3,4},{4,5},{5,6},{6,7},{7,8},{8,9},{9,10},{10,1... | collective-permute-start | bytes 393224 | tf_op jit(solution)/shard_map/ppermute | solution.py:328
  122.6 1.0 copy-start.7
  122.6 1.4 copy-start.8
  124.4 1.0 copy-start.6
  125.9 12.6 %collective-permute-start.10 = (bf16[256,256]{1,0:T(8,128)(2,1)S(1)}, bf16[256,256]{1,0:T(8,128)(2,1)S(1)}, u32[]{:S(2)}, u32[]{:S(2)}) collective-permute-start(bf16[256,256]{1,0:T(8,128)(2,1)S(1)} %pad_maximum_fusion.2), channel_id=1, source_target_pairs={{1,0},{2,1},{3,2},{4,3},{5,4},{6,5},{7,6},{8,7},{9,8},{10,9},{11,1... | collective-permute-start | bytes 393224 | tf_op jit(solution)/shard_map/ppermute | solution.py:328
  138.6 11.3 %collective-permute-start.11 = (bf16[128,256]{1,0:T(8,128)(2,1)S(1)}, bf16[128,256]{1,0:T(8,128)(2,1)S(1)}, u32[]{:S(2)}, u32[]{:S(2)}) collective-permute-start(bf16[128,256]{1,0:T(8,128)(2,1)S(1)} %fusion.21), channel_id=1, source_target_pairs={{2,0},{3,1},{4,2},{5,3},{6,4},{7,5},{8,6},{9,7},{10,8},{11,9},{12,... | collective-permute-start | bytes 196616 | tf_op jit(solution)/shard_map/ppermute | solution.py:328

commit v5 on v1

v5 whole, which is shorter than its diff:
```python
import functools
import math

import jax
import jax.numpy as jnp
from jax import lax
from jax.experimental import pallas as pl
from jax.experimental.pallas import tpu as pltpu
from jax.sharding import PartitionSpec as P

HQ = 8
HD = 128
REACH = 4
ROPE_BASE = 500000.0
MASKED = -1e30
NX, NC, NZ, NY = 4, 2, 16, 4
ALL = ("fsdp", "ctx")


def place(x, c, z, y):
    return (x * NC + c) * (NZ * NY) + z * NY + y


def route(move):
    return [
        (place(x, c, z, y), place(*move(x, c, z, y)))
        for x in range(NX)
        for c in range(NC)
        for z in range(NZ)
        for y in range(NY)
    ]


def along_y(block, distance):
    return lax.ppermute(
        block, ALL, route(lambda x, c, z, y: (x, c, z, (y + distance) % NY))
    )


def along_x(block, distance):
    return lax.ppermute(
        block, ALL, route(lambda x, c, z, y: ((x + distance) % NX, c, z, y))
    )


def swap_cores(block):
    return lax.ppermute(block, ALL, route(lambda x, c, z, y: (x, 1 - c, z, y)))


BLOCK = NZ * NY * 8
SPAN = NZ * 8
TURN = (((1,), (1,)), ((), ()))
VMEM_LIMIT = 14 * 1024 * 1024


def order_matrix(y_me):
    slot = lax.broadcasted_iota(jnp.int32, (BLOCK, BLOCK), 1)
    source = lax.broadcasted_iota(jnp.int32, (BLOCK, BLOCK), 0)
    step, inner = slot // SPAN, slot % SPAN
    wanted = inner // 8 * (NY * 8) + (y_me - step + NY) % NY * 8 + inner % 8
    return (source == wanted).astype(jnp.bfloat16)


def x_block(x_me, step):
    return pl.multiple_of((x_me - step + NX) % NX * BLOCK, BLOCK)


def arrange_body(at, order, features, theirs, out_ref):
    for e in range(NX):
        x_at = (at[0] - e + NX) % NX
        own = features[:, pl.ds(pl.multiple_of((x_at * NC + at[2]) * BLOCK, BLOCK), BLOCK)]
        other = theirs[:, pl.ds(pl.multiple_of(x_at * BLOCK, BLOCK), BLOCK)]
        both = jnp.concatenate([own, other], axis=0)
        rows = both.shape[0]
        out_ref[e * rows : (e + 1) * rows, :] = jnp.dot(
            both, order[...], preferred_element_type=jnp.float32
        ).astype(jnp.bfloat16)


SCALARS = pl.BlockSpec(memory_space=pltpu.SMEM)
WHOLE = pl.BlockSpec(memory_space=pltpu.VMEM)
LEFT = pl.BlockSpec(memory_space=pl.ANY)


def call(body, in_specs, out_shape, flops, mib, **more):
    return pl.pallas_call(
        body,
        in_specs=in_specs,
        out_shape=out_shape,
        compiler_params=pltpu.CompilerParams(vmem_limit_bytes=VMEM_LIMIT),
        cost_estimate=pl.CostEstimate(flops=flops, bytes_accessed=mib << 20, transcendentals=0),
        **more,
    )


def arrange(at, order, features, theirs):
    rows = features.shape[0]
    return call(
        arrange_body,
        [SCALARS] + [WHOLE] * 3,
        pltpu.VMEM((NX * 2 * rows, BLOCK), jnp.bfloat16),
        NX * 4 * rows * BLOCK * BLOCK, 4,
    )(at, in_vmem(order), features, theirs)


def stack_body(at, features, own, first, second, third, a_ref, b_ref, theirs_ref, sems):
    copies = []
    for x in range(NX):
        from_block = pl.ds(pl.multiple_of((x * NC + 1 - at[2]) * BLOCK, BLOCK), BLOCK)
        copies.append(
            pltpu.make_async_copy(
                features.at[:, from_block], theirs_ref.at[:, pl.ds(x * BLOCK, BLOCK)], sems.at[x]
            )
        )
        copies[-1].start()
    rows = own.shape[0]
    for ref, pair in ((a_ref, (own, first)), (b_ref, (second, third))):
        for i, piece in enumerate(pair):
            ref[i * rows : (i + 1) * rows, :] = piece[...]
    for copy in copies:
        copy.wait()


def stack_plane(at, features, pieces):
    rows, columns = pieces[0].shape
    return call(
        stack_body,
        [SCALARS, LEFT] + [WHOLE] * 4,
        [
            pltpu.VMEM((2 * rows, columns), jnp.bfloat16),
            pltpu.VMEM((2 * rows, columns), jnp.bfloat16),
            jax.ShapeDtypeStruct((features.shape[0], NX * BLOCK), jnp.bfloat16),
        ],
        0, 4,
        out_specs=[WHOLE, WHOLE, LEFT],
        scratch_shapes=[pltpu.SemaphoreType.DMA((NX,))],
    )(at, features, *[in_vmem(p) for p in pieces])


def in_vmem(array):
    return pltpu.with_memory_space_constraint(array, pltpu.VMEM)


def put_rows(steps, pieces, rows_ref, sems):
    half, stores = BLOCK // 2, []
    for i, piece in enumerate(pieces):
        at = steps[i // 2] * BLOCK + i % 2 * half
        stores.append(pltpu.make_async_copy(piece, rows_ref.at[pl.ds(at, half)], sems.at[i]))
        stores[-1].start()
    return stores


def products(steps, count, arranged, pieces):
    half, total = BLOCK // 2, 0.0
    for i, step in enumerate(steps):
        left = arranged[step * 2 * count : (step + 1) * 2 * count, :]
        for j in range(2):
            total += jnp.dot(
                left[:, j * half : (j + 1) * half], pieces[2 * i + j][...],
                preferred_element_type=jnp.float32,
            )
    return total[:count], total[count:]


def early_body(steps, arranged, *refs):
    pieces, (mine_ref, theirs_ref, rows_ref, sems) = refs[: 2 * len(steps)], refs[2 * len(steps) :]
    stores = put_rows(steps, pieces, rows_ref, sems)
    mine_ref[...], theirs_ref[...] = products(steps, mine_ref.shape[0], arranged, pieces)
    for store in stores:
        store.wait()


def early_sums(arranged, pieces, steps):
    count, columns = arranged.shape[0] // NX // 2, pieces[0].shape[1]
    return call(
        functools.partial(early_body, steps),
        [WHOLE] * (1 + len(pieces)),
        [
            pltpu.VMEM((count, columns), jnp.float32),
            pltpu.VMEM((count, columns), jnp.float32),
            jax.ShapeDtypeStruct((NX * BLOCK, columns), jnp.bfloat16),
        ],
        len(steps) * 4 * count * BLOCK * columns, len(steps) * 2,
        out_specs=[WHOLE, WHOLE, LEFT],
        scratch_shapes=[pltpu.SemaphoreType.DMA((len(pieces),))],
    )(in_vmem(arranged), *[in_vmem(p) for p in pieces])


def late_body(steps, arranged, mine, theirs, first, second, mine_ref, theirs_ref):
    more, more_theirs = products(steps, mine.shape[0], arranged, (first, second))
    mine_ref[...] = mine[...] + more
    theirs_ref[...] = theirs[...] + more_theirs


def late_sums(arranged, sums, pieces, steps):
    count, columns = sums[0].shape
    return call(
        functools.partial(late_body, steps),
        [WHOLE] * 5,
        [pltpu.VMEM((count, columns), jnp.float32)] * 2,
        len(steps) * 4 * count * BLOCK * columns, 4,
    )(*[in_vmem(x) for x in (arranged, *sums, *pieces)])


def place_body(steps, first, second, after, rows_in, rows_ref, sems):
    for store in put_rows(steps, (first, second), rows_ref, sems):
        store.wait()


def place_rows(pieces, after, rows, steps):
    return call(
        functools.partial(place_body, steps),
        [WHOLE, WHOLE, LEFT, LEFT],
        jax.ShapeDtypeStruct(rows.shape, rows.dtype),
        0, 4,
        out_specs=LEFT,
        scratch_shapes=[pltpu.SemaphoreType.DMA((2,))],
        input_output_aliases={3: 0},
    )(*[in_vmem(p) for p in pieces], after, rows)


def query_part_body(at, order, grads, all_rows, out_ref, weights, sems):
    rows = grads.shape[0]
    loads = []
    for e in range(NX):
        source = all_rows.at[pl.ds(e * BLOCK, BLOCK), pl.ds(0, HQ * HD)]
        loads.append(pltpu.make_async_copy(source, weights.at[e], sems.at[e]))
        loads[-1].start()
    for e in range(NX):
        loads[e].wait()
        part = lax.dot_general(
            grads[...], weights[e], TURN, preferred_element_type=jnp.float32
        )
        high = part.astype(jnp.bfloat16)
        low = (part - high.astype(jnp.float32)).astype(jnp.bfloat16)
        back = lax.dot_general(
            jnp.concatenate([high, low], axis=0), order[...], TURN,
            preferred_element_type=jnp.float32,
        )
        out_ref[:, pl.ds(x_block(at[0], e), BLOCK)] = back[:rows] + back[rows:]


def query_part_of(at, order, grads, all_rows):
    rows = grads.shape[0]
    return call(
        query_part_body,
        [SCALARS, WHOLE, WHOLE, LEFT],
        pltpu.VMEM((rows, NX * BLOCK), jnp.float32),
        NX * 2 * rows * BLOCK * (HQ * HD + 2 * BLOCK), 6,
        scratch_shapes=[
            pltpu.VMEM((NX, BLOCK, HQ * HD), jnp.bfloat16),
            pltpu.SemaphoreType.DMA((NX,)),
        ],
    )(at, in_vmem(order), grads, all_rows)


def pair_weights_body(at, order, all_rows, out_ref, weights, sem):
    load = pltpu.make_async_copy(all_rows.at[:, pl.ds(HQ * HD, 2 * HD)], weights, sem)
    load.start()
    load.wait()
    for e in range(NX):
        out_ref[pl.ds(x_block(at[0], e), BLOCK), :] = jnp.dot(
            order[...], weights[e * BLOCK : (e + 1) * BLOCK, :],
            preferred_element_type=jnp.float32,
        ).astype(jnp.bfloat16)


def pair_weights_of(at, order, all_rows):
    return call(
        pair_weights_body,
        [SCALARS, WHOLE, LEFT],
        pltpu.VMEM((NX * BLOCK, 2 * HD), jnp.bfloat16),
        NX * 2 * BLOCK * BLOCK * 2 * HD, 3,
        scratch_shapes=[
            pltpu.VMEM((NX * BLOCK, 2 * HD), jnp.bfloat16),
            pltpu.SemaphoreType.DMA,
        ],
    )(at, in_vmem(order), all_rows)


def finish_body(at, pair_out, own_part, other_part, own_w, other_w, out_ref):
    for x in range(NX):
        cut = slice(x * BLOCK, (x + 1) * BLOCK)
        for flip, part, w in ((0, own_part, own_w), (1, other_part, other_w)):
            parity = at[2] if flip == 0 else 1 - at[2]
            total = part[:, cut] + lax.dot_general(
                pair_out[...], w[cut, :], TURN, preferred_element_type=jnp.float32
            )
            to_block = pl.ds(pl.multiple_of((x * NC + parity) * BLOCK, BLOCK), BLOCK)
            out_ref[:, to_block] = total.astype(jnp.bfloat16)


def finish(at, pair_out, parts, weights):
    whole = pl.BlockSpec(memory_space=pltpu.VMEM)
    return pl.pallas_call(
        finish_body,
        in_specs=[pl.BlockSpec(memory_space=pltpu.SMEM)] + [whole] * 5,
        out_shape=jax.ShapeDtypeStruct((pair_out.shape[0], NX * NC * BLOCK), jnp.bfloat16),
        compiler_params=pltpu.CompilerParams(vmem_limit_bytes=VMEM_LIMIT),
    )(at, pair_out, *[in_vmem(p) for p in parts], *[in_vmem(w) for w in weights])


def shifted(block, axis, distance):
    devices = range(lax.axis_size(axis))
    return lax.ppermute(block, axis, [(i - distance, i) for i in devices if i - distance in devices])


def angles_for(positions, head_size):
    half_size = head_size // 2
    inverse = jnp.power(
        jnp.float32(ROPE_BASE), -jnp.arange(half_size, dtype=jnp.float32) / half_size
    )
    phase_angle = positions.astype(jnp.float32)[:, None] * inverse[None, :]
    return (jnp.cos(phase_angle), jnp.sin(phase_angle))


def rotate(vectors, cos_part, sin_part):
    half_size = vectors.shape[-1] // 2
    a = vectors[..., :half_size]
    b = vectors[..., half_size:]
    return jnp.concatenate([a * cos_part - b * sin_part, b * cos_part + a * sin_part], axis=-1)


def local(tokens, doc_start, out_grad, w_qkv):
    row_count = tokens.shape[1]
    score_scale = 1.0 / math.sqrt(HD)
    features = tokens[0]
    begin_rows = doc_start[0]
    grad_rows = out_grad[0].reshape(row_count, HQ, HD)
    fsdp, ctx = lax.axis_index("fsdp"), lax.axis_index("ctx")
    x_me, core = fsdp // NC, fsdp % NC
    y_me = ctx % NY

    column = lax.all_gather(
        w_qkv, "ctx", axis=0, tiled=True,
        axis_index_groups=[[z * NY + y for z in range(NZ)] for y in range(NY)],
    )
    second, first, third = (along_y(column, d) for d in (2, 1, 3))

    at = jnp.stack([x_me, y_me, core]).astype(jnp.int32)
    order = order_matrix(y_me)
    a0, b0, theirs = stack_plane(at, features, [column, first, second, third])
    a1, b3 = along_x(a0, 1), along_x(b0, 3)
    b1, a3 = along_x(b0, 1), along_x(a0, 3)
    a2, b2 = along_x(a1, 1), along_x(b3, 3)
    arranged = arrange(at, order, features, swap_cores(theirs))
    *sums, own_w = early_sums(arranged, [a0, b0, a1, b1, a3, b3], (0, 1, 3))
    mine, theirs = late_sums(arranged, sums, [a2, b2], (2,))
    own_w = place_rows([a2, b2], theirs, own_w, (2,))
    projected = mine + swap_cores(theirs)
    other_w = swap_cores(own_w)
    pair_pre, query_pre = projected[:, HQ * HD :], projected[:, : HQ * HD]

    first_row = ctx * row_count
    query_index = first_row + jnp.arange(row_count, dtype=jnp.int32)
    cos_part, sin_part = angles_for(query_index - begin_rows, HD)
    pair_rows = jnp.concatenate(
        [rotate(pair_pre[:, :HD], cos_part, sin_part), pair_pre[:, HD:]], axis=1
    ).astype(jnp.bfloat16)
    projected_at, pair_rows = lax.optimization_barrier((at, pair_rows))
    back2, pair_w_own = lax.optimization_barrier(
        (shifted(pair_rows, "ctx", 2), pair_weights_of(projected_at, order, own_w))
    )
    back31 = shifted(jnp.concatenate([back2, pair_rows], axis=0), "ctx", 1)
    window = jnp.concatenate([back31[:row_count], back2, back31[row_count:], pair_rows], axis=0)

    queries = rotate(
        query_pre.reshape(row_count, HQ, HD), cos_part[:, None, :], sin_part[:, None, :]
    ).astype(jnp.bfloat16)
    keys, values = window[:, :HD], window[:, HD:]
    key_index = first_row - (REACH - 1) * row_count + jnp.arange(REACH * row_count, dtype=jnp.int32)
    allowed = (key_index[None, :] <= query_index[:, None]) & (
        key_index[None, :] >= begin_rows[:, None]
    )
    scores = (
        jnp.einsum("qhd,kd->hqk", queries, keys, preferred_element_type=jnp.float32) * score_scale
    )
    scores = jnp.where(allowed[None], scores, MASKED)
    top = jnp.max(scores, axis=-1, keepdims=True)
    unnormed = jnp.where(allowed[None], jnp.exp(scores - top), 0.0)
    probs = unnormed / jnp.sum(unnormed, axis=-1, keepdims=True)
    probs_low = probs.astype(jnp.bfloat16)
    grad_probs = jnp.einsum("qhd,kd->hqk", grad_rows, values, preferred_element_type=jnp.float32)
    attn_out = jnp.einsum(
        "hqk,kd->hqd", probs_low, values, preferred_element_type=jnp.float32
    ).astype(jnp.bfloat16)
    row_delta = jnp.sum(
        jnp.transpose(grad_rows, (1, 0, 2)).astype(jnp.float32) * attn_out.astype(jnp.float32),
        axis=-1, keepdims=True,
    )
    grad_value = jnp.einsum("hqk,qhd->kd", probs_low, grad_rows, preferred_element_type=jnp.float32)
    grad_scores = (probs * (grad_probs - row_delta)).astype(jnp.bfloat16)
    grad_query = (
        jnp.einsum("hqk,kd->qhd", grad_scores, keys, preferred_element_type=jnp.float32)
        * score_scale
    )
    grad_key = (
        jnp.einsum("hqk,qhd->kd", grad_scores, queries, preferred_element_type=jnp.float32)
        * score_scale
    )
    pair_grad = jnp.concatenate([grad_key, grad_value], axis=1)
    query_out = rotate(grad_query, cos_part[:, None, :], -sin_part[:, None, :]).reshape(
        row_count, HQ * HD
    ).astype(jnp.bfloat16)
    back3, back2, back1, own_grad = (
        pair_grad[i * row_count : (i + 1) * row_count] for i in range(REACH)
    )
    came, part_own = lax.optimization_barrier(
        (
            shifted(jnp.concatenate([back3, back1], axis=0).astype(jnp.bfloat16), "ctx", -1),
            query_part_of(at, order, query_out, own_w),
        )
    )
    came = came.astype(jnp.float32)
    last, part_other, pair_w_other = lax.optimization_barrier(
        (
            shifted((back2 + came[:row_count]).astype(jnp.bfloat16), "ctx", -2),
            query_part_of(at, order, query_out, other_w),
            pair_weights_of(at, order, other_w),
        )
    )
    pair_total = own_grad + came[row_count:] + last.astype(jnp.float32)
    pair_out = jnp.concatenate(
        [rotate(pair_total[:, :HD], cos_part, -sin_part), pair_total[:, HD:]], axis=1
    ).astype(jnp.bfloat16)
    return finish(at, pair_out, [part_own, part_other], [pair_w_own, pair_w_other])[None]


def solution(mesh):
    placed = (
        P("fsdp", "ctx", None),
        P("fsdp", "ctx"),
        P("fsdp", "ctx", None),
        P(("fsdp", "ctx"), None),
    )
    return jax.shard_map(
        local, mesh=mesh, in_specs=placed, out_specs=P("fsdp", "ctx", None), check_vma=False
    )
```

time: 188 us -> 156 us (0.83)
  the two profiles are of different devices: /device:TPU:24 before, /device:TPU:62 now
where the time goes in v5:
time: 156 us; the launch traced here: 155 us
  starting transfers between devices  50.3 us (32%)
  blocking collectives  35.2 us (23%)
  waiting for transfers between devices  28.5 us (18%)
  Pallas kernels  23.6 us (15%)
  local copies, waits for them, and re-layouts  6.69 us (4%)
  matrix products  5.6 us (4%)
  other arithmetic  4.49 us (3%)
    all_gather x1, blocking collectives, local(): lax.all_gather(w_qkv, 'ctx', axis=0, tiled=True, axis_index_groups=[[z *...  35.2 us
    ppermute x6, starting transfers between devices, along_x(): lax.ppermute(block, ALL, route(lambda x, c, z, y: ((x + distance) % NX, c...  18.1 us
    ppermute x4, starting transfers between devices, shifted(): lax.ppermute(block, axis, [(i - distance, i) for i in devices if i - dist...  16.4 us
    ppermute x6, waiting for transfers between devices, along_x(): lax.ppermute(block, ALL, route(lambda x, c, z, y: ((x + distance) % NX, c...  15.7 us
    ppermute x3, starting transfers between devices, along_y(): lax.ppermute(block, ALL, route(lambda x, c, z, y: (x, c, z, (y + distance...  9.58 us
    pallas_call x2, Pallas kernels, query_part_of(): call(query_part_body, [SCALARS, WHOLE, WHOLE, LEFT], pltpu.VMEM((rows, NX...  9.46 us
    ppermute x3, waiting for transfers between devices, along_y(): lax.ppermute(block, ALL, route(lambda x, c, z, y: (x, c, z, (y + distance...  6.74 us
    unnamed x29, local copies, waits for them, and re-layouts  6.45 us
  transfers between devices with their start and end apart: 16, of which 11 were waited for; matrix products, arithmetic and copies ran while one was open for 8% of the time, Pallas kernels for 13%

profile of v5, /device:TPU:62, one launch (start us, length us, event | category | flops | bytes accessed | tf_op | source)
XLA Modules:
  0.0 155.0 jit_solution(15546962884811667217)
XLA Ops:
  0.0 35.2 %all_gather.3.own = bf16[128,1280]{1,0:T(8,128)(2,1)S(1)} all-gather(bf16[8,1280]{1,0:T(8,128)(2,1)} %param.7), channel_id=1, replica_groups={{0,4,8,12,16,20,24,28,32,36,40,44,48,52,56,60},{1,5,9,13,17,21,25,29,33..., dimensions={0}, use_global_device_ids=true | all-gather | bytes 348160 | tf_op jit(solution)/shard_map/all_gather | solution.py:334
  35.2 2.6 %collective-permute-start.2 = (bf16[128,1280]{1,0:T(8,128)(2,1)S(1)}, bf16[128,1280]{1,0:T(8,128)(2,1)S(1)}, u32[]{:S(2)}, u32[]{:S(2)}) collective-permute-start(bf16[128,1280]{1,0:T(8,128)(2,1)S(1)} %all_gather.3.own), channel_id=1, source_target_pairs={{0,3},{1,0},{2,1},{3,2},{4,7},{5,4},{6,5},{7,6},{8,11},{9,8},{10,9... | collective-permute-start | bytes 983048 | tf_op jit(solution)/shard_map/ppermute | solution.py:35
  37.9 2.8 %collective-permute-start.1 = (bf16[128,1280]{1,0:T(8,128)(2,1)S(1)}, bf16[128,1280]{1,0:T(8,128)(2,1)S(1)}, u32[]{:S(2)}, u32[]{:S(2)}) collective-permute-start(bf16[128,1280]{1,0:T(8,128)(2,1)S(1)} %all_gather.3.own), channel_id=1, source_target_pairs={{0,2},{1,3},{2,0},{3,1},{4,6},{5,7},{6,4},{7,5},{8,10},{9,11},{10,... | collective-permute-start | bytes 983048 | tf_op jit(solution)/shard_map/ppermute | solution.py:35
  40.7 4.1 %collective-permute-start = (bf16[128,1280]{1,0:T(8,128)(2,1)S(1)}, bf16[128,1280]{1,0:T(8,128)(2,1)S(1)}, u32[]{:S(2)}, u32[]{:S(2)}) collective-permute-start(bf16[128,1280]{1,0:T(8,128)(2,1)S(1)} %all_gather.3.own), channel_id=1, source_target_pairs={{0,1},{1,2},{2,3},{3,0},{4,5},{5,6},{6,7},{7,4},{8,9},{9,10},{10,1... | collective-permute-start | bytes 983048 | tf_op jit(solution)/shard_map/ppermute | solution.py:35
  44.9 4.0 %collective-permute-done.2.third = bf16[128,1280]{1,0:T(8,128)(2,1)S(1)} collective-permute-done((bf16[128,1280]{1,0:T(8,128)(2,1)S(1)}, bf16[128,1280]{1,0:T(8,128)(2,1)S(1)}, u32[]{:S(2)}, u32[]{:S(2)}) %collective-permute-start.2) | collective-permute-done | bytes 327712 | tf_op jit(solution)/shard_map/ppermute | solution.py:35
  48.9 2.8 %collective-permute-done.first = bf16[128,1280]{1,0:T(8,128)(2,1)S(1)} collective-permute-done((bf16[128,1280]{1,0:T(8,128)(2,1)S(1)}, bf16[128,1280]{1,0:T(8,128)(2,1)S(1)}, u32[]{:S(2)}, u32[]{:S(2)}) %collective-permute-start) | collective-permute-done | bytes 327712 | tf_op jit(solution)/shard_map/ppermute | solution.py:35
  51.7 0.7 copy-done.2
  52.4 1.2 copy-done
  53.6 1.0 copy-done.3
  54.6 0.8 shard_map.46
  55.4 0.8 copy-done.4
  56.2 2.4 %collective-permute-start.4 = (bf16[256,1280]{1,0:T(8,128)(2,1)S(1)}, bf16[256,1280]{1,0:T(8,128)(2,1)S(1)}, u32[]{:S(2)}, u32[]{:S(2)}) collective-permute-start(bf16[256,1280]{1,0:T(8,128)(2,1)S(1)} %get-tuple-element.23.refs_0_), channel_id=1, source_target_pairs={{0,128},{1,129},{2,130},{3,131},{4,132},{5,133},{6,134},{7,135},{8... | collective-permute-start | bytes 1966088 | tf_op jit(solution)/shard_map/ppermute | solution.py:41
  58.6 3.5 %collective-permute-start.7 = (bf16[256,1280]{1,0:T(8,128)(2,1)S(1)}, bf16[256,1280]{1,0:T(8,128)(2,1)}, u32[]{:S(2)}, u32[]{:S(2)}) collective-permute-start(bf16[256,1280]{1,0:T(8,128)(2,1)S(1)} %get-tuple-element.24.refs_1_), channel_id=1, source_target_pairs={{0,384},{1,385},{2,386},{3,387},{4,388},{5,389},{6,390},{7,391},{8... | collective-permute-start | bytes 1966088 | tf_op jit(solution)/shard_map/ppermute | solution.py:41
  62.0 1.8 %copy.8 = bf16[1,128,1024]{1,2,0:T(8,128)(2,1)} copy(bf16[1,128,1024]{2,1,0:T(8,128)(2,1)} %param.6) | data formatting | bytes 524288 | tf_op args[2]
  63.8 2.7 %collective-permute-start.6 = (bf16[256,1280]{1,0:T(8,128)(2,1)S(1)}, bf16[256,1280]{1,0:T(8,128)(2,1)S(1)}, u32[]{:S(2)}, u32[]{:S(2)}) collective-permute-start(bf16[256,1280]{1,0:T(8,128)(2,1)S(1)} %get-tuple-element.23.refs_0_), channel_id=1, source_target_pairs={{0,384},{1,385},{2,386},{3,387},{4,388},{5,389},{6,390},{7,391},{8... | collective-permute-start | bytes 1966088 | tf_op jit(solution)/shard_map/ppermute | solution.py:41
  66.6 4.3 %collective-permute-start.5 = (bf16[256,1280]{1,0:T(8,128)(2,1)S(1)}, bf16[256,1280]{1,0:T(8,128)(2,1)S(1)}, u32[]{:S(2)}, u32[]{:S(2)}) collective-permute-start(bf16[256,1280]{1,0:T(8,128)(2,1)S(1)} %get-tuple-element.24.refs_1_), channel_id=1, source_target_pairs={{0,128},{1,129},{2,130},{3,131},{4,132},{5,133},{6,134},{7,135},{8... | collective-permute-start | bytes 1966088 | tf_op jit(solution)/shard_map/ppermute | solution.py:41
  70.9 1.9 %collective-permute-start.3 = (bf16[128,2048]{1,0:T(8,128)(2,1)}, bf16[128,2048]{1,0:T(8,128)(2,1)S(1)}, u32[]{:S(2)}, u32[]{:S(2)}) collective-permute-start(bf16[128,2048]{1,0:T(8,128)(2,1)} %copy-done.4), channel_id=1, source_target_pairs={{0,64},{1,65},{2,66},{3,67},{4,68},{5,69},{6,70},{7,71},{8,72},{9,... | collective-permute-start | bytes 1572872 | tf_op jit(solution)/shard_map/ppermute | solution.py:47
  72.8 2.0 %collective-permute-done.4.refs_2_ = bf16[256,1280]{1,0:T(8,128)(2,1)S(1)} collective-permute-done((bf16[256,1280]{1,0:T(8,128)(2,1)S(1)}, bf16[256,1280]{1,0:T(8,128)(2,1)S(1)}, u32[]{:S(2)}, u32[]{:S(2)}) %collective-permute-start.4) | collective-permute-done | bytes 655392 | tf_op jit(solution)/shard_map/ppermute | solution.py:41
  74.8 1.9 %collective-permute-start.8 = (bf16[256,1280]{1,0:T(8,128)(2,1)S(1)}, bf16[256,1280]{1,0:T(8,128)(2,1)S(1)}, u32[]{:S(2)}, u32[]{:S(2)}) collective-permute-start(bf16[256,1280]{1,0:T(8,128)(2,1)S(1)} %collective-permute-done.4.refs_2_), channel_id=1, source_target_pairs={{0,128},{1,129},{2,130},{3,131},{4,132},{5,133},{6,134},{7,135},{8... | collective-permute-start | bytes 1966088 | tf_op jit(solution)/shard_map/ppermute | solution.py:41
  76.8 0.6 collective-permute-done.7.refs_5_
  77.4 3.3 %collective-permute-start.9 = (bf16[256,1280]{1,0:T(8,128)(2,1)}, bf16[256,1280]{1,0:T(8,128)(2,1)S(1)}, u32[]{:S(2)}, u32[]{:S(2)}) collective-permute-start(bf16[256,1280]{1,0:T(8,128)(2,1)} %collective-permute-done.7.refs_5_), channel_id=1, source_target_pairs={{0,384},{1,385},{2,386},{3,387},{4,388},{5,389},{6,390},{7,391},{8... | collective-permute-start | bytes 1966088 | tf_op jit(solution)/shard_map/ppermute | solution.py:41
  80.9 1.3 shard_map.47.arranged
  82.2 5.0 %collective-permute-done.6.refs_4_ = bf16[256,1280]{1,0:T(8,128)(2,1)S(1)} collective-permute-done((bf16[256,1280]{1,0:T(8,128)(2,1)S(1)}, bf16[256,1280]{1,0:T(8,128)(2,1)S(1)}, u32[]{:S(2)}, u32[]{:S(2)}) %collective-permute-start.6) | collective-permute-done | bytes 655392 | tf_op jit(solution)/shard_map/ppermute | solution.py:41
  87.5 3.1 %shard_map.48 = (f32[128,1280]{1,0:T(8,128)S(1)}, f32[128,1280]{1,0:T(8,128)S(1)}, bf16[2048,1280]{1,0:T(8,128)(2,1)}) custom-call(bf16[1024,512]{1,0:T(8,128)(2,1)S(1)} %shard_map.47.arranged, bf16[256,1280]{1,0:T(8,128)(2,1)S(1)} %get-tuple-element.23.refs_0_, bf16[256,1280]{1,0:T(8,128)(2,1)S(1)} %get-tuple-element.24.refs_1_, ...), custom_call_target="tpu_custom_call" | custom-call | flops 1006632960 | bytes 6291456 | tf_op jit(solution)/shard_map/pallas_call | solution.py:175
  90.6 6.2 %collective-permute-done.8.first = bf16[256,1280]{1,0:T(8,128)(2,1)S(1)} collective-permute-done((bf16[256,1280]{1,0:T(8,128)(2,1)S(1)}, bf16[256,1280]{1,0:T(8,128)(2,1)S(1)}, u32[]{:S(2)}, u32[]{:S(2)}) %collective-permute-start.8) | collective-permute-done | bytes 655392 | tf_op jit(solution)/shard_map/ppermute | solution.py:41
  96.7 1.6 %collective-permute-done.9.second = bf16[256,1280]{1,0:T(8,128)(2,1)S(1)} collective-permute-done((bf16[256,1280]{1,0:T(8,128)(2,1)}, bf16[256,1280]{1,0:T(8,128)(2,1)S(1)}, u32[]{:S(2)}, u32[]{:S(2)}) %collective-permute-start.9) | collective-permute-done | bytes 655392 | tf_op jit(solution)/shard_map/ppermute | solution.py:41
  98.8 1.9 %collective-permute-start.10 = (f32[128,1280]{1,0:T(8,128)S(1)}, f32[128,1280]{1,0:T(8,128)S(1)}, u32[]{:S(2)}, u32[]{:S(2)}) collective-permute-start(f32[128,1280]{1,0:T(8,128)S(1)} %get-tuple-element.28.after), channel_id=1, source_target_pairs={{0,64},{1,65},{2,66},{3,67},{4,68},{5,69},{6,70},{7,71},{8,72},{9,... | collective-permute-start | bytes 1966088 | tf_op jit(solution)/shard_map/ppermute | solution.py:47
  100.8 1.1 shard_map.50.all_rows
  102.0 2.4 %collective-permute-start.15 = (bf16[2048,1280]{1,0:T(8,128)(2,1)}, bf16[2048,1280]{1,0:T(8,128)(2,1)}, u32[]{:S(2)}, u32[]{:S(2)}) collective-permute-start(bf16[2048,1280]{1,0:T(8,128)(2,1)} %shard_map.50.all_rows), channel_id=1, source_target_pairs={{0,64},{1,65},{2,66},{3,67},{4,68},{5,69},{6,70},{7,71},{8,72},{9,... | collective-permute-start | bytes 15728648 | tf_op jit(solution)/shard_map/ppermute | solution.py:47
  104.8 0.9 fusion.37
  105.8 2.9 %collective-permute-start.11 = (bf16[128,256]{1,0:T(8,128)(2,1)S(1)}, bf16[128,256]{1,0:T(8,128)(2,1)S(1)}, u32[]{:S(2)}, u32[]{:S(2)}) collective-permute-start(bf16[128,256]{1,0:T(8,128)(2,1)S(1)} %pad_maximum_fusion.5), channel_id=1, source_target_pairs={{0,2},{1,3},{2,4},{3,5},{4,6},{5,7},{6,8},{7,9},{8,10},{9,11},{10,... | collective-permute-start | bytes 196616 | tf_op jit(solution)/shard_map/ppermute | solution.py:305
  108.9 2.5 %shard_map.51.own_w = bf16[2048,256]{1,0:T(8,128)(2,1)S(1)} custom-call(s32[3]{0:T(128)S(1)} %pad_add_fusion.at, bf16[512,512]{1,0:T(8,128)(2,1)S(1)} %fusion.21.order, bf16[2048,1280]{1,0:T(8,128)(2,1)} %shard_map.50.all_rows), custom_call_target="tpu_custom_call" | custom-call | flops 536870912 | bytes 3145728 | tf_op jit(solution)/shard_map/pallas_call | solution.py:269
  111.5 2.0 %collective-permute-done.11 = bf16[128,256]{1,0:T(8,128)(2,1)S(1)} collective-permute-done((bf16[128,256]{1,0:T(8,128)(2,1)S(1)}, bf16[128,256]{1,0:T(8,128)(2,1)S(1)}, u32[]{:S(2)}, u32[]{:S(2)}) %collective-permute-start.11) | collective-permute-done | bytes 65568 | tf_op jit(solution)/shard_map/ppermute | solution.py:305
  113.5 4.9 %collective-permute-start.12 = (bf16[256,256]{1,0:T(8,128)(2,1)S(1)}, bf16[256,256]{1,0:T(8,128)(2,1)S(1)}, u32[]{:S(2)}, u32[]{:S(2)}) collective-permute-start(bf16[256,256]{1,0:T(8,128)(2,1)S(1)} %pad_maximum_fusion.3), channel_id=1, source_target_pairs={{0,1},{1,2},{2,3},{3,4},{4,5},{5,6},{6,7},{7,8},{8,9},{9,10},{10,1... | collective-permute-start | bytes 393224 | tf_op jit(solution)/shard_map/ppermute | solution.py:305
  118.7 2.3 %collective-permute-done.12 = bf16[256,256]{1,0:T(8,128)(2,1)S(1)} collective-permute-done((bf16[256,256]{1,0:T(8,128)(2,1)S(1)}, bf16[256,256]{1,0:T(8,128)(2,1)S(1)}, u32[]{:S(2)}, u32[]{:S(2)}) %collective-permute-start.12) | collective-permute-done | bytes 131104 | tf_op jit(solution)/shard_map/ppermute | solution.py:305
  121.0 2.3 %fusion.60 = (f32[8,128]{1,0:T(8,128)S(1)}, f32[8,128,512]{1,2,0:T(8,128)}) fusion(pred[128,512]{0,1:T(8,128)(4,1)S(1)} %compare_and_fusion, bf16[512,256]{1,0:T(8,128)(2,1)S(1)} %pad_maximum_fusion.1, bf16[128,8,64]{2,0,1:T(8,128)(2,1)S(1)} %get-tuple-element.40, bf16[128,8,64]{2,0,1:T(8,128)(2,1)S(1)} %get-tuple-element.39), kind=kOutput, calls=%fused_computation.112 | convolution fusion | flops 137363968 | bytes 2887680 | tf_op jit(solution)/shard_map/sub | solution.py:380
  123.3 1.8 %fusion.23 = bf16[8,128,512]{1,2,0:T(8,128)(2,1)S(1)} fusion(f32[8,128,512]{1,2,0:T(8,128)} %get-tuple-element.59, f32[8,128]{1,0:T(8,128)S(1)} %get-tuple-element.58), kind=kLoop, calls=%fused_computation.42 | loop fusion | flops 1048576 | bytes 3149824 | tf_op jit(solution)/shard_map/convert_element_type | solution.py:382
  126.0 0.8 copy-done.5
  126.8 1.4 fusion.2
  128.2 0.5 fusion.8
  128.8 2.0 %collective-permute-start.13 = (bf16[256,256]{1,0:T(8,128)(2,1)S(1)}, bf16[256,256]{1,0:T(8,128)(2,1)S(1)}, u32[]{:S(2)}, u32[]{:S(2)}) collective-permute-start(bf16[256,256]{1,0:T(8,128)(2,1)S(1)} %pad_maximum_fusion.4), channel_id=1, source_target_pairs={{1,0},{2,1},{3,2},{4,3},{5,4},{6,5},{7,6},{8,7},{9,8},{10,9},{11,1... | collective-permute-start | bytes 393224 | tf_op jit(solution)/shard_map/ppermute | solution.py:305
  130.8 0.6 fusion.4
  131.8 4.7 %shard_map.52.own_part = f32[128,2048]{1,0:T(8,128)S(1)} custom-call(s32[3]{0:T(128)S(1)} %pad_add_fusion.at, bf16[512,512]{1,0:T(8,128)(2,1)S(1)} %fusion.21.order, bf16[128,1024]{1,0:T(8,128)(2,1)S(1)} %copy_bitcast_fusion.grads, bf16[2048,1280]{1,0:T(8,128)(2,1)} %shard_map.50.all_rows), custom_call_target="tpu_custom_call" | custom-call | flops 1073741824 | bytes 6291456 | tf_op jit(solution)/shard_map/pallas_call | solution.py:245
  136.5 1.7 %collective-permute-done.13 = bf16[256,256]{1,0:T(8,128)(2,1)S(1)} collective-permute-done((bf16[256,256]{1,0:T(8,128)(2,1)S(1)}, bf16[256,256]{1,0:T(8,128)(2,1)S(1)}, u32[]{:S(2)}, u32[]{:S(2)}) %collective-permute-start.13) | collective-permute-done | bytes 131104 | tf_op jit(solution)/shard_map/ppermute | solution.py:305
  138.2 6.6 %collective-permute-start.14 = (bf16[128,256]{1,0:T(8,128)(2,1)S(1)}, bf16[128,256]{1,0:T(8,128)(2,1)S(1)}, u32[]{:S(2)}, u32[]{:S(2)}) collective-permute-start(bf16[128,256]{1,0:T(8,128)(2,1)S(1)} %fusion.32), channel_id=1, source_target_pairs={{2,0},{3,1},{4,2},{5,3},{6,4},{7,5},{8,6},{9,7},{10,8},{11,9},{12,... | collective-permute-start | bytes 196616 | tf_op jit(solution)/shard_map/ppermute | solution.py:305
  144.9 4.7 %shard_map.53.other_part = f32[128,2048]{1,0:T(8,128)S(1)} custom-call(s32[3]{0:T(128)S(1)} %pad_add_fusion.at, bf16[512,512]{1,0:T(8,128)(2,1)S(1)} %fusion.21.order, bf16[128,1024]{1,0:T(8,128)(2,1)S(1)} %copy_bitcast_fusion.grads, bf16[2048,1280]{1,0:T(8,128)(2,1)} %collective-permute-done.15.all_rows), custom_call_target="tpu_custom_call" | custom-call | flops 1073741824 | bytes 6291456 | tf_op jit(solution)/shard_map/pallas_call | solution.py:245
  149.6 2.5 %shard_map.54.other_w = bf16[2048,256]{1,0:T(8,128)(2,1)S(1)} custom-call(s32[3]{0:T(128)S(1)} %pad_add_fusion.at, bf16[512,512]{1,0:T(8,128)(2,1)S(1)} %fusion.21.order, bf16[2048,1280]{1,0:T(8,128)(2,1)} %collective-permute-done.15.all_rows), custom_call_target="tpu_custom_call" | custom-call | flops 536870912 | bytes 3145728 | tf_op jit(solution)/shard_map/pallas_call | solution.py:269
  152.6 2.3 %shard_map.55 = bf16[128,4096]{1,0:T(8,128)(2,1)} custom-call(s32[3]{0:T(128)S(1)} %pad_add_fusion.at, bf16[128,256]{1,0:T(8,128)(2,1)S(1)} %pad_maximum_fusion.6.pair_out, f32[128,2048]{1,0:T(8,128)S(1)} %shard_map.52.own_part, f32[128,2048]{1,0:T(8,128)S(1)} %shard_map.53.other_part, bf16[2048,256]{1,0:T(8,128)(2,1)S(1)} %shard_map.51.own_w, ...), custom_call_target="tpu_custom_call" | custom-call | tf_op jit(solution)/shard_map/pallas_call | solution.py:295
  (61 shorter events, 3.8 us)
Async XLA Ops:
  35.2 13.7 %collective-permute-start.2 = (bf16[128,1280]{1,0:T(8,128)(2,1)S(1)}, bf16[128,1280]{1,0:T(8,128)(2,1)S(1)}, u32[]{:S(2)}, u32[]{:S(2)}) collective-permute-start(bf16[128,1280]{1,0:T(8,128)(2,1)S(1)} %all_gather.3.own), channel_id=1, source_target_pairs={{0,3},{1,0},{2,1},{3,2},{4,7},{5,4},{6,5},{7,6},{8,11},{9,8},{10,9... | collective-permute-start | bytes 983048 | tf_op jit(solution)/shard_map/ppermute | solution.py:35
  37.9 11.0 %collective-permute-start.1 = (bf16[128,1280]{1,0:T(8,128)(2,1)S(1)}, bf16[128,1280]{1,0:T(8,128)(2,1)S(1)}, u32[]{:S(2)}, u32[]{:S(2)}) collective-permute-start(bf16[128,1280]{1,0:T(8,128)(2,1)S(1)} %all_gather.3.own), channel_id=1, source_target_pairs={{0,2},{1,3},{2,0},{3,1},{4,6},{5,7},{6,4},{7,5},{8,10},{9,11},{10,... | collective-permute-start | bytes 983048 | tf_op jit(solution)/shard_map/ppermute | solution.py:35
  40.7 10.9 %collective-permute-start = (bf16[128,1280]{1,0:T(8,128)(2,1)S(1)}, bf16[128,1280]{1,0:T(8,128)(2,1)S(1)}, u32[]{:S(2)}, u32[]{:S(2)}) collective-permute-start(bf16[128,1280]{1,0:T(8,128)(2,1)S(1)} %all_gather.3.own), channel_id=1, source_target_pairs={{0,1},{1,2},{2,3},{3,0},{4,5},{5,6},{6,7},{7,4},{8,9},{9,10},{10,1... | collective-permute-start | bytes 983048 | tf_op jit(solution)/shard_map/ppermute | solution.py:35
  51.7 0.7 copy-start.2
  52.4 1.2 copy-start
  53.6 1.0 copy-start.3
  54.6 26.3 %copy-start.1 = (bf16[1,128,4096]{2,1,0:T(8,128)(2,1)S(1)}, bf16[1,128,4096]{2,1,0:T(8,128)(2,1)}, u32[]{:S(2)}) copy-start(bf16[1,128,4096]{2,1,0:T(8,128)(2,1)} %param.4) | copy-start | bytes 3145732
  55.4 0.8 copy-start.4
  56.2 18.7 %collective-permute-start.4 = (bf16[256,1280]{1,0:T(8,128)(2,1)S(1)}, bf16[256,1280]{1,0:T(8,128)(2,1)S(1)}, u32[]{:S(2)}, u32[]{:S(2)}) collective-permute-start(bf16[256,1280]{1,0:T(8,128)(2,1)S(1)} %get-tuple-element.23.refs_0_), channel_id=1, source_target_pairs={{0,128},{1,129},{2,130},{3,131},{4,132},{5,133},{6,134},{7,135},{8... | collective-permute-start | bytes 1966088 | tf_op jit(solution)/shard_map/ppermute | solution.py:41
  58.6 18.8 %collective-permute-start.7 = (bf16[256,1280]{1,0:T(8,128)(2,1)S(1)}, bf16[256,1280]{1,0:T(8,128)(2,1)}, u32[]{:S(2)}, u32[]{:S(2)}) collective-permute-start(bf16[256,1280]{1,0:T(8,128)(2,1)S(1)} %get-tuple-element.24.refs_1_), channel_id=1, source_target_pairs={{0,384},{1,385},{2,386},{3,387},{4,388},{5,389},{6,390},{7,391},{8... | collective-permute-start | bytes 1966088 | tf_op jit(solution)/shard_map/ppermute | solution.py:41
  63.8 23.3 %collective-permute-start.6 = (bf16[256,1280]{1,0:T(8,128)(2,1)S(1)}, bf16[256,1280]{1,0:T(8,128)(2,1)S(1)}, u32[]{:S(2)}, u32[]{:S(2)}) collective-permute-start(bf16[256,1280]{1,0:T(8,128)(2,1)S(1)} %get-tuple-element.23.refs_0_), channel_id=1, source_target_pairs={{0,384},{1,385},{2,386},{3,387},{4,388},{5,389},{6,390},{7,391},{8... | collective-permute-start | bytes 1966088 | tf_op jit(solution)/shard_map/ppermute | solution.py:41
  66.6 20.9 %collective-permute-start.5 = (bf16[256,1280]{1,0:T(8,128)(2,1)S(1)}, bf16[256,1280]{1,0:T(8,128)(2,1)S(1)}, u32[]{:S(2)}, u32[]{:S(2)}) collective-permute-start(bf16[256,1280]{1,0:T(8,128)(2,1)S(1)} %get-tuple-element.24.refs_1_), channel_id=1, source_target_pairs={{0,128},{1,129},{2,130},{3,131},{4,132},{5,133},{6,134},{7,135},{8... | collective-permute-start | bytes 1966088 | tf_op jit(solution)/shard_map/ppermute | solution.py:41
  70.9 10.0 %collective-permute-start.3 = (bf16[128,2048]{1,0:T(8,128)(2,1)}, bf16[128,2048]{1,0:T(8,128)(2,1)S(1)}, u32[]{:S(2)}, u32[]{:S(2)}) collective-permute-start(bf16[128,2048]{1,0:T(8,128)(2,1)} %copy-done.4), channel_id=1, source_target_pairs={{0,64},{1,65},{2,66},{3,67},{4,68},{5,69},{6,70},{7,71},{8,72},{9,... | collective-permute-start | bytes 1572872 | tf_op jit(solution)/shard_map/ppermute | solution.py:47
  74.8 21.9 %collective-permute-start.8 = (bf16[256,1280]{1,0:T(8,128)(2,1)S(1)}, bf16[256,1280]{1,0:T(8,128)(2,1)S(1)}, u32[]{:S(2)}, u32[]{:S(2)}) collective-permute-start(bf16[256,1280]{1,0:T(8,128)(2,1)S(1)} %collective-permute-done.4.refs_2_), channel_id=1, source_target_pairs={{0,128},{1,129},{2,130},{3,131},{4,132},{5,133},{6,134},{7,135},{8... | collective-permute-start | bytes 1966088 | tf_op jit(solution)/shard_map/ppermute | solution.py:41
  77.4 21.0 %collective-permute-start.9 = (bf16[256,1280]{1,0:T(8,128)(2,1)}, bf16[256,1280]{1,0:T(8,128)(2,1)S(1)}, u32[]{:S(2)}, u32[]{:S(2)}) collective-permute-start(bf16[256,1280]{1,0:T(8,128)(2,1)} %collective-permute-done.7.refs_5_), channel_id=1, source_target_pairs={{0,384},{1,385},{2,386},{3,387},{4,388},{5,389},{6,390},{7,391},{8... | collective-permute-start | bytes 1966088 | tf_op jit(solution)/shard_map/ppermute | solution.py:41
  98.8 5.7 %collective-permute-start.10 = (f32[128,1280]{1,0:T(8,128)S(1)}, f32[128,1280]{1,0:T(8,128)S(1)}, u32[]{:S(2)}, u32[]{:S(2)}) collective-permute-start(f32[128,1280]{1,0:T(8,128)S(1)} %get-tuple-element.28.after), channel_id=1, source_target_pairs={{0,64},{1,65},{2,66},{3,67},{4,68},{5,69},{6,70},{7,71},{8,72},{9,... | collective-permute-start | bytes 1966088 | tf_op jit(solution)/shard_map/ppermute | solution.py:47
  100.8 3.6 %copy-start.12 = (s32[1,128]{1,0:T(1,128)S(1)}, s32[1,128]{1,0:T(1,128)}, u32[]{:S(2)}) copy-start(s32[1,128]{1,0:T(1,128)} %param.5) | copy-start | bytes 1540
  102.0 42.9 %collective-permute-start.15 = (bf16[2048,1280]{1,0:T(8,128)(2,1)}, bf16[2048,1280]{1,0:T(8,128)(2,1)}, u32[]{:S(2)}, u32[]{:S(2)}) collective-permute-start(bf16[2048,1280]{1,0:T(8,128)(2,1)} %shard_map.50.all_rows), channel_id=1, source_target_pairs={{0,64},{1,65},{2,66},{3,67},{4,68},{5,69},{6,70},{7,71},{8,72},{9,... | collective-permute-start | bytes 15728648 | tf_op jit(solution)/shard_map/ppermute | solution.py:47
  105.8 7.7 %collective-permute-start.11 = (bf16[128,256]{1,0:T(8,128)(2,1)S(1)}, bf16[128,256]{1,0:T(8,128)(2,1)S(1)}, u32[]{:S(2)}, u32[]{:S(2)}) collective-permute-start(bf16[128,256]{1,0:T(8,128)(2,1)S(1)} %pad_maximum_fusion.5), channel_id=1, source_target_pairs={{0,2},{1,3},{2,4},{3,5},{4,6},{5,7},{6,8},{7,9},{8,10},{9,11},{10,... | collective-permute-start | bytes 196616 | tf_op jit(solution)/shard_map/ppermute | solution.py:305
  113.5 7.4 %collective-permute-start.12 = (bf16[256,256]{1,0:T(8,128)(2,1)S(1)}, bf16[256,256]{1,0:T(8,128)(2,1)S(1)}, u32[]{:S(2)}, u32[]{:S(2)}) collective-permute-start(bf16[256,256]{1,0:T(8,128)(2,1)S(1)} %pad_maximum_fusion.3), channel_id=1, source_target_pairs={{0,1},{1,2},{2,3},{3,4},{4,5},{5,6},{6,7},{7,8},{8,9},{9,10},{10,1... | collective-permute-start | bytes 393224 | tf_op jit(solution)/shard_map/ppermute | solution.py:305
  118.7 4.7 %copy-start.6 = (bf16[128,8,64]{2,0,1:T(8,128)(2,1)}, bf16[128,8,64]{2,0,1:T(8,128)(2,1)S(1)}, u32[]{:S(2)}) copy-start(bf16[128,8,64]{2,0,1:T(8,128)(2,1)S(1)} %get-tuple-element.40) | copy-start | bytes 393220
  121.0 4.6 %copy-start.9 = (bf16[512,256]{1,0:T(8,128)(2,1)}, bf16[512,256]{1,0:T(8,128)(2,1)S(1)}, u32[]{:S(2)}) copy-start(bf16[512,256]{1,0:T(8,128)(2,1)S(1)} %pad_maximum_fusion.1) | copy-start | bytes 786436
  123.3 1.8 %copy-start.8 = (bf16[1,128,1024]{1,2,0:T(8,128)(2,1)S(1)}, bf16[1,128,1024]{1,2,0:T(8,128)(2,1)}, u32[]{:S(2)}) copy-start(bf16[1,128,1024]{1,2,0:T(8,128)(2,1)} %copy.8) | copy-start | bytes 786436
  125.2 1.6 %copy-start.5 = (f32[8,128,512]{1,2,0:T(8,128)S(1)}, f32[8,128,512]{1,2,0:T(8,128)}, u32[]{:S(2)}) copy-start(f32[8,128,512]{1,2,0:T(8,128)} %get-tuple-element.59) | copy-start | bytes 6291460
  126.8 1.4 copy-start.7
  128.2 2.6 %copy-start.10 = (bf16[512,256]{1,0:T(8,128)(2,1)S(1)}, bf16[512,256]{1,0:T(8,128)(2,1)}, u32[]{:S(2)}) copy-start(bf16[512,256]{1,0:T(8,128)(2,1)} %copy-done.9) | copy-start | bytes 786436
  128.2 3.2 %copy-start.11 = (f32[128,64]{1,0:T(8,128)S(1)}, f32[128,64]{1,0:T(8,128)}, u32[]{:S(2)}) copy-start(f32[128,64]{1,0:T(8,128)} %get-tuple-element.53) | copy-start | bytes 98308
  128.8 9.4 %collective-permute-start.13 = (bf16[256,256]{1,0:T(8,128)(2,1)S(1)}, bf16[256,256]{1,0:T(8,128)(2,1)S(1)}, u32[]{:S(2)}, u32[]{:S(2)}) collective-permute-start(bf16[256,256]{1,0:T(8,128)(2,1)S(1)} %pad_maximum_fusion.4), channel_id=1, source_target_pairs={{1,0},{2,1},{3,2},{4,3},{5,4},{6,5},{7,6},{8,7},{9,8},{10,9},{11,1... | collective-permute-start | bytes 393224 | tf_op jit(solution)/shard_map/ppermute | solution.py:305
  138.2 13.9 %collective-permute-start.14 = (bf16[128,256]{1,0:T(8,128)(2,1)S(1)}, bf16[128,256]{1,0:T(8,128)(2,1)S(1)}, u32[]{:S(2)}, u32[]{:S(2)}) collective-permute-start(bf16[128,256]{1,0:T(8,128)(2,1)S(1)} %fusion.32), channel_id=1, source_target_pairs={{2,0},{3,1},{4,2},{5,3},{6,4},{7,5},{8,6},{9,7},{10,8},{11,9},{12,... | collective-permute-start | bytes 196616 | tf_op jit(solution)/shard_map/ppermute | solution.py:305

commit v6 on v5

--- a/solution.py
+++ b/solution.py
@@ -49,7 +49,6 @@
 
 BLOCK = NZ * NY * 8
 SPAN = NZ * 8
-TURN = (((1,), (1,)), ((), ()))
 VMEM_LIMIT = 14 * 1024 * 1024
 
 
@@ -79,7 +78,7 @@
 
 SCALARS = pl.BlockSpec(memory_space=pltpu.SMEM)
 WHOLE = pl.BlockSpec(memory_space=pltpu.VMEM)
-LEFT = pl.BlockSpec(memory_space=pl.ANY)
+LEFT = pl.BlockSpec(memory_space=pltpu.HBM)
 
 
 def call(body, in_specs, out_shape, flops, mib, **more):
@@ -100,72 +99,61 @@
         [SCALARS] + [WHOLE] * 3,
         pltpu.VMEM((NX * 2 * rows, BLOCK), jnp.bfloat16),
         NX * 4 * rows * BLOCK * BLOCK, 4,
-    )(at, in_vmem(order), features, theirs)
-
-
-def stack_body(at, features, own, first, second, third, a_ref, b_ref, theirs_ref, sems):
-    copies = []
+    )(at, order, features, theirs)
+
+
+def pick_body(at, features, theirs_ref):
     for x in range(NX):
         from_block = pl.ds(pl.multiple_of((x * NC + 1 - at[2]) * BLOCK, BLOCK), BLOCK)
-        copies.append(
-            pltpu.make_async_copy(
-                features.at[:, from_block], theirs_ref.at[:, pl.ds(x * BLOCK, BLOCK)], sems.at[x]
-            )
-        )
-        copies[-1].start()
+        theirs_ref[:, x * BLOCK : (x + 1) * BLOCK] = features[:, from_block]
+
+
+def pick(at, features):
+    return call(
+        pick_body,
+        [SCALARS, WHOLE],
+        jax.ShapeDtypeStruct((features.shape[0], NX * BLOCK), jnp.bfloat16),
+        0, 2,
+    )(at, features)
+
+
+def stack_body(own, first, second, third, plane_ref):
     rows = own.shape[0]
-    for ref, pair in ((a_ref, (own, first)), (b_ref, (second, third))):
-        for i, piece in enumerate(pair):
-            ref[i * rows : (i + 1) * rows, :] = piece[...]
-    for copy in copies:
-        copy.wait()
-
-
-def stack_plane(at, features, pieces):
+    for i, piece in enumerate((own, first, second, third)):
+        plane_ref[i * rows : (i + 1) * rows, :] = piece[...]
+
+
+def stack_plane(pieces):
     rows, columns = pieces[0].shape
     return call(
-        stack_body,
-        [SCALARS, LEFT] + [WHOLE] * 4,
-        [
-            pltpu.VMEM((2 * rows, columns), jnp.bfloat16),
-            pltpu.VMEM((2 * rows, columns), jnp.bfloat16),
-            jax.ShapeDtypeStruct((features.shape[0], NX * BLOCK), jnp.bfloat16),
-        ],
-        0, 4,
-        out_specs=[WHOLE, WHOLE, LEFT],
-        scratch_shapes=[pltpu.SemaphoreType.DMA((NX,))],
-    )(at, features, *[in_vmem(p) for p in pieces])
+        stack_body, [WHOLE] * 4, pltpu.VMEM((4 * rows, columns), jnp.bfloat16), 0, 3
+    )(*[in_vmem(p) for p in pieces])
+
+
+def in_hbm(array):
+    return pltpu.with_memory_space_constraint(array, pltpu.HBM)
 
 
 def in_vmem(array):
     return pltpu.with_memory_space_constraint(array, pltpu.VMEM)
 
 
-def put_rows(steps, pieces, rows_ref, sems):
-    half, stores = BLOCK // 2, []
-    for i, piece in enumerate(pieces):
-        at = steps[i // 2] * BLOCK + i % 2 * half
-        stores.append(pltpu.make_async_copy(piece, rows_ref.at[pl.ds(at, half)], sems.at[i]))
-        stores[-1].start()
-    return stores
-
-
-def products(steps, count, arranged, pieces):
-    half, total = BLOCK // 2, 0.0
-    for i, step in enumerate(steps):
-        left = arranged[step * 2 * count : (step + 1) * 2 * count, :]
-        for j in range(2):
-            total += jnp.dot(
-                left[:, j * half : (j + 1) * half], pieces[2 * i + j][...],
-                preferred_element_type=jnp.float32,
-            )
-    return total[:count], total[count:]
-
-
 def early_body(steps, arranged, *refs):
-    pieces, (mine_ref, theirs_ref, rows_ref, sems) = refs[: 2 * len(steps)], refs[2 * len(steps) :]
-    stores = put_rows(steps, pieces, rows_ref, sems)
-    mine_ref[...], theirs_ref[...] = products(steps, mine_ref.shape[0], arranged, pieces)
+    pieces, (mine_ref, theirs_ref, rows_ref, sems) = refs[: len(steps)], refs[len(steps) :]
+    count, stores, total = mine_ref.shape[0], [], 0.0
+    for i, (step, piece) in enumerate(zip(steps, pieces)):
+        store = pltpu.make_async_copy(
+            piece, rows_ref.at[pl.ds(step * BLOCK, BLOCK)], sems.at[i]
+        )
+        store.start()
+        stores.append(store)
+    for step, piece in zip(steps, pieces):
+        total += jnp.dot(
+            arranged[step * 2 * count : (step + 1) * 2 * count, :], piece[...],
+            preferred_element_type=jnp.float32,
+        )
+    mine_ref[...] = total[:count]
+    theirs_ref[...] = total[count:]
     for store in stores:
         store.wait()
 
@@ -186,37 +174,45 @@
     )(in_vmem(arranged), *[in_vmem(p) for p in pieces])
 
 
-def late_body(steps, arranged, mine, theirs, first, second, mine_ref, theirs_ref):
-    more, more_theirs = products(steps, mine.shape[0], arranged, (first, second))
-    mine_ref[...] = mine[...] + more
-    theirs_ref[...] = theirs[...] + more_theirs
-
-
-def late_sums(arranged, sums, pieces, steps):
+def late_body(step, arranged, mine, theirs, first, second, mine_ref, theirs_ref):
+    count, half = mine.shape[0], BLOCK // 2
+    left = arranged[step * 2 * count : (step + 1) * 2 * count, :]
+    more = jnp.dot(left[:, :half], first[...], preferred_element_type=jnp.float32)
+    more += jnp.dot(left[:, half:], second[...], preferred_element_type=jnp.float32)
+    mine_ref[...] = mine[...] + more[:count]
+    theirs_ref[...] = theirs[...] + more[count:]
+
+
+def late_sums(arranged, sums, halves, step):
     count, columns = sums[0].shape
     return call(
-        functools.partial(late_body, steps),
+        functools.partial(late_body, step),
         [WHOLE] * 5,
         [pltpu.VMEM((count, columns), jnp.float32)] * 2,
-        len(steps) * 4 * count * BLOCK * columns, 4,
-    )(*[in_vmem(x) for x in (arranged, *sums, *pieces)])
-
-
-def place_body(steps, first, second, after, rows_in, rows_ref, sems):
-    for store in put_rows(steps, (first, second), rows_ref, sems):
+        4 * count * BLOCK * columns, 4,
+    )(*[in_vmem(x) for x in (arranged, *sums, *halves)])
+
+
+def place_body(step, first, second, after, rows_in, rows_ref, sems):
+    half, stores = BLOCK // 2, []
+    for i, piece in enumerate((first, second)):
+        to_rows = rows_ref.at[pl.ds(step * BLOCK + i * half, half)]
+        stores.append(pltpu.make_async_copy(piece, to_rows, sems.at[i]))
+        stores[-1].start()
+    for store in stores:
         store.wait()
 
 
-def place_rows(pieces, after, rows, steps):
-    return call(
-        functools.partial(place_body, steps),
-        [WHOLE, WHOLE, LEFT, LEFT],
+def place_rows(halves, after, rows, step):
+    return call(
+        functools.partial(place_body, step),
+        [WHOLE, WHOLE, pl.BlockSpec(memory_space=pl.ANY), LEFT],
         jax.ShapeDtypeStruct(rows.shape, rows.dtype),
         0, 4,
         out_specs=LEFT,
         scratch_shapes=[pltpu.SemaphoreType.DMA((2,))],
         input_output_aliases={3: 0},
-    )(*[in_vmem(p) for p in pieces], after, rows)
+    )(*[in_vmem(p) for p in halves], after, rows)
 
 
 def query_part_body(at, order, grads, all_rows, out_ref, weights, sems):
@@ -226,18 +222,16 @@
         source = all_rows.at[pl.ds(e * BLOCK, BLOCK), pl.ds(0, HQ * HD)]
         loads.append(pltpu.make_async_copy(source, weights.at[e], sems.at[e]))
         loads[-1].start()
+    turned = grads[...].T
     for e in range(NX):
         loads[e].wait()
-        part = lax.dot_general(
-            grads[...], weights[e], TURN, preferred_element_type=jnp.float32
-        )
+        part = jnp.dot(weights[e], turned, preferred_element_type=jnp.float32)
         high = part.astype(jnp.bfloat16)
         low = (part - high.astype(jnp.float32)).astype(jnp.bfloat16)
-        back = lax.dot_general(
-            jnp.concatenate([high, low], axis=0), order[...], TURN,
-            preferred_element_type=jnp.float32,
+        back = jnp.dot(
+            order[...], jnp.concatenate([high, low], axis=1), preferred_element_type=jnp.float32
         )
-        out_ref[:, pl.ds(x_block(at[0], e), BLOCK)] = back[:rows] + back[rows:]
+        out_ref[:, pl.ds(x_block(at[0], e), BLOCK)] = (back[:, :rows] + back[:, rows:]).T
 
 
 def query_part_of(at, order, grads, all_rows):
@@ -251,31 +245,33 @@
             pltpu.VMEM((NX, BLOCK, HQ * HD), jnp.bfloat16),
             pltpu.SemaphoreType.DMA((NX,)),
         ],
-    )(at, in_vmem(order), grads, all_rows)
-
-
-def pair_weights_body(at, order, all_rows, out_ref, weights, sem):
-    load = pltpu.make_async_copy(all_rows.at[:, pl.ds(HQ * HD, 2 * HD)], weights, sem)
-    load.start()
-    load.wait()
+    )(at, in_hbm(order), grads, all_rows)
+
+
+def pair_weights_body(at, order_t, all_rows, out_ref, weights, sems):
+    loads = []
     for e in range(NX):
-        out_ref[pl.ds(x_block(at[0], e), BLOCK), :] = jnp.dot(
-            order[...], weights[e * BLOCK : (e + 1) * BLOCK, :],
-            preferred_element_type=jnp.float32,
+        source = all_rows.at[pl.ds(e * BLOCK, BLOCK), pl.ds(HQ * HD, 2 * HD)]
+        loads.append(pltpu.make_async_copy(source, weights.at[e], sems.at[e]))
+        loads[-1].start()
+    for e in range(NX):
+        loads[e].wait()
+        out_ref[:, pl.ds(x_block(at[0], e), BLOCK)] = jnp.dot(
+            weights[e].T, order_t[...], preferred_element_type=jnp.float32
         ).astype(jnp.bfloat16)
 
 
-def pair_weights_of(at, order, all_rows):
+def pair_weights_of(at, order_t, all_rows):
     return call(
         pair_weights_body,
         [SCALARS, WHOLE, LEFT],
-        pltpu.VMEM((NX * BLOCK, 2 * HD), jnp.bfloat16),
+        pltpu.HBM((2 * HD, NX * BLOCK), jnp.bfloat16),
         NX * 2 * BLOCK * BLOCK * 2 * HD, 3,
         scratch_shapes=[
-            pltpu.VMEM((NX * BLOCK, 2 * HD), jnp.bfloat16),
-            pltpu.SemaphoreType.DMA,
+            pltpu.VMEM((NX, BLOCK, 2 * HD), jnp.bfloat16),
+            pltpu.SemaphoreType.DMA((NX,)),
         ],
-    )(at, in_vmem(order), all_rows)
+    )(at, in_hbm(order_t), all_rows)
 
 
 def finish_body(at, pair_out, own_part, other_part, own_w, other_w, out_ref):
@@ -283,8 +279,8 @@
         cut = slice(x * BLOCK, (x + 1) * BLOCK)
         for flip, part, w in ((0, own_part, own_w), (1, other_part, other_w)):
             parity = at[2] if flip == 0 else 1 - at[2]
-            total = part[:, cut] + lax.dot_general(
-                pair_out[...], w[cut, :], TURN, preferred_element_type=jnp.float32
+            total = part[:, cut] + jnp.dot(
+                pair_out[...], w[:, cut], preferred_element_type=jnp.float32
             )
             to_block = pl.ds(pl.multiple_of((x * NC + parity) * BLOCK, BLOCK), BLOCK)
             out_ref[:, to_block] = total.astype(jnp.bfloat16)
@@ -297,7 +293,7 @@
         in_specs=[pl.BlockSpec(memory_space=pltpu.SMEM)] + [whole] * 5,
         out_shape=jax.ShapeDtypeStruct((pair_out.shape[0], NX * NC * BLOCK), jnp.bfloat16),
         compiler_params=pltpu.CompilerParams(vmem_limit_bytes=VMEM_LIMIT),
-    )(at, pair_out, *[in_vmem(p) for p in parts], *[in_vmem(w) for w in weights])
+    )(at, pair_out, *[in_vmem(p) for p in parts], *[in_hbm(w) for w in weights])
 
 
 def shifted(block, axis, distance):
@@ -339,14 +335,17 @@
 
     at = jnp.stack([x_me, y_me, core]).astype(jnp.int32)
     order = order_matrix(y_me)
-    a0, b0, theirs = stack_plane(at, features, [column, first, second, third])
-    a1, b3 = along_x(a0, 1), along_x(b0, 3)
-    b1, a3 = along_x(b0, 1), along_x(a0, 3)
-    a2, b2 = along_x(a1, 1), along_x(b3, 3)
+    order_t = order.T
+    plane, theirs = lax.optimization_barrier(
+        (stack_plane([column, first, second, third]), pick(at, features))
+    )
+    right, left = along_x(plane, 1), along_x(plane, 3)
+    half = BLOCK // 2
+    far_a, far_b = along_x(right[:half], 1), along_x(left[half:], 3)
     arranged = arrange(at, order, features, swap_cores(theirs))
-    *sums, own_w = early_sums(arranged, [a0, b0, a1, b1, a3, b3], (0, 1, 3))
-    mine, theirs = late_sums(arranged, sums, [a2, b2], (2,))
-    own_w = place_rows([a2, b2], theirs, own_w, (2,))
+    *sums, own_w = early_sums(arranged, [plane, right, left], (0, 1, 3))
+    mine, theirs = late_sums(arranged, sums, [far_a, far_b], 2)
+    own_w = place_rows([far_a, far_b], theirs, own_w, 2)
     projected = mine + swap_cores(theirs)
     other_w = swap_cores(own_w)
     pair_pre, query_pre = projected[:, HQ * HD :], projected[:, : HQ * HD]
@@ -359,7 +358,7 @@
     ).astype(jnp.bfloat16)
     projected_at, pair_rows = lax.optimization_barrier((at, pair_rows))
     back2, pair_w_own = lax.optimization_barrier(
-        (shifted(pair_rows, "ctx", 2), pair_weights_of(projected_at, order, own_w))
+        (shifted(pair_rows, "ctx", 2), pair_weights_of(projected_at, order_t, own_w))
     )
     back31 = shifted(jnp.concatenate([back2, pair_rows], axis=0), "ctx", 1)
     window = jnp.concatenate([back31[:row_count], back2, back31[row_count:], pair_rows], axis=0)
@@ -416,7 +415,7 @@
         (
             shifted((back2 + came[:row_count]).astype(jnp.bfloat16), "ctx", -2),
             query_part_of(at, order, query_out, other_w),
-            pair_weights_of(at, order, other_w),
+            pair_weights_of(at, order_t, other_w),
         )
     )
     pair_total = own_grad + came[row_count:] + last.astype(jnp.float32)

time: 156 us -> 160 us (1.026)
  the two profiles are of different devices: /device:TPU:62 before, /device:TPU:56 now
where the time goes in v6:
time: 160 us; the launch traced here: 159 us
  starting transfers between devices  47.8 us (30%)
  blocking collectives  35.2 us (22%)
  Pallas kernels  32.2 us (20%)
  waiting for transfers between devices  30.1 us (19%)
  local copies, waits for them, and re-layouts  5.5 us (3%)
  other arithmetic  4.2 us (3%)
  matrix products  3.35 us (2%)
    all_gather x1, blocking collectives, local(): lax.all_gather(w_qkv, 'ctx', axis=0, tiled=True, axis_index_groups=[[z *...  35.2 us
    ppermute x4, waiting for transfers between devices, along_x(): lax.ppermute(block, ALL, route(lambda x, c, z, y: ((x + distance) % NX, c...  22.9 us
    ppermute x4, starting transfers between devices, shifted(): lax.ppermute(block, axis, [(i - distance, i) for i in devices if i - dist...  18.6 us
    ppermute x4, starting transfers between devices, along_x(): lax.ppermute(block, ALL, route(lambda x, c, z, y: ((x + distance) % NX, c...  13.4 us
    pallas_call x2, Pallas kernels, query_part_of(): call(query_part_body, [SCALARS, WHOLE, WHOLE, LEFT], pltpu.VMEM((rows, NX...  13.3 us
    ppermute x3, starting transfers between devices, along_y(): lax.ppermute(block, ALL, route(lambda x, c, z, y: (x, c, z, (y + distance...  9.58 us
    pallas_call x2, Pallas kernels, pair_weights_of(): call(pair_weights_body, [SCALARS, WHOLE, LEFT], pltpu.HBM((2 * HD, NX * B...  8.65 us
    ppermute x3, starting transfers between devices, swap_cores(): return lax.ppermute(block, ALL, route(lambda x, c, z, y: (x, 1 - c, z, y)))  6.25 us
  transfers between devices with their start and end apart: 14, of which 5 were waited for; matrix products, arithmetic and copies ran while one was open for 7% of the time, Pallas kernels for 18%

profile of v6, /device:TPU:56, one launch (start us, length us, event | category | flops | bytes accessed | tf_op | source)
XLA Modules:
  0.0 158.9 jit_solution(7676282911611420175)
XLA Ops:
  0.0 35.2 %all_gather.3.own = bf16[128,1280]{1,0:T(8,128)(2,1)S(1)} all-gather(bf16[8,1280]{1,0:T(8,128)(2,1)} %param.7), channel_id=1, replica_groups={{0,4,8,12,16,20,24,28,32,36,40,44,48,52,56,60},{1,5,9,13,17,21,25,29,33..., dimensions={0}, use_global_device_ids=true | all-gather | bytes 348160 | tf_op jit(solution)/shard_map/all_gather | solution.py:330
  35.2 2.6 %collective-permute-start.2 = (bf16[128,1280]{1,0:T(8,128)(2,1)S(1)}, bf16[128,1280]{1,0:T(8,128)(2,1)S(1)}, u32[]{:S(2)}, u32[]{:S(2)}) collective-permute-start(bf16[128,1280]{1,0:T(8,128)(2,1)S(1)} %all_gather.3.own), channel_id=1, source_target_pairs={{0,3},{1,0},{2,1},{3,2},{4,7},{5,4},{6,5},{7,6},{8,11},{9,8},{10,9... | collective-permute-start | bytes 983048 | tf_op jit(solution)/shard_map/ppermute | solution.py:35
  37.9 2.8 %collective-permute-start.1 = (bf16[128,1280]{1,0:T(8,128)(2,1)S(1)}, bf16[128,1280]{1,0:T(8,128)(2,1)S(1)}, u32[]{:S(2)}, u32[]{:S(2)}) collective-permute-start(bf16[128,1280]{1,0:T(8,128)(2,1)S(1)} %all_gather.3.own), channel_id=1, source_target_pairs={{0,2},{1,3},{2,0},{3,1},{4,6},{5,7},{6,4},{7,5},{8,10},{9,11},{10,... | collective-permute-start | bytes 983048 | tf_op jit(solution)/shard_map/ppermute | solution.py:35
  40.7 4.1 %collective-permute-start = (bf16[128,1280]{1,0:T(8,128)(2,1)S(1)}, bf16[128,1280]{1,0:T(8,128)(2,1)S(1)}, u32[]{:S(2)}, u32[]{:S(2)}) collective-permute-start(bf16[128,1280]{1,0:T(8,128)(2,1)S(1)} %all_gather.3.own), channel_id=1, source_target_pairs={{0,1},{1,2},{2,3},{3,0},{4,5},{5,6},{6,7},{7,4},{8,9},{9,10},{10,1... | collective-permute-start | bytes 983048 | tf_op jit(solution)/shard_map/ppermute | solution.py:35
  44.9 1.2 copy-done.1
  46.2 0.6 shard_map.47
  46.7 2.2 %collective-permute-done.2.third = bf16[128,1280]{1,0:T(8,128)(2,1)S(1)} collective-permute-done((bf16[128,1280]{1,0:T(8,128)(2,1)S(1)}, bf16[128,1280]{1,0:T(8,128)(2,1)S(1)}, u32[]{:S(2)}, u32[]{:S(2)}) %collective-permute-start.2) | collective-permute-done | bytes 327712 | tf_op jit(solution)/shard_map/ppermute | solution.py:35
  48.9 2.8 %collective-permute-done.first = bf16[128,1280]{1,0:T(8,128)(2,1)S(1)} collective-permute-done((bf16[128,1280]{1,0:T(8,128)(2,1)S(1)}, bf16[128,1280]{1,0:T(8,128)(2,1)S(1)}, u32[]{:S(2)}, u32[]{:S(2)}) %collective-permute-start) | collective-permute-done | bytes 327712 | tf_op jit(solution)/shard_map/ppermute | solution.py:35
  51.8 4.7 %collective-permute-start.5 = (bf16[512,1280]{1,0:T(8,128)(2,1)S(1)}, bf16[512,1280]{1,0:T(8,128)(2,1)}, u32[]{:S(2)}, u32[]{:S(2)}) collective-permute-start(bf16[512,1280]{1,0:T(8,128)(2,1)S(1)} %shard_map.46.refs_0_), channel_id=1, source_target_pairs={{0,384},{1,385},{2,386},{3,387},{4,388},{5,389},{6,390},{7,391},{8... | collective-permute-start | bytes 3932168 | tf_op jit(solution)/shard_map/ppermute | solution.py:41
  56.4 1.9 %collective-permute-start.4 = (bf16[512,1280]{1,0:T(8,128)(2,1)S(1)}, bf16[512,1280]{1,0:T(8,128)(2,1)}, u32[]{:S(2)}, u32[]{:S(2)}) collective-permute-start(bf16[512,1280]{1,0:T(8,128)(2,1)S(1)} %shard_map.46.refs_0_), channel_id=1, source_target_pairs={{0,128},{1,129},{2,130},{3,131},{4,132},{5,133},{6,134},{7,135},{8... | collective-permute-start | bytes 3932168 | tf_op jit(solution)/shard_map/ppermute | solution.py:41
  58.4 0.8 copy.8
  59.3 1.9 %collective-permute-start.3 = (bf16[128,2048]{1,0:T(8,128)(2,1)S(1)}, bf16[128,2048]{1,0:T(8,128)(2,1)S(1)}, u32[]{:S(2)}, u32[]{:S(2)}) collective-permute-start(bf16[128,2048]{1,0:T(8,128)(2,1)S(1)} %shard_map.47), channel_id=1, source_target_pairs={{0,64},{1,65},{2,66},{3,67},{4,68},{5,69},{6,70},{7,71},{8,72},{9,... | collective-permute-start | bytes 1572872 | tf_op jit(solution)/shard_map/ppermute | solution.py:47
  61.2 18.2 %collective-permute-done.5.refs_2_ = bf16[512,1280]{1,0:T(8,128)(2,1)} collective-permute-done((bf16[512,1280]{1,0:T(8,128)(2,1)S(1)}, bf16[512,1280]{1,0:T(8,128)(2,1)}, u32[]{:S(2)}, u32[]{:S(2)}) %collective-permute-start.5) | collective-permute-done | bytes 1310752 | tf_op jit(solution)/shard_map/ppermute | solution.py:41
  79.4 1.1 slice.106
  80.5 4.8 %collective-permute-start.7 = (bf16[256,1280]{1,0:T(8,128)(2,1)S(1)}, bf16[256,1280]{1,0:T(8,128)(2,1)S(1)}, u32[]{:S(2)}, u32[]{:S(2)}) collective-permute-start(bf16[256,1280]{1,0:T(8,128)(2,1)S(1)} %slice.106), channel_id=1, source_target_pairs={{0,384},{1,385},{2,386},{3,387},{4,388},{5,389},{6,390},{7,391},{8... | collective-permute-start | bytes 1966088 | tf_op jit(solution)/shard_map/ppermute | solution.py:41
  85.4 1.1 slice.105
  86.5 1.9 %collective-permute-start.6 = (bf16[256,1280]{1,0:T(8,128)(2,1)S(1)}, bf16[256,1280]{1,0:T(8,128)(2,1)S(1)}, u32[]{:S(2)}, u32[]{:S(2)}) collective-permute-start(bf16[256,1280]{1,0:T(8,128)(2,1)S(1)} %slice.105), channel_id=1, source_target_pairs={{0,128},{1,129},{2,130},{3,131},{4,132},{5,133},{6,134},{7,135},{8... | collective-permute-start | bytes 1966088 | tf_op jit(solution)/shard_map/ppermute | solution.py:41
  88.5 2.1 %fusion.31 = (bf16[512,512]{1,0:T(8,128)(2,1)}, bf16[512,512]{1,0:T(8,128)(2,1)S(1)}) fusion(s32[512]{0:T(512)S(1)} %get-tuple-element.60, s32[512]{0:T(512)S(1)} %get-tuple-element.63, s32[512]{0:T(512)S(1)} %get-tuple-element.61, s32[512]{0:T(512)S(1)} %get-tuple-element.62, s32[]{:T(128)} %select_n.64, pred[512]{0:T(512)(128)(4,1)S(1)} %get-tuple-element.65, ...), kind=kLoop, calls=%fused_computation.61 | loop fusion | flops 20971520 | bytes 1057796 | tf_op jit(solution)/shard_map/convert_element_type | solution.py:60
  90.6 1.2 shard_map.48.arranged
  91.9 3.7 %shard_map.49 = (f32[128,1280]{1,0:T(8,128)S(1)}, f32[128,1280]{1,0:T(8,128)S(1)}, bf16[2048,1280]{1,0:T(8,128)(2,1)}) custom-call(bf16[1024,512]{1,0:T(8,128)(2,1)S(1)} %shard_map.48.arranged, bf16[512,1280]{1,0:T(8,128)(2,1)S(1)} %shard_map.46.refs_0_, bf16[512,1280]{1,0:T(8,128)(2,1)} %collective-permute-done.4.refs_1_, ...), custom_call_target="tpu_custom_call" | custom-call | flops 1006632960 | bytes 6291456 | tf_op jit(solution)/shard_map/pallas_call | solution.py:163
  95.5 4.7 %collective-permute-done.6.first = bf16[256,1280]{1,0:T(8,128)(2,1)S(1)} collective-permute-done((bf16[256,1280]{1,0:T(8,128)(2,1)S(1)}, bf16[256,1280]{1,0:T(8,128)(2,1)S(1)}, u32[]{:S(2)}, u32[]{:S(2)}) %collective-permute-start.6) | collective-permute-done | bytes 655392 | tf_op jit(solution)/shard_map/ppermute | solution.py:41
  100.2 0.5 shard_map.50
  100.7 1.9 %collective-permute-start.8 = (f32[128,1280]{1,0:T(8,128)S(1)}, f32[128,1280]{1,0:T(8,128)S(1)}, u32[]{:S(2)}, u32[]{:S(2)}) collective-permute-start(f32[128,1280]{1,0:T(8,128)S(1)} %get-tuple-element.26.after), channel_id=1, source_target_pairs={{0,64},{1,65},{2,66},{3,67},{4,68},{5,69},{6,70},{7,71},{8,72},{9,... | collective-permute-start | bytes 1966088 | tf_op jit(solution)/shard_map/ppermute | solution.py:47
  102.7 1.2 shard_map.51.all_rows
  103.9 2.4 %collective-permute-start.13 = (bf16[2048,1280]{1,0:T(8,128)(2,1)}, bf16[2048,1280]{1,0:T(8,128)(2,1)}, u32[]{:S(2)}, u32[]{:S(2)}) collective-permute-start(bf16[2048,1280]{1,0:T(8,128)(2,1)} %shard_map.51.all_rows), channel_id=1, source_target_pairs={{0,64},{1,65},{2,66},{3,67},{4,68},{5,69},{6,70},{7,71},{8,72},{9,... | collective-permute-start | bytes 15728648 | tf_op jit(solution)/shard_map/ppermute | solution.py:47
  106.7 0.3 fusion.48
  107.1 3.7 %collective-permute-start.9 = (bf16[128,256]{1,0:T(8,128)(2,1)S(1)}, bf16[128,256]{1,0:T(8,128)(2,1)S(1)}, u32[]{:S(2)}, u32[]{:S(2)}) collective-permute-start(bf16[128,256]{1,0:T(8,128)(2,1)S(1)} %pad_maximum_fusion.5), channel_id=1, source_target_pairs={{0,2},{1,3},{2,4},{3,5},{4,6},{5,7},{6,8},{7,9},{8,10},{9,11},{10,... | collective-permute-start | bytes 196616 | tf_op jit(solution)/shard_map/ppermute | solution.py:301
  110.9 0.2 fusion.68
  111.1 4.3 %shard_map.52.own_w = bf16[256,2048]{1,0:T(8,128)(2,1)} custom-call(s32[3]{0:T(128)S(1)} %pad_add_fusion.at, bf16[512,512]{1,0:T(8,128)(2,1)} %get-tuple-element.51.order_t, bf16[2048,1280]{1,0:T(8,128)(2,1)} %shard_map.51.all_rows), custom_call_target="tpu_custom_call" | custom-call | flops 536870912 | bytes 3145728 | tf_op jit(solution)/shard_map/pallas_call | solution.py:265
  115.4 5.4 %collective-permute-start.10 = (bf16[256,256]{1,0:T(8,128)(2,1)S(1)}, bf16[256,256]{1,0:T(8,128)(2,1)S(1)}, u32[]{:S(2)}, u32[]{:S(2)}) collective-permute-start(bf16[256,256]{1,0:T(8,128)(2,1)S(1)} %pad_maximum_fusion.3), channel_id=1, source_target_pairs={{0,1},{1,2},{2,3},{3,4},{4,5},{5,6},{6,7},{7,8},{8,9},{9,10},{10,1... | collective-permute-start | bytes 393224 | tf_op jit(solution)/shard_map/ppermute | solution.py:301
  120.9 0.2 subtract_convert_fusion.1
  121.1 2.3 %collective-permute-done.10 = bf16[256,256]{1,0:T(8,128)(2,1)S(1)} collective-permute-done((bf16[256,256]{1,0:T(8,128)(2,1)S(1)}, bf16[256,256]{1,0:T(8,128)(2,1)S(1)}, u32[]{:S(2)}, u32[]{:S(2)}) %collective-permute-start.10) | collective-permute-done | bytes 131104 | tf_op jit(solution)/shard_map/ppermute | solution.py:301
  123.4 1.0 fusion.71
  124.5 0.2 fusion.34
  124.7 0.8 copy-done.3
  125.4 0.4 convolution_bitcast_fusion
  125.8 0.4 fusion.7
  126.2 0.4 fusion.2
  126.7 0.5 fusion.8
  127.3 3.3 %collective-permute-start.11 = (bf16[256,256]{1,0:T(8,128)(2,1)S(1)}, bf16[256,256]{1,0:T(8,128)(2,1)S(1)}, u32[]{:S(2)}, u32[]{:S(2)}) collective-permute-start(bf16[256,256]{1,0:T(8,128)(2,1)S(1)} %pad_maximum_fusion.4), channel_id=1, source_target_pairs={{1,0},{2,1},{3,2},{4,3},{5,4},{6,5},{7,6},{8,7},{9,8},{10,9},{11,1... | collective-permute-start | bytes 393224 | tf_op jit(solution)/shard_map/ppermute | solution.py:301
  130.6 0.6 fusion.4
  131.1 0.3 subtract_convert_fusion
  131.5 6.6 %shard_map.53.own_part = f32[128,2048]{1,0:T(8,128)S(1)} custom-call(s32[3]{0:T(128)S(1)} %pad_add_fusion.at, bf16[512,512]{1,0:T(8,128)(2,1)} %copy-done, bf16[128,1024]{1,0:T(8,128)(2,1)S(1)} %copy_bitcast_fusion.grads, bf16[2048,1280]{1,0:T(8,128)(2,1)} %shard_map.51.all_rows), custom_call_target="tpu_custom_call" | custom-call | flops 1073741824 | bytes 6291456 | tf_op jit(solution)/shard_map/pallas_call | solution.py:239
  138.2 6.2 %collective-permute-start.12 = (bf16[128,256]{1,0:T(8,128)(2,1)S(1)}, bf16[128,256]{1,0:T(8,128)(2,1)S(1)}, u32[]{:S(2)}, u32[]{:S(2)}) collective-permute-start(bf16[128,256]{1,0:T(8,128)(2,1)S(1)} %fusion.43), channel_id=1, source_target_pairs={{2,0},{3,1},{4,2},{5,3},{6,4},{7,5},{8,6},{9,7},{10,8},{11,9},{12,... | collective-permute-start | bytes 196616 | tf_op jit(solution)/shard_map/ppermute | solution.py:301
  144.4 6.6 %shard_map.54.other_part = f32[128,2048]{1,0:T(8,128)S(1)} custom-call(s32[3]{0:T(128)S(1)} %pad_add_fusion.at, bf16[512,512]{1,0:T(8,128)(2,1)} %copy-done, bf16[128,1024]{1,0:T(8,128)(2,1)S(1)} %copy_bitcast_fusion.grads, bf16[2048,1280]{1,0:T(8,128)(2,1)} %collective-permute-done.13.all_rows), custom_call_target="tpu_custom_call" | custom-call | flops 1073741824 | bytes 6291456 | tf_op jit(solution)/shard_map/pallas_call | solution.py:239
  151.1 4.3 %shard_map.55.other_w = bf16[256,2048]{1,0:T(8,128)(2,1)} custom-call(s32[3]{0:T(128)S(1)} %pad_add_fusion.at, bf16[512,512]{1,0:T(8,128)(2,1)} %get-tuple-element.51.order_t, bf16[2048,1280]{1,0:T(8,128)(2,1)} %collective-permute-done.13.all_rows), custom_call_target="tpu_custom_call" | custom-call | flops 536870912 | bytes 3145728 | tf_op jit(solution)/shard_map/pallas_call | solution.py:265
  155.5 0.3 fusion.57
  155.9 3.0 %shard_map.56 = bf16[128,4096]{1,0:T(8,128)(2,1)} custom-call(s32[3]{0:T(128)S(1)} %pad_add_fusion.at, bf16[128,256]{1,0:T(8,128)(2,1)S(1)} %pad_maximum_fusion.6.pair_out, f32[128,2048]{1,0:T(8,128)S(1)} %shard_map.53.own_part, f32[128,2048]{1,0:T(8,128)S(1)} %shard_map.54.other_part, bf16[256,2048]{1,0:T(8,128)(2,1)} %shard_map.52.own_w, ...), custom_call_target="tpu_custom_call" | custom-call | tf_op jit(solution)/shard_map/pallas_call | solution.py:291
  (46 shorter events, 1.1 us)
Async XLA Ops:
  35.2 13.7 %collective-permute-start.2 = (bf16[128,1280]{1,0:T(8,128)(2,1)S(1)}, bf16[128,1280]{1,0:T(8,128)(2,1)S(1)}, u32[]{:S(2)}, u32[]{:S(2)}) collective-permute-start(bf16[128,1280]{1,0:T(8,128)(2,1)S(1)} %all_gather.3.own), channel_id=1, source_target_pairs={{0,3},{1,0},{2,1},{3,2},{4,7},{5,4},{6,5},{7,6},{8,11},{9,8},{10,9... | collective-permute-start | bytes 983048 | tf_op jit(solution)/shard_map/ppermute | solution.py:35
  37.9 11.0 %collective-permute-start.1 = (bf16[128,1280]{1,0:T(8,128)(2,1)S(1)}, bf16[128,1280]{1,0:T(8,128)(2,1)S(1)}, u32[]{:S(2)}, u32[]{:S(2)}) collective-permute-start(bf16[128,1280]{1,0:T(8,128)(2,1)S(1)} %all_gather.3.own), channel_id=1, source_target_pairs={{0,2},{1,3},{2,0},{3,1},{4,6},{5,7},{6,4},{7,5},{8,10},{9,11},{10,... | collective-permute-start | bytes 983048 | tf_op jit(solution)/shard_map/ppermute | solution.py:35
  40.7 10.9 %collective-permute-start = (bf16[128,1280]{1,0:T(8,128)(2,1)S(1)}, bf16[128,1280]{1,0:T(8,128)(2,1)S(1)}, u32[]{:S(2)}, u32[]{:S(2)}) collective-permute-start(bf16[128,1280]{1,0:T(8,128)(2,1)S(1)} %all_gather.3.own), channel_id=1, source_target_pairs={{0,1},{1,2},{2,3},{3,0},{4,5},{5,6},{6,7},{7,4},{8,9},{9,10},{10,1... | collective-permute-start | bytes 983048 | tf_op jit(solution)/shard_map/ppermute | solution.py:35
  44.9 1.2 copy-start.1
  46.2 12.2 %copy-start.4 = (bf16[1,128,1024]{2,1,0:T(8,128)(2,1)S(1)}, bf16[1,128,1024]{2,1,0:T(8,128)(2,1)}, u32[]{:S(2)}) copy-start(bf16[1,128,1024]{2,1,0:T(8,128)(2,1)} %param.6) | copy-start | bytes 786436
  51.8 27.6 %collective-permute-start.5 = (bf16[512,1280]{1,0:T(8,128)(2,1)S(1)}, bf16[512,1280]{1,0:T(8,128)(2,1)}, u32[]{:S(2)}, u32[]{:S(2)}) collective-permute-start(bf16[512,1280]{1,0:T(8,128)(2,1)S(1)} %shard_map.46.refs_0_), channel_id=1, source_target_pairs={{0,384},{1,385},{2,386},{3,387},{4,388},{5,389},{6,390},{7,391},{8... | collective-permute-start | bytes 3932168 | tf_op jit(solution)/shard_map/ppermute | solution.py:41
  56.4 28.9 %collective-permute-start.4 = (bf16[512,1280]{1,0:T(8,128)(2,1)S(1)}, bf16[512,1280]{1,0:T(8,128)(2,1)}, u32[]{:S(2)}, u32[]{:S(2)}) collective-permute-start(bf16[512,1280]{1,0:T(8,128)(2,1)S(1)} %shard_map.46.refs_0_), channel_id=1, source_target_pairs={{0,128},{1,129},{2,130},{3,131},{4,132},{5,133},{6,134},{7,135},{8... | collective-permute-start | bytes 3932168 | tf_op jit(solution)/shard_map/ppermute | solution.py:41
  58.4 32.2 %copy-start.2 = (bf16[1,128,4096]{2,1,0:T(8,128)(2,1)S(1)}, bf16[1,128,4096]{2,1,0:T(8,128)(2,1)}, u32[]{:S(2)}) copy-start(bf16[1,128,4096]{2,1,0:T(8,128)(2,1)} %param.4) | copy-start | bytes 3145732
  59.3 31.3 %collective-permute-start.3 = (bf16[128,2048]{1,0:T(8,128)(2,1)S(1)}, bf16[128,2048]{1,0:T(8,128)(2,1)S(1)}, u32[]{:S(2)}, u32[]{:S(2)}) collective-permute-start(bf16[128,2048]{1,0:T(8,128)(2,1)S(1)} %shard_map.47), channel_id=1, source_target_pairs={{0,64},{1,65},{2,66},{3,67},{4,68},{5,69},{6,70},{7,71},{8,72},{9,... | collective-permute-start | bytes 1572872 | tf_op jit(solution)/shard_map/ppermute | solution.py:47
  80.5 15.0 %collective-permute-start.7 = (bf16[256,1280]{1,0:T(8,128)(2,1)S(1)}, bf16[256,1280]{1,0:T(8,128)(2,1)S(1)}, u32[]{:S(2)}, u32[]{:S(2)}) collective-permute-start(bf16[256,1280]{1,0:T(8,128)(2,1)S(1)} %slice.106), channel_id=1, source_target_pairs={{0,384},{1,385},{2,386},{3,387},{4,388},{5,389},{6,390},{7,391},{8... | collective-permute-start | bytes 1966088 | tf_op jit(solution)/shard_map/ppermute | solution.py:41
  86.5 13.7 %collective-permute-start.6 = (bf16[256,1280]{1,0:T(8,128)(2,1)S(1)}, bf16[256,1280]{1,0:T(8,128)(2,1)S(1)}, u32[]{:S(2)}, u32[]{:S(2)}) collective-permute-start(bf16[256,1280]{1,0:T(8,128)(2,1)S(1)} %slice.105), channel_id=1, source_target_pairs={{0,128},{1,129},{2,130},{3,131},{4,132},{5,133},{6,134},{7,135},{8... | collective-permute-start | bytes 1966088 | tf_op jit(solution)/shard_map/ppermute | solution.py:41
  90.6 4.9 %copy-start = (bf16[512,512]{1,0:T(8,128)(2,1)}, bf16[512,512]{1,0:T(8,128)(2,1)S(1)}, u32[]{:S(2)}) copy-start(bf16[512,512]{1,0:T(8,128)(2,1)S(1)} %get-tuple-element.52.order) | copy-start | bytes 1572868
  100.7 5.7 %collective-permute-start.8 = (f32[128,1280]{1,0:T(8,128)S(1)}, f32[128,1280]{1,0:T(8,128)S(1)}, u32[]{:S(2)}, u32[]{:S(2)}) collective-permute-start(f32[128,1280]{1,0:T(8,128)S(1)} %get-tuple-element.26.after), channel_id=1, source_target_pairs={{0,64},{1,65},{2,66},{3,67},{4,68},{5,69},{6,70},{7,71},{8,72},{9,... | collective-permute-start | bytes 1966088 | tf_op jit(solution)/shard_map/ppermute | solution.py:47
  102.7 3.6 %copy-start.5 = (s32[1,128]{1,0:T(1,128)S(1)}, s32[1,128]{1,0:T(1,128)}, u32[]{:S(2)}) copy-start(s32[1,128]{1,0:T(1,128)} %param.5) | copy-start | bytes 1540
  103.9 40.6 %collective-permute-start.13 = (bf16[2048,1280]{1,0:T(8,128)(2,1)}, bf16[2048,1280]{1,0:T(8,128)(2,1)}, u32[]{:S(2)}, u32[]{:S(2)}) collective-permute-start(bf16[2048,1280]{1,0:T(8,128)(2,1)} %shard_map.51.all_rows), channel_id=1, source_target_pairs={{0,64},{1,65},{2,66},{3,67},{4,68},{5,69},{6,70},{7,71},{8,72},{9,... | collective-permute-start | bytes 15728648 | tf_op jit(solution)/shard_map/ppermute | solution.py:47
  107.1 8.3 %collective-permute-start.9 = (bf16[128,256]{1,0:T(8,128)(2,1)S(1)}, bf16[128,256]{1,0:T(8,128)(2,1)S(1)}, u32[]{:S(2)}, u32[]{:S(2)}) collective-permute-start(bf16[128,256]{1,0:T(8,128)(2,1)S(1)} %pad_maximum_fusion.5), channel_id=1, source_target_pairs={{0,2},{1,3},{2,4},{3,5},{4,6},{5,7},{6,8},{7,9},{8,10},{9,11},{10,... | collective-permute-start | bytes 196616 | tf_op jit(solution)/shard_map/ppermute | solution.py:301
  115.4 7.9 %collective-permute-start.10 = (bf16[256,256]{1,0:T(8,128)(2,1)S(1)}, bf16[256,256]{1,0:T(8,128)(2,1)S(1)}, u32[]{:S(2)}, u32[]{:S(2)}) collective-permute-start(bf16[256,256]{1,0:T(8,128)(2,1)S(1)} %pad_maximum_fusion.3), channel_id=1, source_target_pairs={{0,1},{1,2},{2,3},{3,4},{4,5},{5,6},{6,7},{7,8},{8,9},{9,10},{10,1... | collective-permute-start | bytes 393224 | tf_op jit(solution)/shard_map/ppermute | solution.py:301
  124.5 1.0 copy-start.3
  127.3 10.9 %collective-permute-start.11 = (bf16[256,256]{1,0:T(8,128)(2,1)S(1)}, bf16[256,256]{1,0:T(8,128)(2,1)S(1)}, u32[]{:S(2)}, u32[]{:S(2)}) collective-permute-start(bf16[256,256]{1,0:T(8,128)(2,1)S(1)} %pad_maximum_fusion.4), channel_id=1, source_target_pairs={{1,0},{2,1},{3,2},{4,3},{5,4},{6,5},{7,6},{8,7},{9,8},{10,9},{11,1... | collective-permute-start | bytes 393224 | tf_op jit(solution)/shard_map/ppermute | solution.py:301
  138.2 17.2 %collective-permute-start.12 = (bf16[128,256]{1,0:T(8,128)(2,1)S(1)}, bf16[128,256]{1,0:T(8,128)(2,1)S(1)}, u32[]{:S(2)}, u32[]{:S(2)}) collective-permute-start(bf16[128,256]{1,0:T(8,128)(2,1)S(1)} %fusion.43), channel_id=1, source_target_pairs={{2,0},{3,1},{4,2},{5,3},{6,4},{7,5},{8,6},{9,7},{10,8},{11,9},{12,... | collective-permute-start | bytes 196616 | tf_op jit(solution)/shard_map/ppermute | solution.py:301

commit v7 on v6

--- a/solution.py
+++ b/solution.py
@@ -31,16 +31,13 @@
     ]
 
 
-def along_y(block, distance):
-    return lax.ppermute(
-        block, ALL, route(lambda x, c, z, y: (x, c, z, (y + distance) % NY))
-    )
-
-
-def along_x(block, distance):
-    return lax.ppermute(
-        block, ALL, route(lambda x, c, z, y: ((x + distance) % NX, c, z, y))
-    )
+def hop(block, distance, x_core):
+    def move(x, c, z, y):
+        if c == x_core:
+            return (x + distance) % NX, c, z, y
+        return x, c, z, (y + distance) % NY
+
+    return lax.ppermute(block, ALL, route(move))
 
 
 def swap_cores(block):
@@ -65,15 +62,24 @@
 
 
 def arrange_body(at, order, features, theirs, out_ref):
-    for e in range(NX):
-        x_at = (at[0] - e + NX) % NX
+    for s in range(NX):
+        x_at = (at[0] - s + NX) % NX
         own = features[:, pl.ds(pl.multiple_of((x_at * NC + at[2]) * BLOCK, BLOCK), BLOCK)]
         other = theirs[:, pl.ds(pl.multiple_of(x_at * BLOCK, BLOCK), BLOCK)]
         both = jnp.concatenate([own, other], axis=0)
         rows = both.shape[0]
-        out_ref[e * rows : (e + 1) * rows, :] = jnp.dot(
-            both, order[...], preferred_element_type=jnp.float32
-        ).astype(jnp.bfloat16)
+        got = jnp.dot(both, order[...], preferred_element_type=jnp.float32).astype(jnp.bfloat16)
+
+        @pl.when(at[2] == 1)
+        def _():
+            out_ref[s * rows : (s + 1) * rows, :] = got
+
+        @pl.when(at[2] == 0)
+        def _():
+            for e in range(NY):
+                out_ref[e * rows : (e + 1) * rows, s * SPAN : (s + 1) * SPAN] = got[
+                    :, e * SPAN : (e + 1) * SPAN
+                ]
 
 
 SCALARS = pl.BlockSpec(memory_space=pltpu.SMEM)
@@ -174,104 +180,131 @@
     )(in_vmem(arranged), *[in_vmem(p) for p in pieces])
 
 
-def late_body(step, arranged, mine, theirs, first, second, mine_ref, theirs_ref):
-    count, half = mine.shape[0], BLOCK // 2
-    left = arranged[step * 2 * count : (step + 1) * 2 * count, :]
-    more = jnp.dot(left[:, :half], first[...], preferred_element_type=jnp.float32)
-    more += jnp.dot(left[:, half:], second[...], preferred_element_type=jnp.float32)
+def late_body(steps, arranged, mine, theirs, *refs):
+    pieces, (mine_ref, theirs_ref) = refs[: len(steps)], refs[len(steps) :]
+    count, more = mine.shape[0], 0.0
+    for step, piece in zip(steps, pieces):
+        more += jnp.dot(
+            arranged[step * 2 * count : (step + 1) * 2 * count, :], piece[...],
+            preferred_element_type=jnp.float32,
+        )
     mine_ref[...] = mine[...] + more[:count]
     theirs_ref[...] = theirs[...] + more[count:]
 
 
-def late_sums(arranged, sums, halves, step):
+def late_sums(arranged, sums, pieces, steps):
     count, columns = sums[0].shape
     return call(
-        functools.partial(late_body, step),
-        [WHOLE] * 5,
+        functools.partial(late_body, steps),
+        [WHOLE] * (3 + len(pieces)),
         [pltpu.VMEM((count, columns), jnp.float32)] * 2,
-        4 * count * BLOCK * columns, 4,
-    )(*[in_vmem(x) for x in (arranged, *sums, *halves)])
-
-
-def place_body(step, first, second, after, rows_in, rows_ref, sems):
-    half, stores = BLOCK // 2, []
+        len(steps) * 4 * count * BLOCK * columns, 4,
+    )(*[in_vmem(x) for x in (arranged, *sums, *pieces)])
+
+
+def place_body(steps, first, second, after, rows_in, rows_ref, sems):
+    stores = []
     for i, piece in enumerate((first, second)):
-        to_rows = rows_ref.at[pl.ds(step * BLOCK + i * half, half)]
+        to_rows = rows_ref.at[pl.ds(steps[i] * BLOCK, BLOCK)]
         stores.append(pltpu.make_async_copy(piece, to_rows, sems.at[i]))
         stores[-1].start()
     for store in stores:
         store.wait()
 
 
-def place_rows(halves, after, rows, step):
-    return call(
-        functools.partial(place_body, step),
+def place_rows(pieces, after, rows, steps):
+    return call(
+        functools.partial(place_body, steps),
         [WHOLE, WHOLE, pl.BlockSpec(memory_space=pl.ANY), LEFT],
         jax.ShapeDtypeStruct(rows.shape, rows.dtype),
         0, 4,
         out_specs=LEFT,
         scratch_shapes=[pltpu.SemaphoreType.DMA((2,))],
         input_output_aliases={3: 0},
-    )(*[in_vmem(p) for p in halves], after, rows)
-
-
-def query_part_body(at, order, grads, all_rows, out_ref, weights, sems):
+    )(*[in_vmem(p) for p in pieces], after, rows)
+
+
+TURN = (((1,), (1,)), ((), ()))
+
+
+def by_source(pieces, parity, cut, join):
+    for s in range(NX):
+        turned = join([cut(piece, s) for piece in pieces])
+        yield s, jnp.where(parity == 0, turned, pieces[s])
+
+
+def query_part_body(flip, at, order, grads, all_rows, out_ref, weights, held, sems):
+    parity = at[2] if flip == 0 else 1 - at[2]
     rows = grads.shape[0]
     loads = []
     for e in range(NX):
         source = all_rows.at[pl.ds(e * BLOCK, BLOCK), pl.ds(0, HQ * HD)]
         loads.append(pltpu.make_async_copy(source, weights.at[e], sems.at[e]))
         loads[-1].start()
-    turned = grads[...].T
     for e in range(NX):
         loads[e].wait()
-        part = jnp.dot(weights[e], turned, preferred_element_type=jnp.float32)
+        held[e] = lax.dot_general(
+            grads[...], weights[e], TURN, preferred_element_type=jnp.float32
+        )
+    for s, part in by_source(
+        [held[e] for e in range(NX)], parity,
+        lambda piece, d: piece[:, d * SPAN : (d + 1) * SPAN],
+        lambda parts: jnp.concatenate(parts, axis=1),
+    ):
         high = part.astype(jnp.bfloat16)
         low = (part - high.astype(jnp.float32)).astype(jnp.bfloat16)
-        back = jnp.dot(
-            order[...], jnp.concatenate([high, low], axis=1), preferred_element_type=jnp.float32
-        )
-        out_ref[:, pl.ds(x_block(at[0], e), BLOCK)] = (back[:, :rows] + back[:, rows:]).T
-
-
-def query_part_of(at, order, grads, all_rows):
+        back = lax.dot_general(
+            jnp.concatenate([high, low], axis=0), order[...], TURN,
+            preferred_element_type=jnp.float32,
+        )
+        out_ref[:, pl.ds(x_block(at[0], s), BLOCK)] = back[:rows] + back[rows:]
+
+
+def query_part_of(at, order, grads, all_rows, flip):
     rows = grads.shape[0]
     return call(
-        query_part_body,
+        functools.partial(query_part_body, flip),
         [SCALARS, WHOLE, WHOLE, LEFT],
         pltpu.VMEM((rows, NX * BLOCK), jnp.float32),
         NX * 2 * rows * BLOCK * (HQ * HD + 2 * BLOCK), 6,
         scratch_shapes=[
             pltpu.VMEM((NX, BLOCK, HQ * HD), jnp.bfloat16),
+            pltpu.VMEM((NX, rows, BLOCK), jnp.float32),
             pltpu.SemaphoreType.DMA((NX,)),
         ],
     )(at, in_hbm(order), grads, all_rows)
 
 
-def pair_weights_body(at, order_t, all_rows, out_ref, weights, sems):
+def pair_weights_body(flip, at, order, all_rows, out_ref, weights, sems):
+    parity = at[2] if flip == 0 else 1 - at[2]
     loads = []
     for e in range(NX):
         source = all_rows.at[pl.ds(e * BLOCK, BLOCK), pl.ds(HQ * HD, 2 * HD)]
         loads.append(pltpu.make_async_copy(source, weights.at[e], sems.at[e]))
         loads[-1].start()
-    for e in range(NX):
-        loads[e].wait()
-        out_ref[:, pl.ds(x_block(at[0], e), BLOCK)] = jnp.dot(
-            weights[e].T, order_t[...], preferred_element_type=jnp.float32
+    for load in loads:
+        load.wait()
+    for s, part in by_source(
+        [weights[e] for e in range(NX)], parity,
+        lambda piece, d: piece[d * SPAN : (d + 1) * SPAN],
+        lambda parts: jnp.concatenate(parts, axis=0),
+    ):
+        out_ref[pl.ds(x_block(at[0], s), BLOCK), :] = jnp.dot(
+            order[...], part, preferred_element_type=jnp.float32
         ).astype(jnp.bfloat16)
 
 
-def pair_weights_of(at, order_t, all_rows):
-    return call(
-        pair_weights_body,
+def pair_weights_of(at, order, all_rows, flip):
+    return call(
+        functools.partial(pair_weights_body, flip),
         [SCALARS, WHOLE, LEFT],
-        pltpu.HBM((2 * HD, NX * BLOCK), jnp.bfloat16),
+        pltpu.HBM((NX * BLOCK, 2 * HD), jnp.bfloat16),
         NX * 2 * BLOCK * BLOCK * 2 * HD, 3,
         scratch_shapes=[
             pltpu.VMEM((NX, BLOCK, 2 * HD), jnp.bfloat16),
             pltpu.SemaphoreType.DMA((NX,)),
         ],
-    )(at, in_hbm(order_t), all_rows)
+    )(at, in_hbm(order), all_rows)
 
 
 def finish_body(at, pair_out, own_part, other_part, own_w, other_w, out_ref):
@@ -279,8 +312,8 @@
         cut = slice(x * BLOCK, (x + 1) * BLOCK)
         for flip, part, w in ((0, own_part, own_w), (1, other_part, other_w)):
             parity = at[2] if flip == 0 else 1 - at[2]
-            total = part[:, cut] + jnp.dot(
-                pair_out[...], w[:, cut], preferred_element_type=jnp.float32
+            total = part[:, cut] + lax.dot_general(
+                pair_out[...], w[cut, :], TURN, preferred_element_type=jnp.float32
             )
             to_block = pl.ds(pl.multiple_of((x * NC + parity) * BLOCK, BLOCK), BLOCK)
             out_ref[:, to_block] = total.astype(jnp.bfloat16)
@@ -331,21 +364,18 @@
         w_qkv, "ctx", axis=0, tiled=True,
         axis_index_groups=[[z * NY + y for z in range(NZ)] for y in range(NY)],
     )
-    second, first, third = (along_y(column, d) for d in (2, 1, 3))
+    second, first, third = (hop(column, d, 0) for d in (2, 1, 3))
 
     at = jnp.stack([x_me, y_me, core]).astype(jnp.int32)
     order = order_matrix(y_me)
-    order_t = order.T
     plane, theirs = lax.optimization_barrier(
         (stack_plane([column, first, second, third]), pick(at, features))
     )
-    right, left = along_x(plane, 1), along_x(plane, 3)
-    half = BLOCK // 2
-    far_a, far_b = along_x(right[:half], 1), along_x(left[half:], 3)
+    two, one, three = (hop(plane, d, 1) for d in (2, 1, 3))
     arranged = arrange(at, order, features, swap_cores(theirs))
-    *sums, own_w = early_sums(arranged, [plane, right, left], (0, 1, 3))
-    mine, theirs = late_sums(arranged, sums, [far_a, far_b], 2)
-    own_w = place_rows([far_a, far_b], theirs, own_w, 2)
+    *sums, own_w = early_sums(arranged, [plane, three], (0, 3))
+    mine, theirs = late_sums(arranged, sums, [one, two], (1, 2))
+    own_w = place_rows([one, two], theirs, own_w, (1, 2))
     projected = mine + swap_cores(theirs)
     other_w = swap_cores(own_w)
     pair_pre, query_pre = projected[:, HQ * HD :], projected[:, : HQ * HD]
@@ -358,7 +388,7 @@
     ).astype(jnp.bfloat16)
     projected_at, pair_rows = lax.optimization_barrier((at, pair_rows))
     back2, pair_w_own = lax.optimization_barrier(
-        (shifted(pair_rows, "ctx", 2), pair_weights_of(projected_at, order_t, own_w))
+        (shifted(pair_rows, "ctx", 2), pair_weights_of(projected_at, order, own_w, 0))
     )
     back31 = shifted(jnp.concatenate([back2, pair_rows], axis=0), "ctx", 1)
     window = jnp.concatenate([back31[:row_count], back2, back31[row_count:], pair_rows], axis=0)
@@ -407,15 +437,15 @@
     came, part_own = lax.optimization_barrier(
         (
             shifted(jnp.concatenate([back3, back1], axis=0).astype(jnp.bfloat16), "ctx", -1),
-            query_part_of(at, order, query_out, own_w),
+            query_part_of(at, order, query_out, own_w, 0),
         )
     )
     came = came.astype(jnp.float32)
     last, part_other, pair_w_other = lax.optimization_barrier(
         (
             shifted((back2 + came[:row_count]).astype(jnp.bfloat16), "ctx", -2),
-            query_part_of(at, order, query_out, other_w),
-            pair_weights_of(at, order_t, other_w),
+            query_part_of(at, order, query_out, other_w, 1),
+            pair_weights_of(at, order, other_w, 1),
         )
     )
     pair_total = own_grad + came[row_count:] + last.astype(jnp.float32)

time: 160 us -> 150 us (0.938)
  starting transfers between devices: 47.8 us -> 44.2 us
  other arithmetic: 4.2 us -> 2.23 us
  waiting for transfers between devices: 30.1 us -> 28.3 us
    ppermute x7 -> x6, waiting for transfers between devices: 27.8 us -> 23.7 us  [hop(): return lax.ppermute(block, ALL, route(move))]
    ppermute x7 -> x6, starting transfers between devices: 22.9 us -> 19.8 us  [hop(): return lax.ppermute(block, ALL, route(move))]
    slice x2 -> x0, local copies, waits for them, and re-layouts: 2.26 us -> none  [local(): far_a, far_b = (along_x(right[:half], 1), along_x(left[half:], 3))]
    convert_element_type x1, other arithmetic: 2.13 us -> 0.16 us  [order_matrix(): return (source == wanted).astype(jnp.bfloat16)]
    ppermute x3, waiting for transfers between devices: 0.01 us -> 1.69 us  [swap_cores(): return lax.ppermute(block, ALL, route(lambda x, c, z, y: (x, 1 - c, z, y)))]
    unnamed x15 -> x11, local copies, waits for them, and re-layouts: 3 us -> 3.73 us
  transfers between devices with their start and end apart: 14 -> 13, of which waited for: 5 -> 7; matrix products, arithmetic and copies ran while one was open for 7% -> 4% of each run, Pallas kernels for 18% -> 17%
where the time goes in v7:
time: 150 us; the launch traced here: 149 us
  starting transfers between devices  44.2 us (29%)
  blocking collectives  35.2 us (23%)
  Pallas kernels  31.5 us (21%)
  waiting for transfers between devices  28.3 us (19%)
  local copies, waits for them, and re-layouts  3.96 us (3%)
  matrix products  3.36 us (2%)
  other arithmetic  2.23 us (1%)
    all_gather x1, blocking collectives, local(): lax.all_gather(w_qkv, 'ctx', axis=0, tiled=True, axis_index_groups=[[z *...  35.2 us
    ppermute x6, waiting for transfers between devices, hop(): return lax.ppermute(block, ALL, route(move))  23.7 us
    ppermute x6, starting transfers between devices, hop(): return lax.ppermute(block, ALL, route(move))  19.8 us
    ppermute x4, starting transfers between devices, shifted(): lax.ppermute(block, axis, [(i - distance, i) for i in devices if i - dist...  18.2 us
    pallas_call x2, Pallas kernels, query_part_of(): call(functools.partial(query_part_body, flip), [SCALARS, WHOLE, WHOLE, LE...  9.73 us
    pallas_call x2, Pallas kernels, pair_weights_of(): call(functools.partial(pair_weights_body, flip), [SCALARS, WHOLE, LEFT],...  8.03 us
    ppermute x3, starting transfers between devices, swap_cores(): return lax.ppermute(block, ALL, route(lambda x, c, z, y: (x, 1 - c, z, y)))  6.25 us
    unnamed x11, local copies, waits for them, and re-layouts  3.73 us
  transfers between devices with their start and end apart: 13, of which 7 were waited for; matrix products, arithmetic and copies ran while one was open for 4% of the time, Pallas kernels for 17%

profile of v7, /device:TPU:56, one launch (start us, length us, event | category | flops | bytes accessed | tf_op | source)
XLA Modules:
  0.0 149.3 jit_solution(10097070137123369392)
XLA Ops:
  0.0 35.2 %all_gather.3.own = bf16[128,1280]{1,0:T(8,128)(2,1)S(1)} all-gather(bf16[8,1280]{1,0:T(8,128)(2,1)} %param.7), channel_id=1, replica_groups={{0,4,8,12,16,20,24,28,32,36,40,44,48,52,56,60},{1,5,9,13,17,21,25,29,33..., dimensions={0}, use_global_device_ids=true | all-gather | bytes 348160 | tf_op jit(solution)/shard_map/all_gather | solution.py:363
  35.2 4.7 %collective-permute-start.2 = (bf16[128,1280]{1,0:T(8,128)(2,1)S(1)}, bf16[128,1280]{1,0:T(8,128)(2,1)S(1)}, u32[]{:S(2)}, u32[]{:S(2)}) collective-permute-start(bf16[128,1280]{1,0:T(8,128)(2,1)S(1)} %all_gather.3.own), channel_id=1, source_target_pairs={{0,384},{1,385},{2,386},{3,387},{4,388},{5,389},{6,390},{7,391},{8... | collective-permute-start | bytes 983048 | tf_op jit(solution)/shard_map/ppermute | solution.py:40
  39.9 2.7 %collective-permute-start.1 = (bf16[128,1280]{1,0:T(8,128)(2,1)S(1)}, bf16[128,1280]{1,0:T(8,128)(2,1)S(1)}, u32[]{:S(2)}, u32[]{:S(2)}) collective-permute-start(bf16[128,1280]{1,0:T(8,128)(2,1)S(1)} %all_gather.3.own), channel_id=1, source_target_pairs={{0,256},{1,257},{2,258},{3,259},{4,260},{5,261},{6,262},{7,263},{8... | collective-permute-start | bytes 983048 | tf_op jit(solution)/shard_map/ppermute | solution.py:40
  42.6 2.8 %collective-permute-start = (bf16[128,1280]{1,0:T(8,128)(2,1)S(1)}, bf16[128,1280]{1,0:T(8,128)(2,1)S(1)}, u32[]{:S(2)}, u32[]{:S(2)}) collective-permute-start(bf16[128,1280]{1,0:T(8,128)(2,1)S(1)} %all_gather.3.own), channel_id=1, source_target_pairs={{0,128},{1,129},{2,130},{3,131},{4,132},{5,133},{6,134},{7,135},{8... | collective-permute-start | bytes 983048 | tf_op jit(solution)/shard_map/ppermute | solution.py:40
  45.5 1.2 copy-done.1
  46.7 0.6 shard_map.47
  47.3 0.7 collective-permute-done.2.third
  48.0 2.5 %collective-permute-done.1.second = bf16[128,1280]{1,0:T(8,128)(2,1)S(1)} collective-permute-done((bf16[128,1280]{1,0:T(8,128)(2,1)S(1)}, bf16[128,1280]{1,0:T(8,128)(2,1)S(1)}, u32[]{:S(2)}, u32[]{:S(2)}) %collective-permute-start.1) | collective-permute-done | bytes 327712 | tf_op jit(solution)/shard_map/ppermute | solution.py:40
  50.5 3.4 %collective-permute-done.first = bf16[128,1280]{1,0:T(8,128)(2,1)S(1)} collective-permute-done((bf16[128,1280]{1,0:T(8,128)(2,1)S(1)}, bf16[128,1280]{1,0:T(8,128)(2,1)S(1)}, u32[]{:S(2)}, u32[]{:S(2)}) %collective-permute-start) | collective-permute-done | bytes 327712 | tf_op jit(solution)/shard_map/ppermute | solution.py:40
  54.0 2.7 %collective-permute-start.4 = (bf16[512,1280]{1,0:T(8,128)(2,1)S(1)}, bf16[512,1280]{1,0:T(8,128)(2,1)}, u32[]{:S(2)}, u32[]{:S(2)}) collective-permute-start(bf16[512,1280]{1,0:T(8,128)(2,1)S(1)} %shard_map.46.refs_0_), channel_id=1, source_target_pairs={{0,3},{1,0},{2,1},{3,2},{4,7},{5,4},{6,5},{7,6},{8,11},{9,8},{10,9... | collective-permute-start | bytes 3932168 | tf_op jit(solution)/shard_map/ppermute | solution.py:40
  56.6 2.8 %collective-permute-start.6 = (bf16[512,1280]{1,0:T(8,128)(2,1)S(1)}, bf16[512,1280]{1,0:T(8,128)(2,1)S(1)}, u32[]{:S(2)}, u32[]{:S(2)}) collective-permute-start(bf16[512,1280]{1,0:T(8,128)(2,1)S(1)} %shard_map.46.refs_0_), channel_id=1, source_target_pairs={{0,2},{1,3},{2,0},{3,1},{4,6},{5,7},{6,4},{7,5},{8,10},{9,11},{10,... | collective-permute-start | bytes 3932168 | tf_op jit(solution)/shard_map/ppermute | solution.py:40
  59.5 4.1 %collective-permute-start.5 = (bf16[512,1280]{1,0:T(8,128)(2,1)S(1)}, bf16[512,1280]{1,0:T(8,128)(2,1)}, u32[]{:S(2)}, u32[]{:S(2)}) collective-permute-start(bf16[512,1280]{1,0:T(8,128)(2,1)S(1)} %shard_map.46.refs_0_), channel_id=1, source_target_pairs={{0,1},{1,2},{2,3},{3,0},{4,5},{5,6},{6,7},{7,4},{8,9},{9,10},{10,1... | collective-permute-start | bytes 3932168 | tf_op jit(solution)/shard_map/ppermute | solution.py:40
  63.6 1.1 copy.8
  64.7 1.9 %collective-permute-start.3 = (bf16[128,2048]{1,0:T(8,128)(2,1)S(1)}, bf16[128,2048]{1,0:T(8,128)(2,1)S(1)}, u32[]{:S(2)}, u32[]{:S(2)}) collective-permute-start(bf16[128,2048]{1,0:T(8,128)(2,1)S(1)} %shard_map.47), channel_id=1, source_target_pairs={{0,64},{1,65},{2,66},{3,67},{4,68},{5,69},{6,70},{7,71},{8,72},{9,... | collective-permute-start | bytes 1572872 | tf_op jit(solution)/shard_map/ppermute | solution.py:44
  66.7 0.2 fusion.21.order
  66.9 1.7 %collective-permute-done.3.theirs = bf16[128,2048]{1,0:T(8,128)(2,1)S(1)} collective-permute-done((bf16[128,2048]{1,0:T(8,128)(2,1)S(1)}, bf16[128,2048]{1,0:T(8,128)(2,1)S(1)}, u32[]{:S(2)}, u32[]{:S(2)}) %collective-permute-start.3) | collective-permute-done | bytes 524320 | tf_op jit(solution)/shard_map/ppermute | solution.py:44
  68.5 1.2 copy-done.2
  69.8 1.9 %shard_map.48.arranged = bf16[1024,512]{1,0:T(8,128)(2,1)S(1)} custom-call(s32[3]{0:T(128)S(1)} %pad_add_fusion.at, bf16[512,512]{1,0:T(8,128)(2,1)S(1)} %fusion.21.order, bf16[128,4096]{1,0:T(8,128)(2,1)S(1)} %bitcast.62, bf16[128,2048]{1,0:T(8,128)(2,1)S(1)} %collective-permute-done.3.theirs), custom_call_target="tpu_custom_call" | custom-call | flops 536870912 | bytes 4194304 | tf_op jit(solution)/shard_map/pallas_call | solution.py:103
  71.7 17.1 %collective-permute-done.4.refs_1_ = bf16[512,1280]{1,0:T(8,128)(2,1)} collective-permute-done((bf16[512,1280]{1,0:T(8,128)(2,1)S(1)}, bf16[512,1280]{1,0:T(8,128)(2,1)}, u32[]{:S(2)}, u32[]{:S(2)}) %collective-permute-start.4) | collective-permute-done | bytes 1310752 | tf_op jit(solution)/shard_map/ppermute | solution.py:40
  88.8 2.8 %shard_map.49 = (f32[128,1280]{1,0:T(8,128)S(1)}, f32[128,1280]{1,0:T(8,128)S(1)}, bf16[2048,1280]{1,0:T(8,128)(2,1)}) custom-call(bf16[1024,512]{1,0:T(8,128)(2,1)S(1)} %shard_map.48.arranged, bf16[512,1280]{1,0:T(8,128)(2,1)S(1)} %shard_map.46.refs_0_, bf16[512,1280]{1,0:T(8,128)(2,1)} %collective-permute-done.4.refs_1_), custom_call_target="tpu_custom_call" | custom-call | flops 671088640 | bytes 4194304 | tf_op jit(solution)/shard_map/pallas_call | solution.py:169
  91.7 2.2 %shard_map.50 = (f32[128,1280]{1,0:T(8,128)S(1)}, f32[128,1280]{1,0:T(8,128)S(1)}) custom-call(bf16[1024,512]{1,0:T(8,128)(2,1)S(1)} %shard_map.48.arranged, f32[128,1280]{1,0:T(8,128)S(1)} %get-tuple-element.23.mine, f32[128,1280]{1,0:T(8,128)S(1)} %get-tuple-element.24.theirs, bf16[512,1280]{1,0:T(8,128)(2,1)} %collective-permute-done.5.refs_0_.first, ...), custom_call_target="tpu_custom_call" | custom-call | flops 671088640 | bytes 4194304 | tf_op jit(solution)/shard_map/pallas_call | solution.py:197
  93.9 1.9 %collective-permute-start.7 = (f32[128,1280]{1,0:T(8,128)S(1)}, f32[128,1280]{1,0:T(8,128)S(1)}, u32[]{:S(2)}, u32[]{:S(2)}) collective-permute-start(f32[128,1280]{1,0:T(8,128)S(1)} %get-tuple-element.26.after), channel_id=1, source_target_pairs={{0,64},{1,65},{2,66},{3,67},{4,68},{5,69},{6,70},{7,71},{8,72},{9,... | collective-permute-start | bytes 1966088 | tf_op jit(solution)/shard_map/ppermute | solution.py:44
  95.8 2.8 %shard_map.51.all_rows = bf16[2048,1280]{1,0:T(8,128)(2,1)} custom-call(bf16[512,1280]{1,0:T(8,128)(2,1)} %collective-permute-done.5.refs_0_.first, bf16[512,1280]{1,0:T(8,128)(2,1)S(1)} %collective-permute-done.6.refs_1_.second, f32[128,1280]{1,0:T(8,128)S(1)} %get-tuple-element.26.after, ...), custom_call_target="tpu_custom_call", output_to_operand_aliasing={{}: (3, {})} | custom-call | bytes 4194304 | tf_op jit(solution)/shard_map/pallas_call | solution.py:216
  98.6 2.4 %collective-permute-start.12 = (bf16[2048,1280]{1,0:T(8,128)(2,1)}, bf16[2048,1280]{1,0:T(8,128)(2,1)}, u32[]{:S(2)}, u32[]{:S(2)}) collective-permute-start(bf16[2048,1280]{1,0:T(8,128)(2,1)} %shard_map.51.all_rows), channel_id=1, source_target_pairs={{0,64},{1,65},{2,66},{3,67},{4,68},{5,69},{6,70},{7,71},{8,72},{9,... | collective-permute-start | bytes 15728648 | tf_op jit(solution)/shard_map/ppermute | solution.py:44
  101.5 0.3 fusion.37
  101.9 3.9 %collective-permute-start.8 = (bf16[128,256]{1,0:T(8,128)(2,1)S(1)}, bf16[128,256]{1,0:T(8,128)(2,1)S(1)}, u32[]{:S(2)}, u32[]{:S(2)}) collective-permute-start(bf16[128,256]{1,0:T(8,128)(2,1)S(1)} %pad_maximum_fusion.5), channel_id=1, source_target_pairs={{0,2},{1,3},{2,4},{3,5},{4,6},{5,7},{6,8},{7,9},{8,10},{9,11},{10,... | collective-permute-start | bytes 196616 | tf_op jit(solution)/shard_map/ppermute | solution.py:334
  105.8 0.2 fusion.57
  106.0 4.0 %shard_map.52.own_w = bf16[2048,256]{1,0:T(8,128)(2,1)} custom-call(s32[3]{0:T(128)S(1)} %pad_add_fusion.at, bf16[512,512]{1,0:T(8,128)(2,1)} %copy-done, bf16[2048,1280]{1,0:T(8,128)(2,1)} %shard_map.51.all_rows), custom_call_target="tpu_custom_call" | custom-call | flops 536870912 | bytes 3145728 | tf_op jit(solution)/shard_map/pallas_call | solution.py:298
  110.1 5.7 %collective-permute-start.9 = (bf16[256,256]{1,0:T(8,128)(2,1)S(1)}, bf16[256,256]{1,0:T(8,128)(2,1)S(1)}, u32[]{:S(2)}, u32[]{:S(2)}) collective-permute-start(bf16[256,256]{1,0:T(8,128)(2,1)S(1)} %pad_maximum_fusion.3), channel_id=1, source_target_pairs={{0,1},{1,2},{2,3},{3,4},{4,5},{5,6},{6,7},{7,8},{8,9},{9,10},{10,1... | collective-permute-start | bytes 393224 | tf_op jit(solution)/shard_map/ppermute | solution.py:334
  115.8 0.2 subtract_convert_fusion.1
  116.0 2.3 %collective-permute-done.9 = bf16[256,256]{1,0:T(8,128)(2,1)S(1)} collective-permute-done((bf16[256,256]{1,0:T(8,128)(2,1)S(1)}, bf16[256,256]{1,0:T(8,128)(2,1)S(1)}, u32[]{:S(2)}, u32[]{:S(2)}) %collective-permute-start.9) | collective-permute-done | bytes 131104 | tf_op jit(solution)/shard_map/ppermute | solution.py:334
  118.3 1.0 fusion.60
  119.4 0.2 fusion.23
  119.6 0.4 convolution_bitcast_fusion
  120.0 0.4 fusion.7
  120.4 0.4 fusion.2
  120.8 0.5 fusion.8
  121.4 3.0 %collective-permute-start.10 = (bf16[256,256]{1,0:T(8,128)(2,1)S(1)}, bf16[256,256]{1,0:T(8,128)(2,1)S(1)}, u32[]{:S(2)}, u32[]{:S(2)}) collective-permute-start(bf16[256,256]{1,0:T(8,128)(2,1)S(1)} %pad_maximum_fusion.4), channel_id=1, source_target_pairs={{1,0},{2,1},{3,2},{4,3},{5,4},{6,5},{7,6},{8,7},{9,8},{10,9},{11,1... | collective-permute-start | bytes 393224 | tf_op jit(solution)/shard_map/ppermute | solution.py:334
  124.4 0.6 fusion.4
  125.0 0.3 subtract_convert_fusion
  125.2 0.1 copy_bitcast_fusion.grads
  125.4 4.9 %shard_map.53.own_part = f32[128,2048]{1,0:T(8,128)S(1)} custom-call(s32[3]{0:T(128)S(1)} %pad_add_fusion.at, bf16[512,512]{1,0:T(8,128)(2,1)} %copy-done, bf16[128,1024]{1,0:T(8,128)(2,1)S(1)} %copy_bitcast_fusion.grads, bf16[2048,1280]{1,0:T(8,128)(2,1)} %shard_map.51.all_rows), custom_call_target="tpu_custom_call" | custom-call | flops 1073741824 | bytes 6291456 | tf_op jit(solution)/shard_map/pallas_call | solution.py:265
  130.2 0.6 collective-permute-done.10
  130.9 5.7 %collective-permute-start.11 = (bf16[128,256]{1,0:T(8,128)(2,1)S(1)}, bf16[128,256]{1,0:T(8,128)(2,1)S(1)}, u32[]{:S(2)}, u32[]{:S(2)}) collective-permute-start(bf16[128,256]{1,0:T(8,128)(2,1)S(1)} %fusion.32), channel_id=1, source_target_pairs={{2,0},{3,1},{4,2},{5,3},{6,4},{7,5},{8,6},{9,7},{10,8},{11,9},{12,... | collective-permute-start | bytes 196616 | tf_op jit(solution)/shard_map/ppermute | solution.py:334
  136.6 4.9 %shard_map.54.other_part = f32[128,2048]{1,0:T(8,128)S(1)} custom-call(s32[3]{0:T(128)S(1)} %pad_add_fusion.at, bf16[512,512]{1,0:T(8,128)(2,1)} %copy-done, bf16[128,1024]{1,0:T(8,128)(2,1)S(1)} %copy_bitcast_fusion.grads, bf16[2048,1280]{1,0:T(8,128)(2,1)} %collective-permute-done.12.all_rows), custom_call_target="tpu_custom_call" | custom-call | flops 1073741824 | bytes 6291456 | tf_op jit(solution)/shard_map/pallas_call | solution.py:265
  141.4 4.0 %shard_map.55.other_w = bf16[2048,256]{1,0:T(8,128)(2,1)} custom-call(s32[3]{0:T(128)S(1)} %pad_add_fusion.at, bf16[512,512]{1,0:T(8,128)(2,1)} %copy-done, bf16[2048,1280]{1,0:T(8,128)(2,1)} %collective-permute-done.12.all_rows), custom_call_target="tpu_custom_call" | custom-call | flops 536870912 | bytes 3145728 | tf_op jit(solution)/shard_map/pallas_call | solution.py:298
  145.5 0.3 fusion.46
  146.0 3.3 %shard_map.56 = bf16[128,4096]{1,0:T(8,128)(2,1)} custom-call(s32[3]{0:T(128)S(1)} %pad_add_fusion.at, bf16[128,256]{1,0:T(8,128)(2,1)S(1)} %pad_maximum_fusion.6.pair_out, f32[128,2048]{1,0:T(8,128)S(1)} %shard_map.53.own_part, f32[128,2048]{1,0:T(8,128)S(1)} %shard_map.54.other_part, bf16[2048,256]{1,0:T(8,128)(2,1)} %shard_map.52.own_w, ...), custom_call_target="tpu_custom_call" | custom-call | tf_op jit(solution)/shard_map/pallas_call | solution.py:324
  (38 shorter events, 0.9 us)
Async XLA Ops:
  35.2 12.8 %collective-permute-start.2 = (bf16[128,1280]{1,0:T(8,128)(2,1)S(1)}, bf16[128,1280]{1,0:T(8,128)(2,1)S(1)}, u32[]{:S(2)}, u32[]{:S(2)}) collective-permute-start(bf16[128,1280]{1,0:T(8,128)(2,1)S(1)} %all_gather.3.own), channel_id=1, source_target_pairs={{0,384},{1,385},{2,386},{3,387},{4,388},{5,389},{6,390},{7,391},{8... | collective-permute-start | bytes 983048 | tf_op jit(solution)/shard_map/ppermute | solution.py:40
  39.9 10.6 %collective-permute-start.1 = (bf16[128,1280]{1,0:T(8,128)(2,1)S(1)}, bf16[128,1280]{1,0:T(8,128)(2,1)S(1)}, u32[]{:S(2)}, u32[]{:S(2)}) collective-permute-start(bf16[128,1280]{1,0:T(8,128)(2,1)S(1)} %all_gather.3.own), channel_id=1, source_target_pairs={{0,256},{1,257},{2,258},{3,259},{4,260},{5,261},{6,262},{7,263},{8... | collective-permute-start | bytes 983048 | tf_op jit(solution)/shard_map/ppermute | solution.py:40
  42.6 11.3 %collective-permute-start = (bf16[128,1280]{1,0:T(8,128)(2,1)S(1)}, bf16[128,1280]{1,0:T(8,128)(2,1)S(1)}, u32[]{:S(2)}, u32[]{:S(2)}) collective-permute-start(bf16[128,1280]{1,0:T(8,128)(2,1)S(1)} %all_gather.3.own), channel_id=1, source_target_pairs={{0,128},{1,129},{2,130},{3,131},{4,132},{5,133},{6,134},{7,135},{8... | collective-permute-start | bytes 983048 | tf_op jit(solution)/shard_map/ppermute | solution.py:40
  45.5 1.2 copy-start.1
  54.0 34.9 %collective-permute-start.4 = (bf16[512,1280]{1,0:T(8,128)(2,1)S(1)}, bf16[512,1280]{1,0:T(8,128)(2,1)}, u32[]{:S(2)}, u32[]{:S(2)}) collective-permute-start(bf16[512,1280]{1,0:T(8,128)(2,1)S(1)} %shard_map.46.refs_0_), channel_id=1, source_target_pairs={{0,3},{1,0},{2,1},{3,2},{4,7},{5,4},{6,5},{7,6},{8,11},{9,8},{10,9... | collective-permute-start | bytes 3932168 | tf_op jit(solution)/shard_map/ppermute | solution.py:40
  56.6 35.1 %collective-permute-start.6 = (bf16[512,1280]{1,0:T(8,128)(2,1)S(1)}, bf16[512,1280]{1,0:T(8,128)(2,1)S(1)}, u32[]{:S(2)}, u32[]{:S(2)}) collective-permute-start(bf16[512,1280]{1,0:T(8,128)(2,1)S(1)} %shard_map.46.refs_0_), channel_id=1, source_target_pairs={{0,2},{1,3},{2,0},{3,1},{4,6},{5,7},{6,4},{7,5},{8,10},{9,11},{10,... | collective-permute-start | bytes 3932168 | tf_op jit(solution)/shard_map/ppermute | solution.py:40
  59.5 32.2 %collective-permute-start.5 = (bf16[512,1280]{1,0:T(8,128)(2,1)S(1)}, bf16[512,1280]{1,0:T(8,128)(2,1)}, u32[]{:S(2)}, u32[]{:S(2)}) collective-permute-start(bf16[512,1280]{1,0:T(8,128)(2,1)S(1)} %shard_map.46.refs_0_), channel_id=1, source_target_pairs={{0,1},{1,2},{2,3},{3,0},{4,5},{5,6},{6,7},{7,4},{8,9},{9,10},{10,1... | collective-permute-start | bytes 3932168 | tf_op jit(solution)/shard_map/ppermute | solution.py:40
  64.7 3.8 %collective-permute-start.3 = (bf16[128,2048]{1,0:T(8,128)(2,1)S(1)}, bf16[128,2048]{1,0:T(8,128)(2,1)S(1)}, u32[]{:S(2)}, u32[]{:S(2)}) collective-permute-start(bf16[128,2048]{1,0:T(8,128)(2,1)S(1)} %shard_map.47), channel_id=1, source_target_pairs={{0,64},{1,65},{2,66},{3,67},{4,68},{5,69},{6,70},{7,71},{8,72},{9,... | collective-permute-start | bytes 1572872 | tf_op jit(solution)/shard_map/ppermute | solution.py:44
  66.8 24.8 %copy-start = (bf16[512,512]{1,0:T(8,128)(2,1)}, bf16[512,512]{1,0:T(8,128)(2,1)S(1)}, u32[]{:S(2)}) copy-start(bf16[512,512]{1,0:T(8,128)(2,1)S(1)} %fusion.21.order) | copy-start | bytes 1572868
  68.5 1.2 copy-start.2
  93.9 7.4 %collective-permute-start.7 = (f32[128,1280]{1,0:T(8,128)S(1)}, f32[128,1280]{1,0:T(8,128)S(1)}, u32[]{:S(2)}, u32[]{:S(2)}) collective-permute-start(f32[128,1280]{1,0:T(8,128)S(1)} %get-tuple-element.26.after), channel_id=1, source_target_pairs={{0,64},{1,65},{2,66},{3,67},{4,68},{5,69},{6,70},{7,71},{8,72},{9,... | collective-permute-start | bytes 1966088 | tf_op jit(solution)/shard_map/ppermute | solution.py:44
  95.8 5.3 %copy-start.3 = (s32[1,128]{1,0:T(1,128)S(1)}, s32[1,128]{1,0:T(1,128)}, u32[]{:S(2)}) copy-start(s32[1,128]{1,0:T(1,128)} %param.5) | copy-start | bytes 1540
  98.6 37.9 %collective-permute-start.12 = (bf16[2048,1280]{1,0:T(8,128)(2,1)}, bf16[2048,1280]{1,0:T(8,128)(2,1)}, u32[]{:S(2)}, u32[]{:S(2)}) collective-permute-start(bf16[2048,1280]{1,0:T(8,128)(2,1)} %shard_map.51.all_rows), channel_id=1, source_target_pairs={{0,64},{1,65},{2,66},{3,67},{4,68},{5,69},{6,70},{7,71},{8,72},{9,... | collective-permute-start | bytes 15728648 | tf_op jit(solution)/shard_map/ppermute | solution.py:44
  101.9 8.1 %collective-permute-start.8 = (bf16[128,256]{1,0:T(8,128)(2,1)S(1)}, bf16[128,256]{1,0:T(8,128)(2,1)S(1)}, u32[]{:S(2)}, u32[]{:S(2)}) collective-permute-start(bf16[128,256]{1,0:T(8,128)(2,1)S(1)} %pad_maximum_fusion.5), channel_id=1, source_target_pairs={{0,2},{1,3},{2,4},{3,5},{4,6},{5,7},{6,8},{7,9},{8,10},{9,11},{10,... | collective-permute-start | bytes 196616 | tf_op jit(solution)/shard_map/ppermute | solution.py:334
  110.1 8.2 %collective-permute-start.9 = (bf16[256,256]{1,0:T(8,128)(2,1)S(1)}, bf16[256,256]{1,0:T(8,128)(2,1)S(1)}, u32[]{:S(2)}, u32[]{:S(2)}) collective-permute-start(bf16[256,256]{1,0:T(8,128)(2,1)S(1)} %pad_maximum_fusion.3), channel_id=1, source_target_pairs={{0,1},{1,2},{2,3},{3,4},{4,5},{5,6},{6,7},{7,8},{8,9},{9,10},{10,1... | collective-permute-start | bytes 393224 | tf_op jit(solution)/shard_map/ppermute | solution.py:334
  121.4 9.4 %collective-permute-start.10 = (bf16[256,256]{1,0:T(8,128)(2,1)S(1)}, bf16[256,256]{1,0:T(8,128)(2,1)S(1)}, u32[]{:S(2)}, u32[]{:S(2)}) collective-permute-start(bf16[256,256]{1,0:T(8,128)(2,1)S(1)} %pad_maximum_fusion.4), channel_id=1, source_target_pairs={{1,0},{2,1},{3,2},{4,3},{5,4},{6,5},{7,6},{8,7},{9,8},{10,9},{11,1... | collective-permute-start | bytes 393224 | tf_op jit(solution)/shard_map/ppermute | solution.py:334
  130.9 14.6 %collective-permute-start.11 = (bf16[128,256]{1,0:T(8,128)(2,1)S(1)}, bf16[128,256]{1,0:T(8,128)(2,1)S(1)}, u32[]{:S(2)}, u32[]{:S(2)}) collective-permute-start(bf16[128,256]{1,0:T(8,128)(2,1)S(1)} %fusion.32), channel_id=1, source_target_pairs={{2,0},{3,1},{4,2},{5,3},{6,4},{7,5},{8,6},{9,7},{10,8},{11,9},{12,... | collective-permute-start | bytes 196616 | tf_op jit(solution)/shard_map/ppermute | solution.py:334

commit v8 on v7

--- a/solution.py
+++ b/solution.py
@@ -233,7 +233,7 @@
         yield s, jnp.where(parity == 0, turned, pieces[s])
 
 
-def query_part_body(flip, at, order, grads, all_rows, out_ref, weights, held, sems):
+def query_part_body(flip, at, grads, all_rows, out_ref, weights, held, sems):
     parity = at[2] if flip == 0 else 1 - at[2]
     rows = grads.shape[0]
     loads = []
@@ -241,6 +241,7 @@
         source = all_rows.at[pl.ds(e * BLOCK, BLOCK), pl.ds(0, HQ * HD)]
         loads.append(pltpu.make_async_copy(source, weights.at[e], sems.at[e]))
         loads[-1].start()
+    order = order_matrix(at[1])
     for e in range(NX):
         loads[e].wait()
         held[e] = lax.dot_general(
@@ -254,17 +255,17 @@
         high = part.astype(jnp.bfloat16)
         low = (part - high.astype(jnp.float32)).astype(jnp.bfloat16)
         back = lax.dot_general(
-            jnp.concatenate([high, low], axis=0), order[...], TURN,
+            jnp.concatenate([high, low], axis=0), order, TURN,
             preferred_element_type=jnp.float32,
         )
         out_ref[:, pl.ds(x_block(at[0], s), BLOCK)] = back[:rows] + back[rows:]
 
 
-def query_part_of(at, order, grads, all_rows, flip):
+def query_part_of(at, grads, all_rows, flip):
     rows = grads.shape[0]
     return call(
         functools.partial(query_part_body, flip),
-        [SCALARS, WHOLE, WHOLE, LEFT],
+        [SCALARS, WHOLE, LEFT],
         pltpu.VMEM((rows, NX * BLOCK), jnp.float32),
         NX * 2 * rows * BLOCK * (HQ * HD + 2 * BLOCK), 6,
         scratch_shapes=[
@@ -272,39 +273,35 @@
             pltpu.VMEM((NX, rows, BLOCK), jnp.float32),
             pltpu.SemaphoreType.DMA((NX,)),
         ],
-    )(at, in_hbm(order), grads, all_rows)
-
-
-def pair_weights_body(flip, at, order, all_rows, out_ref, weights, sems):
-    parity = at[2] if flip == 0 else 1 - at[2]
-    loads = []
-    for e in range(NX):
-        source = all_rows.at[pl.ds(e * BLOCK, BLOCK), pl.ds(HQ * HD, 2 * HD)]
-        loads.append(pltpu.make_async_copy(source, weights.at[e], sems.at[e]))
-        loads[-1].start()
-    for load in loads:
-        load.wait()
+    )(at, grads, all_rows)
+
+
+def pair_weights_body(at, all_rows, out_ref, weights, sem):
+    load = pltpu.make_async_copy(all_rows.at[:, pl.ds(HQ * HD, 2 * HD)], weights, sem)
+    load.start()
+    order = order_matrix(at[1])
+    load.wait()
     for s, part in by_source(
-        [weights[e] for e in range(NX)], parity,
+        [weights[e * BLOCK : (e + 1) * BLOCK, :] for e in range(NX)], at[2],
         lambda piece, d: piece[d * SPAN : (d + 1) * SPAN],
         lambda parts: jnp.concatenate(parts, axis=0),
     ):
         out_ref[pl.ds(x_block(at[0], s), BLOCK), :] = jnp.dot(
-            order[...], part, preferred_element_type=jnp.float32
+            order, part, preferred_element_type=jnp.float32
         ).astype(jnp.bfloat16)
 
 
-def pair_weights_of(at, order, all_rows, flip):
-    return call(
-        functools.partial(pair_weights_body, flip),
-        [SCALARS, WHOLE, LEFT],
+def pair_weights_of(at, all_rows):
+    return call(
+        pair_weights_body,
+        [SCALARS, LEFT],
         pltpu.HBM((NX * BLOCK, 2 * HD), jnp.bfloat16),
         NX * 2 * BLOCK * BLOCK * 2 * HD, 3,
         scratch_shapes=[
-            pltpu.VMEM((NX, BLOCK, 2 * HD), jnp.bfloat16),
-            pltpu.SemaphoreType.DMA((NX,)),
+            pltpu.VMEM((NX * BLOCK, 2 * HD), jnp.bfloat16),
+            pltpu.SemaphoreType.DMA,
         ],
-    )(at, in_hbm(order), all_rows)
+    )(at, all_rows)
 
 
 def finish_body(at, pair_out, own_part, other_part, own_w, other_w, out_ref):
@@ -326,7 +323,7 @@
         in_specs=[pl.BlockSpec(memory_space=pltpu.SMEM)] + [whole] * 5,
         out_shape=jax.ShapeDtypeStruct((pair_out.shape[0], NX * NC * BLOCK), jnp.bfloat16),
         compiler_params=pltpu.CompilerParams(vmem_limit_bytes=VMEM_LIMIT),
-    )(at, pair_out, *[in_vmem(p) for p in parts], *[in_hbm(w) for w in weights])
+    )(at, pair_out, *[in_vmem(p) for p in parts], in_vmem(weights[0]), weights[1])
 
 
 def shifted(block, axis, distance):
@@ -377,7 +374,6 @@
     mine, theirs = late_sums(arranged, sums, [one, two], (1, 2))
     own_w = place_rows([one, two], theirs, own_w, (1, 2))
     projected = mine + swap_cores(theirs)
-    other_w = swap_cores(own_w)
     pair_pre, query_pre = projected[:, HQ * HD :], projected[:, : HQ * HD]
 
     first_row = ctx * row_count
@@ -386,11 +382,12 @@
     pair_rows = jnp.concatenate(
         [rotate(pair_pre[:, :HD], cos_part, sin_part), pair_pre[:, HD:]], axis=1
     ).astype(jnp.bfloat16)
-    projected_at, pair_rows = lax.optimization_barrier((at, pair_rows))
+    later_at, pair_rows = lax.optimization_barrier((at, pair_rows))
     back2, pair_w_own = lax.optimization_barrier(
-        (shifted(pair_rows, "ctx", 2), pair_weights_of(projected_at, order, own_w, 0))
+        (shifted(pair_rows, "ctx", 2), pair_weights_of(later_at, own_w))
     )
     back31 = shifted(jnp.concatenate([back2, pair_rows], axis=0), "ctx", 1)
+    other_w = swap_cores(own_w)
     window = jnp.concatenate([back31[:row_count], back2, back31[row_count:], pair_rows], axis=0)
 
     queries = rotate(
@@ -437,15 +434,15 @@
     came, part_own = lax.optimization_barrier(
         (
             shifted(jnp.concatenate([back3, back1], axis=0).astype(jnp.bfloat16), "ctx", -1),
-            query_part_of(at, order, query_out, own_w, 0),
+            query_part_of(at, query_out, own_w, 0),
         )
     )
     came = came.astype(jnp.float32)
     last, part_other, pair_w_other = lax.optimization_barrier(
         (
             shifted((back2 + came[:row_count]).astype(jnp.bfloat16), "ctx", -2),
-            query_part_of(at, order, query_out, other_w, 1),
-            pair_weights_of(at, order, other_w, 1),
+            query_part_of(at, query_out, other_w, 1),
+            swap_cores(pair_w_own),
         )
     )
     pair_total = own_grad + came[row_count:] + last.astype(jnp.float32)

time: 150 us -> 149 us (level)
  the two profiles are of different devices: /device:TPU:56 before, /device:TPU:24 now
where the time goes in v8:
time: 149 us; the launch traced here: 147 us
  starting transfers between devices  38.5 us (26%)
  blocking collectives  37.4 us (25%)
  waiting for transfers between devices  32.4 us (22%)
  Pallas kernels  25.1 us (17%)
  local copies, waits for them, and re-layouts  4.93 us (3%)
  matrix products  4.35 us (3%)
  other arithmetic  4.26 us (3%)
    all_gather x1, blocking collectives, local(): lax.all_gather(w_qkv, 'ctx', axis=0, tiled=True, axis_index_groups=[[z *...  37.4 us
    ppermute x6, waiting for transfers between devices, hop(): return lax.ppermute(block, ALL, route(move))  24.2 us
    ppermute x6, starting transfers between devices, hop(): return lax.ppermute(block, ALL, route(move))  19.8 us
    ppermute x4, starting transfers between devices, shifted(): lax.ppermute(block, axis, [(i - distance, i) for i in devices if i - dist...  10.6 us
    pallas_call x2, Pallas kernels, query_part_of(): call(functools.partial(query_part_body, flip), [SCALARS, WHOLE, LEFT], pl...  8.75 us
    ppermute x4, starting transfers between devices, swap_cores(): return lax.ppermute(block, ALL, route(lambda x, c, z, y: (x, 1 - c, z, y)))  8.16 us
    ppermute x4, waiting for transfers between devices, shifted(): lax.ppermute(block, axis, [(i - distance, i) for i in devices if i - dist...  6.45 us
    unnamed x19, local copies, waits for them, and re-layouts  4.7 us
  transfers between devices with their start and end apart: 14, of which 8 were waited for; matrix products, arithmetic and copies ran while one was open for 6% of the time, Pallas kernels for 14%

profile of v8, /device:TPU:24, one launch (start us, length us, event | category | flops | bytes accessed | tf_op | source)
XLA Modules:
  0.0 147.5 jit_solution(17023336100806408675)
XLA Ops:
  0.0 37.4 %all_gather.3.own = bf16[128,1280]{1,0:T(8,128)(2,1)S(1)} all-gather(bf16[8,1280]{1,0:T(8,128)(2,1)} %param.7), channel_id=1, replica_groups={{0,4,8,12,16,20,24,28,32,36,40,44,48,52,56,60},{1,5,9,13,17,21,25,29,33..., dimensions={0}, use_global_device_ids=true | all-gather | bytes 348160 | tf_op jit(solution)/shard_map/all_gather | solution.py:360
  37.4 4.7 %collective-permute-start.2 = (bf16[128,1280]{1,0:T(8,128)(2,1)S(1)}, bf16[128,1280]{1,0:T(8,128)(2,1)S(1)}, u32[]{:S(2)}, u32[]{:S(2)}) collective-permute-start(bf16[128,1280]{1,0:T(8,128)(2,1)S(1)} %all_gather.3.own), channel_id=1, source_target_pairs={{0,384},{1,385},{2,386},{3,387},{4,388},{5,389},{6,390},{7,391},{8... | collective-permute-start | bytes 983048 | tf_op jit(solution)/shard_map/ppermute | solution.py:40
  42.1 2.7 %collective-permute-start.1 = (bf16[128,1280]{1,0:T(8,128)(2,1)S(1)}, bf16[128,1280]{1,0:T(8,128)(2,1)S(1)}, u32[]{:S(2)}, u32[]{:S(2)}) collective-permute-start(bf16[128,1280]{1,0:T(8,128)(2,1)S(1)} %all_gather.3.own), channel_id=1, source_target_pairs={{0,256},{1,257},{2,258},{3,259},{4,260},{5,261},{6,262},{7,263},{8... | collective-permute-start | bytes 983048 | tf_op jit(solution)/shard_map/ppermute | solution.py:40
  44.8 2.8 %collective-permute-start = (bf16[128,1280]{1,0:T(8,128)(2,1)S(1)}, bf16[128,1280]{1,0:T(8,128)(2,1)S(1)}, u32[]{:S(2)}, u32[]{:S(2)}) collective-permute-start(bf16[128,1280]{1,0:T(8,128)(2,1)S(1)} %all_gather.3.own), channel_id=1, source_target_pairs={{0,128},{1,129},{2,130},{3,131},{4,132},{5,133},{6,134},{7,135},{8... | collective-permute-start | bytes 983048 | tf_op jit(solution)/shard_map/ppermute | solution.py:40
  47.7 1.2 copy-done
  49.0 0.6 shard_map.47
  49.6 3.0 %collective-permute-done.1.second = bf16[128,1280]{1,0:T(8,128)(2,1)S(1)} collective-permute-done((bf16[128,1280]{1,0:T(8,128)(2,1)S(1)}, bf16[128,1280]{1,0:T(8,128)(2,1)S(1)}, u32[]{:S(2)}, u32[]{:S(2)}) %collective-permute-start.1) | collective-permute-done | bytes 327712 | tf_op jit(solution)/shard_map/ppermute | solution.py:40
  52.7 3.6 %collective-permute-done.first = bf16[128,1280]{1,0:T(8,128)(2,1)S(1)} collective-permute-done((bf16[128,1280]{1,0:T(8,128)(2,1)S(1)}, bf16[128,1280]{1,0:T(8,128)(2,1)S(1)}, u32[]{:S(2)}, u32[]{:S(2)}) %collective-permute-start) | collective-permute-done | bytes 327712 | tf_op jit(solution)/shard_map/ppermute | solution.py:40
  56.4 2.8 %collective-permute-start.4 = (bf16[512,1280]{1,0:T(8,128)(2,1)S(1)}, bf16[512,1280]{1,0:T(8,128)(2,1)}, u32[]{:S(2)}, u32[]{:S(2)}) collective-permute-start(bf16[512,1280]{1,0:T(8,128)(2,1)S(1)} %shard_map.46.refs_0_), channel_id=1, source_target_pairs={{0,3},{1,0},{2,1},{3,2},{4,7},{5,4},{6,5},{7,6},{8,11},{9,8},{10,9... | collective-permute-start | bytes 3932168 | tf_op jit(solution)/shard_map/ppermute | solution.py:40
  59.2 2.5 %collective-permute-start.6 = (bf16[512,1280]{1,0:T(8,128)(2,1)S(1)}, bf16[512,1280]{1,0:T(8,128)(2,1)S(1)}, u32[]{:S(2)}, u32[]{:S(2)}) collective-permute-start(bf16[512,1280]{1,0:T(8,128)(2,1)S(1)} %shard_map.46.refs_0_), channel_id=1, source_target_pairs={{0,2},{1,3},{2,0},{3,1},{4,6},{5,7},{6,4},{7,5},{8,10},{9,11},{10,... | collective-permute-start | bytes 3932168 | tf_op jit(solution)/shard_map/ppermute | solution.py:40
  61.7 4.3 %collective-permute-start.5 = (bf16[512,1280]{1,0:T(8,128)(2,1)S(1)}, bf16[512,1280]{1,0:T(8,128)(2,1)}, u32[]{:S(2)}, u32[]{:S(2)}) collective-permute-start(bf16[512,1280]{1,0:T(8,128)(2,1)S(1)} %shard_map.46.refs_0_), channel_id=1, source_target_pairs={{0,1},{1,2},{2,3},{3,0},{4,5},{5,6},{6,7},{7,4},{8,9},{9,10},{10,1... | collective-permute-start | bytes 3932168 | tf_op jit(solution)/shard_map/ppermute | solution.py:40
  66.1 0.8 copy.8
  66.9 1.9 %collective-permute-start.3 = (bf16[128,2048]{1,0:T(8,128)(2,1)S(1)}, bf16[128,2048]{1,0:T(8,128)(2,1)S(1)}, u32[]{:S(2)}, u32[]{:S(2)}) collective-permute-start(bf16[128,2048]{1,0:T(8,128)(2,1)S(1)} %shard_map.47), channel_id=1, source_target_pairs={{0,64},{1,65},{2,66},{3,67},{4,68},{5,69},{6,70},{7,71},{8,72},{9,... | collective-permute-start | bytes 1572872 | tf_op jit(solution)/shard_map/ppermute | solution.py:44
  69.0 1.7 %collective-permute-done.3.theirs = bf16[128,2048]{1,0:T(8,128)(2,1)S(1)} collective-permute-done((bf16[128,2048]{1,0:T(8,128)(2,1)S(1)}, bf16[128,2048]{1,0:T(8,128)(2,1)S(1)}, u32[]{:S(2)}, u32[]{:S(2)}) %collective-permute-start.3) | collective-permute-done | bytes 524320 | tf_op jit(solution)/shard_map/ppermute | solution.py:44
  70.7 1.2 copy-done.1
  71.9 1.9 %shard_map.48.arranged = bf16[1024,512]{1,0:T(8,128)(2,1)S(1)} custom-call(s32[3]{0:T(128)S(1)} %pad_add_fusion.at, bf16[512,512]{1,0:T(8,128)(2,1)S(1)} %fusion.21.order, bf16[128,4096]{1,0:T(8,128)(2,1)S(1)} %bitcast.62, bf16[128,2048]{1,0:T(8,128)(2,1)S(1)} %collective-permute-done.3.theirs), custom_call_target="tpu_custom_call" | custom-call | flops 536870912 | bytes 4194304 | tf_op jit(solution)/shard_map/pallas_call | solution.py:103
  73.8 17.4 %collective-permute-done.4.refs_1_ = bf16[512,1280]{1,0:T(8,128)(2,1)} collective-permute-done((bf16[512,1280]{1,0:T(8,128)(2,1)S(1)}, bf16[512,1280]{1,0:T(8,128)(2,1)}, u32[]{:S(2)}, u32[]{:S(2)}) %collective-permute-start.4) | collective-permute-done | bytes 1310752 | tf_op jit(solution)/shard_map/ppermute | solution.py:40
  91.3 2.9 %shard_map.49 = (f32[128,1280]{1,0:T(8,128)S(1)}, f32[128,1280]{1,0:T(8,128)S(1)}, bf16[2048,1280]{1,0:T(8,128)(2,1)}) custom-call(bf16[1024,512]{1,0:T(8,128)(2,1)S(1)} %shard_map.48.arranged, bf16[512,1280]{1,0:T(8,128)(2,1)S(1)} %shard_map.46.refs_0_, bf16[512,1280]{1,0:T(8,128)(2,1)} %collective-permute-done.4.refs_1_), custom_call_target="tpu_custom_call" | custom-call | flops 671088640 | bytes 4194304 | tf_op jit(solution)/shard_map/pallas_call | solution.py:169
  94.2 2.2 %shard_map.50 = (f32[128,1280]{1,0:T(8,128)S(1)}, f32[128,1280]{1,0:T(8,128)S(1)}) custom-call(bf16[1024,512]{1,0:T(8,128)(2,1)S(1)} %shard_map.48.arranged, f32[128,1280]{1,0:T(8,128)S(1)} %get-tuple-element.23.mine, f32[128,1280]{1,0:T(8,128)S(1)} %get-tuple-element.24.theirs, bf16[512,1280]{1,0:T(8,128)(2,1)} %collective-permute-done.5.refs_0_.first, ...), custom_call_target="tpu_custom_call" | custom-call | flops 671088640 | bytes 4194304 | tf_op jit(solution)/shard_map/pallas_call | solution.py:197
  96.4 1.9 %collective-permute-start.7 = (f32[128,1280]{1,0:T(8,128)S(1)}, f32[128,1280]{1,0:T(8,128)S(1)}, u32[]{:S(2)}, u32[]{:S(2)}) collective-permute-start(f32[128,1280]{1,0:T(8,128)S(1)} %get-tuple-element.26.after), channel_id=1, source_target_pairs={{0,64},{1,65},{2,66},{3,67},{4,68},{5,69},{6,70},{7,71},{8,72},{9,... | collective-permute-start | bytes 1966088 | tf_op jit(solution)/shard_map/ppermute | solution.py:44
  98.3 2.9 %shard_map.51.all_rows = bf16[2048,1280]{1,0:T(8,128)(2,1)} custom-call(bf16[512,1280]{1,0:T(8,128)(2,1)} %collective-permute-done.5.refs_0_.first, bf16[512,1280]{1,0:T(8,128)(2,1)S(1)} %collective-permute-done.6.refs_1_.second, f32[128,1280]{1,0:T(8,128)S(1)} %get-tuple-element.26.after, ...), custom_call_target="tpu_custom_call", output_to_operand_aliasing={{}: (3, {})} | custom-call | bytes 4194304 | tf_op jit(solution)/shard_map/pallas_call | solution.py:216
  101.2 2.4 %collective-permute-start.12 = (bf16[2048,1280]{1,0:T(8,128)(2,1)}, bf16[2048,1280]{1,0:T(8,128)(2,1)}, u32[]{:S(2)}, u32[]{:S(2)}) collective-permute-start(bf16[2048,1280]{1,0:T(8,128)(2,1)} %shard_map.51.all_rows), channel_id=1, source_target_pairs={{0,64},{1,65},{2,66},{3,67},{4,68},{5,69},{6,70},{7,71},{8,72},{9,... | collective-permute-start | bytes 15728648 | tf_op jit(solution)/shard_map/ppermute | solution.py:44
  103.7 0.8 compare_and_fusion
  104.7 0.3 fusion.37
  105.1 1.9 %collective-permute-start.8 = (bf16[128,256]{1,0:T(8,128)(2,1)S(1)}, bf16[128,256]{1,0:T(8,128)(2,1)S(1)}, u32[]{:S(2)}, u32[]{:S(2)}) collective-permute-start(bf16[128,256]{1,0:T(8,128)(2,1)S(1)} %pad_maximum_fusion.5), channel_id=1, source_target_pairs={{0,2},{1,3},{2,4},{3,5},{4,6},{5,7},{6,8},{7,9},{8,10},{9,11},{10,... | collective-permute-start | bytes 196616 | tf_op jit(solution)/shard_map/ppermute | solution.py:331
  107.3 3.5 %shard_map.52.own_w = bf16[2048,256]{1,0:T(8,128)(2,1)} custom-call(s32[3]{0:T(128)S(1)} %pad_add_fusion.at, bf16[2048,1280]{1,0:T(8,128)(2,1)} %shard_map.51.all_rows), custom_call_target="tpu_custom_call" | custom-call | flops 536870912 | bytes 3145728 | tf_op jit(solution)/shard_map/pallas_call | solution.py:295
  110.8 2.0 %collective-permute-done.8 = bf16[128,256]{1,0:T(8,128)(2,1)S(1)} collective-permute-done((bf16[128,256]{1,0:T(8,128)(2,1)S(1)}, bf16[128,256]{1,0:T(8,128)(2,1)S(1)}, u32[]{:S(2)}, u32[]{:S(2)}) %collective-permute-start.8) | collective-permute-done | bytes 65568 | tf_op jit(solution)/shard_map/ppermute | solution.py:331
  112.8 4.2 %collective-permute-start.9 = (bf16[256,256]{1,0:T(8,128)(2,1)S(1)}, bf16[256,256]{1,0:T(8,128)(2,1)S(1)}, u32[]{:S(2)}, u32[]{:S(2)}) collective-permute-start(bf16[256,256]{1,0:T(8,128)(2,1)S(1)} %pad_maximum_fusion.3), channel_id=1, source_target_pairs={{0,1},{1,2},{2,3},{3,4},{4,5},{5,6},{6,7},{7,8},{8,9},{9,10},{10,1... | collective-permute-start | bytes 393224 | tf_op jit(solution)/shard_map/ppermute | solution.py:331
  117.0 0.9 subtract_convert_fusion.1
  118.0 1.9 %collective-permute-start.13 = (bf16[2048,256]{1,0:T(8,128)(2,1)}, bf16[2048,256]{1,0:T(8,128)(2,1)S(1)}, u32[]{:S(2)}, u32[]{:S(2)}) collective-permute-start(bf16[2048,256]{1,0:T(8,128)(2,1)} %shard_map.52.own_w), channel_id=1, source_target_pairs={{0,64},{1,65},{2,66},{3,67},{4,68},{5,69},{6,70},{7,71},{8,72},{9,... | collective-permute-start | bytes 3145736 | tf_op jit(solution)/shard_map/ppermute | solution.py:44
  119.9 0.7 pad_maximum_fusion.1
  120.6 2.0 %fusion.60 = (f32[8,128]{1,0:T(8,128)S(1)}, f32[8,128,512]{1,2,0:T(8,128)S(1)}) fusion(pred[128,512]{0,1:T(8,128)(4,1)} %compare_and_fusion, bf16[512,256]{1,0:T(8,128)(2,1)} %pad_maximum_fusion.1, bf16[128,8,64]{2,0,1:T(8,128)(2,1)} %get-tuple-element.38, bf16[128,8,64]{2,0,1:T(8,128)(2,1)S(1)} %get-tuple-element.37), kind=kOutput, calls=%fused_computation.112 | convolution fusion | flops 137363968 | bytes 2756608 | tf_op jit(solution)/shard_map/sub | solution.py:406
  122.9 0.7 copy-done.4
  123.6 0.4 convolution_bitcast_fusion
  124.1 0.4 fusion.7
  124.5 0.4 fusion.2
  124.9 0.5 copy-done.3
  125.4 0.5 fusion.8
  126.0 2.2 %collective-permute-start.10 = (bf16[256,256]{1,0:T(8,128)(2,1)S(1)}, bf16[256,256]{1,0:T(8,128)(2,1)S(1)}, u32[]{:S(2)}, u32[]{:S(2)}) collective-permute-start(bf16[256,256]{1,0:T(8,128)(2,1)S(1)} %pad_maximum_fusion.4), channel_id=1, source_target_pairs={{1,0},{2,1},{3,2},{4,3},{5,4},{6,5},{7,6},{8,7},{9,8},{10,9},{11,1... | collective-permute-start | bytes 393224 | tf_op jit(solution)/shard_map/ppermute | solution.py:331
  128.2 0.6 fusion.4
  128.7 0.3 subtract_convert_fusion
  129.1 4.4 %shard_map.53.own_part = f32[128,2048]{1,0:T(8,128)S(1)} custom-call(s32[3]{0:T(128)S(1)} %pad_add_fusion.at, bf16[128,1024]{1,0:T(8,128)(2,1)S(1)} %copy_bitcast_fusion.grads, bf16[2048,1280]{1,0:T(8,128)(2,1)} %shard_map.51.all_rows), custom_call_target="tpu_custom_call" | custom-call | flops 1073741824 | bytes 6291456 | tf_op jit(solution)/shard_map/pallas_call | solution.py:266
  133.5 2.4 %collective-permute-done.10 = bf16[256,256]{1,0:T(8,128)(2,1)S(1)} collective-permute-done((bf16[256,256]{1,0:T(8,128)(2,1)S(1)}, bf16[256,256]{1,0:T(8,128)(2,1)S(1)}, u32[]{:S(2)}, u32[]{:S(2)}) %collective-permute-start.10) | collective-permute-done | bytes 131104 | tf_op jit(solution)/shard_map/ppermute | solution.py:331
  136.0 2.2 %collective-permute-start.11 = (bf16[128,256]{1,0:T(8,128)(2,1)S(1)}, bf16[128,256]{1,0:T(8,128)(2,1)S(1)}, u32[]{:S(2)}, u32[]{:S(2)}) collective-permute-start(bf16[128,256]{1,0:T(8,128)(2,1)S(1)} %fusion.32), channel_id=1, source_target_pairs={{2,0},{3,1},{4,2},{5,3},{6,4},{7,5},{8,6},{9,7},{10,8},{11,9},{12,... | collective-permute-start | bytes 196616 | tf_op jit(solution)/shard_map/ppermute | solution.py:331
  138.2 4.4 %shard_map.54.other_part = f32[128,2048]{1,0:T(8,128)S(1)} custom-call(s32[3]{0:T(128)S(1)} %pad_add_fusion.at, bf16[128,1024]{1,0:T(8,128)(2,1)S(1)} %copy_bitcast_fusion.grads, bf16[2048,1280]{1,0:T(8,128)(2,1)} %collective-permute-done.12.all_rows), custom_call_target="tpu_custom_call" | custom-call | flops 1073741824 | bytes 6291456 | tf_op jit(solution)/shard_map/pallas_call | solution.py:266
  142.6 2.0 %collective-permute-done.11 = bf16[128,256]{1,0:T(8,128)(2,1)S(1)} collective-permute-done((bf16[128,256]{1,0:T(8,128)(2,1)S(1)}, bf16[128,256]{1,0:T(8,128)(2,1)S(1)}, u32[]{:S(2)}, u32[]{:S(2)}) %collective-permute-start.11) | collective-permute-done | bytes 65568 | tf_op jit(solution)/shard_map/ppermute | solution.py:331
  144.7 0.3 fusion.46
  145.1 2.3 %shard_map.55 = bf16[128,4096]{1,0:T(8,128)(2,1)} custom-call(s32[3]{0:T(128)S(1)} %pad_add_fusion.at, bf16[128,256]{1,0:T(8,128)(2,1)S(1)} %pad_maximum_fusion.6.pair_out, f32[128,2048]{1,0:T(8,128)S(1)} %shard_map.53.own_part, f32[128,2048]{1,0:T(8,128)S(1)} %shard_map.54.other_part, bf16[2048,256]{1,0:T(8,128)(2,1)S(1)} %copy-done.2, ...), custom_call_target="tpu_custom_call" | custom-call | tf_op jit(solution)/shard_map/pallas_call | solution.py:321
  (47 shorter events, 1.6 us)
Async XLA Ops:
  37.4 12.2 %collective-permute-start.2 = (bf16[128,1280]{1,0:T(8,128)(2,1)S(1)}, bf16[128,1280]{1,0:T(8,128)(2,1)S(1)}, u32[]{:S(2)}, u32[]{:S(2)}) collective-permute-start(bf16[128,1280]{1,0:T(8,128)(2,1)S(1)} %all_gather.3.own), channel_id=1, source_target_pairs={{0,384},{1,385},{2,386},{3,387},{4,388},{5,389},{6,390},{7,391},{8... | collective-permute-start | bytes 983048 | tf_op jit(solution)/shard_map/ppermute | solution.py:40
  42.1 10.6 %collective-permute-start.1 = (bf16[128,1280]{1,0:T(8,128)(2,1)S(1)}, bf16[128,1280]{1,0:T(8,128)(2,1)S(1)}, u32[]{:S(2)}, u32[]{:S(2)}) collective-permute-start(bf16[128,1280]{1,0:T(8,128)(2,1)S(1)} %all_gather.3.own), channel_id=1, source_target_pairs={{0,256},{1,257},{2,258},{3,259},{4,260},{5,261},{6,262},{7,263},{8... | collective-permute-start | bytes 983048 | tf_op jit(solution)/shard_map/ppermute | solution.py:40
  44.8 11.5 %collective-permute-start = (bf16[128,1280]{1,0:T(8,128)(2,1)S(1)}, bf16[128,1280]{1,0:T(8,128)(2,1)S(1)}, u32[]{:S(2)}, u32[]{:S(2)}) collective-permute-start(bf16[128,1280]{1,0:T(8,128)(2,1)S(1)} %all_gather.3.own), channel_id=1, source_target_pairs={{0,128},{1,129},{2,130},{3,131},{4,132},{5,133},{6,134},{7,135},{8... | collective-permute-start | bytes 983048 | tf_op jit(solution)/shard_map/ppermute | solution.py:40
  47.7 1.2 copy-start
  49.0 17.1 %copy-start.6 = (bf16[1,128,1024]{2,1,0:T(8,128)(2,1)S(1)}, bf16[1,128,1024]{2,1,0:T(8,128)(2,1)}, u32[]{:S(2)}) copy-start(bf16[1,128,1024]{2,1,0:T(8,128)(2,1)} %param.6) | copy-start | bytes 786436
  56.4 34.9 %collective-permute-start.4 = (bf16[512,1280]{1,0:T(8,128)(2,1)S(1)}, bf16[512,1280]{1,0:T(8,128)(2,1)}, u32[]{:S(2)}, u32[]{:S(2)}) collective-permute-start(bf16[512,1280]{1,0:T(8,128)(2,1)S(1)} %shard_map.46.refs_0_), channel_id=1, source_target_pairs={{0,3},{1,0},{2,1},{3,2},{4,7},{5,4},{6,5},{7,6},{8,11},{9,8},{10,9... | collective-permute-start | bytes 3932168 | tf_op jit(solution)/shard_map/ppermute | solution.py:40
  59.2 35.0 %collective-permute-start.6 = (bf16[512,1280]{1,0:T(8,128)(2,1)S(1)}, bf16[512,1280]{1,0:T(8,128)(2,1)S(1)}, u32[]{:S(2)}, u32[]{:S(2)}) collective-permute-start(bf16[512,1280]{1,0:T(8,128)(2,1)S(1)} %shard_map.46.refs_0_), channel_id=1, source_target_pairs={{0,2},{1,3},{2,0},{3,1},{4,6},{5,7},{6,4},{7,5},{8,10},{9,11},{10,... | collective-permute-start | bytes 3932168 | tf_op jit(solution)/shard_map/ppermute | solution.py:40
  61.7 32.5 %collective-permute-start.5 = (bf16[512,1280]{1,0:T(8,128)(2,1)S(1)}, bf16[512,1280]{1,0:T(8,128)(2,1)}, u32[]{:S(2)}, u32[]{:S(2)}) collective-permute-start(bf16[512,1280]{1,0:T(8,128)(2,1)S(1)} %shard_map.46.refs_0_), channel_id=1, source_target_pairs={{0,1},{1,2},{2,3},{3,0},{4,5},{5,6},{6,7},{7,4},{8,9},{9,10},{10,1... | collective-permute-start | bytes 3932168 | tf_op jit(solution)/shard_map/ppermute | solution.py:40
  66.9 3.8 %collective-permute-start.3 = (bf16[128,2048]{1,0:T(8,128)(2,1)S(1)}, bf16[128,2048]{1,0:T(8,128)(2,1)S(1)}, u32[]{:S(2)}, u32[]{:S(2)}) collective-permute-start(bf16[128,2048]{1,0:T(8,128)(2,1)S(1)} %shard_map.47), channel_id=1, source_target_pairs={{0,64},{1,65},{2,66},{3,67},{4,68},{5,69},{6,70},{7,71},{8,72},{9,... | collective-permute-start | bytes 1572872 | tf_op jit(solution)/shard_map/ppermute | solution.py:44
  70.7 1.2 copy-start.1
  96.4 8.1 %collective-permute-start.7 = (f32[128,1280]{1,0:T(8,128)S(1)}, f32[128,1280]{1,0:T(8,128)S(1)}, u32[]{:S(2)}, u32[]{:S(2)}) collective-permute-start(f32[128,1280]{1,0:T(8,128)S(1)} %get-tuple-element.26.after), channel_id=1, source_target_pairs={{0,64},{1,65},{2,66},{3,67},{4,68},{5,69},{6,70},{7,71},{8,72},{9,... | collective-permute-start | bytes 1966088 | tf_op jit(solution)/shard_map/ppermute | solution.py:44
  98.3 5.4 %copy-start.7 = (s32[1,128]{1,0:T(1,128)S(1)}, s32[1,128]{1,0:T(1,128)}, u32[]{:S(2)}) copy-start(s32[1,128]{1,0:T(1,128)} %param.5) | copy-start | bytes 1540
  101.2 37.0 %collective-permute-start.12 = (bf16[2048,1280]{1,0:T(8,128)(2,1)}, bf16[2048,1280]{1,0:T(8,128)(2,1)}, u32[]{:S(2)}, u32[]{:S(2)}) collective-permute-start(bf16[2048,1280]{1,0:T(8,128)(2,1)} %shard_map.51.all_rows), channel_id=1, source_target_pairs={{0,64},{1,65},{2,66},{3,67},{4,68},{5,69},{6,70},{7,71},{8,72},{9,... | collective-permute-start | bytes 15728648 | tf_op jit(solution)/shard_map/ppermute | solution.py:44
  105.1 7.7 %collective-permute-start.8 = (bf16[128,256]{1,0:T(8,128)(2,1)S(1)}, bf16[128,256]{1,0:T(8,128)(2,1)S(1)}, u32[]{:S(2)}, u32[]{:S(2)}) collective-permute-start(bf16[128,256]{1,0:T(8,128)(2,1)S(1)} %pad_maximum_fusion.5), channel_id=1, source_target_pairs={{0,2},{1,3},{2,4},{3,5},{4,6},{5,7},{6,8},{7,9},{8,10},{9,11},{10,... | collective-permute-start | bytes 196616 | tf_op jit(solution)/shard_map/ppermute | solution.py:331
  112.8 7.1 %collective-permute-start.9 = (bf16[256,256]{1,0:T(8,128)(2,1)S(1)}, bf16[256,256]{1,0:T(8,128)(2,1)S(1)}, u32[]{:S(2)}, u32[]{:S(2)}) collective-permute-start(bf16[256,256]{1,0:T(8,128)(2,1)S(1)} %pad_maximum_fusion.3), channel_id=1, source_target_pairs={{0,1},{1,2},{2,3},{3,4},{4,5},{5,6},{6,7},{7,8},{8,9},{9,10},{10,1... | collective-permute-start | bytes 393224 | tf_op jit(solution)/shard_map/ppermute | solution.py:331
  118.0 26.7 %collective-permute-start.13 = (bf16[2048,256]{1,0:T(8,128)(2,1)}, bf16[2048,256]{1,0:T(8,128)(2,1)S(1)}, u32[]{:S(2)}, u32[]{:S(2)}) collective-permute-start(bf16[2048,256]{1,0:T(8,128)(2,1)} %shard_map.52.own_w), channel_id=1, source_target_pairs={{0,64},{1,65},{2,66},{3,67},{4,68},{5,69},{6,70},{7,71},{8,72},{9,... | collective-permute-start | bytes 3145736 | tf_op jit(solution)/shard_map/ppermute | solution.py:44
  122.7 1.0 copy-start.4
  122.7 1.4 copy-start.5
  124.4 1.0 copy-start.3
  126.0 9.9 %collective-permute-start.10 = (bf16[256,256]{1,0:T(8,128)(2,1)S(1)}, bf16[256,256]{1,0:T(8,128)(2,1)S(1)}, u32[]{:S(2)}, u32[]{:S(2)}) collective-permute-start(bf16[256,256]{1,0:T(8,128)(2,1)S(1)} %pad_maximum_fusion.4), channel_id=1, source_target_pairs={{1,0},{2,1},{3,2},{4,3},{5,4},{6,5},{7,6},{8,7},{9,8},{10,9},{11,1... | collective-permute-start | bytes 393224 | tf_op jit(solution)/shard_map/ppermute | solution.py:331
  136.0 9.2 %copy-start.2 = (bf16[2048,256]{1,0:T(8,128)(2,1)S(1)}, bf16[2048,256]{1,0:T(8,128)(2,1)}, u32[]{:S(2)}) copy-start(bf16[2048,256]{1,0:T(8,128)(2,1)} %shard_map.52.own_w) | copy-start | bytes 3145732
  136.0 8.7 %collective-permute-start.11 = (bf16[128,256]{1,0:T(8,128)(2,1)S(1)}, bf16[128,256]{1,0:T(8,128)(2,1)S(1)}, u32[]{:S(2)}, u32[]{:S(2)}) collective-permute-start(bf16[128,256]{1,0:T(8,128)(2,1)S(1)} %fusion.32), channel_id=1, source_target_pairs={{2,0},{3,1},{4,2},{5,3},{6,4},{7,5},{8,6},{9,7},{10,8},{11,9},{12,... | collective-permute-start | bytes 196616 | tf_op jit(solution)/shard_map/ppermute | solution.py:331

commit v9 on v8

--- a/solution.py
+++ b/solution.py
@@ -181,8 +181,12 @@
 
 
 def late_body(steps, arranged, mine, theirs, *refs):
-    pieces, (mine_ref, theirs_ref) = refs[: len(steps)], refs[len(steps) :]
-    count, more = mine.shape[0], 0.0
+    pieces, (rows_in, mine_ref, theirs_ref, rows_ref, sems) = refs[: len(steps)], refs[len(steps) :]
+    count, stores, more = mine.shape[0], [], 0.0
+    for i, (step, piece) in enumerate(zip(steps, pieces)):
+        to_rows = rows_ref.at[pl.ds(step * BLOCK, BLOCK)]
+        stores.append(pltpu.make_async_copy(piece, to_rows, sems.at[i]))
+        stores[-1].start()
     for step, piece in zip(steps, pieces):
         more += jnp.dot(
             arranged[step * 2 * count : (step + 1) * 2 * count, :], piece[...],
@@ -190,38 +194,26 @@
         )
     mine_ref[...] = mine[...] + more[:count]
     theirs_ref[...] = theirs[...] + more[count:]
-
-
-def late_sums(arranged, sums, pieces, steps):
-    count, columns = sums[0].shape
-    return call(
-        functools.partial(late_body, steps),
-        [WHOLE] * (3 + len(pieces)),
-        [pltpu.VMEM((count, columns), jnp.float32)] * 2,
-        len(steps) * 4 * count * BLOCK * columns, 4,
-    )(*[in_vmem(x) for x in (arranged, *sums, *pieces)])
-
-
-def place_body(steps, first, second, after, rows_in, rows_ref, sems):
-    stores = []
-    for i, piece in enumerate((first, second)):
-        to_rows = rows_ref.at[pl.ds(steps[i] * BLOCK, BLOCK)]
-        stores.append(pltpu.make_async_copy(piece, to_rows, sems.at[i]))
-        stores[-1].start()
     for store in stores:
         store.wait()
 
 
-def place_rows(pieces, after, rows, steps):
-    return call(
-        functools.partial(place_body, steps),
-        [WHOLE, WHOLE, pl.BlockSpec(memory_space=pl.ANY), LEFT],
-        jax.ShapeDtypeStruct(rows.shape, rows.dtype),
-        0, 4,
-        out_specs=LEFT,
-        scratch_shapes=[pltpu.SemaphoreType.DMA((2,))],
-        input_output_aliases={3: 0},
-    )(*[in_vmem(p) for p in pieces], after, rows)
+def late_sums(arranged, sums, pieces, rows, steps):
+    count, columns = sums[0].shape
+    operands = [in_vmem(x) for x in (arranged, *sums, *pieces)]
+    return call(
+        functools.partial(late_body, steps),
+        [WHOLE] * len(operands) + [LEFT],
+        [
+            pltpu.VMEM((count, columns), jnp.float32),
+            pltpu.VMEM((count, columns), jnp.float32),
+            jax.ShapeDtypeStruct(rows.shape, rows.dtype),
+        ],
+        len(steps) * 4 * count * BLOCK * columns, 4,
+        out_specs=[WHOLE, WHOLE, LEFT],
+        scratch_shapes=[pltpu.SemaphoreType.DMA((len(pieces),))],
+        input_output_aliases={len(operands): 2},
+    )(*operands, rows)
 
 
 TURN = (((1,), (1,)), ((), ()))
@@ -323,7 +315,7 @@
         in_specs=[pl.BlockSpec(memory_space=pltpu.SMEM)] + [whole] * 5,
         out_shape=jax.ShapeDtypeStruct((pair_out.shape[0], NX * NC * BLOCK), jnp.bfloat16),
         compiler_params=pltpu.CompilerParams(vmem_limit_bytes=VMEM_LIMIT),
-    )(at, pair_out, *[in_vmem(p) for p in parts], in_vmem(weights[0]), weights[1])
+    )(at, pair_out, *[in_vmem(p) for p in parts], in_vmem(weights[0]), in_hbm(weights[1]))
 
 
 def shifted(block, axis, distance):
@@ -371,8 +363,7 @@
     two, one, three = (hop(plane, d, 1) for d in (2, 1, 3))
     arranged = arrange(at, order, features, swap_cores(theirs))
     *sums, own_w = early_sums(arranged, [plane, three], (0, 3))
-    mine, theirs = late_sums(arranged, sums, [one, two], (1, 2))
-    own_w = place_rows([one, two], theirs, own_w, (1, 2))
+    mine, theirs, own_w = late_sums(arranged, sums, [one, two], own_w, (1, 2))
     projected = mine + swap_cores(theirs)
     pair_pre, query_pre = projected[:, HQ * HD :], projected[:, : HQ * HD]
 

time: 149 us -> 147 us (0.987)
  other arithmetic: 4.26 us -> 2.23 us
    pallas_call x2 -> x1, Pallas kernels: 5.08 us -> 3.54 us  [late_sums(): call(functools.partial(late_body, steps), [WHOLE] * len(operands) + [LEFT...]
  transfers between devices with their start and end apart: 14 -> 14, of which waited for: 8 -> 8; matrix products, arithmetic and copies ran while one was open for 6% -> 5% of each run, Pallas kernels for 14% -> 12%
where the time goes in v9:
time: 147 us; the launch traced here: 144 us
  starting transfers between devices  38 us (26%)
  blocking collectives  37.4 us (25%)
  waiting for transfers between devices  32.5 us (22%)
  Pallas kernels  24.2 us (16%)
  local copies, waits for them, and re-layouts  6.15 us (4%)
  matrix products  3.36 us (2%)
  other arithmetic  2.23 us (2%)
    all_gather x1, blocking collectives, local(): lax.all_gather(w_qkv, 'ctx', axis=0, tiled=True, axis_index_groups=[[z *...  37.4 us
    ppermute x6, waiting for transfers between devices, hop(): return lax.ppermute(block, ALL, route(move))  23.7 us
    ppermute x6, starting transfers between devices, hop(): return lax.ppermute(block, ALL, route(move))  20.3 us
    ppermute x4, starting transfers between devices, shifted(): lax.ppermute(block, axis, [(i - distance, i) for i in devices if i - dist...  9.46 us
    pallas_call x2, Pallas kernels, query_part_of(): call(functools.partial(query_part_body, flip), [SCALARS, WHOLE, LEFT], pl...  8.75 us
    ppermute x4, starting transfers between devices, swap_cores(): return lax.ppermute(block, ALL, route(lambda x, c, z, y: (x, 1 - c, z, y)))  8.17 us
    ppermute x4, waiting for transfers between devices, shifted(): lax.ppermute(block, axis, [(i - distance, i) for i in devices if i - dist...  7.09 us
    unnamed x19, local copies, waits for them, and re-layouts  5.91 us
  transfers between devices with their start and end apart: 14, of which 8 were waited for; matrix products, arithmetic and copies ran while one was open for 5% of the time, Pallas kernels for 12%

profile of v9, /device:TPU:24, one launch (start us, length us, event | category | flops | bytes accessed | tf_op | source)
XLA Modules:
  0.0 144.4 jit_solution(304549826729110797)
XLA Ops:
  0.0 37.4 %all_gather.3.own = bf16[128,1280]{1,0:T(8,128)(2,1)S(1)} all-gather(bf16[8,1280]{1,0:T(8,128)(2,1)} %param.7), channel_id=1, replica_groups={{0,4,8,12,16,20,24,28,32,36,40,44,48,52,56,60},{1,5,9,13,17,21,25,29,33..., dimensions={0}, use_global_device_ids=true | all-gather | bytes 348160 | tf_op jit(solution)/shard_map/all_gather | solution.py:352
  37.4 3.4 %collective-permute-start = (bf16[128,1280]{1,0:T(8,128)(2,1)S(1)}, bf16[128,1280]{1,0:T(8,128)(2,1)S(1)}, u32[]{:S(2)}, u32[]{:S(2)}) collective-permute-start(bf16[128,1280]{1,0:T(8,128)(2,1)S(1)} %all_gather.3.own), channel_id=1, source_target_pairs={{0,128},{1,129},{2,130},{3,131},{4,132},{5,133},{6,134},{7,135},{8... | collective-permute-start | bytes 983048 | tf_op jit(solution)/shard_map/ppermute | solution.py:40
  40.8 4.6 %collective-permute-start.1 = (bf16[128,1280]{1,0:T(8,128)(2,1)S(1)}, bf16[128,1280]{1,0:T(8,128)(2,1)S(1)}, u32[]{:S(2)}, u32[]{:S(2)}) collective-permute-start(bf16[128,1280]{1,0:T(8,128)(2,1)S(1)} %all_gather.3.own), channel_id=1, source_target_pairs={{0,256},{1,257},{2,258},{3,259},{4,260},{5,261},{6,262},{7,263},{8... | collective-permute-start | bytes 983048 | tf_op jit(solution)/shard_map/ppermute | solution.py:40
  45.5 3.3 %collective-permute-start.2 = (bf16[128,1280]{1,0:T(8,128)(2,1)S(1)}, bf16[128,1280]{1,0:T(8,128)(2,1)S(1)}, u32[]{:S(2)}, u32[]{:S(2)}) collective-permute-start(bf16[128,1280]{1,0:T(8,128)(2,1)S(1)} %all_gather.3.own), channel_id=1, source_target_pairs={{0,384},{1,385},{2,386},{3,387},{4,388},{5,389},{6,390},{7,391},{8... | collective-permute-start | bytes 983048 | tf_op jit(solution)/shard_map/ppermute | solution.py:40
  48.9 1.2 copy-done
  50.2 0.6 shard_map.47
  50.8 1.3 collective-permute-done.1.second
  52.1 0.7 copy-done.3
  52.8 3.4 %collective-permute-done.2.third = bf16[128,1280]{1,0:T(8,128)(2,1)S(1)} collective-permute-done((bf16[128,1280]{1,0:T(8,128)(2,1)S(1)}, bf16[128,1280]{1,0:T(8,128)(2,1)S(1)}, u32[]{:S(2)}, u32[]{:S(2)}) %collective-permute-start.2) | collective-permute-done | bytes 327712 | tf_op jit(solution)/shard_map/ppermute | solution.py:40
  56.2 0.7 copy-done.5
  56.9 1.0 copy-done.4
  57.9 1.0 copy-done.6
  59.0 2.7 %collective-permute-start.4 = (bf16[512,1280]{1,0:T(8,128)(2,1)S(1)}, bf16[512,1280]{1,0:T(8,128)(2,1)}, u32[]{:S(2)}, u32[]{:S(2)}) collective-permute-start(bf16[512,1280]{1,0:T(8,128)(2,1)S(1)} %shard_map.46.refs_0_), channel_id=1, source_target_pairs={{0,3},{1,0},{2,1},{3,2},{4,7},{5,4},{6,5},{7,6},{8,11},{9,8},{10,9... | collective-permute-start | bytes 3932168 | tf_op jit(solution)/shard_map/ppermute | solution.py:40
  61.7 4.4 %collective-permute-start.5 = (bf16[512,1280]{1,0:T(8,128)(2,1)S(1)}, bf16[512,1280]{1,0:T(8,128)(2,1)}, u32[]{:S(2)}, u32[]{:S(2)}) collective-permute-start(bf16[512,1280]{1,0:T(8,128)(2,1)S(1)} %shard_map.46.refs_0_), channel_id=1, source_target_pairs={{0,1},{1,2},{2,3},{3,0},{4,5},{5,6},{6,7},{7,4},{8,9},{9,10},{10,1... | collective-permute-start | bytes 3932168 | tf_op jit(solution)/shard_map/ppermute | solution.py:40
  66.0 1.9 %collective-permute-start.6 = (bf16[512,1280]{1,0:T(8,128)(2,1)S(1)}, bf16[512,1280]{1,0:T(8,128)(2,1)}, u32[]{:S(2)}, u32[]{:S(2)}) collective-permute-start(bf16[512,1280]{1,0:T(8,128)(2,1)S(1)} %shard_map.46.refs_0_), channel_id=1, source_target_pairs={{0,2},{1,3},{2,0},{3,1},{4,6},{5,7},{6,4},{7,5},{8,10},{9,11},{10,... | collective-permute-start | bytes 3932168 | tf_op jit(solution)/shard_map/ppermute | solution.py:40
  68.0 1.1 copy.8
  69.1 1.9 %collective-permute-start.3 = (bf16[128,2048]{1,0:T(8,128)(2,1)S(1)}, bf16[128,2048]{1,0:T(8,128)(2,1)S(1)}, u32[]{:S(2)}, u32[]{:S(2)}) collective-permute-start(bf16[128,2048]{1,0:T(8,128)(2,1)S(1)} %shard_map.47), channel_id=1, source_target_pairs={{0,64},{1,65},{2,66},{3,67},{4,68},{5,69},{6,70},{7,71},{8,72},{9,... | collective-permute-start | bytes 1572872 | tf_op jit(solution)/shard_map/ppermute | solution.py:44
  71.2 1.7 %collective-permute-done.3.theirs = bf16[128,2048]{1,0:T(8,128)(2,1)S(1)} collective-permute-done((bf16[128,2048]{1,0:T(8,128)(2,1)S(1)}, bf16[128,2048]{1,0:T(8,128)(2,1)S(1)}, u32[]{:S(2)}, u32[]{:S(2)}) %collective-permute-start.3) | collective-permute-done | bytes 524320 | tf_op jit(solution)/shard_map/ppermute | solution.py:44
  72.9 1.9 %shard_map.48.arranged = bf16[1024,512]{1,0:T(8,128)(2,1)S(1)} custom-call(s32[3]{0:T(128)S(1)} %pad_add_fusion.at, bf16[512,512]{1,0:T(8,128)(2,1)S(1)} %fusion.21.order, bf16[128,4096]{1,0:T(8,128)(2,1)S(1)} %bitcast.62, bf16[128,2048]{1,0:T(8,128)(2,1)S(1)} %collective-permute-done.3.theirs), custom_call_target="tpu_custom_call" | custom-call | flops 536870912 | bytes 4194304 | tf_op jit(solution)/shard_map/pallas_call | solution.py:103
  74.8 19.0 %collective-permute-done.4.refs_1_ = bf16[512,1280]{1,0:T(8,128)(2,1)} collective-permute-done((bf16[512,1280]{1,0:T(8,128)(2,1)S(1)}, bf16[512,1280]{1,0:T(8,128)(2,1)}, u32[]{:S(2)}, u32[]{:S(2)}) %collective-permute-start.4) | collective-permute-done | bytes 1310752 | tf_op jit(solution)/shard_map/ppermute | solution.py:40
  93.8 2.8 %shard_map.49 = (f32[128,1280]{1,0:T(8,128)S(1)}, f32[128,1280]{1,0:T(8,128)S(1)}, bf16[2048,1280]{1,0:T(8,128)(2,1)}) custom-call(bf16[1024,512]{1,0:T(8,128)(2,1)S(1)} %shard_map.48.arranged, bf16[512,1280]{1,0:T(8,128)(2,1)S(1)} %shard_map.46.refs_0_, bf16[512,1280]{1,0:T(8,128)(2,1)} %collective-permute-done.4.refs_1_), custom_call_target="tpu_custom_call" | custom-call | flops 671088640 | bytes 4194304 | tf_op jit(solution)/shard_map/pallas_call | solution.py:169
  96.7 3.5 %shard_map.50 = (f32[128,1280]{1,0:T(8,128)S(1)}, f32[128,1280]{1,0:T(8,128)S(1)}, bf16[2048,1280]{1,0:T(8,128)(2,1)}) custom-call(bf16[1024,512]{1,0:T(8,128)(2,1)S(1)} %shard_map.48.arranged, f32[128,1280]{1,0:T(8,128)S(1)} %get-tuple-element.24.mine, f32[128,1280]{1,0:T(8,128)S(1)} %get-tuple-element.25.theirs, ...), custom_call_target="tpu_custom_call", output_to_operand_aliasing={{2}: (5, {})} | custom-call | flops 671088640 | bytes 4194304 | tf_op jit(solution)/shard_map/pallas_call | solution.py:204
  100.3 1.9 %collective-permute-start.7 = (f32[128,1280]{1,0:T(8,128)S(1)}, f32[128,1280]{1,0:T(8,128)S(1)}, u32[]{:S(2)}, u32[]{:S(2)}) collective-permute-start(f32[128,1280]{1,0:T(8,128)S(1)} %get-tuple-element.28), channel_id=1, source_target_pairs={{0,64},{1,65},{2,66},{3,67},{4,68},{5,69},{6,70},{7,71},{8,72},{9,... | collective-permute-start | bytes 1966088 | tf_op jit(solution)/shard_map/ppermute | solution.py:44
  102.2 2.4 %collective-permute-start.12 = (bf16[2048,1280]{1,0:T(8,128)(2,1)}, bf16[2048,1280]{1,0:T(8,128)(2,1)}, u32[]{:S(2)}, u32[]{:S(2)}) collective-permute-start(bf16[2048,1280]{1,0:T(8,128)(2,1)} %get-tuple-element.31.all_rows), channel_id=1, source_target_pairs={{0,64},{1,65},{2,66},{3,67},{4,68},{5,69},{6,70},{7,71},{8,72},{9,... | collective-permute-start | bytes 15728648 | tf_op jit(solution)/shard_map/ppermute | solution.py:44
  105.1 0.3 fusion.37
  105.5 1.9 %collective-permute-start.8 = (bf16[128,256]{1,0:T(8,128)(2,1)S(1)}, bf16[128,256]{1,0:T(8,128)(2,1)S(1)}, u32[]{:S(2)}, u32[]{:S(2)}) collective-permute-start(bf16[128,256]{1,0:T(8,128)(2,1)S(1)} %pad_maximum_fusion.5), channel_id=1, source_target_pairs={{0,2},{1,3},{2,4},{3,5},{4,6},{5,7},{6,8},{7,9},{8,10},{9,11},{10,... | collective-permute-start | bytes 196616 | tf_op jit(solution)/shard_map/ppermute | solution.py:323
  107.4 0.2 fusion.57
  107.6 3.5 %shard_map.51.own_w = bf16[2048,256]{1,0:T(8,128)(2,1)} custom-call(s32[3]{0:T(128)S(1)} %pad_add_fusion.at, bf16[2048,1280]{1,0:T(8,128)(2,1)} %get-tuple-element.31.all_rows), custom_call_target="tpu_custom_call" | custom-call | flops 536870912 | bytes 3145728 | tf_op jit(solution)/shard_map/pallas_call | solution.py:287
  111.1 2.0 %collective-permute-done.8 = bf16[128,256]{1,0:T(8,128)(2,1)S(1)} collective-permute-done((bf16[128,256]{1,0:T(8,128)(2,1)S(1)}, bf16[128,256]{1,0:T(8,128)(2,1)S(1)}, u32[]{:S(2)}, u32[]{:S(2)}) %collective-permute-start.8) | collective-permute-done | bytes 65568 | tf_op jit(solution)/shard_map/ppermute | solution.py:323
  113.2 3.4 %collective-permute-start.9 = (bf16[256,256]{1,0:T(8,128)(2,1)S(1)}, bf16[256,256]{1,0:T(8,128)(2,1)S(1)}, u32[]{:S(2)}, u32[]{:S(2)}) collective-permute-start(bf16[256,256]{1,0:T(8,128)(2,1)S(1)} %pad_maximum_fusion.3), channel_id=1, source_target_pairs={{0,1},{1,2},{2,3},{3,4},{4,5},{5,6},{6,7},{7,8},{8,9},{9,10},{10,1... | collective-permute-start | bytes 393224 | tf_op jit(solution)/shard_map/ppermute | solution.py:323
  116.6 0.2 subtract_convert_fusion.1
  116.8 1.9 %collective-permute-start.13 = (bf16[2048,256]{1,0:T(8,128)(2,1)}, bf16[2048,256]{1,0:T(8,128)(2,1)}, u32[]{:S(2)}, u32[]{:S(2)}) collective-permute-start(bf16[2048,256]{1,0:T(8,128)(2,1)} %shard_map.51.own_w), channel_id=1, source_target_pairs={{0,64},{1,65},{2,66},{3,67},{4,68},{5,69},{6,70},{7,71},{8,72},{9,... | collective-permute-start | bytes 3145736 | tf_op jit(solution)/shard_map/ppermute | solution.py:44
  118.7 1.3 collective-permute-done.9
  120.1 1.0 fusion.60
  121.3 0.4 convolution_bitcast_fusion
  121.7 0.4 fusion.7
  122.1 0.4 fusion.2
  122.6 0.5 fusion.8
  123.2 1.9 %collective-permute-start.10 = (bf16[256,256]{1,0:T(8,128)(2,1)S(1)}, bf16[256,256]{1,0:T(8,128)(2,1)S(1)}, u32[]{:S(2)}, u32[]{:S(2)}) collective-permute-start(bf16[256,256]{1,0:T(8,128)(2,1)S(1)} %pad_maximum_fusion.4), channel_id=1, source_target_pairs={{1,0},{2,1},{3,2},{4,3},{5,4},{6,5},{7,6},{8,7},{9,8},{10,9},{11,1... | collective-permute-start | bytes 393224 | tf_op jit(solution)/shard_map/ppermute | solution.py:323
  125.1 0.6 fusion.4
  125.7 0.3 subtract_convert_fusion
  126.1 4.4 %shard_map.52.own_part = f32[128,2048]{1,0:T(8,128)S(1)} custom-call(s32[3]{0:T(128)S(1)} %pad_add_fusion.at, bf16[128,1024]{1,0:T(8,128)(2,1)S(1)} %copy_bitcast_fusion.grads, bf16[2048,1280]{1,0:T(8,128)(2,1)} %get-tuple-element.31.all_rows), custom_call_target="tpu_custom_call" | custom-call | flops 1073741824 | bytes 6291456 | tf_op jit(solution)/shard_map/pallas_call | solution.py:258
  130.4 1.7 %collective-permute-done.10 = bf16[256,256]{1,0:T(8,128)(2,1)S(1)} collective-permute-done((bf16[256,256]{1,0:T(8,128)(2,1)S(1)}, bf16[256,256]{1,0:T(8,128)(2,1)S(1)}, u32[]{:S(2)}, u32[]{:S(2)}) %collective-permute-start.10) | collective-permute-done | bytes 131104 | tf_op jit(solution)/shard_map/ppermute | solution.py:323
  132.2 2.2 %collective-permute-start.11 = (bf16[128,256]{1,0:T(8,128)(2,1)S(1)}, bf16[128,256]{1,0:T(8,128)(2,1)S(1)}, u32[]{:S(2)}, u32[]{:S(2)}) collective-permute-start(bf16[128,256]{1,0:T(8,128)(2,1)S(1)} %fusion.32), channel_id=1, source_target_pairs={{2,0},{3,1},{4,2},{5,3},{6,4},{7,5},{8,6},{9,7},{10,8},{11,9},{12,... | collective-permute-start | bytes 196616 | tf_op jit(solution)/shard_map/ppermute | solution.py:323
  134.4 4.4 %shard_map.53.other_part = f32[128,2048]{1,0:T(8,128)S(1)} custom-call(s32[3]{0:T(128)S(1)} %pad_add_fusion.at, bf16[128,1024]{1,0:T(8,128)(2,1)S(1)} %copy_bitcast_fusion.grads, bf16[2048,1280]{1,0:T(8,128)(2,1)} %collective-permute-done.12.all_rows), custom_call_target="tpu_custom_call" | custom-call | flops 1073741824 | bytes 6291456 | tf_op jit(solution)/shard_map/pallas_call | solution.py:258
  138.9 2.0 %collective-permute-done.11 = bf16[128,256]{1,0:T(8,128)(2,1)S(1)} collective-permute-done((bf16[128,256]{1,0:T(8,128)(2,1)S(1)}, bf16[128,256]{1,0:T(8,128)(2,1)S(1)}, u32[]{:S(2)}, u32[]{:S(2)}) %collective-permute-start.11) | collective-permute-done | bytes 65568 | tf_op jit(solution)/shard_map/ppermute | solution.py:323
  140.9 0.3 fusion.46
  141.4 3.0 %shard_map.54 = bf16[128,4096]{1,0:T(8,128)(2,1)} custom-call(s32[3]{0:T(128)S(1)} %pad_add_fusion.at, bf16[128,256]{1,0:T(8,128)(2,1)S(1)} %pad_maximum_fusion.6.pair_out, f32[128,2048]{1,0:T(8,128)S(1)} %shard_map.52.own_part, f32[128,2048]{1,0:T(8,128)S(1)} %shard_map.53.other_part, bf16[2048,256]{1,0:T(8,128)(2,1)S(1)} %copy-done.2, ...), custom_call_target="tpu_custom_call" | custom-call | tf_op jit(solution)/shard_map/pallas_call | solution.py:313
  (46 shorter events, 1.4 us)
Async XLA Ops:
  37.4 13.3 %collective-permute-start = (bf16[128,1280]{1,0:T(8,128)(2,1)S(1)}, bf16[128,1280]{1,0:T(8,128)(2,1)S(1)}, u32[]{:S(2)}, u32[]{:S(2)}) collective-permute-start(bf16[128,1280]{1,0:T(8,128)(2,1)S(1)} %all_gather.3.own), channel_id=1, source_target_pairs={{0,128},{1,129},{2,130},{3,131},{4,132},{5,133},{6,134},{7,135},{8... | collective-permute-start | bytes 983048 | tf_op jit(solution)/shard_map/ppermute | solution.py:40
  40.8 11.3 %collective-permute-start.1 = (bf16[128,1280]{1,0:T(8,128)(2,1)S(1)}, bf16[128,1280]{1,0:T(8,128)(2,1)S(1)}, u32[]{:S(2)}, u32[]{:S(2)}) collective-permute-start(bf16[128,1280]{1,0:T(8,128)(2,1)S(1)} %all_gather.3.own), channel_id=1, source_target_pairs={{0,256},{1,257},{2,258},{3,259},{4,260},{5,261},{6,262},{7,263},{8... | collective-permute-start | bytes 983048 | tf_op jit(solution)/shard_map/ppermute | solution.py:40
  45.5 10.7 %collective-permute-start.2 = (bf16[128,1280]{1,0:T(8,128)(2,1)S(1)}, bf16[128,1280]{1,0:T(8,128)(2,1)S(1)}, u32[]{:S(2)}, u32[]{:S(2)}) collective-permute-start(bf16[128,1280]{1,0:T(8,128)(2,1)S(1)} %all_gather.3.own), channel_id=1, source_target_pairs={{0,384},{1,385},{2,386},{3,387},{4,388},{5,389},{6,390},{7,391},{8... | collective-permute-start | bytes 983048 | tf_op jit(solution)/shard_map/ppermute | solution.py:40
  48.9 1.2 copy-start
  50.8 22.2 %copy-start.1 = (bf16[1,128,4096]{2,1,0:T(8,128)(2,1)S(1)}, bf16[1,128,4096]{2,1,0:T(8,128)(2,1)}, u32[]{:S(2)}) copy-start(bf16[1,128,4096]{2,1,0:T(8,128)(2,1)} %param.4) | copy-start | bytes 3145732
  52.1 0.7 copy-start.3
  56.2 0.7 copy-start.5
  56.9 1.0 copy-start.4
  57.9 1.0 copy-start.6
  59.0 34.9 %collective-permute-start.4 = (bf16[512,1280]{1,0:T(8,128)(2,1)S(1)}, bf16[512,1280]{1,0:T(8,128)(2,1)}, u32[]{:S(2)}, u32[]{:S(2)}) collective-permute-start(bf16[512,1280]{1,0:T(8,128)(2,1)S(1)} %shard_map.46.refs_0_), channel_id=1, source_target_pairs={{0,3},{1,0},{2,1},{3,2},{4,7},{5,4},{6,5},{7,6},{8,11},{9,8},{10,9... | collective-permute-start | bytes 3932168 | tf_op jit(solution)/shard_map/ppermute | solution.py:40
  61.7 35.0 %collective-permute-start.5 = (bf16[512,1280]{1,0:T(8,128)(2,1)S(1)}, bf16[512,1280]{1,0:T(8,128)(2,1)}, u32[]{:S(2)}, u32[]{:S(2)}) collective-permute-start(bf16[512,1280]{1,0:T(8,128)(2,1)S(1)} %shard_map.46.refs_0_), channel_id=1, source_target_pairs={{0,1},{1,2},{2,3},{3,0},{4,5},{5,6},{6,7},{7,4},{8,9},{9,10},{10,1... | collective-permute-start | bytes 3932168 | tf_op jit(solution)/shard_map/ppermute | solution.py:40
  66.0 30.7 %collective-permute-start.6 = (bf16[512,1280]{1,0:T(8,128)(2,1)S(1)}, bf16[512,1280]{1,0:T(8,128)(2,1)}, u32[]{:S(2)}, u32[]{:S(2)}) collective-permute-start(bf16[512,1280]{1,0:T(8,128)(2,1)S(1)} %shard_map.46.refs_0_), channel_id=1, source_target_pairs={{0,2},{1,3},{2,0},{3,1},{4,6},{5,7},{6,4},{7,5},{8,10},{9,11},{10,... | collective-permute-start | bytes 3932168 | tf_op jit(solution)/shard_map/ppermute | solution.py:40
  69.1 3.8 %collective-permute-start.3 = (bf16[128,2048]{1,0:T(8,128)(2,1)S(1)}, bf16[128,2048]{1,0:T(8,128)(2,1)S(1)}, u32[]{:S(2)}, u32[]{:S(2)}) collective-permute-start(bf16[128,2048]{1,0:T(8,128)(2,1)S(1)} %shard_map.47), channel_id=1, source_target_pairs={{0,64},{1,65},{2,66},{3,67},{4,68},{5,69},{6,70},{7,71},{8,72},{9,... | collective-permute-start | bytes 1572872 | tf_op jit(solution)/shard_map/ppermute | solution.py:44
  96.7 7.9 %copy-start.7 = (s32[1,128]{1,0:T(1,128)S(1)}, s32[1,128]{1,0:T(1,128)}, u32[]{:S(2)}) copy-start(s32[1,128]{1,0:T(1,128)} %param.5) | copy-start | bytes 1540
  100.3 4.5 %collective-permute-start.7 = (f32[128,1280]{1,0:T(8,128)S(1)}, f32[128,1280]{1,0:T(8,128)S(1)}, u32[]{:S(2)}, u32[]{:S(2)}) collective-permute-start(f32[128,1280]{1,0:T(8,128)S(1)} %get-tuple-element.28), channel_id=1, source_target_pairs={{0,64},{1,65},{2,66},{3,67},{4,68},{5,69},{6,70},{7,71},{8,72},{9,... | collective-permute-start | bytes 1966088 | tf_op jit(solution)/shard_map/ppermute | solution.py:44
  102.2 32.2 %collective-permute-start.12 = (bf16[2048,1280]{1,0:T(8,128)(2,1)}, bf16[2048,1280]{1,0:T(8,128)(2,1)}, u32[]{:S(2)}, u32[]{:S(2)}) collective-permute-start(bf16[2048,1280]{1,0:T(8,128)(2,1)} %get-tuple-element.31.all_rows), channel_id=1, source_target_pairs={{0,64},{1,65},{2,66},{3,67},{4,68},{5,69},{6,70},{7,71},{8,72},{9,... | collective-permute-start | bytes 15728648 | tf_op jit(solution)/shard_map/ppermute | solution.py:44
  105.5 7.7 %collective-permute-start.8 = (bf16[128,256]{1,0:T(8,128)(2,1)S(1)}, bf16[128,256]{1,0:T(8,128)(2,1)S(1)}, u32[]{:S(2)}, u32[]{:S(2)}) collective-permute-start(bf16[128,256]{1,0:T(8,128)(2,1)S(1)} %pad_maximum_fusion.5), channel_id=1, source_target_pairs={{0,2},{1,3},{2,4},{3,5},{4,6},{5,7},{6,8},{7,9},{8,10},{9,11},{10,... | collective-permute-start | bytes 196616 | tf_op jit(solution)/shard_map/ppermute | solution.py:323
  113.2 6.9 %collective-permute-start.9 = (bf16[256,256]{1,0:T(8,128)(2,1)S(1)}, bf16[256,256]{1,0:T(8,128)(2,1)S(1)}, u32[]{:S(2)}, u32[]{:S(2)}) collective-permute-start(bf16[256,256]{1,0:T(8,128)(2,1)S(1)} %pad_maximum_fusion.3), channel_id=1, source_target_pairs={{0,1},{1,2},{2,3},{3,4},{4,5},{5,6},{6,7},{7,8},{8,9},{9,10},{10,1... | collective-permute-start | bytes 393224 | tf_op jit(solution)/shard_map/ppermute | solution.py:323
  116.8 24.1 %collective-permute-start.13 = (bf16[2048,256]{1,0:T(8,128)(2,1)}, bf16[2048,256]{1,0:T(8,128)(2,1)}, u32[]{:S(2)}, u32[]{:S(2)}) collective-permute-start(bf16[2048,256]{1,0:T(8,128)(2,1)} %shard_map.51.own_w), channel_id=1, source_target_pairs={{0,64},{1,65},{2,66},{3,67},{4,68},{5,69},{6,70},{7,71},{8,72},{9,... | collective-permute-start | bytes 3145736 | tf_op jit(solution)/shard_map/ppermute | solution.py:44
  123.2 9.0 %collective-permute-start.10 = (bf16[256,256]{1,0:T(8,128)(2,1)S(1)}, bf16[256,256]{1,0:T(8,128)(2,1)S(1)}, u32[]{:S(2)}, u32[]{:S(2)}) collective-permute-start(bf16[256,256]{1,0:T(8,128)(2,1)S(1)} %pad_maximum_fusion.4), channel_id=1, source_target_pairs={{1,0},{2,1},{3,2},{4,3},{5,4},{6,5},{7,6},{8,7},{9,8},{10,9},{11,1... | collective-permute-start | bytes 393224 | tf_op jit(solution)/shard_map/ppermute | solution.py:323
  132.2 9.2 %copy-start.2 = (bf16[2048,256]{1,0:T(8,128)(2,1)S(1)}, bf16[2048,256]{1,0:T(8,128)(2,1)}, u32[]{:S(2)}) copy-start(bf16[2048,256]{1,0:T(8,128)(2,1)} %shard_map.51.own_w) | copy-start | bytes 3145732
  132.2 8.7 %collective-permute-start.11 = (bf16[128,256]{1,0:T(8,128)(2,1)S(1)}, bf16[128,256]{1,0:T(8,128)(2,1)S(1)}, u32[]{:S(2)}, u32[]{:S(2)}) collective-permute-start(bf16[128,256]{1,0:T(8,128)(2,1)S(1)} %fusion.32), channel_id=1, source_target_pairs={{2,0},{3,1},{4,2},{5,3},{6,4},{7,5},{8,6},{9,7},{10,8},{11,9},{12,... | collective-permute-start | bytes 196616 | tf_op jit(solution)/shard_map/ppermute | solution.py:323

commit v10 on v9

--- a/solution.py
+++ b/solution.py
@@ -108,19 +108,29 @@
     )(at, order, features, theirs)
 
 
-def pick_body(at, features, theirs_ref):
+def pick_body(at, features, theirs_ref, sems):
+    copies = []
     for x in range(NX):
         from_block = pl.ds(pl.multiple_of((x * NC + 1 - at[2]) * BLOCK, BLOCK), BLOCK)
-        theirs_ref[:, x * BLOCK : (x + 1) * BLOCK] = features[:, from_block]
+        copies.append(
+            pltpu.make_async_copy(
+                features.at[:, from_block], theirs_ref.at[:, pl.ds(x * BLOCK, BLOCK)], sems.at[x]
+            )
+        )
+        copies[-1].start()
+    for copy in copies:
+        copy.wait()
 
 
 def pick(at, features):
     return call(
         pick_body,
-        [SCALARS, WHOLE],
-        jax.ShapeDtypeStruct((features.shape[0], NX * BLOCK), jnp.bfloat16),
+        [SCALARS, LEFT],
+        pltpu.HBM((features.shape[0], NX * BLOCK), jnp.bfloat16),
         0, 2,
-    )(at, features)
+        out_specs=LEFT,
+        scratch_shapes=[pltpu.SemaphoreType.DMA((NX,))],
+    )(at, in_hbm(features))
 
 
 def stack_body(own, first, second, third, plane_ref):
@@ -133,7 +143,7 @@
     rows, columns = pieces[0].shape
     return call(
         stack_body, [WHOLE] * 4, pltpu.VMEM((4 * rows, columns), jnp.bfloat16), 0, 3
-    )(*[in_vmem(p) for p in pieces])
+    )(*[in_vmem(p) for p in pieces[:3]], in_hbm(pieces[3]))
 
 
 def in_hbm(array):
@@ -353,17 +363,17 @@
         w_qkv, "ctx", axis=0, tiled=True,
         axis_index_groups=[[z * NY + y for z in range(NZ)] for y in range(NY)],
     )
-    second, first, third = (hop(column, d, 0) for d in (2, 1, 3))
+    third, first, second = (hop(column, d, 0) for d in (3, 1, 2))
 
     at = jnp.stack([x_me, y_me, core]).astype(jnp.int32)
     order = order_matrix(y_me)
     plane, theirs = lax.optimization_barrier(
         (stack_plane([column, first, second, third]), pick(at, features))
     )
-    two, one, three = (hop(plane, d, 1) for d in (2, 1, 3))
+    three, one, two = (hop(plane, d, 1) for d in (3, 1, 2))
     arranged = arrange(at, order, features, swap_cores(theirs))
-    *sums, own_w = early_sums(arranged, [plane, three], (0, 3))
-    mine, theirs, own_w = late_sums(arranged, sums, [one, two], own_w, (1, 2))
+    *sums, own_w = early_sums(arranged, [plane, two], (0, 2))
+    mine, theirs, own_w = late_sums(arranged, sums, [one, three], own_w, (1, 3))
     projected = mine + swap_cores(theirs)
     pair_pre, query_pre = projected[:, HQ * HD :], projected[:, : HQ * HD]
 

time: 147 us -> 151 us (1.027); the launches traced: 144 us -> 151 us
  Pallas kernels: 24.2 us -> 42.2 us
  waiting for transfers between devices: 32.5 us -> 24.5 us
  local copies, waits for them, and re-layouts: 6.15 us -> 1.52 us
    pallas_call x1, Pallas kernels: 0.58 us -> 17.6 us  [pick(): call(pick_body, [SCALARS, LEFT], pltpu.HBM((features.shape[0], NX * BLOCK...]
    ppermute x6, waiting for transfers between devices: 23.7 us -> 16.1 us  [hop(): return lax.ppermute(block, ALL, route(move))]
    unnamed x19 -> x9, local copies, waits for them, and re-layouts: 5.91 us -> 1.28 us
  transfers between devices with their start and end apart: 14 -> 14, of which waited for: 8 -> 8; matrix products, arithmetic and copies ran while one was open for 5% -> 4% of each run, Pallas kernels for 12% -> 23%
where the time goes in v10:
time: 151 us
  Pallas kernels  42.2 us (28%)
  starting transfers between devices  38.7 us (26%)
  blocking collectives  37.4 us (25%)
  waiting for transfers between devices  24.5 us (16%)
  matrix products  3.36 us (2%)
  other arithmetic  2.23 us (1%)
  local copies, waits for them, and re-layouts  1.52 us (1%)
    all_gather x1, blocking collectives, local(): lax.all_gather(w_qkv, 'ctx', axis=0, tiled=True, axis_index_groups=[[z *...  37.4 us
    ppermute x6, starting transfers between devices, hop(): return lax.ppermute(block, ALL, route(move))  20.5 us
    pallas_call x1, Pallas kernels, pick(): call(pick_body, [SCALARS, LEFT], pltpu.HBM((features.shape[0], NX * BLOCK...  17.6 us
    ppermute x6, waiting for transfers between devices, hop(): return lax.ppermute(block, ALL, route(move))  16.1 us
    ppermute x4, starting transfers between devices, shifted(): lax.ppermute(block, axis, [(i - distance, i) for i in devices if i - dist...  10 us
    pallas_call x2, Pallas kernels, query_part_of(): call(functools.partial(query_part_body, flip), [SCALARS, WHOLE, LEFT], pl...  8.75 us
    ppermute x4, starting transfers between devices, swap_cores(): return lax.ppermute(block, ALL, route(lambda x, c, z, y: (x, 1 - c, z, y)))  8.17 us
    ppermute x4, waiting for transfers between devices, shifted(): lax.ppermute(block, axis, [(i - distance, i) for i in devices if i - dist...  6.51 us
  transfers between devices with their start and end apart: 14, of which 8 were waited for; matrix products, arithmetic and copies ran while one was open for 4% of the time, Pallas kernels for 23%

profile of v10, /device:TPU:24, one launch (start us, length us, event | category | flops | bytes accessed | tf_op | source)
XLA Modules:
  0.0 150.5 jit_solution(4697453194533882982)
XLA Ops:
  0.0 37.4 %all_gather.3.own = bf16[128,1280]{1,0:T(8,128)(2,1)S(1)} all-gather(bf16[8,1280]{1,0:T(8,128)(2,1)} %param.7), channel_id=1, replica_groups={{0,4,8,12,16,20,24,28,32,36,40,44,48,52,56,60},{1,5,9,13,17,21,25,29,33..., dimensions={0}, use_global_device_ids=true | all-gather | bytes 348160 | tf_op jit(solution)/shard_map/all_gather | solution.py:362
  37.4 3.4 %collective-permute-start = (bf16[128,1280]{1,0:T(8,128)(2,1)S(1)}, bf16[128,1280]{1,0:T(8,128)(2,1)S(1)}, u32[]{:S(2)}, u32[]{:S(2)}) collective-permute-start(bf16[128,1280]{1,0:T(8,128)(2,1)S(1)} %all_gather.3.own), channel_id=1, source_target_pairs={{0,128},{1,129},{2,130},{3,131},{4,132},{5,133},{6,134},{7,135},{8... | collective-permute-start | bytes 983048 | tf_op jit(solution)/shard_map/ppermute | solution.py:40
  40.8 4.6 %collective-permute-start.1 = (bf16[128,1280]{1,0:T(8,128)(2,1)S(1)}, bf16[128,1280]{1,0:T(8,128)(2,1)S(1)}, u32[]{:S(2)}, u32[]{:S(2)}) collective-permute-start(bf16[128,1280]{1,0:T(8,128)(2,1)S(1)} %all_gather.3.own), channel_id=1, source_target_pairs={{0,256},{1,257},{2,258},{3,259},{4,260},{5,261},{6,262},{7,263},{8... | collective-permute-start | bytes 983048 | tf_op jit(solution)/shard_map/ppermute | solution.py:40
  45.5 3.3 %collective-permute-start.2 = (bf16[128,1280]{1,0:T(8,128)(2,1)S(1)}, bf16[128,1280]{1,0:T(8,128)(2,1)}, u32[]{:S(2)}, u32[]{:S(2)}) collective-permute-start(bf16[128,1280]{1,0:T(8,128)(2,1)S(1)} %all_gather.3.own), channel_id=1, source_target_pairs={{0,384},{1,385},{2,386},{3,387},{4,388},{5,389},{6,390},{7,391},{8... | collective-permute-start | bytes 983048 | tf_op jit(solution)/shard_map/ppermute | solution.py:40
  48.9 17.6 %shard_map.47 = bf16[128,2048]{1,0:T(8,128)(2,1)} custom-call(s32[3]{0:T(128)S(1)} %pad_add_fusion.at, bf16[128,4096]{1,0:T(8,128)(2,1)} %bitcast.61), custom_call_target="tpu_custom_call" | custom-call | bytes 2097152 | tf_op jit(solution)/shard_map/pallas_call | solution.py:126
  66.6 1.1 shard_map.46.refs_0_
  67.7 3.1 %collective-permute-start.4 = (bf16[512,1280]{1,0:T(8,128)(2,1)S(1)}, bf16[512,1280]{1,0:T(8,128)(2,1)}, u32[]{:S(2)}, u32[]{:S(2)}) collective-permute-start(bf16[512,1280]{1,0:T(8,128)(2,1)S(1)} %shard_map.46.refs_0_), channel_id=1, source_target_pairs={{0,2},{1,3},{2,0},{3,1},{4,6},{5,7},{6,4},{7,5},{8,10},{9,11},{10,... | collective-permute-start | bytes 3932168 | tf_op jit(solution)/shard_map/ppermute | solution.py:40
  70.9 4.1 %collective-permute-start.5 = (bf16[512,1280]{1,0:T(8,128)(2,1)S(1)}, bf16[512,1280]{1,0:T(8,128)(2,1)}, u32[]{:S(2)}, u32[]{:S(2)}) collective-permute-start(bf16[512,1280]{1,0:T(8,128)(2,1)S(1)} %shard_map.46.refs_0_), channel_id=1, source_target_pairs={{0,1},{1,2},{2,3},{3,0},{4,5},{5,6},{6,7},{7,4},{8,9},{9,10},{10,1... | collective-permute-start | bytes 3932168 | tf_op jit(solution)/shard_map/ppermute | solution.py:40
  75.0 1.9 %collective-permute-start.6 = (bf16[512,1280]{1,0:T(8,128)(2,1)S(1)}, bf16[512,1280]{1,0:T(8,128)(2,1)}, u32[]{:S(2)}, u32[]{:S(2)}) collective-permute-start(bf16[512,1280]{1,0:T(8,128)(2,1)S(1)} %shard_map.46.refs_0_), channel_id=1, source_target_pairs={{0,3},{1,0},{2,1},{3,2},{4,7},{5,4},{6,5},{7,6},{8,11},{9,8},{10,9... | collective-permute-start | bytes 3932168 | tf_op jit(solution)/shard_map/ppermute | solution.py:40
  76.9 1.1 copy.8
  78.1 1.9 %collective-permute-start.3 = (bf16[128,2048]{1,0:T(8,128)(2,1)}, bf16[128,2048]{1,0:T(8,128)(2,1)S(1)}, u32[]{:S(2)}, u32[]{:S(2)}) collective-permute-start(bf16[128,2048]{1,0:T(8,128)(2,1)} %shard_map.47), channel_id=1, source_target_pairs={{0,64},{1,65},{2,66},{3,67},{4,68},{5,69},{6,70},{7,71},{8,72},{9,... | collective-permute-start | bytes 1572872 | tf_op jit(solution)/shard_map/ppermute | solution.py:44
  80.0 0.2 fusion.21.order
  80.2 1.9 %collective-permute-done.3.theirs = bf16[128,2048]{1,0:T(8,128)(2,1)S(1)} collective-permute-done((bf16[128,2048]{1,0:T(8,128)(2,1)}, bf16[128,2048]{1,0:T(8,128)(2,1)S(1)}, u32[]{:S(2)}, u32[]{:S(2)}) %collective-permute-start.3) | collective-permute-done | bytes 524320 | tf_op jit(solution)/shard_map/ppermute | solution.py:44
  82.1 1.9 %shard_map.48.arranged = bf16[1024,512]{1,0:T(8,128)(2,1)S(1)} custom-call(s32[3]{0:T(128)S(1)} %pad_add_fusion.at, bf16[512,512]{1,0:T(8,128)(2,1)S(1)} %fusion.21.order, bf16[128,4096]{1,0:T(8,128)(2,1)S(1)} %bitcast.62, bf16[128,2048]{1,0:T(8,128)(2,1)S(1)} %collective-permute-done.3.theirs), custom_call_target="tpu_custom_call" | custom-call | flops 536870912 | bytes 4194304 | tf_op jit(solution)/shard_map/pallas_call | solution.py:103
  84.0 5.0 %collective-permute-done.4.refs_1_ = bf16[512,1280]{1,0:T(8,128)(2,1)} collective-permute-done((bf16[512,1280]{1,0:T(8,128)(2,1)S(1)}, bf16[512,1280]{1,0:T(8,128)(2,1)}, u32[]{:S(2)}, u32[]{:S(2)}) %collective-permute-start.4) | collective-permute-done | bytes 1310752 | tf_op jit(solution)/shard_map/ppermute | solution.py:40
  88.9 2.8 %shard_map.49 = (f32[128,1280]{1,0:T(8,128)S(1)}, f32[128,1280]{1,0:T(8,128)S(1)}, bf16[2048,1280]{1,0:T(8,128)(2,1)}) custom-call(bf16[1024,512]{1,0:T(8,128)(2,1)S(1)} %shard_map.48.arranged, bf16[512,1280]{1,0:T(8,128)(2,1)S(1)} %shard_map.46.refs_0_, bf16[512,1280]{1,0:T(8,128)(2,1)} %collective-permute-done.4.refs_1_), custom_call_target="tpu_custom_call" | custom-call | flops 671088640 | bytes 4194304 | tf_op jit(solution)/shard_map/pallas_call | solution.py:179
  91.7 8.7 %collective-permute-done.5.refs_0_ = bf16[512,1280]{1,0:T(8,128)(2,1)} collective-permute-done((bf16[512,1280]{1,0:T(8,128)(2,1)S(1)}, bf16[512,1280]{1,0:T(8,128)(2,1)}, u32[]{:S(2)}, u32[]{:S(2)}) %collective-permute-start.5) | collective-permute-done | bytes 1310752 | tf_op jit(solution)/shard_map/ppermute | solution.py:40
  100.5 2.4 %collective-permute-done.6.refs_1_ = bf16[512,1280]{1,0:T(8,128)(2,1)} collective-permute-done((bf16[512,1280]{1,0:T(8,128)(2,1)S(1)}, bf16[512,1280]{1,0:T(8,128)(2,1)}, u32[]{:S(2)}, u32[]{:S(2)}) %collective-permute-start.6) | collective-permute-done | bytes 1310752 | tf_op jit(solution)/shard_map/ppermute | solution.py:40
  102.9 3.5 %shard_map.50 = (f32[128,1280]{1,0:T(8,128)S(1)}, f32[128,1280]{1,0:T(8,128)S(1)}, bf16[2048,1280]{1,0:T(8,128)(2,1)}) custom-call(bf16[1024,512]{1,0:T(8,128)(2,1)S(1)} %shard_map.48.arranged, f32[128,1280]{1,0:T(8,128)S(1)} %get-tuple-element.24.mine, f32[128,1280]{1,0:T(8,128)S(1)} %get-tuple-element.25.theirs, ...), custom_call_target="tpu_custom_call", output_to_operand_aliasing={{2}: (5, {})} | custom-call | flops 671088640 | bytes 4194304 | tf_op jit(solution)/shard_map/pallas_call | solution.py:214
  106.4 1.9 %collective-permute-start.7 = (f32[128,1280]{1,0:T(8,128)S(1)}, f32[128,1280]{1,0:T(8,128)S(1)}, u32[]{:S(2)}, u32[]{:S(2)}) collective-permute-start(f32[128,1280]{1,0:T(8,128)S(1)} %get-tuple-element.28), channel_id=1, source_target_pairs={{0,64},{1,65},{2,66},{3,67},{4,68},{5,69},{6,70},{7,71},{8,72},{9,... | collective-permute-start | bytes 1966088 | tf_op jit(solution)/shard_map/ppermute | solution.py:44
  108.3 2.4 %collective-permute-start.12 = (bf16[2048,1280]{1,0:T(8,128)(2,1)}, bf16[2048,1280]{1,0:T(8,128)(2,1)}, u32[]{:S(2)}, u32[]{:S(2)}) collective-permute-start(bf16[2048,1280]{1,0:T(8,128)(2,1)} %get-tuple-element.31.all_rows), channel_id=1, source_target_pairs={{0,64},{1,65},{2,66},{3,67},{4,68},{5,69},{6,70},{7,71},{8,72},{9,... | collective-permute-start | bytes 15728648 | tf_op jit(solution)/shard_map/ppermute | solution.py:44
  110.8 0.1 compare_and_fusion
  111.2 0.3 fusion.37
  111.6 2.4 %collective-permute-start.8 = (bf16[128,256]{1,0:T(8,128)(2,1)S(1)}, bf16[128,256]{1,0:T(8,128)(2,1)S(1)}, u32[]{:S(2)}, u32[]{:S(2)}) collective-permute-start(bf16[128,256]{1,0:T(8,128)(2,1)S(1)} %pad_maximum_fusion.5), channel_id=1, source_target_pairs={{0,2},{1,3},{2,4},{3,5},{4,6},{5,7},{6,8},{7,9},{8,10},{9,11},{10,... | collective-permute-start | bytes 196616 | tf_op jit(solution)/shard_map/ppermute | solution.py:333
  114.0 0.2 fusion.57
  114.2 3.5 %shard_map.51.own_w = bf16[2048,256]{1,0:T(8,128)(2,1)} custom-call(s32[3]{0:T(128)S(1)} %pad_add_fusion.at, bf16[2048,1280]{1,0:T(8,128)(2,1)} %get-tuple-element.31.all_rows), custom_call_target="tpu_custom_call" | custom-call | flops 536870912 | bytes 3145728 | tf_op jit(solution)/shard_map/pallas_call | solution.py:297
  117.8 1.5 %collective-permute-done.8 = bf16[128,256]{1,0:T(8,128)(2,1)S(1)} collective-permute-done((bf16[128,256]{1,0:T(8,128)(2,1)S(1)}, bf16[128,256]{1,0:T(8,128)(2,1)S(1)}, u32[]{:S(2)}, u32[]{:S(2)}) %collective-permute-start.8) | collective-permute-done | bytes 65568 | tf_op jit(solution)/shard_map/ppermute | solution.py:333
  119.3 2.7 %collective-permute-start.9 = (bf16[256,256]{1,0:T(8,128)(2,1)S(1)}, bf16[256,256]{1,0:T(8,128)(2,1)S(1)}, u32[]{:S(2)}, u32[]{:S(2)}) collective-permute-start(bf16[256,256]{1,0:T(8,128)(2,1)S(1)} %pad_maximum_fusion.3), channel_id=1, source_target_pairs={{0,1},{1,2},{2,3},{3,4},{4,5},{5,6},{6,7},{7,8},{8,9},{9,10},{10,1... | collective-permute-start | bytes 393224 | tf_op jit(solution)/shard_map/ppermute | solution.py:333
  122.0 0.2 subtract_convert_fusion.1
  122.2 1.9 %collective-permute-start.13 = (bf16[2048,256]{1,0:T(8,128)(2,1)}, bf16[2048,256]{1,0:T(8,128)(2,1)}, u32[]{:S(2)}, u32[]{:S(2)}) collective-permute-start(bf16[2048,256]{1,0:T(8,128)(2,1)} %shard_map.51.own_w), channel_id=1, source_target_pairs={{0,64},{1,65},{2,66},{3,67},{4,68},{5,69},{6,70},{7,71},{8,72},{9,... | collective-permute-start | bytes 3145736 | tf_op jit(solution)/shard_map/ppermute | solution.py:44
  124.2 2.0 %collective-permute-done.9 = bf16[256,256]{1,0:T(8,128)(2,1)S(1)} collective-permute-done((bf16[256,256]{1,0:T(8,128)(2,1)S(1)}, bf16[256,256]{1,0:T(8,128)(2,1)S(1)}, u32[]{:S(2)}, u32[]{:S(2)}) %collective-permute-start.9) | collective-permute-done | bytes 131104 | tf_op jit(solution)/shard_map/ppermute | solution.py:333
  126.2 1.0 fusion.60
  127.2 0.2 fusion.23
  127.4 0.4 convolution_bitcast_fusion
  127.9 0.4 fusion.7
  128.2 0.4 fusion.2
  128.7 0.5 fusion.8
  129.3 2.7 %collective-permute-start.10 = (bf16[256,256]{1,0:T(8,128)(2,1)S(1)}, bf16[256,256]{1,0:T(8,128)(2,1)S(1)}, u32[]{:S(2)}, u32[]{:S(2)}) collective-permute-start(bf16[256,256]{1,0:T(8,128)(2,1)S(1)} %pad_maximum_fusion.4), channel_id=1, source_target_pairs={{1,0},{2,1},{3,2},{4,3},{5,4},{6,5},{7,6},{8,7},{9,8},{10,9},{11,1... | collective-permute-start | bytes 393224 | tf_op jit(solution)/shard_map/ppermute | solution.py:333
  132.0 0.6 fusion.4
  132.5 0.3 subtract_convert_fusion
  132.8 0.1 copy_bitcast_fusion.grads
  132.9 4.4 %shard_map.52.own_part = f32[128,2048]{1,0:T(8,128)S(1)} custom-call(s32[3]{0:T(128)S(1)} %pad_add_fusion.at, bf16[128,1024]{1,0:T(8,128)(2,1)S(1)} %copy_bitcast_fusion.grads, bf16[2048,1280]{1,0:T(8,128)(2,1)} %get-tuple-element.31.all_rows), custom_call_target="tpu_custom_call" | custom-call | flops 1073741824 | bytes 6291456 | tf_op jit(solution)/shard_map/pallas_call | solution.py:268
  137.3 1.0 collective-permute-done.10
  138.3 2.2 %collective-permute-start.11 = (bf16[128,256]{1,0:T(8,128)(2,1)S(1)}, bf16[128,256]{1,0:T(8,128)(2,1)S(1)}, u32[]{:S(2)}, u32[]{:S(2)}) collective-permute-start(bf16[128,256]{1,0:T(8,128)(2,1)S(1)} %fusion.32), channel_id=1, source_target_pairs={{2,0},{3,1},{4,2},{5,3},{6,4},{7,5},{8,6},{9,7},{10,8},{11,9},{12,... | collective-permute-start | bytes 196616 | tf_op jit(solution)/shard_map/ppermute | solution.py:333
  140.6 4.4 %shard_map.53.other_part = f32[128,2048]{1,0:T(8,128)S(1)} custom-call(s32[3]{0:T(128)S(1)} %pad_add_fusion.at, bf16[128,1024]{1,0:T(8,128)(2,1)S(1)} %copy_bitcast_fusion.grads, bf16[2048,1280]{1,0:T(8,128)(2,1)} %collective-permute-done.12.all_rows), custom_call_target="tpu_custom_call" | custom-call | flops 1073741824 | bytes 6291456 | tf_op jit(solution)/shard_map/pallas_call | solution.py:268
  145.0 2.0 %collective-permute-done.11 = bf16[128,256]{1,0:T(8,128)(2,1)S(1)} collective-permute-done((bf16[128,256]{1,0:T(8,128)(2,1)S(1)}, bf16[128,256]{1,0:T(8,128)(2,1)S(1)}, u32[]{:S(2)}, u32[]{:S(2)}) %collective-permute-start.11) | collective-permute-done | bytes 65568 | tf_op jit(solution)/shard_map/ppermute | solution.py:333
  147.0 0.3 fusion.46
  147.5 3.0 %shard_map.54 = bf16[128,4096]{1,0:T(8,128)(2,1)} custom-call(s32[3]{0:T(128)S(1)} %pad_add_fusion.at, bf16[128,256]{1,0:T(8,128)(2,1)S(1)} %pad_maximum_fusion.6.pair_out, f32[128,2048]{1,0:T(8,128)S(1)} %shard_map.52.own_part, f32[128,2048]{1,0:T(8,128)S(1)} %shard_map.53.other_part, bf16[2048,256]{1,0:T(8,128)(2,1)S(1)} %copy-done.1, ...), custom_call_target="tpu_custom_call" | custom-call | tf_op jit(solution)/shard_map/pallas_call | solution.py:323
  (36 shorter events, 0.7 us)
Async XLA Ops:
  37.4 29.1 %collective-permute-start = (bf16[128,1280]{1,0:T(8,128)(2,1)S(1)}, bf16[128,1280]{1,0:T(8,128)(2,1)S(1)}, u32[]{:S(2)}, u32[]{:S(2)}) collective-permute-start(bf16[128,1280]{1,0:T(8,128)(2,1)S(1)} %all_gather.3.own), channel_id=1, source_target_pairs={{0,128},{1,129},{2,130},{3,131},{4,132},{5,133},{6,134},{7,135},{8... | collective-permute-start | bytes 983048 | tf_op jit(solution)/shard_map/ppermute | solution.py:40
  40.8 25.7 %collective-permute-start.1 = (bf16[128,1280]{1,0:T(8,128)(2,1)S(1)}, bf16[128,1280]{1,0:T(8,128)(2,1)S(1)}, u32[]{:S(2)}, u32[]{:S(2)}) collective-permute-start(bf16[128,1280]{1,0:T(8,128)(2,1)S(1)} %all_gather.3.own), channel_id=1, source_target_pairs={{0,256},{1,257},{2,258},{3,259},{4,260},{5,261},{6,262},{7,263},{8... | collective-permute-start | bytes 983048 | tf_op jit(solution)/shard_map/ppermute | solution.py:40
  45.5 21.1 %collective-permute-start.2 = (bf16[128,1280]{1,0:T(8,128)(2,1)S(1)}, bf16[128,1280]{1,0:T(8,128)(2,1)}, u32[]{:S(2)}, u32[]{:S(2)}) collective-permute-start(bf16[128,1280]{1,0:T(8,128)(2,1)S(1)} %all_gather.3.own), channel_id=1, source_target_pairs={{0,384},{1,385},{2,386},{3,387},{4,388},{5,389},{6,390},{7,391},{8... | collective-permute-start | bytes 983048 | tf_op jit(solution)/shard_map/ppermute | solution.py:40
  66.5 15.6 %copy-start = (bf16[1,128,4096]{2,1,0:T(8,128)(2,1)S(1)}, bf16[1,128,4096]{2,1,0:T(8,128)(2,1)}, u32[]{:S(2)}) copy-start(bf16[1,128,4096]{2,1,0:T(8,128)(2,1)} %param.4) | copy-start | bytes 3145732
  67.7 21.2 %collective-permute-start.4 = (bf16[512,1280]{1,0:T(8,128)(2,1)S(1)}, bf16[512,1280]{1,0:T(8,128)(2,1)}, u32[]{:S(2)}, u32[]{:S(2)}) collective-permute-start(bf16[512,1280]{1,0:T(8,128)(2,1)S(1)} %shard_map.46.refs_0_), channel_id=1, source_target_pairs={{0,2},{1,3},{2,0},{3,1},{4,6},{5,7},{6,4},{7,5},{8,10},{9,11},{10,... | collective-permute-start | bytes 3932168 | tf_op jit(solution)/shard_map/ppermute | solution.py:40
  70.9 29.6 %collective-permute-start.5 = (bf16[512,1280]{1,0:T(8,128)(2,1)S(1)}, bf16[512,1280]{1,0:T(8,128)(2,1)}, u32[]{:S(2)}, u32[]{:S(2)}) collective-permute-start(bf16[512,1280]{1,0:T(8,128)(2,1)S(1)} %shard_map.46.refs_0_), channel_id=1, source_target_pairs={{0,1},{1,2},{2,3},{3,0},{4,5},{5,6},{6,7},{7,4},{8,9},{9,10},{10,1... | collective-permute-start | bytes 3932168 | tf_op jit(solution)/shard_map/ppermute | solution.py:40
  75.0 27.9 %collective-permute-start.6 = (bf16[512,1280]{1,0:T(8,128)(2,1)S(1)}, bf16[512,1280]{1,0:T(8,128)(2,1)}, u32[]{:S(2)}, u32[]{:S(2)}) collective-permute-start(bf16[512,1280]{1,0:T(8,128)(2,1)S(1)} %shard_map.46.refs_0_), channel_id=1, source_target_pairs={{0,3},{1,0},{2,1},{3,2},{4,7},{5,4},{6,5},{7,6},{8,11},{9,8},{10,9... | collective-permute-start | bytes 3932168 | tf_op jit(solution)/shard_map/ppermute | solution.py:40
  78.1 4.0 %collective-permute-start.3 = (bf16[128,2048]{1,0:T(8,128)(2,1)}, bf16[128,2048]{1,0:T(8,128)(2,1)S(1)}, u32[]{:S(2)}, u32[]{:S(2)}) collective-permute-start(bf16[128,2048]{1,0:T(8,128)(2,1)} %shard_map.47), channel_id=1, source_target_pairs={{0,64},{1,65},{2,66},{3,67},{4,68},{5,69},{6,70},{7,71},{8,72},{9,... | collective-permute-start | bytes 1572872 | tf_op jit(solution)/shard_map/ppermute | solution.py:44
  102.9 7.9 %copy-start.2 = (s32[1,128]{1,0:T(1,128)S(1)}, s32[1,128]{1,0:T(1,128)}, u32[]{:S(2)}) copy-start(s32[1,128]{1,0:T(1,128)} %param.5) | copy-start | bytes 1540
  106.4 4.5 %collective-permute-start.7 = (f32[128,1280]{1,0:T(8,128)S(1)}, f32[128,1280]{1,0:T(8,128)S(1)}, u32[]{:S(2)}, u32[]{:S(2)}) collective-permute-start(f32[128,1280]{1,0:T(8,128)S(1)} %get-tuple-element.28), channel_id=1, source_target_pairs={{0,64},{1,65},{2,66},{3,67},{4,68},{5,69},{6,70},{7,71},{8,72},{9,... | collective-permute-start | bytes 1966088 | tf_op jit(solution)/shard_map/ppermute | solution.py:44
  108.3 32.2 %collective-permute-start.12 = (bf16[2048,1280]{1,0:T(8,128)(2,1)}, bf16[2048,1280]{1,0:T(8,128)(2,1)}, u32[]{:S(2)}, u32[]{:S(2)}) collective-permute-start(bf16[2048,1280]{1,0:T(8,128)(2,1)} %get-tuple-element.31.all_rows), channel_id=1, source_target_pairs={{0,64},{1,65},{2,66},{3,67},{4,68},{5,69},{6,70},{7,71},{8,72},{9,... | collective-permute-start | bytes 15728648 | tf_op jit(solution)/shard_map/ppermute | solution.py:44
  111.6 7.7 %collective-permute-start.8 = (bf16[128,256]{1,0:T(8,128)(2,1)S(1)}, bf16[128,256]{1,0:T(8,128)(2,1)S(1)}, u32[]{:S(2)}, u32[]{:S(2)}) collective-permute-start(bf16[128,256]{1,0:T(8,128)(2,1)S(1)} %pad_maximum_fusion.5), channel_id=1, source_target_pairs={{0,2},{1,3},{2,4},{3,5},{4,6},{5,7},{6,8},{7,9},{8,10},{9,11},{10,... | collective-permute-start | bytes 196616 | tf_op jit(solution)/shard_map/ppermute | solution.py:333
  119.3 6.9 %collective-permute-start.9 = (bf16[256,256]{1,0:T(8,128)(2,1)S(1)}, bf16[256,256]{1,0:T(8,128)(2,1)S(1)}, u32[]{:S(2)}, u32[]{:S(2)}) collective-permute-start(bf16[256,256]{1,0:T(8,128)(2,1)S(1)} %pad_maximum_fusion.3), channel_id=1, source_target_pairs={{0,1},{1,2},{2,3},{3,4},{4,5},{5,6},{6,7},{7,8},{8,9},{9,10},{10,1... | collective-permute-start | bytes 393224 | tf_op jit(solution)/shard_map/ppermute | solution.py:333
  122.2 24.8 %collective-permute-start.13 = (bf16[2048,256]{1,0:T(8,128)(2,1)}, bf16[2048,256]{1,0:T(8,128)(2,1)}, u32[]{:S(2)}, u32[]{:S(2)}) collective-permute-start(bf16[2048,256]{1,0:T(8,128)(2,1)} %shard_map.51.own_w), channel_id=1, source_target_pairs={{0,64},{1,65},{2,66},{3,67},{4,68},{5,69},{6,70},{7,71},{8,72},{9,... | collective-permute-start | bytes 3145736 | tf_op jit(solution)/shard_map/ppermute | solution.py:44
  129.3 9.0 %collective-permute-start.10 = (bf16[256,256]{1,0:T(8,128)(2,1)S(1)}, bf16[256,256]{1,0:T(8,128)(2,1)S(1)}, u32[]{:S(2)}, u32[]{:S(2)}) collective-permute-start(bf16[256,256]{1,0:T(8,128)(2,1)S(1)} %pad_maximum_fusion.4), channel_id=1, source_target_pairs={{1,0},{2,1},{3,2},{4,3},{5,4},{6,5},{7,6},{8,7},{9,8},{10,9},{11,1... | collective-permute-start | bytes 393224 | tf_op jit(solution)/shard_map/ppermute | solution.py:333
  138.3 9.2 %copy-start.1 = (bf16[2048,256]{1,0:T(8,128)(2,1)S(1)}, bf16[2048,256]{1,0:T(8,128)(2,1)}, u32[]{:S(2)}) copy-start(bf16[2048,256]{1,0:T(8,128)(2,1)} %shard_map.51.own_w) | copy-start | bytes 3145732
  138.3 8.7 %collective-permute-start.11 = (bf16[128,256]{1,0:T(8,128)(2,1)S(1)}, bf16[128,256]{1,0:T(8,128)(2,1)S(1)}, u32[]{:S(2)}, u32[]{:S(2)}) collective-permute-start(bf16[128,256]{1,0:T(8,128)(2,1)S(1)} %fusion.32), channel_id=1, source_target_pairs={{2,0},{3,1},{4,2},{5,3},{6,4},{7,5},{8,6},{9,7},{10,8},{11,9},{12,... | collective-permute-start | bytes 196616 | tf_op jit(solution)/shard_map/ppermute | solution.py:333

commit v11 on v9

--- a/solution.py
+++ b/solution.py
@@ -133,7 +133,7 @@
     rows, columns = pieces[0].shape
     return call(
         stack_body, [WHOLE] * 4, pltpu.VMEM((4 * rows, columns), jnp.bfloat16), 0, 3
-    )(*[in_vmem(p) for p in pieces])
+    )(*[in_vmem(p) for p in pieces[:2]], *[in_hbm(p) for p in pieces[2:]])
 
 
 def in_hbm(array):
@@ -353,17 +353,17 @@
         w_qkv, "ctx", axis=0, tiled=True,
         axis_index_groups=[[z * NY + y for z in range(NZ)] for y in range(NY)],
     )
-    second, first, third = (hop(column, d, 0) for d in (2, 1, 3))
+    third, first, second = (hop(column, d, 0) for d in (3, 1, 2))
 
     at = jnp.stack([x_me, y_me, core]).astype(jnp.int32)
     order = order_matrix(y_me)
     plane, theirs = lax.optimization_barrier(
         (stack_plane([column, first, second, third]), pick(at, features))
     )
-    two, one, three = (hop(plane, d, 1) for d in (2, 1, 3))
+    three, one, two = (hop(plane, d, 1) for d in (3, 1, 2))
     arranged = arrange(at, order, features, swap_cores(theirs))
-    *sums, own_w = early_sums(arranged, [plane, three], (0, 3))
-    mine, theirs, own_w = late_sums(arranged, sums, [one, two], own_w, (1, 2))
+    *sums, own_w = early_sums(arranged, [plane, two], (0, 2))
+    mine, theirs, own_w = late_sums(arranged, sums, [one, three], own_w, (1, 3))
     projected = mine + swap_cores(theirs)
     pair_pre, query_pre = projected[:, HQ * HD :], projected[:, : HQ * HD]
 

time: 147 us -> 154 us (1.048)
  the two profiles are of different devices: /device:TPU:24 before, /device:TPU:26 now
where the time goes in v11:
time: 154 us; the launch traced here: 153 us
  waiting for transfers between devices  46.6 us (30%)
  blocking collectives  37.4 us (24%)
  starting transfers between devices  34.4 us (22%)
  Pallas kernels  25.2 us (16%)
  local copies, waits for them, and re-layouts  3.47 us (2%)
  matrix products  3.36 us (2%)
  other arithmetic  2.23 us (1%)
    all_gather x1, blocking collectives, local(): lax.all_gather(w_qkv, 'ctx', axis=0, tiled=True, axis_index_groups=[[z *...  37.4 us
    ppermute x6, waiting for transfers between devices, hop(): return lax.ppermute(block, ALL, route(move))  36.3 us
    ppermute x6, starting transfers between devices, hop(): return lax.ppermute(block, ALL, route(move))  18.2 us
    pallas_call x2, Pallas kernels, query_part_of(): call(functools.partial(query_part_body, flip), [SCALARS, WHOLE, LEFT], pl...  8.75 us
    ppermute x4, waiting for transfers between devices, shifted(): lax.ppermute(block, axis, [(i - distance, i) for i in devices if i - dist...  8.57 us
    ppermute x4, starting transfers between devices, swap_cores(): return lax.ppermute(block, ALL, route(lambda x, c, z, y: (x, 1 - c, z, y)))  8.17 us
    ppermute x4, starting transfers between devices, shifted(): lax.ppermute(block, axis, [(i - distance, i) for i in devices if i - dist...  7.99 us
    pallas_call x1, Pallas kernels, late_sums(): call(functools.partial(late_body, steps), [WHOLE] * len(operands) + [LEFT...  3.52 us
  transfers between devices with their start and end apart: 14, of which 9 were waited for; matrix products, arithmetic and copies ran while one was open for 4% of the time, Pallas kernels for 11%

profile of v11, /device:TPU:26, one launch (start us, length us, event | category | flops | bytes accessed | tf_op | source)
XLA Modules:
  0.0 153.2 jit_solution(15206661026767329875)
XLA Ops:
  0.0 37.4 %all_gather.3.own = bf16[128,1280]{1,0:T(8,128)(2,1)S(1)} all-gather(bf16[8,1280]{1,0:T(8,128)(2,1)} %param.7), channel_id=1, replica_groups={{0,4,8,12,16,20,24,28,32,36,40,44,48,52,56,60},{1,5,9,13,17,21,25,29,33..., dimensions={0}, use_global_device_ids=true | all-gather | bytes 348160 | tf_op jit(solution)/shard_map/all_gather | solution.py:352
  37.4 3.4 %collective-permute-start = (bf16[128,1280]{1,0:T(8,128)(2,1)S(1)}, bf16[128,1280]{1,0:T(8,128)(2,1)S(1)}, u32[]{:S(2)}, u32[]{:S(2)}) collective-permute-start(bf16[128,1280]{1,0:T(8,128)(2,1)S(1)} %all_gather.3.own), channel_id=1, source_target_pairs={{0,128},{1,129},{2,130},{3,131},{4,132},{5,133},{6,134},{7,135},{8... | collective-permute-start | bytes 983048 | tf_op jit(solution)/shard_map/ppermute | solution.py:40
  40.8 3.0 %collective-permute-start.1 = (bf16[128,1280]{1,0:T(8,128)(2,1)S(1)}, bf16[128,1280]{1,0:T(8,128)(2,1)S(1)}, u32[]{:S(2)}, u32[]{:S(2)}) collective-permute-start(bf16[128,1280]{1,0:T(8,128)(2,1)S(1)} %all_gather.3.own), channel_id=1, source_target_pairs={{0,256},{1,257},{2,258},{3,259},{4,260},{5,261},{6,262},{7,263},{8... | collective-permute-start | bytes 983048 | tf_op jit(solution)/shard_map/ppermute | solution.py:40
  43.9 4.1 %collective-permute-start.2 = (bf16[128,1280]{1,0:T(8,128)(2,1)S(1)}, bf16[128,1280]{1,0:T(8,128)(2,1)}, u32[]{:S(2)}, u32[]{:S(2)}) collective-permute-start(bf16[128,1280]{1,0:T(8,128)(2,1)S(1)} %all_gather.3.own), channel_id=1, source_target_pairs={{0,384},{1,385},{2,386},{3,387},{4,388},{5,389},{6,390},{7,391},{8... | collective-permute-start | bytes 983048 | tf_op jit(solution)/shard_map/ppermute | solution.py:40
  48.1 1.2 copy-done
  49.3 0.6 shard_map.47
  49.9 1.5 %collective-permute-done.1.second = bf16[128,1280]{1,0:T(8,128)(2,1)S(1)} collective-permute-done((bf16[128,1280]{1,0:T(8,128)(2,1)S(1)}, bf16[128,1280]{1,0:T(8,128)(2,1)S(1)}, u32[]{:S(2)}, u32[]{:S(2)}) %collective-permute-start.1) | collective-permute-done | bytes 327712 | tf_op jit(solution)/shard_map/ppermute | solution.py:40
  51.4 0.7 copy-done.3
  52.1 17.1 %collective-permute-done.2.third = bf16[128,1280]{1,0:T(8,128)(2,1)} collective-permute-done((bf16[128,1280]{1,0:T(8,128)(2,1)S(1)}, bf16[128,1280]{1,0:T(8,128)(2,1)}, u32[]{:S(2)}, u32[]{:S(2)}) %collective-permute-start.2) | collective-permute-done | bytes 327712 | tf_op jit(solution)/shard_map/ppermute | solution.py:40
  69.3 1.2 shard_map.46.refs_0_
  70.4 1.9 %collective-permute-start.4 = (bf16[512,1280]{1,0:T(8,128)(2,1)S(1)}, bf16[512,1280]{1,0:T(8,128)(2,1)}, u32[]{:S(2)}, u32[]{:S(2)}) collective-permute-start(bf16[512,1280]{1,0:T(8,128)(2,1)S(1)} %shard_map.46.refs_0_), channel_id=1, source_target_pairs={{0,2},{1,3},{2,0},{3,1},{4,6},{5,7},{6,4},{7,5},{8,10},{9,11},{10,... | collective-permute-start | bytes 3932168 | tf_op jit(solution)/shard_map/ppermute | solution.py:40
  72.4 1.9 %collective-permute-start.5 = (bf16[512,1280]{1,0:T(8,128)(2,1)S(1)}, bf16[512,1280]{1,0:T(8,128)(2,1)}, u32[]{:S(2)}, u32[]{:S(2)}) collective-permute-start(bf16[512,1280]{1,0:T(8,128)(2,1)S(1)} %shard_map.46.refs_0_), channel_id=1, source_target_pairs={{0,1},{1,2},{2,3},{3,0},{4,5},{5,6},{6,7},{7,4},{8,9},{9,10},{10,1... | collective-permute-start | bytes 3932168 | tf_op jit(solution)/shard_map/ppermute | solution.py:40
  74.3 3.9 %collective-permute-start.6 = (bf16[512,1280]{1,0:T(8,128)(2,1)S(1)}, bf16[512,1280]{1,0:T(8,128)(2,1)}, u32[]{:S(2)}, u32[]{:S(2)}) collective-permute-start(bf16[512,1280]{1,0:T(8,128)(2,1)S(1)} %shard_map.46.refs_0_), channel_id=1, source_target_pairs={{0,3},{1,0},{2,1},{3,2},{4,7},{5,4},{6,5},{7,6},{8,11},{9,8},{10,9... | collective-permute-start | bytes 3932168 | tf_op jit(solution)/shard_map/ppermute | solution.py:40
  78.2 1.1 copy.8
  79.4 1.9 %collective-permute-start.3 = (bf16[128,2048]{1,0:T(8,128)(2,1)S(1)}, bf16[128,2048]{1,0:T(8,128)(2,1)S(1)}, u32[]{:S(2)}, u32[]{:S(2)}) collective-permute-start(bf16[128,2048]{1,0:T(8,128)(2,1)S(1)} %shard_map.47), channel_id=1, source_target_pairs={{0,64},{1,65},{2,66},{3,67},{4,68},{5,69},{6,70},{7,71},{8,72},{9,... | collective-permute-start | bytes 1572872 | tf_op jit(solution)/shard_map/ppermute | solution.py:44
  81.5 1.7 %collective-permute-done.3.theirs = bf16[128,2048]{1,0:T(8,128)(2,1)S(1)} collective-permute-done((bf16[128,2048]{1,0:T(8,128)(2,1)S(1)}, bf16[128,2048]{1,0:T(8,128)(2,1)S(1)}, u32[]{:S(2)}, u32[]{:S(2)}) %collective-permute-start.3) | collective-permute-done | bytes 524320 | tf_op jit(solution)/shard_map/ppermute | solution.py:44
  83.2 1.9 %shard_map.48.arranged = bf16[1024,512]{1,0:T(8,128)(2,1)S(1)} custom-call(s32[3]{0:T(128)S(1)} %pad_add_fusion.at, bf16[512,512]{1,0:T(8,128)(2,1)S(1)} %fusion.21.order, bf16[128,4096]{1,0:T(8,128)(2,1)S(1)} %bitcast.62, bf16[128,2048]{1,0:T(8,128)(2,1)S(1)} %collective-permute-done.3.theirs), custom_call_target="tpu_custom_call" | custom-call | flops 536870912 | bytes 4194304 | tf_op jit(solution)/shard_map/pallas_call | solution.py:103
  85.1 6.6 %collective-permute-done.4.refs_1_ = bf16[512,1280]{1,0:T(8,128)(2,1)} collective-permute-done((bf16[512,1280]{1,0:T(8,128)(2,1)S(1)}, bf16[512,1280]{1,0:T(8,128)(2,1)}, u32[]{:S(2)}, u32[]{:S(2)}) %collective-permute-start.4) | collective-permute-done | bytes 1310752 | tf_op jit(solution)/shard_map/ppermute | solution.py:40
  91.6 2.8 %shard_map.49 = (f32[128,1280]{1,0:T(8,128)S(1)}, f32[128,1280]{1,0:T(8,128)S(1)}, bf16[2048,1280]{1,0:T(8,128)(2,1)}) custom-call(bf16[1024,512]{1,0:T(8,128)(2,1)S(1)} %shard_map.48.arranged, bf16[512,1280]{1,0:T(8,128)(2,1)S(1)} %shard_map.46.refs_0_, bf16[512,1280]{1,0:T(8,128)(2,1)} %collective-permute-done.4.refs_1_), custom_call_target="tpu_custom_call" | custom-call | flops 671088640 | bytes 4194304 | tf_op jit(solution)/shard_map/pallas_call | solution.py:169
  94.5 11.1 %collective-permute-done.6.refs_1_ = bf16[512,1280]{1,0:T(8,128)(2,1)} collective-permute-done((bf16[512,1280]{1,0:T(8,128)(2,1)S(1)}, bf16[512,1280]{1,0:T(8,128)(2,1)}, u32[]{:S(2)}, u32[]{:S(2)}) %collective-permute-start.6) | collective-permute-done | bytes 1310752 | tf_op jit(solution)/shard_map/ppermute | solution.py:40
  105.6 3.5 %shard_map.50 = (f32[128,1280]{1,0:T(8,128)S(1)}, f32[128,1280]{1,0:T(8,128)S(1)}, bf16[2048,1280]{1,0:T(8,128)(2,1)}) custom-call(bf16[1024,512]{1,0:T(8,128)(2,1)S(1)} %shard_map.48.arranged, f32[128,1280]{1,0:T(8,128)S(1)} %get-tuple-element.24.mine, f32[128,1280]{1,0:T(8,128)S(1)} %get-tuple-element.25.theirs, ...), custom_call_target="tpu_custom_call", output_to_operand_aliasing={{2}: (5, {})} | custom-call | flops 671088640 | bytes 4194304 | tf_op jit(solution)/shard_map/pallas_call | solution.py:204
  109.1 1.9 %collective-permute-start.7 = (f32[128,1280]{1,0:T(8,128)S(1)}, f32[128,1280]{1,0:T(8,128)S(1)}, u32[]{:S(2)}, u32[]{:S(2)}) collective-permute-start(f32[128,1280]{1,0:T(8,128)S(1)} %get-tuple-element.28), channel_id=1, source_target_pairs={{0,64},{1,65},{2,66},{3,67},{4,68},{5,69},{6,70},{7,71},{8,72},{9,... | collective-permute-start | bytes 1966088 | tf_op jit(solution)/shard_map/ppermute | solution.py:44
  111.1 2.4 %collective-permute-start.12 = (bf16[2048,1280]{1,0:T(8,128)(2,1)}, bf16[2048,1280]{1,0:T(8,128)(2,1)}, u32[]{:S(2)}, u32[]{:S(2)}) collective-permute-start(bf16[2048,1280]{1,0:T(8,128)(2,1)} %get-tuple-element.31.all_rows), channel_id=1, source_target_pairs={{0,64},{1,65},{2,66},{3,67},{4,68},{5,69},{6,70},{7,71},{8,72},{9,... | collective-permute-start | bytes 15728648 | tf_op jit(solution)/shard_map/ppermute | solution.py:44
  113.9 0.3 fusion.37
  114.3 1.9 %collective-permute-start.8 = (bf16[128,256]{1,0:T(8,128)(2,1)S(1)}, bf16[128,256]{1,0:T(8,128)(2,1)S(1)}, u32[]{:S(2)}, u32[]{:S(2)}) collective-permute-start(bf16[128,256]{1,0:T(8,128)(2,1)S(1)} %pad_maximum_fusion.5), channel_id=1, source_target_pairs={{0,2},{1,3},{2,4},{3,5},{4,6},{5,7},{6,8},{7,9},{8,10},{9,11},{10,... | collective-permute-start | bytes 196616 | tf_op jit(solution)/shard_map/ppermute | solution.py:323
  116.3 0.2 fusion.57
  116.5 3.5 %shard_map.51.own_w = bf16[2048,256]{1,0:T(8,128)(2,1)} custom-call(s32[3]{0:T(128)S(1)} %pad_add_fusion.at, bf16[2048,1280]{1,0:T(8,128)(2,1)} %get-tuple-element.31.all_rows), custom_call_target="tpu_custom_call" | custom-call | flops 536870912 | bytes 3145728 | tf_op jit(solution)/shard_map/pallas_call | solution.py:287
  120.0 2.0 %collective-permute-done.8 = bf16[128,256]{1,0:T(8,128)(2,1)S(1)} collective-permute-done((bf16[128,256]{1,0:T(8,128)(2,1)S(1)}, bf16[128,256]{1,0:T(8,128)(2,1)S(1)}, u32[]{:S(2)}, u32[]{:S(2)}) %collective-permute-start.8) | collective-permute-done | bytes 65568 | tf_op jit(solution)/shard_map/ppermute | solution.py:323
  122.0 1.9 %collective-permute-start.9 = (bf16[256,256]{1,0:T(8,128)(2,1)S(1)}, bf16[256,256]{1,0:T(8,128)(2,1)S(1)}, u32[]{:S(2)}, u32[]{:S(2)}) collective-permute-start(bf16[256,256]{1,0:T(8,128)(2,1)S(1)} %pad_maximum_fusion.3), channel_id=1, source_target_pairs={{0,1},{1,2},{2,3},{3,4},{4,5},{5,6},{6,7},{7,8},{8,9},{9,10},{10,1... | collective-permute-start | bytes 393224 | tf_op jit(solution)/shard_map/ppermute | solution.py:323
  123.9 0.2 subtract_convert_fusion.1
  124.2 1.9 %collective-permute-start.13 = (bf16[2048,256]{1,0:T(8,128)(2,1)}, bf16[2048,256]{1,0:T(8,128)(2,1)}, u32[]{:S(2)}, u32[]{:S(2)}) collective-permute-start(bf16[2048,256]{1,0:T(8,128)(2,1)} %shard_map.51.own_w), channel_id=1, source_target_pairs={{0,64},{1,65},{2,66},{3,67},{4,68},{5,69},{6,70},{7,71},{8,72},{9,... | collective-permute-start | bytes 3145736 | tf_op jit(solution)/shard_map/ppermute | solution.py:44
  126.1 2.8 %collective-permute-done.9 = bf16[256,256]{1,0:T(8,128)(2,1)S(1)} collective-permute-done((bf16[256,256]{1,0:T(8,128)(2,1)S(1)}, bf16[256,256]{1,0:T(8,128)(2,1)S(1)}, u32[]{:S(2)}, u32[]{:S(2)}) %collective-permute-start.9) | collective-permute-done | bytes 131104 | tf_op jit(solution)/shard_map/ppermute | solution.py:323
  128.9 1.0 fusion.60
  130.0 0.2 fusion.23
  130.1 0.4 convolution_bitcast_fusion
  130.6 0.4 fusion.7
  131.0 0.4 fusion.2
  131.4 0.5 fusion.8
  132.0 1.9 %collective-permute-start.10 = (bf16[256,256]{1,0:T(8,128)(2,1)S(1)}, bf16[256,256]{1,0:T(8,128)(2,1)S(1)}, u32[]{:S(2)}, u32[]{:S(2)}) collective-permute-start(bf16[256,256]{1,0:T(8,128)(2,1)S(1)} %pad_maximum_fusion.4), channel_id=1, source_target_pairs={{1,0},{2,1},{3,2},{4,3},{5,4},{6,5},{7,6},{8,7},{9,8},{10,9},{11,1... | collective-permute-start | bytes 393224 | tf_op jit(solution)/shard_map/ppermute | solution.py:323
  133.9 0.6 fusion.4
  134.5 0.3 subtract_convert_fusion
  134.9 4.4 %shard_map.52.own_part = f32[128,2048]{1,0:T(8,128)S(1)} custom-call(s32[3]{0:T(128)S(1)} %pad_add_fusion.at, bf16[128,1024]{1,0:T(8,128)(2,1)S(1)} %copy_bitcast_fusion.grads, bf16[2048,1280]{1,0:T(8,128)(2,1)} %get-tuple-element.31.all_rows), custom_call_target="tpu_custom_call" | custom-call | flops 1073741824 | bytes 6291456 | tf_op jit(solution)/shard_map/pallas_call | solution.py:258
  139.3 1.7 %collective-permute-done.10 = bf16[256,256]{1,0:T(8,128)(2,1)S(1)} collective-permute-done((bf16[256,256]{1,0:T(8,128)(2,1)S(1)}, bf16[256,256]{1,0:T(8,128)(2,1)S(1)}, u32[]{:S(2)}, u32[]{:S(2)}) %collective-permute-start.10) | collective-permute-done | bytes 131104 | tf_op jit(solution)/shard_map/ppermute | solution.py:323
  141.0 2.2 %collective-permute-start.11 = (bf16[128,256]{1,0:T(8,128)(2,1)S(1)}, bf16[128,256]{1,0:T(8,128)(2,1)S(1)}, u32[]{:S(2)}, u32[]{:S(2)}) collective-permute-start(bf16[128,256]{1,0:T(8,128)(2,1)S(1)} %fusion.32), channel_id=1, source_target_pairs={{2,0},{3,1},{4,2},{5,3},{6,4},{7,5},{8,6},{9,7},{10,8},{11,9},{12,... | collective-permute-start | bytes 196616 | tf_op jit(solution)/shard_map/ppermute | solution.py:323
  143.3 4.4 %shard_map.53.other_part = f32[128,2048]{1,0:T(8,128)S(1)} custom-call(s32[3]{0:T(128)S(1)} %pad_add_fusion.at, bf16[128,1024]{1,0:T(8,128)(2,1)S(1)} %copy_bitcast_fusion.grads, bf16[2048,1280]{1,0:T(8,128)(2,1)} %collective-permute-done.12.all_rows), custom_call_target="tpu_custom_call" | custom-call | flops 1073741824 | bytes 6291456 | tf_op jit(solution)/shard_map/pallas_call | solution.py:258
  147.7 2.0 %collective-permute-done.11 = bf16[128,256]{1,0:T(8,128)(2,1)S(1)} collective-permute-done((bf16[128,256]{1,0:T(8,128)(2,1)S(1)}, bf16[128,256]{1,0:T(8,128)(2,1)S(1)}, u32[]{:S(2)}, u32[]{:S(2)}) %collective-permute-start.11) | collective-permute-done | bytes 65568 | tf_op jit(solution)/shard_map/ppermute | solution.py:323
  149.8 0.3 fusion.46
  150.2 3.0 %shard_map.54 = bf16[128,4096]{1,0:T(8,128)(2,1)} custom-call(s32[3]{0:T(128)S(1)} %pad_add_fusion.at, bf16[128,256]{1,0:T(8,128)(2,1)S(1)} %pad_maximum_fusion.6.pair_out, f32[128,2048]{1,0:T(8,128)S(1)} %shard_map.52.own_part, f32[128,2048]{1,0:T(8,128)S(1)} %shard_map.53.other_part, bf16[2048,256]{1,0:T(8,128)(2,1)S(1)} %copy-done.2, ...), custom_call_target="tpu_custom_call" | custom-call | tf_op jit(solution)/shard_map/pallas_call | solution.py:313
  (40 shorter events, 1.1 us)
Async XLA Ops:
  37.4 12.4 %collective-permute-start = (bf16[128,1280]{1,0:T(8,128)(2,1)S(1)}, bf16[128,1280]{1,0:T(8,128)(2,1)S(1)}, u32[]{:S(2)}, u32[]{:S(2)}) collective-permute-start(bf16[128,1280]{1,0:T(8,128)(2,1)S(1)} %all_gather.3.own), channel_id=1, source_target_pairs={{0,128},{1,129},{2,130},{3,131},{4,132},{5,133},{6,134},{7,135},{8... | collective-permute-start | bytes 983048 | tf_op jit(solution)/shard_map/ppermute | solution.py:40
  40.8 10.6 %collective-permute-start.1 = (bf16[128,1280]{1,0:T(8,128)(2,1)S(1)}, bf16[128,1280]{1,0:T(8,128)(2,1)S(1)}, u32[]{:S(2)}, u32[]{:S(2)}) collective-permute-start(bf16[128,1280]{1,0:T(8,128)(2,1)S(1)} %all_gather.3.own), channel_id=1, source_target_pairs={{0,256},{1,257},{2,258},{3,259},{4,260},{5,261},{6,262},{7,263},{8... | collective-permute-start | bytes 983048 | tf_op jit(solution)/shard_map/ppermute | solution.py:40
  43.9 25.4 %collective-permute-start.2 = (bf16[128,1280]{1,0:T(8,128)(2,1)S(1)}, bf16[128,1280]{1,0:T(8,128)(2,1)}, u32[]{:S(2)}, u32[]{:S(2)}) collective-permute-start(bf16[128,1280]{1,0:T(8,128)(2,1)S(1)} %all_gather.3.own), channel_id=1, source_target_pairs={{0,384},{1,385},{2,386},{3,387},{4,388},{5,389},{6,390},{7,391},{8... | collective-permute-start | bytes 983048 | tf_op jit(solution)/shard_map/ppermute | solution.py:40
  48.0 1.2 copy-start
  49.9 33.3 %copy-start.1 = (bf16[1,128,4096]{2,1,0:T(8,128)(2,1)S(1)}, bf16[1,128,4096]{2,1,0:T(8,128)(2,1)}, u32[]{:S(2)}) copy-start(bf16[1,128,4096]{2,1,0:T(8,128)(2,1)} %param.4) | copy-start | bytes 3145732
  51.4 0.7 copy-start.3
  70.4 21.2 %collective-permute-start.4 = (bf16[512,1280]{1,0:T(8,128)(2,1)S(1)}, bf16[512,1280]{1,0:T(8,128)(2,1)}, u32[]{:S(2)}, u32[]{:S(2)}) collective-permute-start(bf16[512,1280]{1,0:T(8,128)(2,1)S(1)} %shard_map.46.refs_0_), channel_id=1, source_target_pairs={{0,2},{1,3},{2,0},{3,1},{4,6},{5,7},{6,4},{7,5},{8,10},{9,11},{10,... | collective-permute-start | bytes 3932168 | tf_op jit(solution)/shard_map/ppermute | solution.py:40
  72.4 22.1 %collective-permute-start.5 = (bf16[512,1280]{1,0:T(8,128)(2,1)S(1)}, bf16[512,1280]{1,0:T(8,128)(2,1)}, u32[]{:S(2)}, u32[]{:S(2)}) collective-permute-start(bf16[512,1280]{1,0:T(8,128)(2,1)S(1)} %shard_map.46.refs_0_), channel_id=1, source_target_pairs={{0,1},{1,2},{2,3},{3,0},{4,5},{5,6},{6,7},{7,4},{8,9},{9,10},{10,1... | collective-permute-start | bytes 3932168 | tf_op jit(solution)/shard_map/ppermute | solution.py:40
  74.3 31.3 %collective-permute-start.6 = (bf16[512,1280]{1,0:T(8,128)(2,1)S(1)}, bf16[512,1280]{1,0:T(8,128)(2,1)}, u32[]{:S(2)}, u32[]{:S(2)}) collective-permute-start(bf16[512,1280]{1,0:T(8,128)(2,1)S(1)} %shard_map.46.refs_0_), channel_id=1, source_target_pairs={{0,3},{1,0},{2,1},{3,2},{4,7},{5,4},{6,5},{7,6},{8,11},{9,8},{10,9... | collective-permute-start | bytes 3932168 | tf_op jit(solution)/shard_map/ppermute | solution.py:40
  79.4 3.8 %collective-permute-start.3 = (bf16[128,2048]{1,0:T(8,128)(2,1)S(1)}, bf16[128,2048]{1,0:T(8,128)(2,1)S(1)}, u32[]{:S(2)}, u32[]{:S(2)}) collective-permute-start(bf16[128,2048]{1,0:T(8,128)(2,1)S(1)} %shard_map.47), channel_id=1, source_target_pairs={{0,64},{1,65},{2,66},{3,67},{4,68},{5,69},{6,70},{7,71},{8,72},{9,... | collective-permute-start | bytes 1572872 | tf_op jit(solution)/shard_map/ppermute | solution.py:44
  105.6 7.9 %copy-start.4 = (s32[1,128]{1,0:T(1,128)S(1)}, s32[1,128]{1,0:T(1,128)}, u32[]{:S(2)}) copy-start(s32[1,128]{1,0:T(1,128)} %param.5) | copy-start | bytes 1540
  109.1 4.5 %collective-permute-start.7 = (f32[128,1280]{1,0:T(8,128)S(1)}, f32[128,1280]{1,0:T(8,128)S(1)}, u32[]{:S(2)}, u32[]{:S(2)}) collective-permute-start(f32[128,1280]{1,0:T(8,128)S(1)} %get-tuple-element.28), channel_id=1, source_target_pairs={{0,64},{1,65},{2,66},{3,67},{4,68},{5,69},{6,70},{7,71},{8,72},{9,... | collective-permute-start | bytes 1966088 | tf_op jit(solution)/shard_map/ppermute | solution.py:44
  111.1 32.2 %collective-permute-start.12 = (bf16[2048,1280]{1,0:T(8,128)(2,1)}, bf16[2048,1280]{1,0:T(8,128)(2,1)}, u32[]{:S(2)}, u32[]{:S(2)}) collective-permute-start(bf16[2048,1280]{1,0:T(8,128)(2,1)} %get-tuple-element.31.all_rows), channel_id=1, source_target_pairs={{0,64},{1,65},{2,66},{3,67},{4,68},{5,69},{6,70},{7,71},{8,72},{9,... | collective-permute-start | bytes 15728648 | tf_op jit(solution)/shard_map/ppermute | solution.py:44
  114.3 7.7 %collective-permute-start.8 = (bf16[128,256]{1,0:T(8,128)(2,1)S(1)}, bf16[128,256]{1,0:T(8,128)(2,1)S(1)}, u32[]{:S(2)}, u32[]{:S(2)}) collective-permute-start(bf16[128,256]{1,0:T(8,128)(2,1)S(1)} %pad_maximum_fusion.5), channel_id=1, source_target_pairs={{0,2},{1,3},{2,4},{3,5},{4,6},{5,7},{6,8},{7,9},{8,10},{9,11},{10,... | collective-permute-start | bytes 196616 | tf_op jit(solution)/shard_map/ppermute | solution.py:323
  122.0 6.9 %collective-permute-start.9 = (bf16[256,256]{1,0:T(8,128)(2,1)S(1)}, bf16[256,256]{1,0:T(8,128)(2,1)S(1)}, u32[]{:S(2)}, u32[]{:S(2)}) collective-permute-start(bf16[256,256]{1,0:T(8,128)(2,1)S(1)} %pad_maximum_fusion.3), channel_id=1, source_target_pairs={{0,1},{1,2},{2,3},{3,4},{4,5},{5,6},{6,7},{7,8},{8,9},{9,10},{10,1... | collective-permute-start | bytes 393224 | tf_op jit(solution)/shard_map/ppermute | solution.py:323
  124.2 25.6 %collective-permute-start.13 = (bf16[2048,256]{1,0:T(8,128)(2,1)}, bf16[2048,256]{1,0:T(8,128)(2,1)}, u32[]{:S(2)}, u32[]{:S(2)}) collective-permute-start(bf16[2048,256]{1,0:T(8,128)(2,1)} %shard_map.51.own_w), channel_id=1, source_target_pairs={{0,64},{1,65},{2,66},{3,67},{4,68},{5,69},{6,70},{7,71},{8,72},{9,... | collective-permute-start | bytes 3145736 | tf_op jit(solution)/shard_map/ppermute | solution.py:44
  132.0 9.0 %collective-permute-start.10 = (bf16[256,256]{1,0:T(8,128)(2,1)S(1)}, bf16[256,256]{1,0:T(8,128)(2,1)S(1)}, u32[]{:S(2)}, u32[]{:S(2)}) collective-permute-start(bf16[256,256]{1,0:T(8,128)(2,1)S(1)} %pad_maximum_fusion.4), channel_id=1, source_target_pairs={{1,0},{2,1},{3,2},{4,3},{5,4},{6,5},{7,6},{8,7},{9,8},{10,9},{11,1... | collective-permute-start | bytes 393224 | tf_op jit(solution)/shard_map/ppermute | solution.py:323
  141.0 9.2 %copy-start.2 = (bf16[2048,256]{1,0:T(8,128)(2,1)S(1)}, bf16[2048,256]{1,0:T(8,128)(2,1)}, u32[]{:S(2)}) copy-start(bf16[2048,256]{1,0:T(8,128)(2,1)} %shard_map.51.own_w) | copy-start | bytes 3145732
  141.0 8.7 %collective-permute-start.11 = (bf16[128,256]{1,0:T(8,128)(2,1)S(1)}, bf16[128,256]{1,0:T(8,128)(2,1)S(1)}, u32[]{:S(2)}, u32[]{:S(2)}) collective-permute-start(bf16[128,256]{1,0:T(8,128)(2,1)S(1)} %fusion.32), channel_id=1, source_target_pairs={{2,0},{3,1},{4,2},{5,3},{6,4},{7,5},{8,6},{9,7},{10,8},{11,9},{12,... | collective-permute-start | bytes 196616 | tf_op jit(solution)/shard_map/ppermute | solution.py:323
